TPU v7x, 32 devices: a whole 2x2x4 slice. The times are simulated.
32 devices in a mesh: wide: 8 (over y, x, core), narrow: 4 (over z).
Axes of the slice: x: 2, y: 2, z: 4, core: 2. Of those that a mesh axis runs over, the one named last changes fastest.
Arguments:
- volumes: bfloat16 [4, 1, 4, 32, 4096], P('narrow', None, None, 'wide'), may hold values from -6 to 6
- first_kernel: bfloat16 [27, 32, 4], replicated, may hold values from -0.625 to 0.625
- second_kernel: bfloat16 [27, 64, 32], replicated, may hold values from -0.21875 to 0.21875
- cotangent: bfloat16 [4, 1, 64, 16384], P('narrow', None, None, 'wide'), may hold values from -6 to 6
Outputs:
- activations: bfloat16 [4, 1, 64, 16384], P('narrow', None, None, 'wide')
- weight_grad: float32 [27, 64, 32], P(None, 'narrow')
All inputs are finite; a program needn't handle non-finite values.
Results may differ from a plain program's by a relative error of at most 0.023.
The roundings to bfloat16 on the way count: a program that leaves them out, or rounds other values in their place, can miss the bound.
Values may be sent and summed in bfloat16 or wider, within the bound.
No kernel may reach another device: no remote copies, remote signals or barrier semaphores. Data moves between devices by JAX's collectives and lax.ppermute only.
A program may use at most 64 MiB of HBM per device.

v0:
```python
import math

import jax
import jax.numpy as jnp
from jax import lax
from jax.sharding import PartitionSpec as P

CIN = 4
YCELLS = 64
XCELLS = 64


neg_slope = 0.3


def passed_along(block, axis, distance):
    devices = range(lax.axis_size(axis))
    route = [(i - distance, i) for i in devices if i - distance in devices]
    return lax.ppermute(block, axis, route)


def with_halo(x, sides, width):
    for axis, dim in sides:
        size, length = (lax.axis_size(axis), x.shape[dim])
        up = [(i, (i + 1) % size) for i in range(size - 1)]
        down = [(j, i) for i, j in up]
        last = lax.slice_in_dim(x, length - width, length, axis=dim)
        first = lax.slice_in_dim(x, 0, width, axis=dim)
        before = lax.ppermute(last, axis, up)
        after = lax.ppermute(first, axis, down)
        x = jnp.concatenate([before, x, after], axis=dim)
    return x


def leaky_relu(value):
    return jnp.where(value > 0, value, neg_slope * value)


def edge_masks():
    half_x = XCELLS // 2
    plane = YCELLS // 2 * half_x
    column = jnp.arange(plane, dtype=jnp.int32) % half_x
    left_ok = jnp.where(column > 0, 1.0, 0.0).astype(jnp.bfloat16)
    right_ok = jnp.where(column < half_x - 1, 1.0, 0.0).astype(jnp.bfloat16)
    return (left_ok, right_ok)


def conv_first(stacked, out_depth, first_kernel):
    batch = stacked.shape[0]
    depth_in = stacked.shape[2]
    half_y = YCELLS // 2
    half_x = XCELLS // 2
    plane = half_y * half_x
    margin = half_x + 1
    left_ok, right_ok = edge_masks()
    grid = stacked.reshape(batch, CIN, depth_in, half_y, 2, half_x, 2)
    parity = grid.transpose(0, 1, 2, 4, 6, 3, 5).reshape(batch, CIN, depth_in, 2, 2, plane)
    flat = jnp.pad(parity, ((0, 0), (0, 0), (0, 0), (0, 0), (0, 0), (margin, 0)))
    pieces = []
    for shift_z in range(3):
        chosen = flat[:, :, shift_z : shift_z + 2 * out_depth - 1 : 2]
        for shift_y in range(3):
            row_par = 0 if shift_y == 1 else 1
            row_off = -1 if shift_y == 0 else 0
            for shift_x in range(3):
                col_par = 0 if shift_x == 1 else 1
                col_off = -1 if shift_x == 0 else 0
                begin = margin + row_off * half_x + col_off
                part = chosen[:, :, :, row_par, col_par, begin : begin + plane]
                if col_off == -1:
                    part = part * left_ok
                pieces.append(part)
    taps = jnp.stack(pieces, axis=1).reshape(batch, 27, CIN, out_depth * plane)
    total = jnp.einsum("toc,btcp->bop", first_kernel, taps, preferred_element_type=jnp.float32)
    first_act = leaky_relu(total).astype(jnp.bfloat16)
    return first_act.reshape(batch, first_kernel.shape[1], out_depth, plane)


def depth_taps(flat, shift_z, depth_out):
    half_x = XCELLS // 2
    plane = YCELLS // 2 * half_x
    margin = half_x + 1
    left_ok, right_ok = edge_masks()
    chosen = flat[:, :, shift_z : shift_z + depth_out]
    pieces = []
    for shift_y in range(3):
        for shift_x in range(3):
            begin = margin + (shift_y - 1) * half_x + (shift_x - 1)
            part = chosen[:, :, :, begin : begin + plane]
            if shift_x == 0:
                part = part * left_ok
            if shift_x == 2:
                part = part * right_ok
            pieces.append(part)
    stacked = jnp.stack(pieces, axis=1)
    return stacked.reshape(stacked.shape[0], 9, stacked.shape[2], depth_out * plane)


def body(volumes, first_kernel, second_kernel, cotangent):
    local = volumes[0]
    batch = local.shape[0]
    planes = local.shape[2]
    depth_out = planes // 2
    lower_plane = passed_along(local[:, :, planes - 1 :], "wide", 1)
    stacked = jnp.concatenate([lower_plane, local], axis=2)
    first_act = conv_first(stacked, depth_out, first_kernel)
    rimmed = with_halo(first_act, (("wide", 2),), 1)
    margin = XCELLS // 2 + 1
    flat = jnp.pad(rimmed, ((0, 0), (0, 0), (0, 0), (margin, margin)))
    cells_out = depth_out * (YCELLS // 2) * (XCELLS // 2)
    pre = jnp.zeros((batch, second_kernel.shape[1], cells_out), jnp.float32)
    for shift_z in range(3):
        taps = depth_taps(flat, shift_z, depth_out)
        pre = pre + jnp.einsum(
            "toc,btcp->bop",
            second_kernel[9 * shift_z : 9 * shift_z + 9],
            taps,
            preferred_element_type=jnp.float32,
        )
    output = leaky_relu(pre).astype(jnp.bfloat16)
    back = (cotangent[0].astype(jnp.float32) * jnp.where(pre > 0, 1.0, neg_slope)).astype(
        jnp.bfloat16
    )
    terms = []
    for shift_z in range(3):
        taps = depth_taps(flat, shift_z, depth_out)
        terms.append(jnp.einsum("bop,btcp->toc", back, taps, preferred_element_type=jnp.float32))
    count = lax.axis_size("wide") * lax.axis_size("narrow") * batch * cells_out
    local_term = jnp.concatenate(terms, axis=0) * (1.0 / math.sqrt(count))
    partial_rows = lax.psum_scatter(
        local_term.astype(jnp.bfloat16), "narrow", scatter_dimension=1, tiled=True
    ).astype(jnp.float32)
    weight_grad = lax.psum(partial_rows, "wide")
    return (output.reshape(1, batch, output.shape[1], cells_out), weight_grad)


def solution(mesh):
    return jax.shard_map(
        body,
        mesh=mesh,
        in_specs=(P("narrow", None, None, "wide", None), P(), P(), P("narrow", None, None, "wide")),
        out_specs=(P("narrow", None, None, "wide"), P(None, "narrow", None)),
        check_vma=False,
    )
```

profile of v0, /device:TPU:0, one launch (start us, length us, event | category | flops | bytes accessed | tf_op | source)
XLA Modules:
  0.0 152.0 jit_solution(7802893537868011982)
XLA Ops:
  7.2 1.0 slice.314
  8.2 2.4 %collective-permute-start = (bf16[1,4,1,4096]{3,2,1,0:T(2,128)(2,1)S(1)}, bf16[1,4,1,4096]{3,2,1,0:T(2,128)(2,1)S(1)}, u32[]{:S(2)}, u32[]{:S(2)}) collective-permute-start(bf16[1,4,1,4096]{3,2,1,0:T(2,128)(2,1)S(1)} %slice.314), channel_id=1, source_target_pairs={{0,4},{4,8},{8,12},{12,16},{16,20},{20,24},{24,28},{1,5},{5,9},{9,... | collective-permute-start | bytes 98312 | tf_op jit(solution)/shard_map/ppermute | solution.py:19
  10.6 4.0 %copy.44 = bf16[1,1,4,4,4096]{3,4,2,1,0:T(8,128)(2,1)} copy(bf16[1,1,4,4,4096]{4,3,2,1,0:T(4,128)(2,1)} %param.4) | data formatting | bytes 262144 | tf_op args[0]
  14.6 10.7 %copy.46 = bf16[1,4,4,32,2,32,2]{5,3,6,4,2,1,0:T(8,128)(2,1)S(1)} copy(bf16[1,4,4,32,2,32,2]{2,6,5,4,3,1,0:T(2,128)(2,1)} %bitcast.117) | data formatting | bytes 262144 | tf_op jit(solution)/shard_map/concatenate | solution.py:105
  25.9 1.4 copy.45
  29.8 1.3 stack.186
  31.6 4.5 %collective-permute-start.1 = (bf16[1,32,1,1024]{3,2,1,0:T(2,128)(2,1)S(1)}, bf16[1,32,1,1024]{3,2,1,0:T(2,128)(2,1)S(1)}, u32[]{:S(2)}, u32[]{:S(2)}) collective-permute-start(bf16[1,32,1,1024]{3,2,1,0:T(2,128)(2,1)S(1)} %get-tuple-element.39), channel_id=1, source_target_pairs={{0,4},{4,8},{8,12},{12,16},{16,20},{20,24},{24,28},{1,5},{5,9},{9,... | collective-permute-start | bytes 196616 | tf_op jit(solution)/shard_map/ppermute | solution.py:29
  36.1 1.5 collective-permute-start.2
  37.6 1.7 %collective-permute-done.2 = bf16[1,32,1,1024]{3,2,1,0:T(2,128)(2,1)S(1)} collective-permute-done((bf16[1,32,1,1024]{3,2,1,0:T(2,128)(2,1)S(1)}, bf16[1,32,1,1024]{3,2,1,0:T(2,128)(2,1)S(1)}, u32[]{:S(2)}, u32[]{:S(2)}) %collective-permute-start.2) | collective-permute-done | bytes 65568 | tf_op jit(solution)/shard_map/ppermute | solution.py:30
  39.4 1.0 select_maximum_fusion
  40.4 2.5 %slice_multiply_fusion.13 = (bf16[1,32,2,1024]{3,2,1,0:T(2,128)(2,1)}, bf16[1,32,2,1024]{3,2,1,0:T(2,128)(2,1)}, bf16[1,32,2,1024]{3,2,1,0:T(2,128)(2,1)}, bf16[...) fusion(bf16[1,32,4,1090]{3,2,1,0:T(4,128)(2,1)S(1)} %select_max, ...), kind=kLoop, calls=%fused_computation.51 | loop fusion | flops 589824 | bytes 2361344 | tf_op jit(solution)/shard_map/mul | solution.py:91
  43.0 3.3 %slice_multiply_fusion.12 = (bf16[1,32,2,1024]{3,2,1,0:T(2,128)(2,1)S(1)}, bf16[1,32,2,1024]{3,2,1,0:T(2,128)(2,1)S(1)}, bf16[1,32,2,1024]{3,2,1,0:T(2,128)(2,1)...) fusion(bf16[1,32,4,1090]{3,2,1,0:T(4,128)(2,1)S(1)} %select_max, ...), kind=kLoop, calls=%fused_computation.50 | loop fusion | flops 589824 | bytes 3934208 | tf_op jit(solution)/shard_map/mul | solution.py:93
  46.4 0.7 stack.188
  47.8 1.7 %stack.190 = bf16[1,1,32,2048]{3,2,1,0:T(8,128)(2,1)} reshape(bf16[1,32,2,1024]{3,2,1,0:T(2,128)(2,1)} %get-tuple-element.26) | data formatting | bytes 262144 | tf_op jit(solution)/shard_map/stack | solution.py:95
  49.5 2.1 %pad_maximum_fusion.1 = (bf16[1,32,2,1024]{3,2,1,0:T(2,128)(2,1)S(1)}, bf16[1,32,2,1024]{3,2,1,0:T(2,128)(2,1)}) fusion(bf16[1,32,2,1024]{3,2,1,0:T(2,128)(2,1)S(1)} %reshape.486, bf16[1,32,1,1024]{3,2,1,0:T(2,128)(2,1)S(1)} %collective-permute-done.1, bf16[1,32,1,1024]{3,2,1,0:T(2,128)(2,1)} %copy-done.11), kind=kLoop, calls=%fused_computation.53 | loop fusion | flops 524288 | bytes 524288 | tf_op jit(solution)/shard_map/concatenate | solution.py:31
  51.6 0.7 stack.191
  52.4 0.7 stack.192
  53.1 1.6 %stack.193 = bf16[1,1,32,2048]{3,2,1,0:T(8,128)(2,1)} reshape(bf16[1,32,2,1024]{3,2,1,0:T(2,128)(2,1)} %get-tuple-element.19) | data formatting | bytes 262144 | tf_op jit(solution)/shard_map/stack | solution.py:95
  56.2 0.7 stack.197
  56.9 0.9 constant_dynamic-update-slice_fusion.16
  57.8 1.6 %stack.198 = bf16[1,1,32,2048]{3,2,1,0:T(8,128)(2,1)} reshape(bf16[1,32,2,1024]{3,2,1,0:T(2,128)(2,1)} %get-tuple-element.31) | data formatting | bytes 262144 | tf_op jit(solution)/shard_map/stack | solution.py:95
  59.5 1.6 %stack.199 = bf16[1,1,32,2048]{3,2,1,0:T(8,128)(2,1)} reshape(bf16[1,32,2,1024]{3,2,1,0:T(2,128)(2,1)} %get-tuple-element.15) | data formatting | bytes 262144 | tf_op jit(solution)/shard_map/stack | solution.py:95
  61.1 1.6 %stack.200 = bf16[1,1,32,2048]{3,2,1,0:T(8,128)(2,1)} reshape(bf16[1,32,2,1024]{3,2,1,0:T(2,128)(2,1)} %get-tuple-element.24) | data formatting | bytes 262144 | tf_op jit(solution)/shard_map/stack | solution.py:95
  62.7 0.9 constant_dynamic-update-slice_fusion.15
  63.6 0.9 constant_dynamic-update-slice_fusion.14
  64.5 0.9 constant_dynamic-update-slice_fusion.13
  65.5 1.8 %stack.202 = bf16[1,1,32,2048]{3,2,1,0:T(8,128)(2,1)} reshape(bf16[1,32,2,1024]{3,2,1,0:T(2,128)(2,1)} %get-tuple-element.14) | data formatting | bytes 262144 | tf_op jit(solution)/shard_map/stack | solution.py:95
  67.3 1.6 %stack.203 = bf16[1,1,32,2048]{3,2,1,0:T(8,128)(2,1)} reshape(bf16[1,32,2,1024]{3,2,1,0:T(2,128)(2,1)} %get-tuple-element.23) | data formatting | bytes 262144 | tf_op jit(solution)/shard_map/stack | solution.py:95
  68.9 0.7 stack.204
  69.6 0.7 stack.205
  70.3 1.0 stack.211
  71.3 1.6 %stack.207 = bf16[1,1,32,2048]{3,2,1,0:T(8,128)(2,1)} reshape(bf16[1,32,2,1024]{3,2,1,0:T(2,128)(2,1)} %get-tuple-element.22) | data formatting | bytes 262144 | tf_op jit(solution)/shard_map/stack | solution.py:95
  73.0 0.9 constant_dynamic-update-slice_fusion.25
  73.9 0.7 stack.208
  74.6 0.7 stack.209
  75.3 1.6 %stack.210 = bf16[1,1,32,2048]{3,2,1,0:T(8,128)(2,1)} reshape(bf16[1,32,2,1024]{3,2,1,0:T(2,128)(2,1)} %get-tuple-element.21) | data formatting | bytes 262144 | tf_op jit(solution)/shard_map/stack | solution.py:95
  77.1 1.0 stack.213
  78.2 1.6 %constant_dynamic-update-slice_fusion.12 = bf16[1,9,32,2048]{3,2,1,0:T(8,128)(2,1)} fusion(bf16[1,9,32,2048]{3,2,1,0:T(8,128)(2,1)} %copy-done.1, bf16[1,1,32,2048]{3,2,1,0:T(8,128)(2,1)} %stack.202), kind=kLoop, calls=%fused_computation.73 | loop fusion | bytes 262144
  79.8 1.6 %constant_dynamic-update-slice_fusion.11 = bf16[1,9,32,2048]{3,2,1,0:T(8,128)(2,1)} fusion(bf16[1,9,32,2048]{3,2,1,0:T(8,128)(2,1)} %constant_dynamic-update-slice_fusion.12, bf16[1,1,32,2048]{3,2,1,0:T(8,128)(2,1)} %stack.203), kind=kLoop, calls=%fused_computation.72 | loop fusion | bytes 262144
  81.3 1.6 %constant_dynamic-update-slice_fusion.10 = bf16[1,9,32,2048]{3,2,1,0:T(8,128)(2,1)} fusion(bf16[1,9,32,2048]{3,2,1,0:T(8,128)(2,1)} %constant_dynamic-update-slice_fusion.11, bf16[1,1,32,2048]{3,2,1,0:T(8,128)(2,1)} %stack.204), kind=kLoop, calls=%fused_computation.71 | loop fusion | bytes 262144
  83.6 1.7 %convolution_bitcast_fusion.1 = f32[2048,64]{0,1:T(8,128)S(1)} fusion(bf16[1,9,32,2048]{3,2,1,0:T(8,128)(2,1)} %constant_dynamic-update-slice_fusion.9, bf16[27,64,32]{1,2,0:T(8,128)(2,1)} %param.6), kind=kOutput, calls=%fused_computation.1 | convolution fusion | flops 75497472 | bytes 1777664 | tf_op jit(solution)/shard_map/toc,btcp->bop/dot_general | solution.py:114
  85.5 0.7 copy-done.18
  87.8 1.2 fusion.33
  89.5 0.8 copy-done.2
  91.3 1.5 %copy.75 = bf16[27,64,32]{2,0,1:T(8,128)(2,1)} copy(bf16[27,64,32]{1,2,0:T(8,128)(2,1)S(1)} %fusion.26) | data formatting | bytes 221184 | tf_op jit(solution)/shard_map/convert_element_type | solution.py:131
  92.8 25.7 %reduce-scatter.2.cloned.1.call-done = bf16[27,16,32]{2,0,1:T(8,128)(2,1)} async-done(((bf16[27,64,32]{2,0,1:T(8,128)(2,1)}), bf16[27,16,32]{2,0,1:T(8,128)(2,1)}) %reduce-scatter.2.cloned.1.call-update) | async-done | bytes 27664 | tf_op jit(solution)/shard_map/reduce_scatter | solution.py:130
  118.6 25.8 %psum.7 = f32[27,16,32]{2,0,1:T(8,128)S(1)} all-reduce(bf16[27,16,32]{2,0,1:T(8,128)(2,1)} %reduce-scatter.2.cloned.1.call-done), channel_id=1, replica_groups=mesh['wide'=8,'narrow'=4] {'wide'}, use_global_device_ids=true, to_apply=%region_1.2 | all-reduce | flops 13824 | bytes 82944 | tf_op jit(solution)/shard_map/psum | solution.py:133
  144.4 0.8 copy.76
  (85 shorter events, 9.8 us)
Async XLA Ops:
  7.2 23.9 %copy-start = (bf16[27,32,4]{1,2,0:T(4,128)(2,1)S(1)}, bf16[27,32,4]{1,2,0:T(4,128)(2,1)}, u32[]{:S(2)}) copy-start(bf16[27,32,4]{1,2,0:T(4,128)(2,1)} %param.5) | copy-start | bytes 20740
  7.2 111.4 %reduce-scatter.2.cloned.1.call-start = ((), (), s32[]{:S(2)}) async-start(), calls=%async_computation.1 | async-start | bytes 655360 | tf_op jit(solution)/shard_map/reduce_scatter | solution.py:130
  8.2 17.1 %collective-permute-start = (bf16[1,4,1,4096]{3,2,1,0:T(2,128)(2,1)S(1)}, bf16[1,4,1,4096]{3,2,1,0:T(2,128)(2,1)S(1)}, u32[]{:S(2)}, u32[]{:S(2)}) collective-permute-start(bf16[1,4,1,4096]{3,2,1,0:T(2,128)(2,1)S(1)} %slice.314), channel_id=1, source_target_pairs={{0,4},{4,8},{8,12},{12,16},{16,20},{20,24},{24,28},{1,5},{5,9},{9,... | collective-permute-start | bytes 98312 | tf_op jit(solution)/shard_map/ppermute | solution.py:19
  31.6 6.0 %collective-permute-start.1 = (bf16[1,32,1,1024]{3,2,1,0:T(2,128)(2,1)S(1)}, bf16[1,32,1,1024]{3,2,1,0:T(2,128)(2,1)S(1)}, u32[]{:S(2)}, u32[]{:S(2)}) collective-permute-start(bf16[1,32,1,1024]{3,2,1,0:T(2,128)(2,1)S(1)} %get-tuple-element.39), channel_id=1, source_target_pairs={{0,4},{4,8},{8,12},{12,16},{16,20},{20,24},{24,28},{1,5},{5,9},{9,... | collective-permute-start | bytes 196616 | tf_op jit(solution)/shard_map/ppermute | solution.py:29
  36.1 3.2 %collective-permute-start.2 = (bf16[1,32,1,1024]{3,2,1,0:T(2,128)(2,1)S(1)}, bf16[1,32,1,1024]{3,2,1,0:T(2,128)(2,1)S(1)}, u32[]{:S(2)}, u32[]{:S(2)}) collective-permute-start(bf16[1,32,1,1024]{3,2,1,0:T(2,128)(2,1)S(1)} %get-tuple-element.40), channel_id=1, source_target_pairs={{4,0},{8,4},{12,8},{16,12},{20,16},{24,20},{28,24},{5,1},{9,5},{13... | collective-permute-start | bytes 196616 | tf_op jit(solution)/shard_map/ppermute | solution.py:30
  39.4 3.5 %copy-start.11 = (bf16[1,32,1,1024]{3,2,1,0:T(2,128)(2,1)}, bf16[1,32,1,1024]{3,2,1,0:T(2,128)(2,1)S(1)}, u32[]{:S(2)}) copy-start(bf16[1,32,1,1024]{3,2,1,0:T(2,128)(2,1)S(1)} %collective-permute-done.2) | copy-start | bytes 196612
  47.8 8.3 %copy-start.16 = (bf16[1,32,2,1024]{3,2,1,0:T(2,128)(2,1)S(1)}, bf16[1,32,2,1024]{3,2,1,0:T(2,128)(2,1)}, u32[]{:S(2)}) copy-start(bf16[1,32,2,1024]{3,2,1,0:T(2,128)(2,1)} %get-tuple-element.25) | copy-start | bytes 393220
  65.5 5.9 %copy-start.1 = (bf16[1,9,32,2048]{3,2,1,0:T(8,128)(2,1)}, bf16[1,9,32,2048]{3,2,1,0:T(8,128)(2,1)S(1)}, u32[]{:S(2)}) copy-start(bf16[1,9,32,2048]{3,2,1,0:T(8,128)(2,1)S(1)} %bitcast_dynamic-update-slice_fusion) | copy-start | bytes 3538948
  74.6 8.3 %copy-start.12 = (bf16[1,1,32,2048]{3,2,1,0:T(8,128)(2,1)S(1)}, bf16[1,1,32,2048]{3,2,1,0:T(8,128)(2,1)}, u32[]{:S(2)}) copy-start(bf16[1,1,32,2048]{3,2,1,0:T(8,128)(2,1)} %stack.205) | copy-start | bytes 393220
  81.3 4.0 %copy-start.14 = (bf16[1,1,32,2048]{3,2,1,0:T(8,128)(2,1)S(1)}, bf16[1,1,32,2048]{3,2,1,0:T(8,128)(2,1)}, u32[]{:S(2)}) copy-start(bf16[1,1,32,2048]{3,2,1,0:T(8,128)(2,1)} %stack.208) | copy-start | bytes 393220
  82.9 2.4 %copy-start.15 = (bf16[1,1,32,2048]{3,2,1,0:T(8,128)(2,1)S(1)}, bf16[1,1,32,2048]{3,2,1,0:T(8,128)(2,1)}, u32[]{:S(2)}) copy-start(bf16[1,1,32,2048]{3,2,1,0:T(8,128)(2,1)} %stack.209) | copy-start | bytes 393220
  83.6 1.8 %copy-start.13 = (bf16[1,1,32,2048]{3,2,1,0:T(8,128)(2,1)S(1)}, bf16[1,1,32,2048]{3,2,1,0:T(8,128)(2,1)}, u32[]{:S(2)}) copy-start(bf16[1,1,32,2048]{3,2,1,0:T(8,128)(2,1)} %stack.210) | copy-start | bytes 393220
  85.3 0.9 copy-start.18
  85.5 1.2 copy-start.4
  85.5 1.3 copy-start.5
  86.3 0.9 copy-start.3
  86.3 1.0 copy-start.10
  86.3 1.1 copy-start.9
  86.3 1.1 copy-start.8
  86.7 1.0 copy-start.7
  86.7 1.0 copy-start.6
  86.7 1.1 copy-start.17
  89.0 1.3 copy-start.2
Sparse Core Ops, SparseCore 0:
  93.0 25.5 reduce-scatter.1
where the time goes:
time: 153 us; the launch traced here: 152 us
  local copies, waits for them, and re-layouts  61.3 us (40%)
  waiting for transfers between devices  27.5 us (18%)
  blocking collectives  25.8 us (17%)
  between operations  14.5 us (9%)
  other arithmetic  9.54 us (6%)
  starting transfers between devices  8.38 us (5%)
  matrix products  4.98 us (3%)
    psum x1, blocking collectives, body(): weight_grad = lax.psum(partial_rows, 'wide')  25.8 us
    another operation x29, local copies, waits for them, and re-layouts, depth_taps(): stacked = jnp.stack(pieces, axis=1)  25.8 us
    reduce_scatter x1, waiting for transfers between devices, body(): lax.psum_scatter(local_term.astype(jnp.bfloat16), 'narrow', scatter_dimen...  25.7 us
    unnamed x66, local copies, waits for them, and re-layouts  16.9 us
    concatenate x2, local copies, waits for them, and re-layouts, body(): stacked = jnp.concatenate([lower_plane, local], axis=2)  12 us
    ppermute x1, starting transfers between devices, with_halo(): before = lax.ppermute(last, axis, up)  4.51 us
    dot_general x3, matrix products, body(): jnp.einsum('toc,btcp->bop', second_kernel[9 * shift_z:9 * shift_z + 9], t...  3.36 us
    mul x1, other arithmetic, depth_taps(): part = part * right_ok  3.35 us
  transfers between devices with their start and end apart: 4, of which 2 were waited for; matrix products, arithmetic and copies ran while one was open for 10% of the time, Pallas kernels for 0%

commit v1 on v0

v1 whole, which is shorter than its diff:
```python
import functools
import math

import jax
import jax.numpy as jnp
import numpy as np
from jax import lax
from jax.experimental import pallas as pl
from jax.experimental.pallas import tpu as pltpu
from jax.sharding import PartitionSpec as P

CIN = 4
C1 = 32
C2 = 64
PLANES = 4
CELLS = 4096
HALF = 32
PLANE = 1024
LANES = 128
ROWS = 3 * CIN * PLANES
WINDOW = 640
PACKED = 7 * LANES
neg_slope = 0.3


def selection():
    table = np.zeros((WINDOW, 9, LANES), np.float32)
    for b in range(3):
        for c in range(3):
            for lane in range(LANES):
                row, col = divmod(lane, HALF)
                x = 2 * col + c - 1
                if x >= 0:
                    table[(2 * row + b + 1) * 64 + x, 3 * b + c, lane] = 1
    return table.reshape(WINDOW, 9 * LANES)


def placement():
    table = np.zeros((27, CIN, 4, 512), np.float32)
    for a in range(3):
        for bc in range(9):
            for i in range(CIN):
                for q in range(4):
                    src, zp = divmod(2 * q + a + 1, PLANES)
                    table[9 * a + bc, i, q, bc * ROWS + src * 16 + i * PLANES + zp] = 1
    return table.reshape(27 * CIN, 4 * 512)


def leaky_relu(value):
    return jnp.where(value > 0, value, neg_slope * value)


def slots():
    where = {}
    free = [(tile, 3) for tile in range(6)]
    for bc in range(9):
        for a in range(3):
            where[9 * a + bc] = (bc, a) if bc < 7 else free.pop(0)
    return where


def prepare_kernel(k1_ref, place_ref, k2_ref, w1_ref, w2_ref):
    spread = jnp.dot(k1_ref[...], place_ref[...], preferred_element_type=jnp.float32)
    for q in range(4):
        w1_ref[q * C1 : (q + 1) * C1, :] = spread[:, 512 * q : 512 * q + 9 * ROWS].astype(jnp.bfloat16)
    blank = jnp.zeros((C2, C1), jnp.bfloat16)
    for bc in range(9):
        taps = [k2_ref[9 * a + bc] for a in range(3)]
        here = slice(bc * LANES, (bc + 1) * LANES)
        w2_ref[0:C2, here] = jnp.concatenate(taps + [blank], axis=1)
        w2_ref[C2 : 2 * C2, here] = jnp.concatenate([blank] + taps, axis=1)


def main_kernel(
    wide, scale, before_ref, own_ref, after_ref, select_ref, w1_ref, w2_ref, cot_ref,
    out_ref, grad_ref, x_ref, window_ref, taps_ref, act_ref, shifted_ref, back_ref,
):
    for s, ref in enumerate((before_ref, own_ref, after_ref)):
        for i in range(CIN):
            row = 16 * s + PLANES * i
            x_ref[row : row + PLANES, :] = ref[0, 0, i].astype(jnp.float32)
    window_ref[0:ROWS, 0:LANES] = jnp.zeros((ROWS, LANES), jnp.bfloat16)
    for j in range(8):
        rows = slice(j * ROWS, (j + 1) * ROWS)
        if j:
            window_ref[rows, 0:LANES] = x_ref[:, 512 * j - LANES : 512 * j].astype(jnp.bfloat16)
        window_ref[rows, LANES:WINDOW] = x_ref[:, 512 * j : 512 * j + 512].astype(jnp.bfloat16)
    for first in range(0, 9, 2):
        count = min(2, 9 - first)
        picked = jnp.dot(
            window_ref[...], select_ref[:, first * LANES : (first + count) * LANES],
            preferred_element_type=jnp.float32,
        ).astype(jnp.bfloat16)
        for k in range(count):
            for j in range(8):
                taps_ref[(first + k) * ROWS : (first + k + 1) * ROWS, j * LANES : (j + 1) * LANES] = picked[
                    j * ROWS : (j + 1) * ROWS, k * LANES : (k + 1) * LANES
                ]
    inside = jnp.where(lax.axis_index("wide") < wide - 1, 1.0, 0.0)
    margin = jnp.zeros((4 * C1, LANES), jnp.bfloat16)
    act_ref[:, 0:LANES] = margin
    act_ref[:, LANES + PLANE :] = margin
    for n in range(4):
        first_pre = jnp.dot(w1_ref[...], taps_ref[:, 256 * n : 256 * n + 256], preferred_element_type=jnp.float32)
        first_act = leaky_relu(first_pre)
        here = slice(LANES + 256 * n, LANES + 256 * n + 256)
        act_ref[0 : 3 * C1, here] = first_act[0 : 3 * C1].astype(jnp.bfloat16)
        act_ref[3 * C1 :, here] = (first_act[3 * C1 :] * inside).astype(jnp.bfloat16)
    column = lax.broadcasted_iota(jnp.int32, (1, PLANE), 1) % HALF
    left_ok = jnp.where(column > 0, 1.0, 0.0).astype(jnp.bfloat16)
    right_ok = jnp.where(column < HALF - 1, 1.0, 0.0).astype(jnp.bfloat16)
    for b in range(3):
        for c in range(3):
            begin = LANES + (b - 1) * HALF + (c - 1)
            part = act_ref[:, begin : begin + PLANE]
            if c == 0:
                part = part * left_ok
            if c == 2:
                part = part * right_ok
            shifted_ref[(3 * b + c) * LANES : (3 * b + c + 1) * LANES, :] = part
    for n in range(4):
        here = slice(256 * n, 256 * n + 256)
        pre = jnp.dot(w2_ref[...], shifted_ref[:, here], preferred_element_type=jnp.float32)
        output = leaky_relu(pre).astype(jnp.bfloat16)
        slope = jnp.where(pre > 0, 1.0, neg_slope)
        for z in range(2):
            cells = slice(z * PLANE + 256 * n, z * PLANE + 256 * n + 256)
            rows = slice(z * C2, (z + 1) * C2)
            out_ref[0, 0, :, cells] = output[rows]
            back_ref[rows, here] = (cot_ref[0, 0, :, cells].astype(jnp.float32) * slope[rows]).astype(jnp.bfloat16)
    where = slots()
    group = lax.broadcasted_iota(jnp.int32, (C2, LANES), 1) // C1
    tiles = [None] * 9
    for first in range(0, 9, 2):
        count = min(2, 9 - first)
        sums = lax.dot_general(
            back_ref[...], shifted_ref[first * LANES : (first + count) * LANES, :],
            (((1,), (1,)), ((), ())), preferred_element_type=jnp.float32,
        )
        for k in range(count):
            tile = sums[:, k * LANES : (k + 1) * LANES]
            tiles[first + k] = (tile[0:C2] + pltpu.roll(tile[C2:], LANES - C1, 1)) * scale
    for bc in (7, 8):
        for a in range(3):
            tile, place = where[9 * a + bc]
            moved = pltpu.roll(tiles[bc], ((place - a) * C1) % LANES, 1)
            tiles[tile] = jnp.where(group == place, moved, tiles[tile])
    for tile in range(7):
        grad_ref[:, tile * LANES : (tile + 1) * LANES] = tiles[tile].astype(jnp.bfloat16)


def finish_kernel(parts_ref, grad_ref):
    total = parts_ref[0].astype(jnp.float32)
    for k in range(1, parts_ref.shape[0]):
        total = total + parts_ref[k].astype(jnp.float32)
    for tap, (tile, place) in slots().items():
        begin = tile * LANES + place * C1
        grad_ref[tap] = total[:, begin : begin + C1]


def body(volumes, first_kernel, second_kernel, cotangent):
    wide = lax.axis_size("wide")
    narrow = lax.axis_size("narrow")
    cells_out = cotangent.shape[3]
    scale = 1.0 / math.sqrt(wide * narrow * cells_out)
    before = lax.ppermute(volumes, "wide", [(k, k + 1) for k in range(wide - 1)])
    after = lax.ppermute(volumes, "wide", [(k + 1, k) for k in range(wide - 1)])
    k1 = first_kernel.transpose(1, 0, 2).reshape(C1, 27 * CIN)
    w1, w2 = pl.pallas_call(
        prepare_kernel,
        out_shape=(
            jax.ShapeDtypeStruct((4 * C1, 9 * ROWS), jnp.bfloat16),
            jax.ShapeDtypeStruct((2 * C2, 9 * LANES), jnp.bfloat16),
        ),
        name="prepare",
    )(k1, jnp.asarray(placement(), jnp.bfloat16), second_kernel)
    output, term = pl.pallas_call(
        functools.partial(main_kernel, wide, scale),
        out_shape=(
            jax.ShapeDtypeStruct((1, 1, C2, cells_out), jnp.bfloat16),
            jax.ShapeDtypeStruct((C2, PACKED), jnp.bfloat16),
        ),
        scratch_shapes=[
            pltpu.VMEM((ROWS, CELLS), jnp.float32),
            pltpu.VMEM((8 * ROWS, WINDOW), jnp.bfloat16),
            pltpu.VMEM((9 * ROWS, PLANE), jnp.bfloat16),
            pltpu.VMEM((4 * C1, PLANE + 2 * LANES), jnp.bfloat16),
            pltpu.VMEM((9 * LANES, PLANE), jnp.bfloat16),
            pltpu.VMEM((2 * C2, PLANE), jnp.bfloat16),
        ],
        compiler_params=pltpu.CompilerParams(vmem_limit_bytes=24 * 2**20),
        name="local",
    )(before, volumes, after, jnp.asarray(selection(), jnp.bfloat16), w1, w2, cotangent)
    rows = C2 // narrow
    owned = lax.all_to_all(term, "narrow", 0, 0, tiled=True)
    partial = jnp.sum(owned.reshape(narrow, rows, PACKED).astype(jnp.float32), axis=0).astype(jnp.bfloat16)
    copies = jnp.broadcast_to(partial[None], (wide, rows, PACKED))
    parts = lax.all_to_all(copies, "wide", 0, 0, tiled=True)
    weight_grad = pl.pallas_call(
        finish_kernel,
        out_shape=jax.ShapeDtypeStruct((27, rows, C1), jnp.float32),
        name="finish",
    )(parts)
    return (output, weight_grad)


def solution(mesh):
    return jax.shard_map(
        body,
        mesh=mesh,
        in_specs=(P("narrow", None, None, "wide", None), P(), P(), P("narrow", None, None, "wide")),
        out_specs=(P("narrow", None, None, "wide"), P(None, "narrow", None)),
        check_vma=False,
    )
```

time: 153 us -> 42.3 us (0.28)
  local copies, waits for them, and re-layouts: 61.3 us -> 6.18 us
  waiting for transfers between devices: 27.5 us -> 0.01 us
  between operations: 14.5 us -> 0.71 us
  other arithmetic: 9.54 us -> 0.02 us
  Pallas kernels: 0 us -> 7.02 us
  matrix products: 4.98 us -> 0 us
  starting transfers between devices: 8.38 us -> 3.79 us
  blocking collectives: 25.8 us -> 24.1 us
    another operation x30 -> x0, local copies, waits for them, and re-layouts: 27.1 us -> none  [the longest x29 25.8 us: depth_taps(): stacked = jnp.stack(pieces, axis=1)]
    psum x1 -> x0, blocking collectives: 25.8 us -> none  [body(): weight_grad = lax.psum(partial_rows, 'wide')]
    reduce_scatter x1 -> x0, waiting for transfers between devices: 25.7 us -> none  [body(): lax.psum_scatter(local_term.astype(jnp.bfloat16), 'narrow', scatter_dimen...]
    all_to_all x0 -> x2, blocking collectives: none -> 24.1 us  [the longest x1 12.7 us: body(): parts = lax.all_to_all(copies, 'wide', 0, 0, tiled=True)]
    unnamed x66 -> x11, local copies, waits for them, and re-layouts: 16.9 us -> 4.71 us
    concatenate x2 -> x0, local copies, waits for them, and re-layouts: 12 us -> none  [body(): stacked = jnp.concatenate([lower_plane, local], axis=2)]
    pallas_call x0 -> x3, Pallas kernels: none -> 7.02 us  [the longest x1 3.14 us: body(): pl.pallas_call(functools.partial(main_kernel, wide, scale), out_shape=(ja...]
    mul x3 -> x0, other arithmetic: 6.16 us -> none  [the longest x1 3.35 us: depth_taps(): part = part * right_ok]
  transfers between devices with their start and end apart: 4 -> 2, of which waited for: 2 -> 0; matrix products, arithmetic and copies ran while one was open for 10% -> 8% of each run, Pallas kernels for 0% -> 5%
where the time goes in v1:
time: 42.3 us; the launch traced here: 41.8 us
  blocking collectives  24.1 us (57%)
  Pallas kernels  7.02 us (17%)
  local copies, waits for them, and re-layouts  6.18 us (15%)
  starting transfers between devices  3.79 us (9%)
  between operations  0.71 us (2%)
    all_to_all x1, blocking collectives, body(): parts = lax.all_to_all(copies, 'wide', 0, 0, tiled=True)  12.7 us
    all_to_all x1, blocking collectives, body(): owned = lax.all_to_all(term, 'narrow', 0, 0, tiled=True)  11.4 us
    unnamed x11, local copies, waits for them, and re-layouts  4.71 us
    pallas_call x1, Pallas kernels, body(): pl.pallas_call(functools.partial(main_kernel, wide, scale), out_shape=(ja...  3.14 us
    ppermute x1, starting transfers between devices, body(): lax.ppermute(volumes, 'wide', [(k, k + 1) for k in range(wide - 1)])  2.5 us
    pallas_call x1, Pallas kernels, body(): pl.pallas_call(prepare_kernel, out_shape=(jax.ShapeDtypeStruct((4 * C1, 9...  2.15 us
    pallas_call x1, Pallas kernels, body(): pl.pallas_call(finish_kernel, out_shape=jax.ShapeDtypeStruct((27, rows, C...  1.74 us
    reshape x2, local copies, waits for them, and re-layouts, body(): k1 = first_kernel.transpose(1, 0, 2).reshape(C1, 27 * CIN)  1.45 us
  transfers between devices with their start and end apart: 2, of which 0 were waited for; matrix products, arithmetic and copies ran while one was open for 8% of the time, Pallas kernels for 5%

profile of v1, /device:TPU:0, one launch (start us, length us, event | category | flops | bytes accessed | tf_op | source)
XLA Modules:
  0.0 41.8 jit_solution(13143779850366673330)
XLA Ops:
  0.6 0.0 copy-start
  0.6 0.0 copy-start.3
  0.7 2.5 %collective-permute-start = (bf16[1,1,4,4,4096]{4,3,2,1,0:T(4,128)(2,1)}, bf16[1,1,4,4,4096]{4,3,2,1,0:T(4,128)(2,1)S(1)}, u32[]{:S(2)}, u32[]{:S(2)}) collective-permute-start(bf16[1,1,4,4,4096]{4,3,2,1,0:T(4,128)(2,1)} %own_ref.1), channel_id=1, source_target_pairs={{0,4},{4,8},{8,12},{12,16},{16,20},{20,24},{24,28},{1,5},{5,9},{9,... | collective-permute-start | bytes 393224 | tf_op jit(solution)/shard_map/ppermute | solution.py:166
  3.2 1.3 %collective-permute-start.1 = (bf16[1,1,4,4,4096]{4,3,2,1,0:T(4,128)(2,1)}, bf16[1,1,4,4,4096]{4,3,2,1,0:T(4,128)(2,1)S(1)}, u32[]{:S(2)}, u32[]{:S(2)}) collective-permute-start(bf16[1,1,4,4,4096]{4,3,2,1,0:T(4,128)(2,1)} %own_ref.1), channel_id=1, source_target_pairs={{4,0},{8,4},{12,8},{16,12},{20,16},{24,20},{28,24},{5,1},{9,5},{13... | collective-permute-start | bytes 393224 | tf_op jit(solution)/shard_map/ppermute | solution.py:167
  4.5 1.9 %copy.11.k2_ref = bf16[27,64,32]{2,1,0:T(8,128)(2,1)} copy(bf16[27,64,32]{1,2,0:T(8,128)(2,1)} %param.8) | data formatting | bytes 221184 | tf_op args[2]
  6.3 0.8 %reshape.12 = bf16[32,108]{0,1:T(8,128)(2,1)S(1)} reshape(bf16[32,27,4]{0,2,1:T(4,128)(2,1)} %bitcast.5) | data formatting | bytes 13824 | tf_op jit(solution)/shard_map/reshape | solution.py:168
  7.1 0.7 %copy.10.k1_ref = bf16[32,108]{1,0:T(8,128)(2,1)} copy(bf16[32,108]{0,1:T(8,128)(2,1)S(1)} %reshape.12) | data formatting | bytes 13824 | tf_op jit(solution)/shard_map/reshape | solution.py:168
  7.8 2.1 %prepare.1 = (bf16[128,432]{1,0:T(8,128)(2,1)}, bf16[128,1152]{1,0:T(8,128)(2,1)}) custom-call(bf16[32,108]{1,0:T(8,128)(2,1)} %copy.10.k1_ref, bf16[108,2048]{1,0:T(8,128)(2,1)} %constant.7.clone.place_ref, bf16[27,64,32]{2,1,0:T(8,128)(2,1)} %copy.11.k2_ref), custom_call_target="tpu_custom_call" | custom-call | tf_op jit(solution)/shard_map/prepare/pallas_call | solution.py:169
  10.0 0.0 collective-permute-done.before_ref
  10.0 0.0 collective-permute-done.1.after_ref
  10.0 0.0 copy-done
  10.0 0.0 copy-done.3
  10.0 0.0 copy-start.1
  10.0 1.0 %copy-done.1 = bf16[128,1152]{1,0:T(8,128)(2,1)S(1)} copy-done((bf16[128,1152]{1,0:T(8,128)(2,1)S(1)}, bf16[128,1152]{1,0:T(8,128)(2,1)}, u32[]{:S(2)}) %copy-start.1) | copy-done | bytes 294936
  10.9 0.0 copy-start.2
  10.9 0.9 %copy-done.2 = bf16[1,1,64,2048]{3,2,1,0:T(8,128)(2,1)S(1)} copy-done((bf16[1,1,64,2048]{3,2,1,0:T(8,128)(2,1)S(1)}, bf16[1,1,64,2048]{3,2,1,0:T(8,128)(2,1)}, u32[]{:S(2)}) %copy-start.2) | copy-done | bytes 262168
  11.9 0.0 copy-start.4
  11.9 0.9 %copy-done.4 = bf16[128,432]{1,0:T(8,128)(2,1)S(1)} copy-done((bf16[128,432]{1,0:T(8,128)(2,1)S(1)}, bf16[128,432]{1,0:T(8,128)(2,1)}, u32[]{:S(2)}) %copy-start.4) | copy-done | bytes 110616
  12.8 3.1 %local.1 = (bf16[1,1,64,2048]{3,2,1,0:T(8,128)(2,1)}, bf16[64,896]{1,0:T(8,128)(2,1)S(1)}) custom-call(bf16[1,1,4,4,4096]{4,3,2,1,0:T(4,128)(2,1)S(1)} %collective-permute-done.before_ref, bf16[1,1,4,4,4096]{4,3,2,1,0:T(4,128)(2,1)S(1)} %copy-done.3, bf16[1,1,4,4,4096]{4,3,2,1,0:T(4,128)(2,1)S(1)} %collective-permute-done.1.after_ref, ...), custom_call_target="tpu_custom_call" | custom-call | tf_op jit(solution)/shard_map/local/pallas_call | solution.py:177
  15.9 11.4 %all_to_all.14 = bf16[4,16,896]{2,1,0:T(8,128)(2,1)S(1)} all-to-all(bf16[4,16,896]{2,1,0:T(8,128)(2,1)S(1)} %bitcast.4), channel_id=1, replica_groups=mesh['wide'=8,'narrow'=4] {'narrow'}, dimensions={0} | all-to-all | bytes 229376 | tf_op jit(solution)/shard_map/all_to_all | solution.py:195
  27.4 12.7 %all_to_all.15.parts_ref = bf16[8,16,896]{2,1,0:T(8,128)(2,1)} all-to-all(bf16[8,16,896]{2,1,0:T(8,128)(2,1)S(1)} %broadcast_in_dim.2), channel_id=1, replica_groups=mesh['wide'=8,'narrow'=4] {'wide'}, dimensions={0} | all-to-all | bytes 458752 | tf_op jit(solution)/shard_map/all_to_all | solution.py:198
  40.1 1.7 %finish.1 = f32[27,16,32]{2,1,0:T(8,128)} custom-call(bf16[8,16,896]{2,1,0:T(8,128)(2,1)} %all_to_all.15.parts_ref), custom_call_target="tpu_custom_call" | custom-call | tf_op jit(solution)/shard_map/finish/pallas_call | solution.py:199
  (2 shorter events, 0.0 us)
Async XLA Ops:
  0.6 9.3 %copy-start = (bf16[640,1152]{1,0:T(8,128)(2,1)S(1)}, bf16[640,1152]{1,0:T(8,128)(2,1)}, u32[]{:S(2)}) copy-start(bf16[640,1152]{1,0:T(8,128)(2,1)} %constant.8.clone.select_ref) | copy-start | bytes 4423684
  0.6 9.3 %copy-start.3 = (bf16[1,1,4,4,4096]{4,3,2,1,0:T(4,128)(2,1)S(1)}, bf16[1,1,4,4,4096]{4,3,2,1,0:T(4,128)(2,1)}, u32[]{:S(2)}) copy-start(bf16[1,1,4,4,4096]{4,3,2,1,0:T(4,128)(2,1)} %own_ref.1) | copy-start | bytes 393220
  0.7 9.3 %collective-permute-start = (bf16[1,1,4,4,4096]{4,3,2,1,0:T(4,128)(2,1)}, bf16[1,1,4,4,4096]{4,3,2,1,0:T(4,128)(2,1)S(1)}, u32[]{:S(2)}, u32[]{:S(2)}) collective-permute-start(bf16[1,1,4,4,4096]{4,3,2,1,0:T(4,128)(2,1)} %own_ref.1), channel_id=1, source_target_pairs={{0,4},{4,8},{8,12},{12,16},{16,20},{20,24},{24,28},{1,5},{5,9},{9,... | collective-permute-start | bytes 393224 | tf_op jit(solution)/shard_map/ppermute | solution.py:166
  3.2 6.8 %collective-permute-start.1 = (bf16[1,1,4,4,4096]{4,3,2,1,0:T(4,128)(2,1)}, bf16[1,1,4,4,4096]{4,3,2,1,0:T(4,128)(2,1)S(1)}, u32[]{:S(2)}, u32[]{:S(2)}) collective-permute-start(bf16[1,1,4,4,4096]{4,3,2,1,0:T(4,128)(2,1)} %own_ref.1), channel_id=1, source_target_pairs={{4,0},{8,4},{12,8},{16,12},{20,16},{24,20},{28,24},{5,1},{9,5},{13... | collective-permute-start | bytes 393224 | tf_op jit(solution)/shard_map/ppermute | solution.py:167
  10.0 1.0 %copy-start.1 = (bf16[128,1152]{1,0:T(8,128)(2,1)S(1)}, bf16[128,1152]{1,0:T(8,128)(2,1)}, u32[]{:S(2)}) copy-start(bf16[128,1152]{1,0:T(8,128)(2,1)} %get-tuple-element.7.w2_ref) | copy-start | bytes 884740
  10.9 0.9 %copy-start.2 = (bf16[1,1,64,2048]{3,2,1,0:T(8,128)(2,1)S(1)}, bf16[1,1,64,2048]{3,2,1,0:T(8,128)(2,1)}, u32[]{:S(2)}) copy-start(bf16[1,1,64,2048]{3,2,1,0:T(8,128)(2,1)} %cot_ref.1) | copy-start | bytes 786436
  11.9 0.9 %copy-start.4 = (bf16[128,432]{1,0:T(8,128)(2,1)S(1)}, bf16[128,432]{1,0:T(8,128)(2,1)}, u32[]{:S(2)}) copy-start(bf16[128,432]{1,0:T(8,128)(2,1)} %get-tuple-element.6.w1_ref) | copy-start | bytes 331780

commit v2 on v1

--- a/solution.py
+++ b/solution.py
@@ -59,22 +59,30 @@
     return where
 
 
-def prepare_kernel(k1_ref, place_ref, k2_ref, w1_ref, w2_ref):
-    spread = jnp.dot(k1_ref[...], place_ref[...], preferred_element_type=jnp.float32)
+def prepare_kernel(k1_ref, place_ref, k2_ref, w1_ref, w2_ref, rows_ref):
+    for tap in range(27):
+        rows_ref[CIN * tap : CIN * (tap + 1), :] = k1_ref[tap].astype(jnp.float32)
+    spread = lax.dot_general(
+        rows_ref[...].astype(jnp.bfloat16), place_ref[...],
+        (((0,), (0,)), ((), ())), preferred_element_type=jnp.float32,
+    )
     for q in range(4):
         w1_ref[q * C1 : (q + 1) * C1, :] = spread[:, 512 * q : 512 * q + 9 * ROWS].astype(jnp.bfloat16)
-    blank = jnp.zeros((C2, C1), jnp.bfloat16)
+    blank = jnp.zeros((C1, C2), jnp.bfloat16)
     for bc in range(9):
         taps = [k2_ref[9 * a + bc] for a in range(3)]
         here = slice(bc * LANES, (bc + 1) * LANES)
-        w2_ref[0:C2, here] = jnp.concatenate(taps + [blank], axis=1)
-        w2_ref[C2 : 2 * C2, here] = jnp.concatenate([blank] + taps, axis=1)
+        lower = jnp.concatenate(taps + [blank], axis=0)
+        upper = jnp.concatenate([blank] + taps, axis=0)
+        w2_ref[:, here] = jnp.concatenate([lower, upper], axis=1).T
 
 
 def main_kernel(
-    wide, scale, before_ref, own_ref, after_ref, select_ref, w1_ref, w2_ref, cot_ref,
-    out_ref, grad_ref, x_ref, window_ref, taps_ref, act_ref, shifted_ref, back_ref,
+    wide, scale, before_ref, own_ref, after_ref, select_ref, w1_ref, w2_ref, cot_hbm,
+    out_hbm, grad_ref, x_ref, window_ref, taps_ref, act_ref, shifted_ref, back_ref, cot_ref, out_ref, cot_sem, out_sem,
 ):
+    cot_copy = pltpu.make_async_copy(cot_hbm, cot_ref, cot_sem)
+    cot_copy.start()
     for s, ref in enumerate((before_ref, own_ref, after_ref)):
         for i in range(CIN):
             row = 16 * s + PLANES * i
@@ -118,6 +126,7 @@
             if c == 2:
                 part = part * right_ok
             shifted_ref[(3 * b + c) * LANES : (3 * b + c + 1) * LANES, :] = part
+    cot_copy.wait()
     for n in range(4):
         here = slice(256 * n, 256 * n + 256)
         pre = jnp.dot(w2_ref[...], shifted_ref[:, here], preferred_element_type=jnp.float32)
@@ -128,6 +137,8 @@
             rows = slice(z * C2, (z + 1) * C2)
             out_ref[0, 0, :, cells] = output[rows]
             back_ref[rows, here] = (cot_ref[0, 0, :, cells].astype(jnp.float32) * slope[rows]).astype(jnp.bfloat16)
+    out_copy = pltpu.make_async_copy(out_ref, out_hbm, out_sem)
+    out_copy.start()
     where = slots()
     group = lax.broadcasted_iota(jnp.int32, (C2, LANES), 1) // C1
     tiles = [None] * 9
@@ -147,6 +158,7 @@
             tiles[tile] = jnp.where(group == place, moved, tiles[tile])
     for tile in range(7):
         grad_ref[:, tile * LANES : (tile + 1) * LANES] = tiles[tile].astype(jnp.bfloat16)
+    out_copy.wait()
 
 
 def finish_kernel(parts_ref, grad_ref):
@@ -165,17 +177,20 @@
     scale = 1.0 / math.sqrt(wide * narrow * cells_out)
     before = lax.ppermute(volumes, "wide", [(k, k + 1) for k in range(wide - 1)])
     after = lax.ppermute(volumes, "wide", [(k + 1, k) for k in range(wide - 1)])
-    k1 = first_kernel.transpose(1, 0, 2).reshape(C1, 27 * CIN)
     w1, w2 = pl.pallas_call(
         prepare_kernel,
         out_shape=(
             jax.ShapeDtypeStruct((4 * C1, 9 * ROWS), jnp.bfloat16),
             jax.ShapeDtypeStruct((2 * C2, 9 * LANES), jnp.bfloat16),
         ),
+        scratch_shapes=[pltpu.VMEM((27 * CIN, C1), jnp.float32)],
+        compiler_params=pltpu.CompilerParams(vmem_limit_bytes=8 * 2**20),
         name="prepare",
-    )(k1, jnp.asarray(placement(), jnp.bfloat16), second_kernel)
+    )(first_kernel.transpose(0, 2, 1), jnp.asarray(placement(), jnp.bfloat16), second_kernel.transpose(0, 2, 1))
     output, term = pl.pallas_call(
         functools.partial(main_kernel, wide, scale),
+        in_specs=[pl.BlockSpec(memory_space=pltpu.VMEM)] * 6 + [pl.BlockSpec(memory_space=pl.ANY)],
+        out_specs=(pl.BlockSpec(memory_space=pl.ANY), pl.BlockSpec(memory_space=pltpu.VMEM)),
         out_shape=(
             jax.ShapeDtypeStruct((1, 1, C2, cells_out), jnp.bfloat16),
             jax.ShapeDtypeStruct((C2, PACKED), jnp.bfloat16),
@@ -187,6 +202,10 @@
             pltpu.VMEM((4 * C1, PLANE + 2 * LANES), jnp.bfloat16),
             pltpu.VMEM((9 * LANES, PLANE), jnp.bfloat16),
             pltpu.VMEM((2 * C2, PLANE), jnp.bfloat16),
+            pltpu.VMEM((1, 1, C2, cells_out), jnp.bfloat16),
+            pltpu.VMEM((1, 1, C2, cells_out), jnp.bfloat16),
+            pltpu.SemaphoreType.DMA,
+            pltpu.SemaphoreType.DMA,
         ],
         compiler_params=pltpu.CompilerParams(vmem_limit_bytes=24 * 2**20),
         name="local",
@@ -199,6 +218,7 @@
     weight_grad = pl.pallas_call(
         finish_kernel,
         out_shape=jax.ShapeDtypeStruct((27, rows, C1), jnp.float32),
+        compiler_params=pltpu.CompilerParams(vmem_limit_bytes=8 * 2**20),
         name="finish",
     )(parts)
     return (output, weight_grad)

time: 42.3 us -> 39.7 us (0.939)
  Pallas kernels: 7.02 us -> 4.58 us
  waiting for transfers between devices: 0.01 us -> 1.18 us
  blocking collectives: 24.1 us -> 23.1 us
    pallas_call x1, Pallas kernels: 2.15 us -> 0.35 us  [body(): pl.pallas_call(prepare_kernel, out_shape=(jax.ShapeDtypeStruct((4 * C1, 9...]
    reshape x2 -> x0, local copies, waits for them, and re-layouts: 1.45 us -> none  [body(): k1 = first_kernel.transpose(1, 0, 2).reshape(C1, 27 * CIN)]
    unnamed x11 -> x12, local copies, waits for them, and re-layouts: 4.71 us -> 5.92 us
    ppermute x1, waiting for transfers between devices: 0.01 us -> 1.18 us  [body(): after = lax.ppermute(volumes, 'wide', [(k + 1, k) for k in range(wide - 1)])]
    pallas_call x1, Pallas kernels: 1.74 us -> 0.8 us  [body(): pl.pallas_call(finish_kernel, out_shape=jax.ShapeDtypeStruct((27, rows, C...]
    all_to_all x1, blocking collectives: 11.4 us -> 10.6 us  [body(): owned = lax.all_to_all(term, 'narrow', 0, 0, tiled=True)]
  transfers between devices with their start and end apart: 2 -> 2, of which waited for: 0 -> 1; matrix products, arithmetic and copies ran while one was open for 8% -> 0% of each run, Pallas kernels for 5% -> 1%
where the time goes in v2:
time: 39.7 us; the launch traced here: 39.2 us
  blocking collectives  23.1 us (58%)
  local copies, waits for them, and re-layouts  5.94 us (15%)
  Pallas kernels  4.58 us (12%)
  starting transfers between devices  3.66 us (9%)
  waiting for transfers between devices  1.18 us (3%)
  between operations  0.7 us (2%)
    all_to_all x1, blocking collectives, body(): parts = lax.all_to_all(copies, 'wide', 0, 0, tiled=True)  12.6 us
    all_to_all x1, blocking collectives, body(): owned = lax.all_to_all(term, 'narrow', 0, 0, tiled=True)  10.6 us
    unnamed x12, local copies, waits for them, and re-layouts  5.92 us
    pallas_call x1, Pallas kernels, body(): pl.pallas_call(functools.partial(main_kernel, wide, scale), in_specs=[pl....  3.43 us
    ppermute x1, starting transfers between devices, body(): lax.ppermute(volumes, 'wide', [(k, k + 1) for k in range(wide - 1)])  2.37 us
    ppermute x1, starting transfers between devices, body(): after = lax.ppermute(volumes, 'wide', [(k + 1, k) for k in range(wide - 1)])  1.29 us
    ppermute x1, waiting for transfers between devices, body(): after = lax.ppermute(volumes, 'wide', [(k + 1, k) for k in range(wide - 1)])  1.18 us
    pallas_call x1, Pallas kernels, body(): pl.pallas_call(finish_kernel, out_shape=jax.ShapeDtypeStruct((27, rows, C...  0.8 us
  transfers between devices with their start and end apart: 2, of which 1 were waited for; matrix products, arithmetic and copies ran while one was open for 0% of the time, Pallas kernels for 1%

profile of v2, /device:TPU:0, one launch (start us, length us, event | category | flops | bytes accessed | tf_op | source)
XLA Modules:
  0.0 39.2 jit_solution(17849226549538566253)
XLA Ops:
  0.6 2.4 %collective-permute-start = (bf16[1,1,4,4,4096]{4,3,2,1,0:T(4,128)(2,1)}, bf16[1,1,4,4,4096]{4,3,2,1,0:T(4,128)(2,1)S(1)}, u32[]{:S(2)}, u32[]{:S(2)}) collective-permute-start(bf16[1,1,4,4,4096]{4,3,2,1,0:T(4,128)(2,1)} %own_ref.1), channel_id=1, source_target_pairs={{0,4},{4,8},{8,12},{12,16},{16,20},{20,24},{24,28},{1,5},{5,9},{9,... | collective-permute-start | bytes 393224 | tf_op jit(solution)/shard_map/ppermute | solution.py:178
  3.0 1.3 %collective-permute-start.1 = (bf16[1,1,4,4,4096]{4,3,2,1,0:T(4,128)(2,1)}, bf16[1,1,4,4,4096]{4,3,2,1,0:T(4,128)(2,1)S(1)}, u32[]{:S(2)}, u32[]{:S(2)}) collective-permute-start(bf16[1,1,4,4,4096]{4,3,2,1,0:T(4,128)(2,1)} %own_ref.1), channel_id=1, source_target_pairs={{4,0},{8,4},{12,8},{16,12},{20,16},{24,20},{28,24},{5,1},{9,5},{13... | collective-permute-start | bytes 393224 | tf_op jit(solution)/shard_map/ppermute | solution.py:179
  4.3 0.0 copy-start.1
  4.3 1.0 %copy-done.1 = bf16[108,2048]{1,0:T(8,128)(2,1)S(1)} copy-done((bf16[108,2048]{1,0:T(8,128)(2,1)S(1)}, bf16[108,2048]{1,0:T(8,128)(2,1)}, u32[]{:S(2)}) %copy-start.1) | copy-done | bytes 442392
  5.3 0.0 copy-start.3
  5.3 0.9 %copy-done.3 = bf16[27,64,32]{1,2,0:T(8,128)(2,1)S(1)} copy-done((bf16[27,64,32]{1,2,0:T(8,128)(2,1)S(1)}, bf16[27,64,32]{1,2,0:T(8,128)(2,1)}, u32[]{:S(2)}) %copy-start.3) | copy-done | bytes 110616
  6.3 0.0 copy-start.5
  6.3 0.7 %copy-done.5 = bf16[27,32,4]{1,2,0:T(4,128)(2,1)S(1)} copy-done((bf16[27,32,4]{1,2,0:T(4,128)(2,1)S(1)}, bf16[27,32,4]{1,2,0:T(4,128)(2,1)}, u32[]{:S(2)}) %copy-start.5) | copy-done | bytes 6936
  7.0 0.4 prepare.1
  7.4 0.0 collective-permute-done.before_ref
  7.4 1.2 %collective-permute-done.1.after_ref = bf16[1,1,4,4,4096]{4,3,2,1,0:T(4,128)(2,1)S(1)} collective-permute-done((bf16[1,1,4,4,4096]{4,3,2,1,0:T(4,128)(2,1)}, bf16[1,1,4,4,4096]{4,3,2,1,0:T(4,128)(2,1)S(1)}, u32[]{:S(2)}, u32[]{:S(2)}) %collective-permute-start.1) | collective-permute-done | bytes 131104 | tf_op jit(solution)/shard_map/ppermute | solution.py:179
  8.6 0.0 copy-start
  8.6 1.4 %copy-done = bf16[640,1152]{1,0:T(8,128)(2,1)S(1)} copy-done((bf16[640,1152]{1,0:T(8,128)(2,1)S(1)}, bf16[640,1152]{1,0:T(8,128)(2,1)}, u32[]{:S(2)}) %copy-start) | copy-done | bytes 1474584
  9.9 0.0 copy-start.2
  9.9 0.9 %copy-done.2 = bf16[1,1,64,2048]{3,2,1,0:T(8,128)(2,1)S(1)} copy-done((bf16[1,1,64,2048]{3,2,1,0:T(8,128)(2,1)S(1)}, bf16[1,1,64,2048]{3,2,1,0:T(8,128)(2,1)}, u32[]{:S(2)}) %copy-start.2) | copy-done | bytes 262168
  10.9 0.0 copy-start.4
  10.9 0.9 %copy-done.4 = bf16[1,1,4,4,4096]{4,3,2,1,0:T(4,128)(2,1)S(1)} copy-done((bf16[1,1,4,4,4096]{4,3,2,1,0:T(4,128)(2,1)S(1)}, bf16[1,1,4,4,4096]{4,3,2,1,0:T(4,128)(2,1)}, u32[]{:S(2)}) %copy-start.4) | copy-done | bytes 131096
  11.8 3.4 %local.1 = (bf16[1,1,64,2048]{3,2,1,0:T(8,128)(2,1)}, bf16[64,896]{1,0:T(8,128)(2,1)S(1)}) custom-call(bf16[1,1,4,4,4096]{4,3,2,1,0:T(4,128)(2,1)S(1)} %collective-permute-done.before_ref, bf16[1,1,4,4,4096]{4,3,2,1,0:T(4,128)(2,1)S(1)} %copy-done.4, bf16[1,1,4,4,4096]{4,3,2,1,0:T(4,128)(2,1)S(1)} %collective-permute-done.1.after_ref, ...), custom_call_target="tpu_custom_call" | custom-call | tf_op jit(solution)/shard_map/local/pallas_call | solution.py:190
  15.2 10.6 %all_to_all.14 = bf16[4,16,896]{2,1,0:T(8,128)(2,1)S(1)} all-to-all(bf16[4,16,896]{2,1,0:T(8,128)(2,1)S(1)} %bitcast.4), channel_id=1, replica_groups=mesh['wide'=8,'narrow'=4] {'narrow'}, dimensions={0} | all-to-all | bytes 229376 | tf_op jit(solution)/shard_map/all_to_all | solution.py:214
  25.8 12.6 %all_to_all.15.parts_ref = bf16[8,16,896]{2,1,0:T(8,128)(2,1)S(1)} all-to-all(bf16[8,16,896]{2,1,0:T(8,128)(2,1)S(1)} %broadcast_in_dim.2), channel_id=1, replica_groups=mesh['wide'=8,'narrow'=4] {'wide'}, dimensions={0} | all-to-all | bytes 458752 | tf_op jit(solution)/shard_map/all_to_all | solution.py:217
  38.4 0.8 %finish.1 = f32[27,16,32]{2,1,0:T(8,128)} custom-call(bf16[8,16,896]{2,1,0:T(8,128)(2,1)S(1)} %all_to_all.15.parts_ref), custom_call_target="tpu_custom_call" | custom-call | tf_op jit(solution)/shard_map/finish/pallas_call | solution.py:218
  (2 shorter events, 0.0 us)
Async XLA Ops:
  0.6 6.7 %collective-permute-start = (bf16[1,1,4,4,4096]{4,3,2,1,0:T(4,128)(2,1)}, bf16[1,1,4,4,4096]{4,3,2,1,0:T(4,128)(2,1)S(1)}, u32[]{:S(2)}, u32[]{:S(2)}) collective-permute-start(bf16[1,1,4,4,4096]{4,3,2,1,0:T(4,128)(2,1)} %own_ref.1), channel_id=1, source_target_pairs={{0,4},{4,8},{8,12},{12,16},{16,20},{20,24},{24,28},{1,5},{5,9},{9,... | collective-permute-start | bytes 393224 | tf_op jit(solution)/shard_map/ppermute | solution.py:178
  3.0 5.6 %collective-permute-start.1 = (bf16[1,1,4,4,4096]{4,3,2,1,0:T(4,128)(2,1)}, bf16[1,1,4,4,4096]{4,3,2,1,0:T(4,128)(2,1)S(1)}, u32[]{:S(2)}, u32[]{:S(2)}) collective-permute-start(bf16[1,1,4,4,4096]{4,3,2,1,0:T(4,128)(2,1)} %own_ref.1), channel_id=1, source_target_pairs={{4,0},{8,4},{12,8},{16,12},{20,16},{24,20},{28,24},{5,1},{9,5},{13... | collective-permute-start | bytes 393224 | tf_op jit(solution)/shard_map/ppermute | solution.py:179
  4.3 1.0 %copy-start.1 = (bf16[108,2048]{1,0:T(8,128)(2,1)S(1)}, bf16[108,2048]{1,0:T(8,128)(2,1)}, u32[]{:S(2)}) copy-start(bf16[108,2048]{1,0:T(8,128)(2,1)} %constant.7.clone.place_ref) | copy-start | bytes 1327108
  5.3 0.9 %copy-start.3 = (bf16[27,64,32]{1,2,0:T(8,128)(2,1)S(1)}, bf16[27,64,32]{1,2,0:T(8,128)(2,1)}, u32[]{:S(2)}) copy-start(bf16[27,64,32]{1,2,0:T(8,128)(2,1)} %param.8) | copy-start | bytes 331780
  6.3 0.7 %copy-start.5 = (bf16[27,32,4]{1,2,0:T(4,128)(2,1)S(1)}, bf16[27,32,4]{1,2,0:T(4,128)(2,1)}, u32[]{:S(2)}) copy-start(bf16[27,32,4]{1,2,0:T(4,128)(2,1)} %param.7) | copy-start | bytes 20740
  8.6 1.4 %copy-start = (bf16[640,1152]{1,0:T(8,128)(2,1)S(1)}, bf16[640,1152]{1,0:T(8,128)(2,1)}, u32[]{:S(2)}) copy-start(bf16[640,1152]{1,0:T(8,128)(2,1)} %constant.8.clone.select_ref) | copy-start | bytes 4423684
  9.9 0.9 %copy-start.2 = (bf16[1,1,64,2048]{3,2,1,0:T(8,128)(2,1)S(1)}, bf16[1,1,64,2048]{3,2,1,0:T(8,128)(2,1)}, u32[]{:S(2)}) copy-start(bf16[1,1,64,2048]{3,2,1,0:T(8,128)(2,1)} %cot_hbm.1) | copy-start | bytes 786436
  10.9 0.9 %copy-start.4 = (bf16[1,1,4,4,4096]{4,3,2,1,0:T(4,128)(2,1)S(1)}, bf16[1,1,4,4,4096]{4,3,2,1,0:T(4,128)(2,1)}, u32[]{:S(2)}) copy-start(bf16[1,1,4,4,4096]{4,3,2,1,0:T(4,128)(2,1)} %own_ref.1) | copy-start | bytes 393220

commit v3 on v1

--- a/solution.py
+++ b/solution.py
@@ -19,7 +19,8 @@
 LANES = 128
 ROWS = 3 * CIN * PLANES
 WINDOW = 640
-PACKED = 7 * LANES
+PACKED = 8 * LANES
+MIB = 2**20
 neg_slope = 0.3
 
 
@@ -51,40 +52,60 @@
 
 
 def slots():
-    where = {}
-    free = [(tile, 3) for tile in range(6)]
-    for bc in range(9):
-        for a in range(3):
-            where[9 * a + bc] = (bc, a) if bc < 7 else free.pop(0)
-    return where
-
-
-def prepare_kernel(k1_ref, place_ref, k2_ref, w1_ref, w2_ref):
-    spread = jnp.dot(k1_ref[...], place_ref[...], preferred_element_type=jnp.float32)
-    for q in range(4):
-        w1_ref[q * C1 : (q + 1) * C1, :] = spread[:, 512 * q : 512 * q + 9 * ROWS].astype(jnp.bfloat16)
-    blank = jnp.zeros((C2, C1), jnp.bfloat16)
+    return {9 * a + bc: (bc, a) if bc < 8 else (a, 3) for a in range(3) for bc in range(9)}
+
+
+def plane_rows(volume_ref, rows_ref):
+    for i in range(CIN):
+        rows_ref[PLANES * i : PLANES * (i + 1), :] = volume_ref[0, 0, i].astype(jnp.float32)
+    return rows_ref[...].astype(jnp.bfloat16)
+
+
+def prepare_kernel(
+    k1_hbm, place_hbm, k2_hbm, own_hbm, select_hbm, cot_hbm, w1_ref, w2_ref, mine_ref, select_ref, cot_ref,
+    k1_ref, place_ref, k2_ref, own_ref, k1_rows_ref, rows_ref, sems,
+):
+    moves = ((k2_hbm, k2_ref), (own_hbm, own_ref), (k1_hbm, k1_ref), (place_hbm, place_ref), (select_hbm, select_ref), (cot_hbm, cot_ref))
+    copies = [pltpu.make_async_copy(src, dst, sems.at[k]) for k, (src, dst) in enumerate(moves)]
+    for copy in copies:
+        copy.start()
+    copies[0].wait()
+    blank = jnp.zeros((C1, C2), jnp.bfloat16)
     for bc in range(9):
         taps = [k2_ref[9 * a + bc] for a in range(3)]
         here = slice(bc * LANES, (bc + 1) * LANES)
-        w2_ref[0:C2, here] = jnp.concatenate(taps + [blank], axis=1)
-        w2_ref[C2 : 2 * C2, here] = jnp.concatenate([blank] + taps, axis=1)
+        lower = jnp.concatenate(taps + [blank], axis=0)
+        upper = jnp.concatenate([blank] + taps, axis=0)
+        w2_ref[:, here] = jnp.concatenate([lower, upper], axis=1).T
+    copies[1].wait()
+    mine_ref[...] = plane_rows(own_ref, rows_ref)
+    copies[2].wait()
+    for tap in range(27):
+        k1_rows_ref[CIN * tap : CIN * (tap + 1), :] = k1_ref[tap].astype(jnp.float32)
+    copies[3].wait()
+    spread = lax.dot_general(
+        k1_rows_ref[...].astype(jnp.bfloat16), place_ref[...],
+        (((0,), (0,)), ((), ())), preferred_element_type=jnp.float32,
+    )
+    for q in range(4):
+        w1_ref[q * C1 : (q + 1) * C1, :] = spread[:, 512 * q : 512 * q + 9 * ROWS].astype(jnp.bfloat16)
+    copies[4].wait()
+    copies[5].wait()
 
 
 def main_kernel(
-    wide, scale, before_ref, own_ref, after_ref, select_ref, w1_ref, w2_ref, cot_ref,
-    out_ref, grad_ref, x_ref, window_ref, taps_ref, act_ref, shifted_ref, back_ref,
+    wide, scale, before_ref, mine_ref, after_ref, select_ref, w1_ref, w2_ref, cot_ref, out_hbm, grad_ref,
+    rows_ref, window_ref, taps_ref, act_ref, shifted_ref, back_ref, out_ref, out_sem,
 ):
-    for s, ref in enumerate((before_ref, own_ref, after_ref)):
-        for i in range(CIN):
-            row = 16 * s + PLANES * i
-            x_ref[row : row + PLANES, :] = ref[0, 0, i].astype(jnp.float32)
-    window_ref[0:ROWS, 0:LANES] = jnp.zeros((ROWS, LANES), jnp.bfloat16)
-    for j in range(8):
-        rows = slice(j * ROWS, (j + 1) * ROWS)
-        if j:
-            window_ref[rows, 0:LANES] = x_ref[:, 512 * j - LANES : 512 * j].astype(jnp.bfloat16)
-        window_ref[rows, LANES:WINDOW] = x_ref[:, 512 * j : 512 * j + 512].astype(jnp.bfloat16)
+    sources = (plane_rows(before_ref, rows_ref.at[0]), mine_ref[...], plane_rows(after_ref, rows_ref.at[1]))
+    for s, rows in enumerate(sources):
+        for j in range(8):
+            top = j * ROWS + 16 * s
+            if j:
+                window_ref[top : top + 16, 0:LANES] = rows[:, 512 * j - LANES : 512 * j]
+            else:
+                window_ref[top : top + 16, 0:LANES] = jnp.zeros((16, LANES), jnp.bfloat16)
+            window_ref[top : top + 16, LANES:WINDOW] = rows[:, 512 * j : 512 * j + 512]
     for first in range(0, 9, 2):
         count = min(2, 9 - first)
         picked = jnp.dot(
@@ -128,9 +149,10 @@
             rows = slice(z * C2, (z + 1) * C2)
             out_ref[0, 0, :, cells] = output[rows]
             back_ref[rows, here] = (cot_ref[0, 0, :, cells].astype(jnp.float32) * slope[rows]).astype(jnp.bfloat16)
-    where = slots()
+    out_copy = pltpu.make_async_copy(out_ref, out_hbm, out_sem)
+    out_copy.start()
     group = lax.broadcasted_iota(jnp.int32, (C2, LANES), 1) // C1
-    tiles = [None] * 9
+    tiles = []
     for first in range(0, 9, 2):
         count = min(2, 9 - first)
         sums = lax.dot_general(
@@ -139,23 +161,26 @@
         )
         for k in range(count):
             tile = sums[:, k * LANES : (k + 1) * LANES]
-            tiles[first + k] = (tile[0:C2] + pltpu.roll(tile[C2:], LANES - C1, 1)) * scale
-    for bc in (7, 8):
-        for a in range(3):
-            tile, place = where[9 * a + bc]
-            moved = pltpu.roll(tiles[bc], ((place - a) * C1) % LANES, 1)
-            tiles[tile] = jnp.where(group == place, moved, tiles[tile])
-    for tile in range(7):
-        grad_ref[:, tile * LANES : (tile + 1) * LANES] = tiles[tile].astype(jnp.bfloat16)
+            tiles.append((tile[0:C2] + pltpu.roll(tile[C2:], LANES - C1, 1)) * scale)
+    last = tiles.pop()
+    for a in range(3):
+        tiles[a] = jnp.where(group == 3, pltpu.roll(last, (3 - a) * C1, 1), tiles[a])
+    pieces, rows, lanes = grad_ref.shape
+    narrow = C2 // rows
+    for tile in range(8):
+        rounded = tiles[tile].astype(jnp.bfloat16)
+        for n in range(narrow):
+            part = rounded[n * rows : (n + 1) * rows]
+            if pieces > 1:
+                grad_ref[tile * narrow + n] = part
+            else:
+                grad_ref[0, n * rows : (n + 1) * rows, tile * LANES : (tile + 1) * LANES] = part
+    out_copy.wait()
 
 
 def finish_kernel(parts_ref, grad_ref):
-    total = parts_ref[0].astype(jnp.float32)
-    for k in range(1, parts_ref.shape[0]):
-        total = total + parts_ref[k].astype(jnp.float32)
     for tap, (tile, place) in slots().items():
-        begin = tile * LANES + place * C1
-        grad_ref[tap] = total[:, begin : begin + C1]
+        grad_ref[tap] = parts_ref[tile, :, place * C1 : (place + 1) * C1]
 
 
 def body(volumes, first_kernel, second_kernel, cotangent):
@@ -165,40 +190,71 @@
     scale = 1.0 / math.sqrt(wide * narrow * cells_out)
     before = lax.ppermute(volumes, "wide", [(k, k + 1) for k in range(wide - 1)])
     after = lax.ppermute(volumes, "wide", [(k + 1, k) for k in range(wide - 1)])
-    k1 = first_kernel.transpose(1, 0, 2).reshape(C1, 27 * CIN)
-    w1, w2 = pl.pallas_call(
+    pinned = pl.BlockSpec(memory_space=pltpu.HBM)
+    fast = pl.BlockSpec(memory_space=pltpu.VMEM)
+    w1, w2, mine, select, cot = pl.pallas_call(
         prepare_kernel,
+        in_specs=[pinned] * 6,
+        out_specs=(fast,) * 5,
         out_shape=(
             jax.ShapeDtypeStruct((4 * C1, 9 * ROWS), jnp.bfloat16),
             jax.ShapeDtypeStruct((2 * C2, 9 * LANES), jnp.bfloat16),
+            jax.ShapeDtypeStruct((CIN * PLANES, CELLS), jnp.bfloat16),
+            jax.ShapeDtypeStruct((WINDOW, 9 * LANES), jnp.bfloat16),
+            jax.ShapeDtypeStruct(cotangent.shape, jnp.bfloat16),
         ),
+        scratch_shapes=[
+            pltpu.VMEM((27, CIN, C1), jnp.bfloat16),
+            pltpu.VMEM((27 * CIN, 4 * 512), jnp.bfloat16),
+            pltpu.VMEM((27, C1, C2), jnp.bfloat16),
+            pltpu.VMEM(volumes.shape, jnp.bfloat16),
+            pltpu.VMEM((27 * CIN, C1), jnp.float32),
+            pltpu.VMEM((CIN * PLANES, CELLS), jnp.float32),
+            pltpu.SemaphoreType.DMA((6,)),
+        ],
+        compiler_params=pltpu.CompilerParams(vmem_limit_bytes=16 * MIB),
+        cost_estimate=pl.CostEstimate(flops=10**9, bytes_accessed=4 * MIB, transcendentals=0),
         name="prepare",
-    )(k1, jnp.asarray(placement(), jnp.bfloat16), second_kernel)
+    )(*(pltpu.with_memory_space_constraint(x, pltpu.HBM) for x in (
+        first_kernel.transpose(0, 2, 1), jnp.asarray(placement(), jnp.bfloat16), second_kernel.transpose(0, 2, 1),
+        volumes, jnp.asarray(selection(), jnp.bfloat16), cotangent,
+    )))
+    rows = C2 // narrow
+    direct = rows % 16 == 0 and wide * LANES == PACKED
+    pieces = (wide * narrow, rows, LANES) if direct else (1, C2, PACKED)
     output, term = pl.pallas_call(
         functools.partial(main_kernel, wide, scale),
+        in_specs=[fast] * 7,
+        out_specs=(pl.BlockSpec(memory_space=pl.ANY), fast),
         out_shape=(
             jax.ShapeDtypeStruct((1, 1, C2, cells_out), jnp.bfloat16),
-            jax.ShapeDtypeStruct((C2, PACKED), jnp.bfloat16),
+            jax.ShapeDtypeStruct(pieces, jnp.bfloat16),
         ),
         scratch_shapes=[
-            pltpu.VMEM((ROWS, CELLS), jnp.float32),
+            pltpu.VMEM((2, CIN * PLANES, CELLS), jnp.float32),
             pltpu.VMEM((8 * ROWS, WINDOW), jnp.bfloat16),
             pltpu.VMEM((9 * ROWS, PLANE), jnp.bfloat16),
             pltpu.VMEM((4 * C1, PLANE + 2 * LANES), jnp.bfloat16),
             pltpu.VMEM((9 * LANES, PLANE), jnp.bfloat16),
             pltpu.VMEM((2 * C2, PLANE), jnp.bfloat16),
+            pltpu.VMEM((1, 1, C2, cells_out), jnp.bfloat16),
+            pltpu.SemaphoreType.DMA,
         ],
-        compiler_params=pltpu.CompilerParams(vmem_limit_bytes=24 * 2**20),
+        compiler_params=pltpu.CompilerParams(vmem_limit_bytes=24 * MIB),
         name="local",
-    )(before, volumes, after, jnp.asarray(selection(), jnp.bfloat16), w1, w2, cotangent)
-    rows = C2 // narrow
-    owned = lax.all_to_all(term, "narrow", 0, 0, tiled=True)
-    partial = jnp.sum(owned.reshape(narrow, rows, PACKED).astype(jnp.float32), axis=0).astype(jnp.bfloat16)
-    copies = jnp.broadcast_to(partial[None], (wide, rows, PACKED))
-    parts = lax.all_to_all(copies, "wide", 0, 0, tiled=True)
+    )(before, mine, after, select, w1, w2, cot)
+    lanes = PACKED // wide
+    if not direct:
+        term = term.reshape(narrow, rows, wide, lanes).transpose(2, 0, 1, 3).reshape(wide * narrow, rows, lanes)
+    received = lax.all_to_all(term, ("wide", "narrow"), 0, 0, tiled=True)
+    owned = jnp.sum(received.astype(jnp.float32), axis=0)
+    parts = lax.all_to_all(jnp.broadcast_to(owned[None], (wide, rows, lanes)), "wide", 0, 0, tiled=True)
+    if not direct:
+        parts = parts.transpose(1, 0, 2).reshape(rows, PACKED // LANES, LANES).transpose(1, 0, 2)
     weight_grad = pl.pallas_call(
         finish_kernel,
         out_shape=jax.ShapeDtypeStruct((27, rows, C1), jnp.float32),
+        compiler_params=pltpu.CompilerParams(vmem_limit_bytes=8 * MIB),
         name="finish",
     )(parts)
     return (output, weight_grad)

time: 42.3 us -> 37.2 us (0.88)
  local copies, waits for them, and re-layouts: 6.18 us -> 0.01 us
  waiting for transfers between devices: 0.01 us -> 2.45 us
  Pallas kernels: 7.02 us -> 5.62 us
  blocking collectives: 24.1 us -> 24.6 us
    unnamed x11 -> x0, local copies, waits for them, and re-layouts: 4.71 us -> none
    ppermute x1, waiting for transfers between devices: 0.01 us -> 2.45 us  [body(): after = lax.ppermute(volumes, 'wide', [(k + 1, k) for k in range(wide - 1)])]
    reshape x2 -> x0, local copies, waits for them, and re-layouts: 1.45 us -> none  [body(): k1 = first_kernel.transpose(1, 0, 2).reshape(C1, 27 * CIN)]
    pallas_call x1, Pallas kernels: 1.74 us -> 0.79 us  [body(): pl.pallas_call(finish_kernel, out_shape=jax.ShapeDtypeStruct((27, rows, C...]
    pallas_call x2, Pallas kernels: 5.28 us -> 4.83 us  [the longest x1 3.04 us: body(): pl.pallas_call(functools.partial(main_kernel, wide, scale), in_specs=[fas...]
    all_to_all x2, blocking collectives: 24.1 us -> 24.6 us  [the longest x1 17.2 us: body(): received = lax.all_to_all(term, ('wide', 'narrow'), 0, 0, tiled=True)]
  transfers between devices with their start and end apart: 2 -> 2, of which waited for: 0 -> 1; matrix products, arithmetic and copies ran while one was open for 8% -> 0% of each run, Pallas kernels for 5% -> 5%
where the time goes in v3:
time: 37.2 us; the launch traced here: 37 us
  blocking collectives  24.6 us (66%)
  Pallas kernels  5.62 us (15%)
  starting transfers between devices  3.66 us (10%)
  waiting for transfers between devices  2.45 us (7%)
  between operations  0.68 us (2%)
    all_to_all x1, blocking collectives, body(): received = lax.all_to_all(term, ('wide', 'narrow'), 0, 0, tiled=True)  17.2 us
    all_to_all x1, blocking collectives, body(): lax.all_to_all(jnp.broadcast_to(owned[None], (wide, rows, lanes)), 'wide'...  7.4 us
    pallas_call x1, Pallas kernels, body(): pl.pallas_call(functools.partial(main_kernel, wide, scale), in_specs=[fas...  3.04 us
    ppermute x1, waiting for transfers between devices, body(): after = lax.ppermute(volumes, 'wide', [(k + 1, k) for k in range(wide - 1)])  2.45 us
    ppermute x1, starting transfers between devices, body(): lax.ppermute(volumes, 'wide', [(k, k + 1) for k in range(wide - 1)])  2.36 us
    pallas_call x1, Pallas kernels, body(): pl.pallas_call(prepare_kernel, in_specs=[pinned] * 6, out_specs=(fast,) *...  1.78 us
    ppermute x1, starting transfers between devices, body(): after = lax.ppermute(volumes, 'wide', [(k + 1, k) for k in range(wide - 1)])  1.29 us
    pallas_call x1, Pallas kernels, body(): pl.pallas_call(finish_kernel, out_shape=jax.ShapeDtypeStruct((27, rows, C...  0.79 us
  transfers between devices with their start and end apart: 2, of which 1 were waited for; matrix products, arithmetic and copies ran while one was open for 0% of the time, Pallas kernels for 5%

profile of v3, /device:TPU:0, one launch (start us, length us, event | category | flops | bytes accessed | tf_op | source)
XLA Modules:
  0.0 37.0 jit_solution(17059890732660705093)
XLA Ops:
  0.6 2.4 %collective-permute-start = (bf16[1,1,4,4,4096]{4,3,2,1,0:T(4,128)(2,1)}, bf16[1,1,4,4,4096]{4,3,2,1,0:T(4,128)(2,1)S(1)}, u32[]{:S(2)}, u32[]{:S(2)}) collective-permute-start(bf16[1,1,4,4,4096]{4,3,2,1,0:T(4,128)(2,1)} %own_hbm.1), channel_id=1, source_target_pairs={{0,4},{4,8},{8,12},{12,16},{16,20},{20,24},{24,28},{1,5},{5,9},{9,... | collective-permute-start | bytes 393224 | tf_op jit(solution)/shard_map/ppermute | solution.py:191
  3.0 1.3 %collective-permute-start.1 = (bf16[1,1,4,4,4096]{4,3,2,1,0:T(4,128)(2,1)}, bf16[1,1,4,4,4096]{4,3,2,1,0:T(4,128)(2,1)S(1)}, u32[]{:S(2)}, u32[]{:S(2)}) collective-permute-start(bf16[1,1,4,4,4096]{4,3,2,1,0:T(4,128)(2,1)} %own_hbm.1), channel_id=1, source_target_pairs={{4,0},{8,4},{12,8},{16,12},{20,16},{24,20},{28,24},{5,1},{9,5},{13... | collective-permute-start | bytes 393224 | tf_op jit(solution)/shard_map/ppermute | solution.py:192
  4.3 1.8 %prepare.1 = (bf16[128,432]{1,0:T(8,128)(2,1)S(1)}, bf16[128,1152]{1,0:T(8,128)(2,1)S(1)}, bf16[16,4096]{1,0:T(8,128)(2,1)S(1)}, bf16[640,1152]{1,0:T(8,128)(2,1)S(1)}, bf16[1,1,64,2048]{3,2,1,0:T(8,128)(2,1)S(1)}) custom-call(bf16[27,4,32]{2,1,0:T(4,128)(2,1)} %bitcast.3, bf16[108,2048]{1,0:T(8,128)(2,1)} %constant.6.clone.place_hbm, ...), custom_call_target="tpu_custom_call" | custom-call | flops 1000000000 | bytes 4194304 | tf_op jit(solution)/shard_map/prepare/pallas_call | solution.py:195
  6.1 0.0 collective-permute-done.before_ref
  6.1 2.5 %collective-permute-done.1.after_ref = bf16[1,1,4,4,4096]{4,3,2,1,0:T(4,128)(2,1)S(1)} collective-permute-done((bf16[1,1,4,4,4096]{4,3,2,1,0:T(4,128)(2,1)}, bf16[1,1,4,4,4096]{4,3,2,1,0:T(4,128)(2,1)S(1)}, u32[]{:S(2)}, u32[]{:S(2)}) %collective-permute-start.1) | collective-permute-done | bytes 131104 | tf_op jit(solution)/shard_map/ppermute | solution.py:192
  8.6 3.0 %local.1 = (bf16[1,1,64,2048]{3,2,1,0:T(8,128)(2,1)}, bf16[32,16,128]{2,1,0:T(8,128)(2,1)S(1)}) custom-call(bf16[1,1,4,4,4096]{4,3,2,1,0:T(4,128)(2,1)S(1)} %collective-permute-done.before_ref, bf16[16,4096]{1,0:T(8,128)(2,1)S(1)} %get-tuple-element.9.mine_ref, bf16[1,1,4,4,4096]{4,3,2,1,0:T(4,128)(2,1)S(1)} %collective-permute-done.1.after_ref, ...), custom_call_target="tpu_custom_call" | custom-call | tf_op jit(solution)/shard_map/local/pallas_call | solution.py:225
  11.6 17.2 %all_to_all.10 = bf16[32,16,128]{2,1,0:T(8,128)(2,1)S(1)} all-to-all(bf16[32,16,128]{2,1,0:T(8,128)(2,1)S(1)} %get-tuple-element.15), channel_id=1, replica_groups=mesh['wide'=8,'narrow'=4] {'wide','narrow'}, dimensions={0} | all-to-all | bytes 262144 | tf_op jit(solution)/shard_map/all_to_all | solution.py:249
  28.8 7.4 %all_to_all.11.parts_ref = f32[8,16,128]{2,1,0:T(8,128)S(1)} all-to-all(f32[8,16,128]{2,1,0:T(8,128)S(1)} %broadcast_in_dim.2), channel_id=1, replica_groups=mesh['wide'=8,'narrow'=4] {'wide'}, dimensions={0} | all-to-all | bytes 131072 | tf_op jit(solution)/shard_map/all_to_all | solution.py:251
  36.2 0.8 %finish.1 = f32[27,16,32]{2,1,0:T(8,128)} custom-call(f32[8,16,128]{2,1,0:T(8,128)S(1)} %all_to_all.11.parts_ref), custom_call_target="tpu_custom_call" | custom-call | tf_op jit(solution)/shard_map/finish/pallas_call | solution.py:254
  (2 shorter events, 0.0 us)
Async XLA Ops:
  0.6 5.5 %collective-permute-start = (bf16[1,1,4,4,4096]{4,3,2,1,0:T(4,128)(2,1)}, bf16[1,1,4,4,4096]{4,3,2,1,0:T(4,128)(2,1)S(1)}, u32[]{:S(2)}, u32[]{:S(2)}) collective-permute-start(bf16[1,1,4,4,4096]{4,3,2,1,0:T(4,128)(2,1)} %own_hbm.1), channel_id=1, source_target_pairs={{0,4},{4,8},{8,12},{12,16},{16,20},{20,24},{24,28},{1,5},{5,9},{9,... | collective-permute-start | bytes 393224 | tf_op jit(solution)/shard_map/ppermute | solution.py:191
  3.0 5.6 %collective-permute-start.1 = (bf16[1,1,4,4,4096]{4,3,2,1,0:T(4,128)(2,1)}, bf16[1,1,4,4,4096]{4,3,2,1,0:T(4,128)(2,1)S(1)}, u32[]{:S(2)}, u32[]{:S(2)}) collective-permute-start(bf16[1,1,4,4,4096]{4,3,2,1,0:T(4,128)(2,1)} %own_hbm.1), channel_id=1, source_target_pairs={{4,0},{8,4},{12,8},{16,12},{20,16},{24,20},{28,24},{5,1},{9,5},{13... | collective-permute-start | bytes 393224 | tf_op jit(solution)/shard_map/ppermute | solution.py:192

commit v4 on v3

--- a/solution.py
+++ b/solution.py
@@ -19,7 +19,7 @@
 LANES = 128
 ROWS = 3 * CIN * PLANES
 WINDOW = 640
-PACKED = 8 * LANES
+PACKED = 7 * LANES
 MIB = 2**20
 neg_slope = 0.3
 
@@ -52,13 +52,17 @@
 
 
 def slots():
-    return {9 * a + bc: (bc, a) if bc < 8 else (a, 3) for a in range(3) for bc in range(9)}
+    where = {}
+    free = [(tile, 3) for tile in range(6)]
+    for bc in range(9):
+        for a in range(3):
+            where[9 * a + bc] = (bc, a) if bc < 7 else free.pop(0)
+    return where
 
 
 def plane_rows(volume_ref, rows_ref):
     for i in range(CIN):
         rows_ref[PLANES * i : PLANES * (i + 1), :] = volume_ref[0, 0, i].astype(jnp.float32)
-    return rows_ref[...].astype(jnp.bfloat16)
 
 
 def prepare_kernel(
@@ -78,7 +82,8 @@
         upper = jnp.concatenate([blank] + taps, axis=0)
         w2_ref[:, here] = jnp.concatenate([lower, upper], axis=1).T
     copies[1].wait()
-    mine_ref[...] = plane_rows(own_ref, rows_ref)
+    plane_rows(own_ref, rows_ref)
+    mine_ref[...] = rows_ref[...].astype(jnp.bfloat16)
     copies[2].wait()
     for tap in range(27):
         k1_rows_ref[CIN * tap : CIN * (tap + 1), :] = k1_ref[tap].astype(jnp.float32)
@@ -94,10 +99,14 @@
 
 
 def main_kernel(
-    wide, scale, before_ref, mine_ref, after_ref, select_ref, w1_ref, w2_ref, cot_ref, out_hbm, grad_ref,
+    wide, scale, across_ref, mine_ref, within_ref, select_ref, w1_ref, w2_ref, cot_ref, out_hbm, grad_ref,
     rows_ref, window_ref, taps_ref, act_ref, shifted_ref, back_ref, out_ref, out_sem,
 ):
-    sources = (plane_rows(before_ref, rows_ref.at[0]), mine_ref[...], plane_rows(after_ref, rows_ref.at[1]))
+    place = lax.axis_index("wide")
+    odd = lax.rem(place, 2)
+    plane_rows(across_ref, rows_ref.at[odd])
+    plane_rows(within_ref, rows_ref.at[1 - odd])
+    sources = (rows_ref[0].astype(jnp.bfloat16), mine_ref[...], rows_ref[1].astype(jnp.bfloat16))
     for s, rows in enumerate(sources):
         for j in range(8):
             top = j * ROWS + 16 * s
@@ -117,7 +126,7 @@
                 taps_ref[(first + k) * ROWS : (first + k + 1) * ROWS, j * LANES : (j + 1) * LANES] = picked[
                     j * ROWS : (j + 1) * ROWS, k * LANES : (k + 1) * LANES
                 ]
-    inside = jnp.where(lax.axis_index("wide") < wide - 1, 1.0, 0.0)
+    inside = jnp.where(place < wide - 1, 1.0, 0.0)
     margin = jnp.zeros((4 * C1, LANES), jnp.bfloat16)
     act_ref[:, 0:LANES] = margin
     act_ref[:, LANES + PLANE :] = margin
@@ -162,25 +171,23 @@
         for k in range(count):
             tile = sums[:, k * LANES : (k + 1) * LANES]
             tiles.append((tile[0:C2] + pltpu.roll(tile[C2:], LANES - C1, 1)) * scale)
-    last = tiles.pop()
-    for a in range(3):
-        tiles[a] = jnp.where(group == 3, pltpu.roll(last, (3 - a) * C1, 1), tiles[a])
-    pieces, rows, lanes = grad_ref.shape
-    narrow = C2 // rows
-    for tile in range(8):
-        rounded = tiles[tile].astype(jnp.bfloat16)
-        for n in range(narrow):
-            part = rounded[n * rows : (n + 1) * rows]
-            if pieces > 1:
-                grad_ref[tile * narrow + n] = part
-            else:
-                grad_ref[0, n * rows : (n + 1) * rows, tile * LANES : (tile + 1) * LANES] = part
+    where = slots()
+    for bc in (7, 8):
+        for a in range(3):
+            tile, slot = where[9 * a + bc]
+            tiles[tile] = jnp.where(group == slot, pltpu.roll(tiles[bc], (slot - a) * C1, 1), tiles[tile])
+    for tile in range(7):
+        grad_ref[:, tile * LANES : (tile + 1) * LANES] = tiles[tile].astype(jnp.bfloat16)
     out_copy.wait()
 
 
 def finish_kernel(parts_ref, grad_ref):
-    for tap, (tile, place) in slots().items():
-        grad_ref[tap] = parts_ref[tile, :, place * C1 : (place + 1) * C1]
+    total = parts_ref[0].astype(jnp.float32)
+    for k in range(1, parts_ref.shape[0]):
+        total = total + parts_ref[k].astype(jnp.float32)
+    for tap, (tile, slot) in slots().items():
+        begin = tile * LANES + slot * C1
+        grad_ref[tap] = total[:, begin : begin + C1]
 
 
 def body(volumes, first_kernel, second_kernel, cotangent):
@@ -188,8 +195,8 @@
     narrow = lax.axis_size("narrow")
     cells_out = cotangent.shape[3]
     scale = 1.0 / math.sqrt(wide * narrow * cells_out)
-    before = lax.ppermute(volumes, "wide", [(k, k + 1) for k in range(wide - 1)])
-    after = lax.ppermute(volumes, "wide", [(k + 1, k) for k in range(wide - 1)])
+    across = lax.ppermute(volumes, "wide", [p for k in range(1, wide - 1, 2) for p in ((k, k + 1), (k + 1, k))])
+    within = lax.ppermute(volumes, "wide", [p for k in range(0, wide - 1, 2) for p in ((k, k + 1), (k + 1, k))])
     pinned = pl.BlockSpec(memory_space=pltpu.HBM)
     fast = pl.BlockSpec(memory_space=pltpu.VMEM)
     w1, w2, mine, select, cot = pl.pallas_call(
@@ -220,15 +227,13 @@
         volumes, jnp.asarray(selection(), jnp.bfloat16), cotangent,
     )))
     rows = C2 // narrow
-    direct = rows % 16 == 0 and wide * LANES == PACKED
-    pieces = (wide * narrow, rows, LANES) if direct else (1, C2, PACKED)
     output, term = pl.pallas_call(
         functools.partial(main_kernel, wide, scale),
         in_specs=[fast] * 7,
         out_specs=(pl.BlockSpec(memory_space=pl.ANY), fast),
         out_shape=(
             jax.ShapeDtypeStruct((1, 1, C2, cells_out), jnp.bfloat16),
-            jax.ShapeDtypeStruct(pieces, jnp.bfloat16),
+            jax.ShapeDtypeStruct((C2, PACKED), jnp.bfloat16),
         ),
         scratch_shapes=[
             pltpu.VMEM((2, CIN * PLANES, CELLS), jnp.float32),
@@ -242,15 +247,10 @@
         ],
         compiler_params=pltpu.CompilerParams(vmem_limit_bytes=24 * MIB),
         name="local",
-    )(before, mine, after, select, w1, w2, cot)
-    lanes = PACKED // wide
-    if not direct:
-        term = term.reshape(narrow, rows, wide, lanes).transpose(2, 0, 1, 3).reshape(wide * narrow, rows, lanes)
-    received = lax.all_to_all(term, ("wide", "narrow"), 0, 0, tiled=True)
-    owned = jnp.sum(received.astype(jnp.float32), axis=0)
-    parts = lax.all_to_all(jnp.broadcast_to(owned[None], (wide, rows, lanes)), "wide", 0, 0, tiled=True)
-    if not direct:
-        parts = parts.transpose(1, 0, 2).reshape(rows, PACKED // LANES, LANES).transpose(1, 0, 2)
+    )(across, mine, within, select, w1, w2, cot)
+    received = lax.all_to_all(term, "narrow", 0, 0, tiled=True)
+    owned = jnp.sum(received.reshape(narrow, rows, PACKED).astype(jnp.float32), axis=0).astype(jnp.bfloat16)
+    parts = lax.all_to_all(jnp.broadcast_to(owned[None], (wide, rows, PACKED)), "wide", 0, 0, tiled=True)
     weight_grad = pl.pallas_call(
         finish_kernel,
         out_shape=jax.ShapeDtypeStruct((27, rows, C1), jnp.float32),

time: 37.2 us -> 34.9 us (0.938)
  waiting for transfers between devices: 2.45 us -> 0.01 us
  blocking collectives: 24.6 us -> 23.1 us
  starting transfers between devices: 3.66 us -> 5.03 us
    ppermute x2, waiting for transfers between devices: 2.45 us -> 0.01 us  [the longest x1 0.01 us: body(): lax.ppermute(volumes, 'wide', [p for k in range(1, wide - 1, 2) for p in...]
    all_to_all x2, blocking collectives: 24.6 us -> 23.1 us  [the longest x1 12.4 us: body(): lax.all_to_all(jnp.broadcast_to(owned[None], (wide, rows, PACKED)), 'wide...]
    ppermute x2, starting transfers between devices: 3.66 us -> 5.03 us  [the longest x1 4.36 us: body(): lax.ppermute(volumes, 'wide', [p for k in range(0, wide - 1, 2) for p in...]
  transfers between devices with their start and end apart: 2 -> 2, of which waited for: 1 -> 0; matrix products, arithmetic and copies ran while one was open for 0% -> 0% of each run, Pallas kernels for 5% -> 5%
where the time goes in v4:
time: 34.9 us; the launch traced here: 34.6 us
  blocking collectives  23.1 us (66%)
  Pallas kernels  5.76 us (17%)
  starting transfers between devices  5.03 us (14%)
  between operations  0.68 us (2%)
    all_to_all x1, blocking collectives, body(): lax.all_to_all(jnp.broadcast_to(owned[None], (wide, rows, PACKED)), 'wide...  12.4 us
    all_to_all x1, blocking collectives, body(): received = lax.all_to_all(term, 'narrow', 0, 0, tiled=True)  10.7 us
    ppermute x1, starting transfers between devices, body(): lax.ppermute(volumes, 'wide', [p for k in range(0, wide - 1, 2) for p in...  4.36 us
    pallas_call x1, Pallas kernels, body(): pl.pallas_call(functools.partial(main_kernel, wide, scale), in_specs=[fas...  3.18 us
    pallas_call x1, Pallas kernels, body(): pl.pallas_call(prepare_kernel, in_specs=[pinned] * 6, out_specs=(fast,) *...  1.78 us
    pallas_call x1, Pallas kernels, body(): pl.pallas_call(finish_kernel, out_shape=jax.ShapeDtypeStruct((27, rows, C...  0.8 us
  transfers between devices with their start and end apart: 2, of which 0 were waited for; matrix products, arithmetic and copies ran while one was open for 0% of the time, Pallas kernels for 5%

profile of v4, /device:TPU:0, one launch (start us, length us, event | category | flops | bytes accessed | tf_op | source)
XLA Modules:
  0.0 34.6 jit_solution(18118972012293013254)
XLA Ops:
  0.6 0.7 %collective-permute-start = (bf16[1,1,4,4,4096]{4,3,2,1,0:T(4,128)(2,1)}, bf16[1,1,4,4,4096]{4,3,2,1,0:T(4,128)(2,1)S(1)}, u32[]{:S(2)}, u32[]{:S(2)}) collective-permute-start(bf16[1,1,4,4,4096]{4,3,2,1,0:T(4,128)(2,1)} %own_hbm.1), channel_id=1, source_target_pairs={{4,8},{8,4},{12,16},{16,12},{20,24},{24,20},{5,9},{9,5},{13,17},{1... | collective-permute-start | bytes 393224 | tf_op jit(solution)/shard_map/ppermute | solution.py:198
  1.3 4.4 %collective-permute-start.1 = (bf16[1,1,4,4,4096]{4,3,2,1,0:T(4,128)(2,1)}, bf16[1,1,4,4,4096]{4,3,2,1,0:T(4,128)(2,1)S(1)}, u32[]{:S(2)}, u32[]{:S(2)}) collective-permute-start(bf16[1,1,4,4,4096]{4,3,2,1,0:T(4,128)(2,1)} %own_hbm.1), channel_id=1, source_target_pairs={{0,4},{4,0},{8,12},{12,8},{16,20},{20,16},{24,28},{28,24},{1,5},{5... | collective-permute-start | bytes 393224 | tf_op jit(solution)/shard_map/ppermute | solution.py:199
  5.7 1.8 %prepare.1 = (bf16[128,432]{1,0:T(8,128)(2,1)S(1)}, bf16[128,1152]{1,0:T(8,128)(2,1)S(1)}, bf16[16,4096]{1,0:T(8,128)(2,1)S(1)}, bf16[640,1152]{1,0:T(8,128)(2,1)S(1)}, bf16[1,1,64,2048]{3,2,1,0:T(8,128)(2,1)S(1)}) custom-call(bf16[27,4,32]{2,1,0:T(4,128)(2,1)} %bitcast.5, bf16[108,2048]{1,0:T(8,128)(2,1)} %constant.7.clone.place_hbm, ...), custom_call_target="tpu_custom_call" | custom-call | flops 1000000000 | bytes 4194304 | tf_op jit(solution)/shard_map/prepare/pallas_call | solution.py:202
  7.5 0.0 collective-permute-done.across_ref
  7.5 0.0 collective-permute-done.1.within_ref
  7.5 3.2 %local.1 = (bf16[1,1,64,2048]{3,2,1,0:T(8,128)(2,1)}, bf16[64,896]{1,0:T(8,128)(2,1)S(1)}) custom-call(bf16[1,1,4,4,4096]{4,3,2,1,0:T(4,128)(2,1)S(1)} %collective-permute-done.across_ref, bf16[16,4096]{1,0:T(8,128)(2,1)S(1)} %get-tuple-element.9.mine_ref, bf16[1,1,4,4,4096]{4,3,2,1,0:T(4,128)(2,1)S(1)} %collective-permute-done.1.within_ref, ...), custom_call_target="tpu_custom_call" | custom-call | tf_op jit(solution)/shard_map/local/pallas_call | solution.py:230
  10.7 10.7 %all_to_all.14 = bf16[4,16,896]{2,1,0:T(8,128)(2,1)S(1)} all-to-all(bf16[4,16,896]{2,1,0:T(8,128)(2,1)S(1)} %bitcast.3), channel_id=1, replica_groups=mesh['wide'=8,'narrow'=4] {'narrow'}, dimensions={0} | all-to-all | bytes 229376 | tf_op jit(solution)/shard_map/all_to_all | solution.py:251
  21.4 12.4 %all_to_all.15.parts_ref = bf16[8,16,896]{2,1,0:T(8,128)(2,1)S(1)} all-to-all(bf16[8,16,896]{2,1,0:T(8,128)(2,1)S(1)} %broadcast_in_dim.2), channel_id=1, replica_groups=mesh['wide'=8,'narrow'=4] {'wide'}, dimensions={0} | all-to-all | bytes 458752 | tf_op jit(solution)/shard_map/all_to_all | solution.py:253
  33.8 0.8 %finish.1 = f32[27,16,32]{2,1,0:T(8,128)} custom-call(bf16[8,16,896]{2,1,0:T(8,128)(2,1)S(1)} %all_to_all.15.parts_ref), custom_call_target="tpu_custom_call" | custom-call | tf_op jit(solution)/shard_map/finish/pallas_call | solution.py:254
  (2 shorter events, 0.0 us)
Async XLA Ops:
  0.6 6.8 %collective-permute-start = (bf16[1,1,4,4,4096]{4,3,2,1,0:T(4,128)(2,1)}, bf16[1,1,4,4,4096]{4,3,2,1,0:T(4,128)(2,1)S(1)}, u32[]{:S(2)}, u32[]{:S(2)}) collective-permute-start(bf16[1,1,4,4,4096]{4,3,2,1,0:T(4,128)(2,1)} %own_hbm.1), channel_id=1, source_target_pairs={{4,8},{8,4},{12,16},{16,12},{20,24},{24,20},{5,9},{9,5},{13,17},{1... | collective-permute-start | bytes 393224 | tf_op jit(solution)/shard_map/ppermute | solution.py:198
  1.3 6.2 %collective-permute-start.1 = (bf16[1,1,4,4,4096]{4,3,2,1,0:T(4,128)(2,1)}, bf16[1,1,4,4,4096]{4,3,2,1,0:T(4,128)(2,1)S(1)}, u32[]{:S(2)}, u32[]{:S(2)}) collective-permute-start(bf16[1,1,4,4,4096]{4,3,2,1,0:T(4,128)(2,1)} %own_hbm.1), channel_id=1, source_target_pairs={{0,4},{4,0},{8,12},{12,8},{16,20},{20,16},{24,28},{28,24},{1,5},{5... | collective-permute-start | bytes 393224 | tf_op jit(solution)/shard_map/ppermute | solution.py:199

commit v5 on v4

--- a/solution.py
+++ b/solution.py
@@ -21,6 +21,7 @@
 WINDOW = 640
 PACKED = 7 * LANES
 MIB = 2**20
+WIDE = ("chip", "core")
 neg_slope = 0.3
 
 
@@ -102,8 +103,8 @@
     wide, scale, across_ref, mine_ref, within_ref, select_ref, w1_ref, w2_ref, cot_ref, out_hbm, grad_ref,
     rows_ref, window_ref, taps_ref, act_ref, shifted_ref, back_ref, out_ref, out_sem,
 ):
-    place = lax.axis_index("wide")
-    odd = lax.rem(place, 2)
+    place = 2 * lax.axis_index("chip") + lax.axis_index("core")
+    odd = lax.axis_index("core")
     plane_rows(across_ref, rows_ref.at[odd])
     plane_rows(within_ref, rows_ref.at[1 - odd])
     sources = (rows_ref[0].astype(jnp.bfloat16), mine_ref[...], rows_ref[1].astype(jnp.bfloat16))
@@ -182,21 +183,23 @@
 
 
 def finish_kernel(parts_ref, grad_ref):
-    total = parts_ref[0].astype(jnp.float32)
-    for k in range(1, parts_ref.shape[0]):
-        total = total + parts_ref[k].astype(jnp.float32)
-    for tap, (tile, slot) in slots().items():
-        begin = tile * LANES + slot * C1
-        grad_ref[tap] = total[:, begin : begin + C1]
+    wide, half, _ = parts_ref.shape
+    for core in range(2):
+        total = parts_ref[core].astype(jnp.float32)
+        for k in range(core + 2, wide, 2):
+            total = total + parts_ref[k].astype(jnp.float32)
+        for tap, (tile, slot) in slots().items():
+            begin = tile * LANES + slot * C1
+            grad_ref[tap, core * half : (core + 1) * half, :] = total[:, begin : begin + C1]
 
 
 def body(volumes, first_kernel, second_kernel, cotangent):
-    wide = lax.axis_size("wide")
+    wide = lax.axis_size(WIDE)
     narrow = lax.axis_size("narrow")
     cells_out = cotangent.shape[3]
     scale = 1.0 / math.sqrt(wide * narrow * cells_out)
-    across = lax.ppermute(volumes, "wide", [p for k in range(1, wide - 1, 2) for p in ((k, k + 1), (k + 1, k))])
-    within = lax.ppermute(volumes, "wide", [p for k in range(0, wide - 1, 2) for p in ((k, k + 1), (k + 1, k))])
+    across = lax.ppermute(volumes, WIDE, [p for k in range(1, wide - 1, 2) for p in ((k, k + 1), (k + 1, k))])
+    within = lax.ppermute(volumes, WIDE, [p for k in range(0, wide - 1, 2) for p in ((k, k + 1), (k + 1, k))])
     pinned = pl.BlockSpec(memory_space=pltpu.HBM)
     fast = pl.BlockSpec(memory_space=pltpu.VMEM)
     w1, w2, mine, select, cot = pl.pallas_call(
@@ -248,9 +251,10 @@
         compiler_params=pltpu.CompilerParams(vmem_limit_bytes=24 * MIB),
         name="local",
     )(across, mine, within, select, w1, w2, cot)
-    received = lax.all_to_all(term, "narrow", 0, 0, tiled=True)
-    owned = jnp.sum(received.reshape(narrow, rows, PACKED).astype(jnp.float32), axis=0).astype(jnp.bfloat16)
-    parts = lax.all_to_all(jnp.broadcast_to(owned[None], (wide, rows, PACKED)), "wide", 0, 0, tiled=True)
+    half = rows // 2
+    received = lax.all_to_all(term, ("narrow", "core"), 0, 0, tiled=True)
+    owned = jnp.sum(received.reshape(2 * narrow, half, PACKED).astype(jnp.float32), axis=0).astype(jnp.bfloat16)
+    parts = lax.all_to_all(jnp.broadcast_to(owned[None], (wide, half, PACKED)), WIDE, 0, 0, tiled=True)
     weight_grad = pl.pallas_call(
         finish_kernel,
         out_shape=jax.ShapeDtypeStruct((27, rows, C1), jnp.float32),
@@ -261,10 +265,12 @@
 
 
 def solution(mesh):
+    wide, narrow = mesh.devices.shape
+    split = jax.sharding.Mesh(mesh.devices.reshape(wide // 2, 2, narrow), ("chip", "core", "narrow"))
     return jax.shard_map(
         body,
-        mesh=mesh,
-        in_specs=(P("narrow", None, None, "wide", None), P(), P(), P("narrow", None, None, "wide")),
-        out_specs=(P("narrow", None, None, "wide"), P(None, "narrow", None)),
+        mesh=split,
+        in_specs=(P("narrow", None, None, WIDE, None), P(), P(), P("narrow", None, None, WIDE)),
+        out_specs=(P("narrow", None, None, WIDE), P(None, "narrow", None)),
         check_vma=False,
     )

time: 34.9 us -> 34.3 us (0.983)
  blocking collectives: 23.1 us -> 22.6 us
    all_to_all x2, blocking collectives: 23.1 us -> 22.6 us  [the longest x1 12.3 us: body(): received = lax.all_to_all(term, ('narrow', 'core'), 0, 0, tiled=True)]
where the time goes in v5:
time: 34.3 us; the launch traced here: 34.1 us
  blocking collectives  22.6 us (66%)
  Pallas kernels  5.75 us (17%)
  starting transfers between devices  5.03 us (15%)
  between operations  0.68 us (2%)
    all_to_all x1, blocking collectives, body(): received = lax.all_to_all(term, ('narrow', 'core'), 0, 0, tiled=True)  12.3 us
    all_to_all x1, blocking collectives, body(): lax.all_to_all(jnp.broadcast_to(owned[None], (wide, half, PACKED)), WIDE,...  10.2 us
    ppermute x1, starting transfers between devices, body(): lax.ppermute(volumes, WIDE, [p for k in range(0, wide - 1, 2) for p in ((...  4.36 us
    pallas_call x1, Pallas kernels, body(): pl.pallas_call(functools.partial(main_kernel, wide, scale), in_specs=[fas...  3.18 us
    pallas_call x1, Pallas kernels, body(): pl.pallas_call(prepare_kernel, in_specs=[pinned] * 6, out_specs=(fast,) *...  1.78 us
    pallas_call x1, Pallas kernels, body(): pl.pallas_call(finish_kernel, out_shape=jax.ShapeDtypeStruct((27, rows, C...  0.8 us
  transfers between devices with their start and end apart: 2, of which 0 were waited for; matrix products, arithmetic and copies ran while one was open for 0% of the time, Pallas kernels for 5%

profile of v5, /device:TPU:0, one launch (start us, length us, event | category | flops | bytes accessed | tf_op | source)
XLA Modules:
  0.0 34.1 jit_solution(16857907846864684498)
XLA Ops:
  0.6 0.7 %collective-permute-start = (bf16[1,1,4,4,4096]{4,3,2,1,0:T(4,128)(2,1)}, bf16[1,1,4,4,4096]{4,3,2,1,0:T(4,128)(2,1)S(1)}, u32[]{:S(2)}, u32[]{:S(2)}) collective-permute-start(bf16[1,1,4,4,4096]{4,3,2,1,0:T(4,128)(2,1)} %own_hbm.1), channel_id=1, source_target_pairs={{4,8},{8,4},{12,16},{16,12},{20,24},{24,20},{5,9},{9,5},{13,17},{1... | collective-permute-start | bytes 393224 | tf_op jit(solution)/shard_map/ppermute | solution.py:201
  1.3 4.4 %collective-permute-start.1 = (bf16[1,1,4,4,4096]{4,3,2,1,0:T(4,128)(2,1)}, bf16[1,1,4,4,4096]{4,3,2,1,0:T(4,128)(2,1)S(1)}, u32[]{:S(2)}, u32[]{:S(2)}) collective-permute-start(bf16[1,1,4,4,4096]{4,3,2,1,0:T(4,128)(2,1)} %own_hbm.1), channel_id=1, source_target_pairs={{0,4},{4,0},{8,12},{12,8},{16,20},{20,16},{24,28},{28,24},{1,5},{5... | collective-permute-start | bytes 393224 | tf_op jit(solution)/shard_map/ppermute | solution.py:202
  5.7 1.8 %prepare.1 = (bf16[128,432]{1,0:T(8,128)(2,1)S(1)}, bf16[128,1152]{1,0:T(8,128)(2,1)S(1)}, bf16[16,4096]{1,0:T(8,128)(2,1)S(1)}, bf16[640,1152]{1,0:T(8,128)(2,1)S(1)}, bf16[1,1,64,2048]{3,2,1,0:T(8,128)(2,1)S(1)}) custom-call(bf16[27,4,32]{2,1,0:T(4,128)(2,1)} %bitcast.5, bf16[108,2048]{1,0:T(8,128)(2,1)} %constant.7.clone.place_hbm, ...), custom_call_target="tpu_custom_call" | custom-call | flops 1000000000 | bytes 4194304 | tf_op jit(solution)/shard_map/prepare/pallas_call | solution.py:205
  7.5 0.0 collective-permute-done.across_ref
  7.5 0.0 collective-permute-done.1.within_ref
  7.5 3.2 %local.1 = (bf16[1,1,64,2048]{3,2,1,0:T(8,128)(2,1)}, bf16[64,896]{1,0:T(8,128)(2,1)S(1)}) custom-call(bf16[1,1,4,4,4096]{4,3,2,1,0:T(4,128)(2,1)S(1)} %collective-permute-done.across_ref, bf16[16,4096]{1,0:T(8,128)(2,1)S(1)} %get-tuple-element.9.mine_ref, bf16[1,1,4,4,4096]{4,3,2,1,0:T(4,128)(2,1)S(1)} %collective-permute-done.1.within_ref, ...), custom_call_target="tpu_custom_call" | custom-call | tf_op jit(solution)/shard_map/local/pallas_call | solution.py:233
  10.7 12.3 %all_to_all.14 = bf16[8,8,896]{2,1,0:T(8,128)(2,1)S(1)} all-to-all(bf16[8,8,896]{2,1,0:T(8,128)(2,1)S(1)} %bitcast.3), channel_id=1, replica_groups=mesh['chip'=4,'core'=2,'narrow'=4] {'narrow','core'}, dimensions={0} | all-to-all | bytes 229376 | tf_op jit(solution)/shard_map/all_to_all | solution.py:255
  23.0 10.2 %all_to_all.15.parts_ref = bf16[8,8,896]{2,1,0:T(8,128)(2,1)S(1)} all-to-all(bf16[8,8,896]{2,1,0:T(8,128)(2,1)S(1)} %broadcast_in_dim.2), channel_id=1, replica_groups=mesh['chip'=4,'core'=2,'narrow'=4] {'chip','core'}, dimensions={0} | all-to-all | bytes 229376 | tf_op jit(solution)/shard_map/all_to_all | solution.py:257
  33.3 0.8 %finish.1 = f32[27,16,32]{2,1,0:T(8,128)} custom-call(bf16[8,8,896]{2,1,0:T(8,128)(2,1)S(1)} %all_to_all.15.parts_ref), custom_call_target="tpu_custom_call" | custom-call | tf_op jit(solution)/shard_map/finish/pallas_call | solution.py:258
  (2 shorter events, 0.0 us)
Async XLA Ops:
  0.6 6.8 %collective-permute-start = (bf16[1,1,4,4,4096]{4,3,2,1,0:T(4,128)(2,1)}, bf16[1,1,4,4,4096]{4,3,2,1,0:T(4,128)(2,1)S(1)}, u32[]{:S(2)}, u32[]{:S(2)}) collective-permute-start(bf16[1,1,4,4,4096]{4,3,2,1,0:T(4,128)(2,1)} %own_hbm.1), channel_id=1, source_target_pairs={{4,8},{8,4},{12,16},{16,12},{20,24},{24,20},{5,9},{9,5},{13,17},{1... | collective-permute-start | bytes 393224 | tf_op jit(solution)/shard_map/ppermute | solution.py:201
  1.3 6.2 %collective-permute-start.1 = (bf16[1,1,4,4,4096]{4,3,2,1,0:T(4,128)(2,1)}, bf16[1,1,4,4,4096]{4,3,2,1,0:T(4,128)(2,1)S(1)}, u32[]{:S(2)}, u32[]{:S(2)}) collective-permute-start(bf16[1,1,4,4,4096]{4,3,2,1,0:T(4,128)(2,1)} %own_hbm.1), channel_id=1, source_target_pairs={{0,4},{4,0},{8,12},{12,8},{16,20},{20,16},{24,28},{28,24},{1,5},{5... | collective-permute-start | bytes 393224 | tf_op jit(solution)/shard_map/ppermute | solution.py:202

commit v6 on v5

v6 whole, which is shorter than its diff:
```python
import functools
import math

import jax
import jax.numpy as jnp
import numpy as np
from jax import lax
from jax.experimental import pallas as pl
from jax.experimental.pallas import tpu as pltpu
from jax.sharding import PartitionSpec as P

CIN = 4
C1 = 32
C2 = 64
PLANES = 4
CELLS = 4096
HALF = 32
PLANE = 1024
LANES = 128
ROWS = CIN * PLANES
CHUNK = 512
PACKED = 7 * LANES
MIB = 2**20
WIDE = ("chip", "core")
neg_slope = 0.3


def selection():
    table = np.zeros((CHUNK, 2, 2, 4, HALF), np.float32)
    for py in range(2):
        for px in range(2):
            for row in range(4):
                for col in range(HALF):
                    table[(2 * row + py) * 64 + 2 * col + px, py, px, row, col] = 1
    return table.reshape(CHUNK, CHUNK)


def placement():
    table = np.zeros((2, 27, CIN, 4, CHUNK), np.float32)
    for odd in range(2):
        for a in range(3):
            for bc in range(9):
                for i in range(CIN):
                    for q in range(4):
                        slab, plane = divmod(2 * q + a + 1, PLANES)
                        inner = i * PLANES + plane
                        if slab == 1:
                            column = bc * 2 * ROWS + inner
                        elif (slab == 0) == (odd == 1):
                            column = bc * 2 * ROWS + ROWS + inner
                        else:
                            column = 18 * ROWS + bc * ROWS + inner
                        table[odd, 9 * a + bc, i, q, column] = 1
    return table.reshape(2, 27 * CIN, 4 * CHUNK)


def leaky_relu(value):
    return jnp.where(value > 0, value, neg_slope * value)


def plane_rows(volume_ref, rows_ref):
    for i in range(CIN):
        rows_ref[PLANES * i : PLANES * (i + 1), :] = volume_ref[0, 0, i].astype(jnp.float32)


def column_masks():
    column = lax.broadcasted_iota(jnp.int32, (1, PLANE), 1) % HALF
    left_ok = jnp.where(column > 0, 1.0, 0.0).astype(jnp.bfloat16)
    right_ok = jnp.where(column < HALF - 1, 1.0, 0.0).astype(jnp.bfloat16)
    return left_ok, right_ok


def strided_taps(rows, select_ref, parity_ref, taps_ref):
    count = rows.shape[0]
    left_ok, _ = column_masks()
    chunks = jnp.concatenate([rows[:, CHUNK * j : CHUNK * (j + 1)] for j in range(8)], axis=0)
    for p in range(4):
        parity_ref[p, :, 0:LANES] = jnp.zeros((count, LANES), jnp.bfloat16)
    for py in range(2):
        parts = jnp.dot(
            chunks, select_ref[:, 256 * py : 256 * py + 256], preferred_element_type=jnp.float32
        ).astype(jnp.bfloat16)
        for px in range(2):
            for j in range(8):
                parity_ref[2 * py + px, :, LANES * (j + 1) : LANES * (j + 2)] = parts[
                    j * count : (j + 1) * count, px * LANES : (px + 1) * LANES
                ]
    for b in range(3):
        for c in range(3):
            begin = LANES - HALF * (b == 0) - (c == 0)
            part = parity_ref[2 * (b != 1) + (c != 1), :, begin : begin + PLANE]
            if c == 0:
                part = part * left_ok
            taps_ref[(3 * b + c) * count : (3 * b + c + 1) * count, :] = part


def shifted_taps(act_ref, shifted_ref):
    left_ok, right_ok = column_masks()
    for b in range(3):
        for c in range(3):
            begin = LANES + (b - 1) * HALF + (c - 1)
            part = act_ref[:, begin : begin + PLANE]
            if c == 0:
                part = part * left_ok
            if c == 2:
                part = part * right_ok
            shifted_ref[(3 * b + c) * 2 * C1 : (3 * b + c + 1) * 2 * C1, :] = part


def clear_margins(act_ref):
    margin = jnp.zeros((2 * C1, LANES), jnp.bfloat16)
    act_ref[:, 0:LANES] = margin
    act_ref[:, LANES + PLANE :] = margin


def prepare_kernel(
    k1_hbm, place_hbm, k2_hbm, select_hbm, cot_hbm, w1_near_ref, w1_far_ref, w2_ref, select_ref, cot_ref,
    k1_ref, place_ref, k2_ref, k1_rows_ref, sems,
):
    odd = lax.axis_index("core")
    moves = ((k1_hbm, k1_ref), (k2_hbm, k2_ref), (place_hbm.at[odd], place_ref), (select_hbm, select_ref), (cot_hbm, cot_ref))
    copies = [pltpu.make_async_copy(src, dst, sems.at[k]) for k, (src, dst) in enumerate(moves)]
    for copy in copies:
        copy.start()
    copies[0].wait()
    for tap in range(27):
        k1_rows_ref[CIN * tap : CIN * (tap + 1), :] = k1_ref[tap].astype(jnp.float32)
    copies[1].wait()
    blank = jnp.zeros((C1, C2), jnp.bfloat16)

    def stacked(bc, pair):
        k = [blank] + [k2_ref[9 * a + bc] for a in range(3)] + [blank]
        lower = jnp.concatenate(k[1 + 2 * pair : 3 + 2 * pair], axis=0)
        upper = jnp.concatenate(k[2 * pair : 2 + 2 * pair], axis=0)
        return jnp.concatenate([lower, upper], axis=1)

    for pair in range(2):
        for bc in range(0, 8, 2):
            both = jnp.concatenate([stacked(bc, pair), stacked(bc + 1, pair)], axis=0)
            w2_ref[pair, :, C2 * bc : C2 * bc + LANES] = both.T
        alone = jnp.concatenate([stacked(8, pair), jnp.zeros((2 * C1, LANES), jnp.bfloat16)], axis=0)
        w2_ref[pair, :, C2 * 8 : C2 * 9] = alone.T[:, 0 : 2 * C1]
    copies[2].wait()
    spread = lax.dot_general(
        k1_rows_ref[...].astype(jnp.bfloat16), place_ref[...],
        (((0,), (0,)), ((), ())), preferred_element_type=jnp.float32,
    ).astype(jnp.bfloat16)
    for q in range(4):
        rows = slice(q % 2 * C1, (q % 2 + 1) * C1)
        w1_near_ref[q // 2, rows, :] = spread[:, CHUNK * q : CHUNK * q + 18 * ROWS]
        w1_far_ref[q // 2, rows, :] = spread[:, CHUNK * q + 18 * ROWS : CHUNK * q + 27 * ROWS]
    copies[3].wait()
    copies[4].wait()


def near_kernel(
    own_ref, within_ref, select_ref, w1_ref, w2_ref, first_ref, shifted_ref, pre_ref, rows_ref, parity_ref, taps_ref, act_ref,
):
    odd = lax.axis_index("core")
    plane_rows(own_ref, rows_ref.at[0:ROWS])
    plane_rows(within_ref, rows_ref.at[ROWS : 2 * ROWS])
    strided_taps(rows_ref[...].astype(jnp.bfloat16), select_ref, parity_ref, taps_ref)
    clear_margins(act_ref)
    for n in range(4):
        here = slice(256 * n, 256 * n + 256)
        first_ref[:, here] = jnp.dot(w1_ref[odd], taps_ref[:, here], preferred_element_type=jnp.float32)
        complete = jnp.dot(w1_ref[1 - odd], taps_ref[:, here], preferred_element_type=jnp.float32)
        act_ref[:, LANES + 256 * n : LANES + 256 * n + 256] = leaky_relu(complete).astype(jnp.bfloat16)
    shifted_taps(act_ref, shifted_ref)
    for n in range(4):
        here = slice(256 * n, 256 * n + 256)
        pre_ref[:, here] = jnp.dot(w2_ref[1 - odd], shifted_ref[:, here], preferred_element_type=jnp.float32)


def far_kernel(
    chips, scale, across_ref, select_ref, w1_ref, w2_ref, cot_ref, first_ref, near_ref, pre_ref, out_hbm, grad_ref,
    rows_ref, parity_ref, taps_ref, act_ref, shifted_ref, back_ref, sums_ref, out_ref, out_sem,
):
    odd = lax.axis_index("core")
    last = (lax.axis_index("chip") == chips - 1) & (odd == 1)
    inside = jnp.where(last, 0.0, 1.0)
    plane_rows(across_ref, rows_ref)
    strided_taps(rows_ref[...].astype(jnp.bfloat16), select_ref, parity_ref, taps_ref)
    clear_margins(act_ref)
    for n in range(4):
        here = slice(256 * n, 256 * n + 256)
        first_pre = first_ref[:, here] + jnp.dot(w1_ref[odd], taps_ref[:, here], preferred_element_type=jnp.float32)
        first_act = leaky_relu(first_pre)
        there = slice(LANES + 256 * n, LANES + 256 * n + 256)
        act_ref[0:C1, there] = first_act[0:C1].astype(jnp.bfloat16)
        act_ref[C1:, there] = (first_act[C1:] * inside).astype(jnp.bfloat16)
    shifted_taps(act_ref, shifted_ref)
    for n in range(4):
        here = slice(256 * n, 256 * n + 256)
        pre = pre_ref[:, here] + jnp.dot(w2_ref[odd], shifted_ref[:, here], preferred_element_type=jnp.float32)
        output = leaky_relu(pre).astype(jnp.bfloat16)
        slope = jnp.where(pre > 0, 1.0, neg_slope)
        for z in range(2):
            cells = slice(z * PLANE + 256 * n, z * PLANE + 256 * n + 256)
            rows = slice(z * C2, (z + 1) * C2)
            out_ref[0, 0, :, cells] = output[rows]
            back_ref[rows, here] = (cot_ref[0, 0, :, cells].astype(jnp.float32) * slope[rows]).astype(jnp.bfloat16)
    out_copy = pltpu.make_async_copy(out_ref, out_hbm, out_sem)
    out_copy.start()
    for pair, ref in ((1 - odd, near_ref), (odd, shifted_ref)):
        sums_ref[pair] = lax.dot_general(
            ref[...], back_ref[...], (((1,), (1,)), ((), ())), preferred_element_type=jnp.float32
        )
    low = lax.broadcasted_iota(jnp.int32, (C1, LANES), 1) < C2

    def plane_sums(bc, q):
        begin = 2 * C1 * bc + C1 * (q % 2)
        return sums_ref[q // 2, begin : begin + C1, :]

    def two_taps(first, second):
        a, bc = divmod(first, 9)
        here, above = plane_sums(bc, a), pltpu.roll(plane_sums(bc, a + 1), C2, 1)
        if second > 26:
            return here + above
        a, bc = divmod(second, 9)
        there, beyond = pltpu.roll(plane_sums(bc, a), C2, 1), plane_sums(bc, a + 1)
        return jnp.where(low, here, there) + jnp.where(low, above, beyond)

    for block in range(4):
        tall = jnp.concatenate([two_taps(min(8 * block + g, 26), 8 * block + 4 + g) for g in range(4)], axis=0)
        flat = (tall * scale).T.astype(jnp.bfloat16)
        grad_ref[:, 2 * block * LANES : (2 * block + 1) * LANES] = flat[0:C2]
        if block < 3:
            grad_ref[:, (2 * block + 1) * LANES : (2 * block + 2) * LANES] = flat[C2:]
    out_copy.wait()


def finish_kernel(parts_ref, grad_ref):
    wide, half, _ = parts_ref.shape
    for core in range(2):
        total = parts_ref[core].astype(jnp.float32)
        for k in range(core + 2, wide, 2):
            total = total + parts_ref[k].astype(jnp.float32)
        for tap in range(27):
            grad_ref[tap, core * half : (core + 1) * half, :] = total[:, tap * C1 : (tap + 1) * C1]


def body(volumes, first_kernel, second_kernel, cotangent):
    wide = lax.axis_size(WIDE)
    narrow = lax.axis_size("narrow")
    cells_out = cotangent.shape[3]
    scale = 1.0 / math.sqrt(wide * narrow * cells_out)
    across = lax.ppermute(volumes, WIDE, [p for k in range(1, wide - 1, 2) for p in ((k, k + 1), (k + 1, k))])
    within = lax.ppermute(volumes, WIDE, [p for k in range(0, wide - 1, 2) for p in ((k, k + 1), (k + 1, k))])
    pinned = pl.BlockSpec(memory_space=pltpu.HBM)
    fast = pl.BlockSpec(memory_space=pltpu.VMEM)
    bf16 = functools.partial(jax.ShapeDtypeStruct, dtype=jnp.bfloat16)
    f32 = functools.partial(jax.ShapeDtypeStruct, dtype=jnp.float32)
    stored = (
        first_kernel.transpose(0, 2, 1), jnp.asarray(placement(), jnp.bfloat16), second_kernel.transpose(0, 2, 1),
        jnp.asarray(selection(), jnp.bfloat16), cotangent,
    )
    w1_near, w1_far, w2, select, cot = pl.pallas_call(
        prepare_kernel,
        in_specs=[pinned] * 5,
        out_specs=(fast,) * 5,
        out_shape=(
            bf16((2, 2 * C1, 18 * ROWS)), bf16((2, 2 * C1, 9 * ROWS)), bf16((2, 2 * C2, 18 * C1)),
            bf16((CHUNK, CHUNK)), bf16(cotangent.shape),
        ),
        scratch_shapes=[
            pltpu.VMEM((27, CIN, C1), jnp.bfloat16),
            pltpu.VMEM((27 * CIN, 4 * CHUNK), jnp.bfloat16),
            pltpu.VMEM((27, C1, C2), jnp.bfloat16),
            pltpu.VMEM((27 * CIN, C1), jnp.float32),
            pltpu.SemaphoreType.DMA((5,)),
        ],
        compiler_params=pltpu.CompilerParams(vmem_limit_bytes=12 * MIB),
        cost_estimate=pl.CostEstimate(flops=10**9, bytes_accessed=4 * MIB, transcendentals=0),
        name="prepare",
    )(*(pltpu.with_memory_space_constraint(x, pltpu.HBM) for x in stored))
    first, near, pre = pl.pallas_call(
        near_kernel,
        in_specs=[fast] * 5,
        out_specs=(fast,) * 3,
        out_shape=(f32((2 * C1, PLANE)), bf16((18 * C1, PLANE)), f32((2 * C2, PLANE))),
        scratch_shapes=[
            pltpu.VMEM((2 * ROWS, CELLS), jnp.float32),
            pltpu.VMEM((4, 2 * ROWS, LANES + PLANE), jnp.bfloat16),
            pltpu.VMEM((18 * ROWS, PLANE), jnp.bfloat16),
            pltpu.VMEM((2 * C1, PLANE + 2 * LANES), jnp.bfloat16),
        ],
        compiler_params=pltpu.CompilerParams(vmem_limit_bytes=16 * MIB),
        cost_estimate=pl.CostEstimate(flops=10**9, bytes_accessed=4 * MIB, transcendentals=0),
        name="near",
    )(volumes, within, select, w1_near, w2)
    rows = C2 // narrow
    output, term = pl.pallas_call(
        functools.partial(far_kernel, wide // 2, scale),
        in_specs=[fast] * 8,
        out_specs=(pl.BlockSpec(memory_space=pl.ANY), fast),
        out_shape=(bf16((1, 1, C2, cells_out)), bf16((C2, PACKED))),
        scratch_shapes=[
            pltpu.VMEM((ROWS, CELLS), jnp.float32),
            pltpu.VMEM((4, ROWS, LANES + PLANE), jnp.bfloat16),
            pltpu.VMEM((9 * ROWS, PLANE), jnp.bfloat16),
            pltpu.VMEM((2 * C1, PLANE + 2 * LANES), jnp.bfloat16),
            pltpu.VMEM((18 * C1, PLANE), jnp.bfloat16),
            pltpu.VMEM((2 * C2, PLANE), jnp.bfloat16),
            pltpu.VMEM((2, 18 * C1, LANES), jnp.float32),
            pltpu.VMEM((1, 1, C2, cells_out), jnp.bfloat16),
            pltpu.SemaphoreType.DMA,
        ],
        compiler_params=pltpu.CompilerParams(vmem_limit_bytes=16 * MIB),
        name="far",
    )(across, select, w1_far, w2, cot, first, near, pre)
    half = rows // 2
    received = lax.all_to_all(term, ("narrow", "core"), 0, 0, tiled=True)
    owned = jnp.sum(received.reshape(2 * narrow, half, PACKED).astype(jnp.float32), axis=0).astype(jnp.bfloat16)
    parts = lax.all_to_all(jnp.broadcast_to(owned[None], (wide, half, PACKED)), WIDE, 0, 0, tiled=True)
    weight_grad = pl.pallas_call(
        finish_kernel,
        out_shape=jax.ShapeDtypeStruct((27, rows, C1), jnp.float32),
        compiler_params=pltpu.CompilerParams(vmem_limit_bytes=8 * MIB),
        name="finish",
    )(parts)
    return (output, weight_grad)


def solution(mesh):
    wide, narrow = mesh.devices.shape
    split = jax.sharding.Mesh(mesh.devices.reshape(wide // 2, 2, narrow), ("chip", "core", "narrow"))
    return jax.shard_map(
        body,
        mesh=split,
        in_specs=(P("narrow", None, None, WIDE, None), P(), P(), P("narrow", None, None, WIDE)),
        out_specs=(P("narrow", None, None, WIDE), P(None, "narrow", None)),
        check_vma=False,
    )
```

time: 34.3 us -> 33.6 us (0.980)
  starting transfers between devices: 5.03 us -> 1.17 us
  blocking collectives: 22.6 us -> 25 us
  Pallas kernels: 5.75 us -> 6.5 us
    all_to_all x1, blocking collectives: 12.3 us -> 16.2 us  [body(): received = lax.all_to_all(term, ('narrow', 'core'), 0, 0, tiled=True)]
    ppermute x1, starting transfers between devices: 4.36 us -> 0.52 us  [body(): lax.ppermute(volumes, WIDE, [p for k in range(0, wide - 1, 2) for p in ((...]
    all_to_all x1, blocking collectives: 10.2 us -> 8.77 us  [body(): lax.all_to_all(jnp.broadcast_to(owned[None], (wide, half, PACKED)), WIDE,...]
    pallas_call x2 -> x3, Pallas kernels: 4.95 us -> 5.7 us  [the longest x1 2.67 us: body(): pl.pallas_call(functools.partial(far_kernel, wide // 2, scale), in_specs=...]
  transfers between devices with their start and end apart: 2 -> 2, of which waited for: 0 -> 0; matrix products, arithmetic and copies ran while one was open for 0% -> 0% of each run, Pallas kernels for 5% -> 9%
where the time goes in v6:
time: 33.6 us; the launch traced here: 33.4 us
  blocking collectives  25 us (74%)
  Pallas kernels  6.5 us (19%)
  starting transfers between devices  1.17 us (3%)
  between operations  0.7 us (2%)
    all_to_all x1, blocking collectives, body(): received = lax.all_to_all(term, ('narrow', 'core'), 0, 0, tiled=True)  16.2 us
    all_to_all x1, blocking collectives, body(): lax.all_to_all(jnp.broadcast_to(owned[None], (wide, half, PACKED)), WIDE,...  8.77 us
    pallas_call x1, Pallas kernels, body(): pl.pallas_call(functools.partial(far_kernel, wide // 2, scale), in_specs=...  2.67 us
    pallas_call x1, Pallas kernels, body(): pl.pallas_call(prepare_kernel, in_specs=[pinned] * 5, out_specs=(fast,) *...  1.7 us
    pallas_call x1, Pallas kernels, body(): pl.pallas_call(near_kernel, in_specs=[fast] * 5, out_specs=(fast,) * 3, o...  1.32 us
    pallas_call x1, Pallas kernels, body(): pl.pallas_call(finish_kernel, out_shape=jax.ShapeDtypeStruct((27, rows, C...  0.8 us
  transfers between devices with their start and end apart: 2, of which 0 were waited for; matrix products, arithmetic and copies ran while one was open for 0% of the time, Pallas kernels for 9%

profile of v6, /device:TPU:0, one launch (start us, length us, event | category | flops | bytes accessed | tf_op | source)
XLA Modules:
  0.0 33.4 jit_solution(2950707941015367518)
XLA Ops:
  0.6 0.5 %collective-permute-start.1 = (bf16[1,1,4,4,4096]{4,3,2,1,0:T(4,128)(2,1)}, bf16[1,1,4,4,4096]{4,3,2,1,0:T(4,128)(2,1)S(1)}, u32[]{:S(2)}, u32[]{:S(2)}) collective-permute-start(bf16[1,1,4,4,4096]{4,3,2,1,0:T(4,128)(2,1)} %own_ref.1), channel_id=1, source_target_pairs={{0,4},{4,0},{8,12},{12,8},{16,20},{20,16},{24,28},{28,24},{1,5},{5... | collective-permute-start | bytes 393224 | tf_op jit(solution)/shard_map/ppermute | solution.py:249
  1.1 0.7 %collective-permute-start = (bf16[1,1,4,4,4096]{4,3,2,1,0:T(4,128)(2,1)}, bf16[1,1,4,4,4096]{4,3,2,1,0:T(4,128)(2,1)S(1)}, u32[]{:S(2)}, u32[]{:S(2)}) collective-permute-start(bf16[1,1,4,4,4096]{4,3,2,1,0:T(4,128)(2,1)} %own_ref.1), channel_id=1, source_target_pairs={{4,8},{8,4},{12,16},{16,12},{20,24},{24,20},{5,9},{9,5},{13,17},{1... | collective-permute-start | bytes 393224 | tf_op jit(solution)/shard_map/ppermute | solution.py:248
  1.8 0.0 copy-start
  1.8 1.7 %prepare.1 = (bf16[2,64,288]{2,1,0:T(8,128)(2,1)S(1)}, bf16[2,64,144]{2,1,0:T(8,128)(2,1)S(1)}, bf16[2,128,576]{2,1,0:T(8,128)(2,1)S(1)}, bf16[512,512]{1,0:T(8,128)(2,1)S(1)}, bf16[1,1,64,2048]{3,2,1,0:T(8,128)(2,1)S(1)}) custom-call(bf16[27,4,32]{2,1,0:T(4,128)(2,1)} %bitcast.5, bf16[2,108,2048]{2,1,0:T(8,128)(2,1)} %constant.7.clone.place_hbm, ...), custom_call_target="tpu_custom_call" | custom-call | flops 1000000000 | bytes 4194304 | tf_op jit(solution)/shard_map/prepare/pallas_call | solution.py:258
  3.5 0.0 collective-permute-done.1.within_ref
  3.5 0.0 copy-done
  3.6 1.3 %near.1 = (f32[64,1024]{1,0:T(8,128)S(1)}, bf16[576,1024]{1,0:T(8,128)(2,1)S(1)}, f32[128,1024]{1,0:T(8,128)S(1)}) custom-call(bf16[1,1,4,4,4096]{4,3,2,1,0:T(4,128)(2,1)S(1)} %copy-done, bf16[1,1,4,4,4096]{4,3,2,1,0:T(4,128)(2,1)S(1)} %collective-permute-done.1.within_ref, bf16[512,512]{1,0:T(8,128)(2,1)S(1)} %get-tuple-element.12.select_ref, ...), custom_call_target="tpu_custom_call" | custom-call | flops 1000000000 | bytes 4194304 | tf_op jit(solution)/shard_map/near/pallas_call | solution.py:277
  4.9 0.0 collective-permute-done.across_ref
  4.9 2.7 %far.1 = (bf16[1,1,64,2048]{3,2,1,0:T(8,128)(2,1)}, bf16[64,896]{1,0:T(8,128)(2,1)S(1)}) custom-call(bf16[1,1,4,4,4096]{4,3,2,1,0:T(4,128)(2,1)S(1)} %collective-permute-done.across_ref, bf16[512,512]{1,0:T(8,128)(2,1)S(1)} %get-tuple-element.12.select_ref, bf16[2,64,144]{2,1,0:T(8,128)(2,1)S(1)} %get-tuple-element.13.w1_ref, ...), custom_call_target="tpu_custom_call" | custom-call | tf_op jit(solution)/shard_map/far/pallas_call | solution.py:293
  7.6 16.2 %all_to_all.14 = bf16[8,8,896]{2,1,0:T(8,128)(2,1)S(1)} all-to-all(bf16[8,8,896]{2,1,0:T(8,128)(2,1)S(1)} %bitcast.3), channel_id=1, replica_groups=mesh['chip'=4,'core'=2,'narrow'=4] {'narrow','core'}, dimensions={0} | all-to-all | bytes 229376 | tf_op jit(solution)/shard_map/all_to_all | solution.py:313
  23.8 8.8 %all_to_all.15.parts_ref = bf16[8,8,896]{2,1,0:T(8,128)(2,1)S(1)} all-to-all(bf16[8,8,896]{2,1,0:T(8,128)(2,1)S(1)} %broadcast_in_dim.2), channel_id=1, replica_groups=mesh['chip'=4,'core'=2,'narrow'=4] {'chip','core'}, dimensions={0} | all-to-all | bytes 229376 | tf_op jit(solution)/shard_map/all_to_all | solution.py:315
  32.6 0.8 %finish.1 = f32[27,16,32]{2,1,0:T(8,128)} custom-call(bf16[8,8,896]{2,1,0:T(8,128)(2,1)S(1)} %all_to_all.15.parts_ref), custom_call_target="tpu_custom_call" | custom-call | tf_op jit(solution)/shard_map/finish/pallas_call | solution.py:316
  (2 shorter events, 0.0 us)
Async XLA Ops:
  0.6 2.9 %collective-permute-start.1 = (bf16[1,1,4,4,4096]{4,3,2,1,0:T(4,128)(2,1)}, bf16[1,1,4,4,4096]{4,3,2,1,0:T(4,128)(2,1)S(1)}, u32[]{:S(2)}, u32[]{:S(2)}) collective-permute-start(bf16[1,1,4,4,4096]{4,3,2,1,0:T(4,128)(2,1)} %own_ref.1), channel_id=1, source_target_pairs={{0,4},{4,0},{8,12},{12,8},{16,20},{20,16},{24,28},{28,24},{1,5},{5... | collective-permute-start | bytes 393224 | tf_op jit(solution)/shard_map/ppermute | solution.py:249
  1.1 3.7 %collective-permute-start = (bf16[1,1,4,4,4096]{4,3,2,1,0:T(4,128)(2,1)}, bf16[1,1,4,4,4096]{4,3,2,1,0:T(4,128)(2,1)S(1)}, u32[]{:S(2)}, u32[]{:S(2)}) collective-permute-start(bf16[1,1,4,4,4096]{4,3,2,1,0:T(4,128)(2,1)} %own_ref.1), channel_id=1, source_target_pairs={{4,8},{8,4},{12,16},{16,12},{20,24},{24,20},{5,9},{9,5},{13,17},{1... | collective-permute-start | bytes 393224 | tf_op jit(solution)/shard_map/ppermute | solution.py:248
  1.8 1.7 %copy-start = (bf16[1,1,4,4,4096]{4,3,2,1,0:T(4,128)(2,1)S(1)}, bf16[1,1,4,4,4096]{4,3,2,1,0:T(4,128)(2,1)}, u32[]{:S(2)}) copy-start(bf16[1,1,4,4,4096]{4,3,2,1,0:T(4,128)(2,1)} %own_ref.1) | copy-start | bytes 393220

commit v7 on v6

--- a/solution.py
+++ b/solution.py
@@ -94,17 +94,35 @@
             taps_ref[(3 * b + c) * count : (3 * b + c + 1) * count, :] = part
 
 
-def shifted_taps(act_ref, shifted_ref):
+def shifted_columns(act_ref, columns_ref):
     left_ok, right_ok = column_masks()
-    for b in range(3):
-        for c in range(3):
-            begin = LANES + (b - 1) * HALF + (c - 1)
-            part = act_ref[:, begin : begin + PLANE]
-            if c == 0:
-                part = part * left_ok
-            if c == 2:
-                part = part * right_ok
-            shifted_ref[(3 * b + c) * 2 * C1 : (3 * b + c + 1) * 2 * C1, :] = part
+    for c in range(3):
+        begin = LANES + c - 1
+        part = act_ref[:, begin : begin + PLANE]
+        if c == 0:
+            part = part * left_ok
+        if c == 2:
+            part = part * right_ok
+        columns_ref[c * 2 * C1 : (c + 1) * 2 * C1, :] = part
+
+
+def second_layer(w2, columns_ref, rowed_ref):
+    blank = jnp.zeros((2 * C2, LANES), jnp.float32)
+    for b in (0, 2):
+        rowed_ref[b, :, 0:LANES] = blank
+        rowed_ref[b, :, LANES + PLANE :] = blank
+    for n in range(4):
+        sums = jnp.dot(w2, columns_ref[:, 256 * n : 256 * n + 256], preferred_element_type=jnp.float32)
+        for b in range(3):
+            rowed_ref[b, :, LANES + 256 * n : LANES + 256 * n + 256] = sums[b * 2 * C2 : (b + 1) * 2 * C2]
+
+
+def row_sum(rowed_ref, n):
+    total = rowed_ref[1, :, LANES + 256 * n : LANES + 256 * n + 256]
+    for b in (0, 2):
+        begin = LANES + HALF * (b - 1) + 256 * n
+        total = total + rowed_ref[b, :, begin : begin + 256]
+    return total
 
 
 def clear_margins(act_ref):
@@ -134,12 +152,14 @@
         upper = jnp.concatenate(k[2 * pair : 2 + 2 * pair], axis=0)
         return jnp.concatenate([lower, upper], axis=1)
 
-    for pair in range(2):
-        for bc in range(0, 8, 2):
-            both = jnp.concatenate([stacked(bc, pair), stacked(bc + 1, pair)], axis=0)
-            w2_ref[pair, :, C2 * bc : C2 * bc + LANES] = both.T
-        alone = jnp.concatenate([stacked(8, pair), jnp.zeros((2 * C1, LANES), jnp.bfloat16)], axis=0)
-        w2_ref[pair, :, C2 * 8 : C2 * 9] = alone.T[:, 0 : 2 * C1]
+    for b in range(3):
+        rows = slice(b * 2 * C2, (b + 1) * 2 * C2)
+        for pair in range(2):
+            both = jnp.concatenate([stacked(3 * b, pair), stacked(3 * b + 1, pair)], axis=0)
+            w2_ref[pair, rows, 0:LANES] = both.T
+        both = jnp.concatenate([stacked(3 * b + 2, 0), stacked(3 * b + 2, 1)], axis=0).T
+        for pair in range(2):
+            w2_ref[pair, rows, LANES : LANES + 2 * C1] = both[:, pair * 2 * C1 : (pair + 1) * 2 * C1]
     copies[2].wait()
     spread = lax.dot_general(
         k1_rows_ref[...].astype(jnp.bfloat16), place_ref[...],
@@ -154,7 +174,8 @@
 
 
 def near_kernel(
-    own_ref, within_ref, select_ref, w1_ref, w2_ref, first_ref, shifted_ref, pre_ref, rows_ref, parity_ref, taps_ref, act_ref,
+    own_ref, within_ref, select_ref, w1_ref, w2_ref, first_ref, columns_ref, pre_ref,
+    rows_ref, parity_ref, taps_ref, act_ref, rowed_ref,
 ):
     odd = lax.axis_index("core")
     plane_rows(own_ref, rows_ref.at[0:ROWS])
@@ -166,15 +187,15 @@
         first_ref[:, here] = jnp.dot(w1_ref[odd], taps_ref[:, here], preferred_element_type=jnp.float32)
         complete = jnp.dot(w1_ref[1 - odd], taps_ref[:, here], preferred_element_type=jnp.float32)
         act_ref[:, LANES + 256 * n : LANES + 256 * n + 256] = leaky_relu(complete).astype(jnp.bfloat16)
-    shifted_taps(act_ref, shifted_ref)
-    for n in range(4):
-        here = slice(256 * n, 256 * n + 256)
-        pre_ref[:, here] = jnp.dot(w2_ref[1 - odd], shifted_ref[:, here], preferred_element_type=jnp.float32)
+    shifted_columns(act_ref, columns_ref)
+    second_layer(w2_ref[1 - odd], columns_ref, rowed_ref)
+    for n in range(4):
+        pre_ref[:, 256 * n : 256 * n + 256] = row_sum(rowed_ref, n)
 
 
 def far_kernel(
     chips, scale, across_ref, select_ref, w1_ref, w2_ref, cot_ref, first_ref, near_ref, pre_ref, out_hbm, grad_ref,
-    rows_ref, parity_ref, taps_ref, act_ref, shifted_ref, back_ref, sums_ref, out_ref, out_sem,
+    rows_ref, parity_ref, taps_ref, act_ref, columns_ref, rowed_ref, back_ref, sums_ref, out_ref, out_sem,
 ):
     odd = lax.axis_index("core")
     last = (lax.axis_index("chip") == chips - 1) & (odd == 1)
@@ -189,28 +210,35 @@
         there = slice(LANES + 256 * n, LANES + 256 * n + 256)
         act_ref[0:C1, there] = first_act[0:C1].astype(jnp.bfloat16)
         act_ref[C1:, there] = (first_act[C1:] * inside).astype(jnp.bfloat16)
-    shifted_taps(act_ref, shifted_ref)
-    for n in range(4):
-        here = slice(256 * n, 256 * n + 256)
-        pre = pre_ref[:, here] + jnp.dot(w2_ref[odd], shifted_ref[:, here], preferred_element_type=jnp.float32)
+    shifted_columns(act_ref, columns_ref)
+    second_layer(w2_ref[odd], columns_ref, rowed_ref)
+    margin = jnp.zeros((HALF, LANES), jnp.bfloat16)
+    back_ref[0:HALF, :] = margin
+    back_ref[HALF + PLANE :, :] = margin
+    for n in range(4):
+        pre = pre_ref[:, 256 * n : 256 * n + 256] + row_sum(rowed_ref, n)
         output = leaky_relu(pre).astype(jnp.bfloat16)
         slope = jnp.where(pre > 0, 1.0, neg_slope)
+        backs = []
         for z in range(2):
             cells = slice(z * PLANE + 256 * n, z * PLANE + 256 * n + 256)
             rows = slice(z * C2, (z + 1) * C2)
             out_ref[0, 0, :, cells] = output[rows]
-            back_ref[rows, here] = (cot_ref[0, 0, :, cells].astype(jnp.float32) * slope[rows]).astype(jnp.bfloat16)
+            backs.append((cot_ref[0, 0, :, cells].astype(jnp.float32) * slope[rows]).astype(jnp.bfloat16))
+        back_ref[HALF + 256 * n : HALF + 256 * n + 256, :] = jnp.concatenate(backs, axis=0).T
     out_copy = pltpu.make_async_copy(out_ref, out_hbm, out_sem)
     out_copy.start()
-    for pair, ref in ((1 - odd, near_ref), (odd, shifted_ref)):
-        sums_ref[pair] = lax.dot_general(
-            ref[...], back_ref[...], (((1,), (1,)), ((), ())), preferred_element_type=jnp.float32
-        )
+    columns = jnp.concatenate([near_ref[...], columns_ref[...]], axis=0)
+    rowed_back = jnp.concatenate([back_ref[(2 - b) * HALF : (2 - b) * HALF + PLANE, :] for b in range(3)], axis=1)
+    sums = jnp.dot(columns, rowed_back, preferred_element_type=jnp.float32)
+    sums_ref[1 - odd] = sums[0 : 6 * C1]
+    sums_ref[odd] = sums[6 * C1 :]
     low = lax.broadcasted_iota(jnp.int32, (C1, LANES), 1) < C2
 
     def plane_sums(bc, q):
-        begin = 2 * C1 * bc + C1 * (q % 2)
-        return sums_ref[q // 2, begin : begin + C1, :]
+        b, c = divmod(bc, 3)
+        begin = 2 * C1 * c + C1 * (q % 2)
+        return sums_ref[q // 2, begin : begin + C1, b * LANES : (b + 1) * LANES]
 
     def two_taps(first, second):
         a, bc = divmod(first, 9)
@@ -260,7 +288,7 @@
         in_specs=[pinned] * 5,
         out_specs=(fast,) * 5,
         out_shape=(
-            bf16((2, 2 * C1, 18 * ROWS)), bf16((2, 2 * C1, 9 * ROWS)), bf16((2, 2 * C2, 18 * C1)),
+            bf16((2, 2 * C1, 18 * ROWS)), bf16((2, 2 * C1, 9 * ROWS)), bf16((2, 6 * C2, 6 * C1)),
             bf16((CHUNK, CHUNK)), bf16(cotangent.shape),
         ),
         scratch_shapes=[
@@ -278,12 +306,13 @@
         near_kernel,
         in_specs=[fast] * 5,
         out_specs=(fast,) * 3,
-        out_shape=(f32((2 * C1, PLANE)), bf16((18 * C1, PLANE)), f32((2 * C2, PLANE))),
+        out_shape=(f32((2 * C1, PLANE)), bf16((6 * C1, PLANE)), f32((2 * C2, PLANE))),
         scratch_shapes=[
             pltpu.VMEM((2 * ROWS, CELLS), jnp.float32),
             pltpu.VMEM((4, 2 * ROWS, LANES + PLANE), jnp.bfloat16),
             pltpu.VMEM((18 * ROWS, PLANE), jnp.bfloat16),
             pltpu.VMEM((2 * C1, PLANE + 2 * LANES), jnp.bfloat16),
+            pltpu.VMEM((3, 2 * C2, PLANE + 2 * LANES), jnp.float32),
         ],
         compiler_params=pltpu.CompilerParams(vmem_limit_bytes=16 * MIB),
         cost_estimate=pl.CostEstimate(flops=10**9, bytes_accessed=4 * MIB, transcendentals=0),
@@ -300,9 +329,10 @@
             pltpu.VMEM((4, ROWS, LANES + PLANE), jnp.bfloat16),
             pltpu.VMEM((9 * ROWS, PLANE), jnp.bfloat16),
             pltpu.VMEM((2 * C1, PLANE + 2 * LANES), jnp.bfloat16),
-            pltpu.VMEM((18 * C1, PLANE), jnp.bfloat16),
-            pltpu.VMEM((2 * C2, PLANE), jnp.bfloat16),
-            pltpu.VMEM((2, 18 * C1, LANES), jnp.float32),
+            pltpu.VMEM((6 * C1, PLANE), jnp.bfloat16),
+            pltpu.VMEM((3, 2 * C2, PLANE + 2 * LANES), jnp.float32),
+            pltpu.VMEM((PLANE + 2 * HALF, LANES), jnp.bfloat16),
+            pltpu.VMEM((2, 6 * C1, 3 * LANES), jnp.float32),
             pltpu.VMEM((1, 1, C2, cells_out), jnp.bfloat16),
             pltpu.SemaphoreType.DMA,
         ],

time: 33.6 us -> 33.2 us (0.988)
    pallas_call x1, Pallas kernels: 2.67 us -> 2.27 us  [body(): pl.pallas_call(functools.partial(far_kernel, wide // 2, scale), in_specs=...]
  transfers between devices with their start and end apart: 2 -> 2, of which waited for: 0 -> 0; matrix products, arithmetic and copies ran while one was open for 0% -> 0% of each run, Pallas kernels for 9% -> 10%
where the time goes in v7:
time: 33.2 us; the launch traced here: 33 us
  blocking collectives  24.7 us (74%)
  Pallas kernels  6.3 us (19%)
  starting transfers between devices  1.17 us (4%)
  between operations  0.7 us (2%)
    all_to_all x1, blocking collectives, body(): received = lax.all_to_all(term, ('narrow', 'core'), 0, 0, tiled=True)  16 us
    all_to_all x1, blocking collectives, body(): lax.all_to_all(jnp.broadcast_to(owned[None], (wide, half, PACKED)), WIDE,...  8.77 us
    pallas_call x1, Pallas kernels, body(): pl.pallas_call(functools.partial(far_kernel, wide // 2, scale), in_specs=...  2.27 us
    pallas_call x1, Pallas kernels, body(): pl.pallas_call(prepare_kernel, in_specs=[pinned] * 5, out_specs=(fast,) *...  1.85 us
    pallas_call x1, Pallas kernels, body(): pl.pallas_call(near_kernel, in_specs=[fast] * 5, out_specs=(fast,) * 3, o...  1.39 us
    pallas_call x1, Pallas kernels, body(): pl.pallas_call(finish_kernel, out_shape=jax.ShapeDtypeStruct((27, rows, C...  0.8 us
  transfers between devices with their start and end apart: 2, of which 0 were waited for; matrix products, arithmetic and copies ran while one was open for 0% of the time, Pallas kernels for 10%

profile of v7, /device:TPU:0, one launch (start us, length us, event | category | flops | bytes accessed | tf_op | source)
XLA Modules:
  0.0 33.0 jit_solution(6276048520126436739)
XLA Ops:
  0.6 0.5 %collective-permute-start.1 = (bf16[1,1,4,4,4096]{4,3,2,1,0:T(4,128)(2,1)}, bf16[1,1,4,4,4096]{4,3,2,1,0:T(4,128)(2,1)S(1)}, u32[]{:S(2)}, u32[]{:S(2)}) collective-permute-start(bf16[1,1,4,4,4096]{4,3,2,1,0:T(4,128)(2,1)} %own_ref.1), channel_id=1, source_target_pairs={{0,4},{4,0},{8,12},{12,8},{16,20},{20,16},{24,28},{28,24},{1,5},{5... | collective-permute-start | bytes 393224 | tf_op jit(solution)/shard_map/ppermute | solution.py:277
  1.1 0.7 %collective-permute-start = (bf16[1,1,4,4,4096]{4,3,2,1,0:T(4,128)(2,1)}, bf16[1,1,4,4,4096]{4,3,2,1,0:T(4,128)(2,1)S(1)}, u32[]{:S(2)}, u32[]{:S(2)}) collective-permute-start(bf16[1,1,4,4,4096]{4,3,2,1,0:T(4,128)(2,1)} %own_ref.1), channel_id=1, source_target_pairs={{4,8},{8,4},{12,16},{16,12},{20,24},{24,20},{5,9},{9,5},{13,17},{1... | collective-permute-start | bytes 393224 | tf_op jit(solution)/shard_map/ppermute | solution.py:276
  1.8 0.0 copy-start
  1.8 1.9 %prepare.1 = (bf16[2,64,288]{2,1,0:T(8,128)(2,1)S(1)}, bf16[2,64,144]{2,1,0:T(8,128)(2,1)S(1)}, bf16[2,384,192]{2,1,0:T(8,128)(2,1)S(1)}, bf16[512,512]{1,0:T(8,128)(2,1)S(1)}, bf16[1,1,64,2048]{3,2,1,0:T(8,128)(2,1)S(1)}) custom-call(bf16[27,4,32]{2,1,0:T(4,128)(2,1)} %bitcast.5, bf16[2,108,2048]{2,1,0:T(8,128)(2,1)} %constant.7.clone.place_hbm, ...), custom_call_target="tpu_custom_call" | custom-call | flops 1000000000 | bytes 4194304 | tf_op jit(solution)/shard_map/prepare/pallas_call | solution.py:286
  3.7 0.0 collective-permute-done.1.within_ref
  3.7 0.0 copy-done
  3.7 1.4 %near.1 = (f32[64,1024]{1,0:T(8,128)S(1)}, bf16[192,1024]{1,0:T(8,128)(2,1)S(1)}, f32[128,1024]{1,0:T(8,128)S(1)}) custom-call(bf16[1,1,4,4,4096]{4,3,2,1,0:T(4,128)(2,1)S(1)} %copy-done, bf16[1,1,4,4,4096]{4,3,2,1,0:T(4,128)(2,1)S(1)} %collective-permute-done.1.within_ref, bf16[512,512]{1,0:T(8,128)(2,1)S(1)} %get-tuple-element.12.select_ref, ...), custom_call_target="tpu_custom_call" | custom-call | flops 1000000000 | bytes 4194304 | tf_op jit(solution)/shard_map/near/pallas_call | solution.py:305
  5.1 0.0 collective-permute-done.across_ref
  5.1 2.3 %far.1 = (bf16[1,1,64,2048]{3,2,1,0:T(8,128)(2,1)}, bf16[64,896]{1,0:T(8,128)(2,1)S(1)}) custom-call(bf16[1,1,4,4,4096]{4,3,2,1,0:T(4,128)(2,1)S(1)} %collective-permute-done.across_ref, bf16[512,512]{1,0:T(8,128)(2,1)S(1)} %get-tuple-element.12.select_ref, bf16[2,64,144]{2,1,0:T(8,128)(2,1)S(1)} %get-tuple-element.13.w1_ref, ...), custom_call_target="tpu_custom_call" | custom-call | tf_op jit(solution)/shard_map/far/pallas_call | solution.py:322
  7.4 16.0 %all_to_all.14 = bf16[8,8,896]{2,1,0:T(8,128)(2,1)S(1)} all-to-all(bf16[8,8,896]{2,1,0:T(8,128)(2,1)S(1)} %bitcast.3), channel_id=1, replica_groups=mesh['chip'=4,'core'=2,'narrow'=4] {'narrow','core'}, dimensions={0} | all-to-all | bytes 229376 | tf_op jit(solution)/shard_map/all_to_all | solution.py:343
  23.4 8.8 %all_to_all.15.parts_ref = bf16[8,8,896]{2,1,0:T(8,128)(2,1)S(1)} all-to-all(bf16[8,8,896]{2,1,0:T(8,128)(2,1)S(1)} %broadcast_in_dim.2), channel_id=1, replica_groups=mesh['chip'=4,'core'=2,'narrow'=4] {'chip','core'}, dimensions={0} | all-to-all | bytes 229376 | tf_op jit(solution)/shard_map/all_to_all | solution.py:345
  32.2 0.8 %finish.1 = f32[27,16,32]{2,1,0:T(8,128)} custom-call(bf16[8,8,896]{2,1,0:T(8,128)(2,1)S(1)} %all_to_all.15.parts_ref), custom_call_target="tpu_custom_call" | custom-call | tf_op jit(solution)/shard_map/finish/pallas_call | solution.py:346
  (2 shorter events, 0.0 us)
Async XLA Ops:
  0.6 3.1 %collective-permute-start.1 = (bf16[1,1,4,4,4096]{4,3,2,1,0:T(4,128)(2,1)}, bf16[1,1,4,4,4096]{4,3,2,1,0:T(4,128)(2,1)S(1)}, u32[]{:S(2)}, u32[]{:S(2)}) collective-permute-start(bf16[1,1,4,4,4096]{4,3,2,1,0:T(4,128)(2,1)} %own_ref.1), channel_id=1, source_target_pairs={{0,4},{4,0},{8,12},{12,8},{16,20},{20,16},{24,28},{28,24},{1,5},{5... | collective-permute-start | bytes 393224 | tf_op jit(solution)/shard_map/ppermute | solution.py:277
  1.1 4.0 %collective-permute-start = (bf16[1,1,4,4,4096]{4,3,2,1,0:T(4,128)(2,1)}, bf16[1,1,4,4,4096]{4,3,2,1,0:T(4,128)(2,1)S(1)}, u32[]{:S(2)}, u32[]{:S(2)}) collective-permute-start(bf16[1,1,4,4,4096]{4,3,2,1,0:T(4,128)(2,1)} %own_ref.1), channel_id=1, source_target_pairs={{4,8},{8,4},{12,16},{16,12},{20,24},{24,20},{5,9},{9,5},{13,17},{1... | collective-permute-start | bytes 393224 | tf_op jit(solution)/shard_map/ppermute | solution.py:276
  1.8 1.9 %copy-start = (bf16[1,1,4,4,4096]{4,3,2,1,0:T(4,128)(2,1)S(1)}, bf16[1,1,4,4,4096]{4,3,2,1,0:T(4,128)(2,1)}, u32[]{:S(2)}) copy-start(bf16[1,1,4,4,4096]{4,3,2,1,0:T(4,128)(2,1)} %own_ref.1) | copy-start | bytes 393220

commit v8 on v7

--- a/solution.py
+++ b/solution.py
@@ -194,7 +194,7 @@
 
 
 def far_kernel(
-    chips, scale, across_ref, select_ref, w1_ref, w2_ref, cot_ref, first_ref, near_ref, pre_ref, out_hbm, grad_ref,
+    chips, narrow, scale, across_ref, select_ref, w1_ref, w2_ref, cot_ref, first_ref, near_ref, pre_ref, out_hbm, keep_ref, give_ref,
     rows_ref, parity_ref, taps_ref, act_ref, columns_ref, rowed_ref, back_ref, sums_ref, out_ref, out_sem,
 ):
     odd = lax.axis_index("core")
@@ -249,12 +249,23 @@
         there, beyond = pltpu.roll(plane_sums(bc, a), C2, 1), plane_sums(bc, a + 1)
         return jnp.where(low, here, there) + jnp.where(low, above, beyond)
 
+    half = C2 // (2 * narrow)
+
+    def put(tile, sums):
+        here = slice(tile * LANES, (tile + 1) * LANES)
+        for n in range(narrow):
+            lower = sums[2 * n * half : (2 * n + 1) * half]
+            upper = sums[(2 * n + 1) * half : (2 * n + 2) * half]
+            rows = slice(n * half, (n + 1) * half)
+            keep_ref[rows, here] = jnp.where(odd == 1, upper, lower).astype(jnp.bfloat16)
+            give_ref[rows, here] = jnp.where(odd == 1, lower, upper).astype(jnp.bfloat16)
+
     for block in range(4):
         tall = jnp.concatenate([two_taps(min(8 * block + g, 26), 8 * block + 4 + g) for g in range(4)], axis=0)
-        flat = (tall * scale).T.astype(jnp.bfloat16)
-        grad_ref[:, 2 * block * LANES : (2 * block + 1) * LANES] = flat[0:C2]
+        flat = (tall * scale).T
+        put(2 * block, flat[0:C2])
         if block < 3:
-            grad_ref[:, (2 * block + 1) * LANES : (2 * block + 2) * LANES] = flat[C2:]
+            put(2 * block + 1, flat[C2:])
     out_copy.wait()
 
 
@@ -274,7 +285,8 @@
     cells_out = cotangent.shape[3]
     scale = 1.0 / math.sqrt(wide * narrow * cells_out)
     across = lax.ppermute(volumes, WIDE, [p for k in range(1, wide - 1, 2) for p in ((k, k + 1), (k + 1, k))])
-    within = lax.ppermute(volumes, WIDE, [p for k in range(0, wide - 1, 2) for p in ((k, k + 1), (k + 1, k))])
+    pairs = [p for k in range(0, wide - 1, 2) for p in ((k, k + 1), (k + 1, k))]
+    within = lax.ppermute(volumes, WIDE, pairs)
     pinned = pl.BlockSpec(memory_space=pltpu.HBM)
     fast = pl.BlockSpec(memory_space=pltpu.VMEM)
     bf16 = functools.partial(jax.ShapeDtypeStruct, dtype=jnp.bfloat16)
@@ -319,11 +331,11 @@
         name="near",
     )(volumes, within, select, w1_near, w2)
     rows = C2 // narrow
-    output, term = pl.pallas_call(
-        functools.partial(far_kernel, wide // 2, scale),
+    output, keep, give = pl.pallas_call(
+        functools.partial(far_kernel, wide // 2, narrow, scale),
         in_specs=[fast] * 8,
-        out_specs=(pl.BlockSpec(memory_space=pl.ANY), fast),
-        out_shape=(bf16((1, 1, C2, cells_out)), bf16((C2, PACKED))),
+        out_specs=(pl.BlockSpec(memory_space=pl.ANY), fast, fast),
+        out_shape=(bf16((1, 1, C2, cells_out)), bf16((C2 // 2, PACKED)), bf16((C2 // 2, PACKED))),
         scratch_shapes=[
             pltpu.VMEM((ROWS, CELLS), jnp.float32),
             pltpu.VMEM((4, ROWS, LANES + PLANE), jnp.bfloat16),
@@ -340,8 +352,10 @@
         name="far",
     )(across, select, w1_far, w2, cot, first, near, pre)
     half = rows // 2
-    received = lax.all_to_all(term, ("narrow", "core"), 0, 0, tiled=True)
-    owned = jnp.sum(received.reshape(2 * narrow, half, PACKED).astype(jnp.float32), axis=0).astype(jnp.bfloat16)
+    got = lax.ppermute(give, WIDE, pairs)
+    term = (keep.astype(jnp.float32) + got.astype(jnp.float32)).astype(jnp.bfloat16)
+    received = lax.all_to_all(term, "narrow", 0, 0, tiled=True)
+    owned = jnp.sum(received.reshape(narrow, half, PACKED).astype(jnp.float32), axis=0).astype(jnp.bfloat16)
     parts = lax.all_to_all(jnp.broadcast_to(owned[None], (wide, half, PACKED)), WIDE, 0, 0, tiled=True)
     weight_grad = pl.pallas_call(
         finish_kernel,

time: 33.2 us -> 33.7 us (1.015)
  blocking collectives: 24.7 us -> 20.3 us
  starting transfers between devices: 1.17 us -> 5.18 us
  waiting for transfers between devices: 0.01 us -> 0.9 us
    all_to_all x1, blocking collectives: 16 us -> 11.6 us  [body(): received = lax.all_to_all(term, 'narrow', 0, 0, tiled=True)]
    ppermute x1 -> x2, starting transfers between devices: 0.52 us -> 4.52 us  [the longest x1 4 us: body(): got = lax.ppermute(give, WIDE, pairs)]
    ppermute x1 -> x2, waiting for transfers between devices: 0.01 us -> 0.89 us  [the longest x1 0.89 us: body(): got = lax.ppermute(give, WIDE, pairs)]
  transfers between devices with their start and end apart: 2 -> 3, of which waited for: 0 -> 1; matrix products, arithmetic and copies ran while one was open for 0% -> 0% of each run, Pallas kernels for 10% -> 10%
where the time goes in v8:
time: 33.7 us; the launch traced here: 33.4 us
  blocking collectives  20.3 us (60%)
  Pallas kernels  6.3 us (19%)
  starting transfers between devices  5.18 us (15%)
  waiting for transfers between devices  0.9 us (3%)
  between operations  0.71 us (2%)
    all_to_all x1, blocking collectives, body(): received = lax.all_to_all(term, 'narrow', 0, 0, tiled=True)  11.6 us
    all_to_all x1, blocking collectives, body(): lax.all_to_all(jnp.broadcast_to(owned[None], (wide, half, PACKED)), WIDE,...  8.72 us
    ppermute x1, starting transfers between devices, body(): got = lax.ppermute(give, WIDE, pairs)  4 us
    pallas_call x1, Pallas kernels, body(): pl.pallas_call(functools.partial(far_kernel, wide // 2, narrow, scale), i...  2.27 us
    pallas_call x1, Pallas kernels, body(): pl.pallas_call(prepare_kernel, in_specs=[pinned] * 5, out_specs=(fast,) *...  1.85 us
    pallas_call x1, Pallas kernels, body(): pl.pallas_call(near_kernel, in_specs=[fast] * 5, out_specs=(fast,) * 3, o...  1.39 us
    ppermute x1, waiting for transfers between devices, body(): got = lax.ppermute(give, WIDE, pairs)  0.89 us
    pallas_call x1, Pallas kernels, body(): pl.pallas_call(finish_kernel, out_shape=jax.ShapeDtypeStruct((27, rows, C...  0.8 us
  transfers between devices with their start and end apart: 3, of which 1 were waited for; matrix products, arithmetic and copies ran while one was open for 0% of the time, Pallas kernels for 10%

profile of v8, /device:TPU:0, one launch (start us, length us, event | category | flops | bytes accessed | tf_op | source)
XLA Modules:
  0.0 33.4 jit_solution(10069464506474932089)
XLA Ops:
  0.6 0.5 %collective-permute-start.1 = (bf16[1,1,4,4,4096]{4,3,2,1,0:T(4,128)(2,1)}, bf16[1,1,4,4,4096]{4,3,2,1,0:T(4,128)(2,1)S(1)}, u32[]{:S(2)}, u32[]{:S(2)}) collective-permute-start(bf16[1,1,4,4,4096]{4,3,2,1,0:T(4,128)(2,1)} %own_ref.1), channel_id=1, source_target_pairs={{0,4},{4,0},{8,12},{12,8},{16,20},{20,16},{24,28},{28,24},{1,5},{5... | collective-permute-start | bytes 393224 | tf_op jit(solution)/shard_map/ppermute | solution.py:289
  1.1 0.7 %collective-permute-start = (bf16[1,1,4,4,4096]{4,3,2,1,0:T(4,128)(2,1)}, bf16[1,1,4,4,4096]{4,3,2,1,0:T(4,128)(2,1)S(1)}, u32[]{:S(2)}, u32[]{:S(2)}) collective-permute-start(bf16[1,1,4,4,4096]{4,3,2,1,0:T(4,128)(2,1)} %own_ref.1), channel_id=1, source_target_pairs={{4,8},{8,4},{12,16},{16,12},{20,24},{24,20},{5,9},{9,5},{13,17},{1... | collective-permute-start | bytes 393224 | tf_op jit(solution)/shard_map/ppermute | solution.py:287
  1.8 0.0 copy-start
  1.8 1.9 %prepare.1 = (bf16[2,64,288]{2,1,0:T(8,128)(2,1)S(1)}, bf16[2,64,144]{2,1,0:T(8,128)(2,1)S(1)}, bf16[2,384,192]{2,1,0:T(8,128)(2,1)S(1)}, bf16[512,512]{1,0:T(8,128)(2,1)S(1)}, bf16[1,1,64,2048]{3,2,1,0:T(8,128)(2,1)S(1)}) custom-call(bf16[27,4,32]{2,1,0:T(4,128)(2,1)} %bitcast.5, bf16[2,108,2048]{2,1,0:T(8,128)(2,1)} %constant.7.clone.place_hbm, ...), custom_call_target="tpu_custom_call" | custom-call | flops 1000000000 | bytes 4194304 | tf_op jit(solution)/shard_map/prepare/pallas_call | solution.py:298
  3.7 0.0 collective-permute-done.1.within_ref
  3.7 0.0 copy-done
  3.7 1.4 %near.1 = (f32[64,1024]{1,0:T(8,128)S(1)}, bf16[192,1024]{1,0:T(8,128)(2,1)S(1)}, f32[128,1024]{1,0:T(8,128)S(1)}) custom-call(bf16[1,1,4,4,4096]{4,3,2,1,0:T(4,128)(2,1)S(1)} %copy-done, bf16[1,1,4,4,4096]{4,3,2,1,0:T(4,128)(2,1)S(1)} %collective-permute-done.1.within_ref, bf16[512,512]{1,0:T(8,128)(2,1)S(1)} %get-tuple-element.13.select_ref, ...), custom_call_target="tpu_custom_call" | custom-call | flops 1000000000 | bytes 4194304 | tf_op jit(solution)/shard_map/near/pallas_call | solution.py:317
  5.1 0.0 collective-permute-done.across_ref
  5.1 2.3 %far.1 = (bf16[1,1,64,2048]{3,2,1,0:T(8,128)(2,1)}, bf16[32,896]{1,0:T(8,128)(2,1)S(1)}, bf16[32,896]{1,0:T(8,128)(2,1)S(1)}) custom-call(bf16[1,1,4,4,4096]{4,3,2,1,0:T(4,128)(2,1)S(1)} %collective-permute-done.across_ref, bf16[512,512]{1,0:T(8,128)(2,1)S(1)} %get-tuple-element.13.select_ref, bf16[2,64,144]{2,1,0:T(8,128)(2,1)S(1)} %get-tuple-element.14.w1_ref, ...), custom_call_target="tpu_custom_call" | custom-call | tf_op jit(solution)/shard_map/far/pallas_call | solution.py:334
  7.4 4.0 %collective-permute-start.2 = (bf16[32,896]{1,0:T(8,128)(2,1)S(1)}, bf16[32,896]{1,0:T(8,128)(2,1)S(1)}, u32[]{:S(2)}, u32[]{:S(2)}) collective-permute-start(bf16[32,896]{1,0:T(8,128)(2,1)S(1)} %get-tuple-element.23), channel_id=1, source_target_pairs={{0,4},{4,0},{8,12},{12,8},{16,20},{20,16},{24,28},{28,24},{1,5},{5... | collective-permute-start | bytes 172040 | tf_op jit(solution)/shard_map/ppermute | solution.py:355
  11.4 0.9 %collective-permute-done.2 = bf16[32,896]{1,0:T(8,128)(2,1)S(1)} collective-permute-done((bf16[32,896]{1,0:T(8,128)(2,1)S(1)}, bf16[32,896]{1,0:T(8,128)(2,1)S(1)}, u32[]{:S(2)}, u32[]{:S(2)}) %collective-permute-start.2) | collective-permute-done | bytes 57376 | tf_op jit(solution)/shard_map/ppermute | solution.py:355
  12.3 11.6 %all_to_all.14 = bf16[4,8,896]{2,1,0:T(8,128)(2,1)S(1)} all-to-all(bf16[4,8,896]{2,1,0:T(8,128)(2,1)S(1)} %fusion), channel_id=1, replica_groups=mesh['chip'=4,'core'=2,'narrow'=4] {'narrow'}, dimensions={0} | all-to-all | bytes 114688 | tf_op jit(solution)/shard_map/all_to_all | solution.py:357
  23.9 8.7 %all_to_all.15.parts_ref = bf16[8,8,896]{2,1,0:T(8,128)(2,1)S(1)} all-to-all(bf16[8,8,896]{2,1,0:T(8,128)(2,1)S(1)} %broadcast_in_dim.2), channel_id=1, replica_groups=mesh['chip'=4,'core'=2,'narrow'=4] {'chip','core'}, dimensions={0} | all-to-all | bytes 229376 | tf_op jit(solution)/shard_map/all_to_all | solution.py:359
  32.6 0.8 %finish.1 = f32[27,16,32]{2,1,0:T(8,128)} custom-call(bf16[8,8,896]{2,1,0:T(8,128)(2,1)S(1)} %all_to_all.15.parts_ref), custom_call_target="tpu_custom_call" | custom-call | tf_op jit(solution)/shard_map/finish/pallas_call | solution.py:360
  (3 shorter events, 0.0 us)
Async XLA Ops:
  0.6 3.1 %collective-permute-start.1 = (bf16[1,1,4,4,4096]{4,3,2,1,0:T(4,128)(2,1)}, bf16[1,1,4,4,4096]{4,3,2,1,0:T(4,128)(2,1)S(1)}, u32[]{:S(2)}, u32[]{:S(2)}) collective-permute-start(bf16[1,1,4,4,4096]{4,3,2,1,0:T(4,128)(2,1)} %own_ref.1), channel_id=1, source_target_pairs={{0,4},{4,0},{8,12},{12,8},{16,20},{20,16},{24,28},{28,24},{1,5},{5... | collective-permute-start | bytes 393224 | tf_op jit(solution)/shard_map/ppermute | solution.py:289
  1.1 4.0 %collective-permute-start = (bf16[1,1,4,4,4096]{4,3,2,1,0:T(4,128)(2,1)}, bf16[1,1,4,4,4096]{4,3,2,1,0:T(4,128)(2,1)S(1)}, u32[]{:S(2)}, u32[]{:S(2)}) collective-permute-start(bf16[1,1,4,4,4096]{4,3,2,1,0:T(4,128)(2,1)} %own_ref.1), channel_id=1, source_target_pairs={{4,8},{8,4},{12,16},{16,12},{20,24},{24,20},{5,9},{9,5},{13,17},{1... | collective-permute-start | bytes 393224 | tf_op jit(solution)/shard_map/ppermute | solution.py:287
  1.8 1.9 %copy-start = (bf16[1,1,4,4,4096]{4,3,2,1,0:T(4,128)(2,1)S(1)}, bf16[1,1,4,4,4096]{4,3,2,1,0:T(4,128)(2,1)}, u32[]{:S(2)}) copy-start(bf16[1,1,4,4,4096]{4,3,2,1,0:T(4,128)(2,1)} %own_ref.1) | copy-start | bytes 393220
  7.4 4.9 %collective-permute-start.2 = (bf16[32,896]{1,0:T(8,128)(2,1)S(1)}, bf16[32,896]{1,0:T(8,128)(2,1)S(1)}, u32[]{:S(2)}, u32[]{:S(2)}) collective-permute-start(bf16[32,896]{1,0:T(8,128)(2,1)S(1)} %get-tuple-element.23), channel_id=1, source_target_pairs={{0,4},{4,0},{8,12},{12,8},{16,20},{20,16},{24,28},{28,24},{1,5},{5... | collective-permute-start | bytes 172040 | tf_op jit(solution)/shard_map/ppermute | solution.py:355

commit v9 on v7

--- a/solution.py
+++ b/solution.py
@@ -342,7 +342,7 @@
     half = rows // 2
     received = lax.all_to_all(term, ("narrow", "core"), 0, 0, tiled=True)
     owned = jnp.sum(received.reshape(2 * narrow, half, PACKED).astype(jnp.float32), axis=0).astype(jnp.bfloat16)
-    parts = lax.all_to_all(jnp.broadcast_to(owned[None], (wide, half, PACKED)), WIDE, 0, 0, tiled=True)
+    parts = lax.all_gather(owned, WIDE)
     weight_grad = pl.pallas_call(
         finish_kernel,
         out_shape=jax.ShapeDtypeStruct((27, rows, C1), jnp.float32),

time: 33.2 us -> 34.5 us (1.039)
  blocking collectives: 24.7 us -> 26 us
    all_gather x0 -> x1, blocking collectives: none -> 10.1 us  [body(): parts = lax.all_gather(owned, WIDE)]
    all_to_all x1 -> x0, blocking collectives: 8.77 us -> none  [body(): lax.all_to_all(jnp.broadcast_to(owned[None], (wide, half, PACKED)), WIDE,...]
  transfers between devices with their start and end apart: 2 -> 2, of which waited for: 0 -> 0; matrix products, arithmetic and copies ran while one was open for 0% -> 0% of each run, Pallas kernels for 10% -> 9%
where the time goes in v9:
time: 34.5 us; the launch traced here: 34.2 us
  blocking collectives  26 us (75%)
  Pallas kernels  6.3 us (18%)
  starting transfers between devices  1.17 us (3%)
  between operations  0.7 us (2%)
    all_to_all x1, blocking collectives, body(): received = lax.all_to_all(term, ('narrow', 'core'), 0, 0, tiled=True)  16 us
    all_gather x1, blocking collectives, body(): parts = lax.all_gather(owned, WIDE)  10.1 us
    pallas_call x1, Pallas kernels, body(): pl.pallas_call(functools.partial(far_kernel, wide // 2, scale), in_specs=...  2.27 us
    pallas_call x1, Pallas kernels, body(): pl.pallas_call(prepare_kernel, in_specs=[pinned] * 5, out_specs=(fast,) *...  1.85 us
    pallas_call x1, Pallas kernels, body(): pl.pallas_call(near_kernel, in_specs=[fast] * 5, out_specs=(fast,) * 3, o...  1.39 us
    pallas_call x1, Pallas kernels, body(): pl.pallas_call(finish_kernel, out_shape=jax.ShapeDtypeStruct((27, rows, C...  0.8 us
  transfers between devices with their start and end apart: 2, of which 0 were waited for; matrix products, arithmetic and copies ran while one was open for 0% of the time, Pallas kernels for 9%

profile of v9, /device:TPU:0, one launch (start us, length us, event | category | flops | bytes accessed | tf_op | source)
XLA Modules:
  0.0 34.2 jit_solution(2488767368002047847)
XLA Ops:
  0.6 0.5 %collective-permute-start.1 = (bf16[1,1,4,4,4096]{4,3,2,1,0:T(4,128)(2,1)}, bf16[1,1,4,4,4096]{4,3,2,1,0:T(4,128)(2,1)S(1)}, u32[]{:S(2)}, u32[]{:S(2)}) collective-permute-start(bf16[1,1,4,4,4096]{4,3,2,1,0:T(4,128)(2,1)} %own_ref.1), channel_id=1, source_target_pairs={{0,4},{4,0},{8,12},{12,8},{16,20},{20,16},{24,28},{28,24},{1,5},{5... | collective-permute-start | bytes 393224 | tf_op jit(solution)/shard_map/ppermute | solution.py:277
  1.1 0.7 %collective-permute-start = (bf16[1,1,4,4,4096]{4,3,2,1,0:T(4,128)(2,1)}, bf16[1,1,4,4,4096]{4,3,2,1,0:T(4,128)(2,1)S(1)}, u32[]{:S(2)}, u32[]{:S(2)}) collective-permute-start(bf16[1,1,4,4,4096]{4,3,2,1,0:T(4,128)(2,1)} %own_ref.1), channel_id=1, source_target_pairs={{4,8},{8,4},{12,16},{16,12},{20,24},{24,20},{5,9},{9,5},{13,17},{1... | collective-permute-start | bytes 393224 | tf_op jit(solution)/shard_map/ppermute | solution.py:276
  1.8 0.0 copy-start
  1.8 1.9 %prepare.1 = (bf16[2,64,288]{2,1,0:T(8,128)(2,1)S(1)}, bf16[2,64,144]{2,1,0:T(8,128)(2,1)S(1)}, bf16[2,384,192]{2,1,0:T(8,128)(2,1)S(1)}, bf16[512,512]{1,0:T(8,128)(2,1)S(1)}, bf16[1,1,64,2048]{3,2,1,0:T(8,128)(2,1)S(1)}) custom-call(bf16[27,4,32]{2,1,0:T(4,128)(2,1)} %bitcast.7, bf16[2,108,2048]{2,1,0:T(8,128)(2,1)} %constant.7.clone.place_hbm, ...), custom_call_target="tpu_custom_call" | custom-call | flops 1000000000 | bytes 4194304 | tf_op jit(solution)/shard_map/prepare/pallas_call | solution.py:286
  3.7 0.0 collective-permute-done.1.within_ref
  3.7 0.0 copy-done
  3.7 1.4 %near.1 = (f32[64,1024]{1,0:T(8,128)S(1)}, bf16[192,1024]{1,0:T(8,128)(2,1)S(1)}, f32[128,1024]{1,0:T(8,128)S(1)}) custom-call(bf16[1,1,4,4,4096]{4,3,2,1,0:T(4,128)(2,1)S(1)} %copy-done, bf16[1,1,4,4,4096]{4,3,2,1,0:T(4,128)(2,1)S(1)} %collective-permute-done.1.within_ref, bf16[512,512]{1,0:T(8,128)(2,1)S(1)} %get-tuple-element.12.select_ref, ...), custom_call_target="tpu_custom_call" | custom-call | flops 1000000000 | bytes 4194304 | tf_op jit(solution)/shard_map/near/pallas_call | solution.py:305
  5.1 0.0 collective-permute-done.across_ref
  5.1 2.3 %far.1 = (bf16[1,1,64,2048]{3,2,1,0:T(8,128)(2,1)}, bf16[64,896]{1,0:T(8,128)(2,1)S(1)}) custom-call(bf16[1,1,4,4,4096]{4,3,2,1,0:T(4,128)(2,1)S(1)} %collective-permute-done.across_ref, bf16[512,512]{1,0:T(8,128)(2,1)S(1)} %get-tuple-element.12.select_ref, bf16[2,64,144]{2,1,0:T(8,128)(2,1)S(1)} %get-tuple-element.13.w1_ref, ...), custom_call_target="tpu_custom_call" | custom-call | tf_op jit(solution)/shard_map/far/pallas_call | solution.py:322
  7.4 16.0 %all_to_all.9 = bf16[8,8,896]{2,1,0:T(8,128)(2,1)S(1)} all-to-all(bf16[8,8,896]{2,1,0:T(8,128)(2,1)S(1)} %bitcast.5), channel_id=1, replica_groups=mesh['chip'=4,'core'=2,'narrow'=4] {'narrow','core'}, dimensions={0} | all-to-all | bytes 229376 | tf_op jit(solution)/shard_map/all_to_all | solution.py:343
  23.4 10.1 %all-gather = bf16[64,896]{1,0:T(8,128)(2,1)S(1)} all-gather(bf16[8,896]{1,0:T(8,128)(2,1)S(1)} %reduce_sum.12), channel_id=2, replica_groups=mesh['chip'=4,'core'=2,'narrow'=4] {'chip','core'}, dimensions={0}, use_global_device_ids=true | all-gather | bytes 129024 | tf_op jit(solution)/shard_map/all_gather | solution.py:345
  33.4 0.8 %finish.1 = f32[27,16,32]{2,1,0:T(8,128)} custom-call(bf16[8,8,896]{2,1,0:T(8,128)(2,1)S(1)} %bitcast.4), custom_call_target="tpu_custom_call" | custom-call | tf_op jit(solution)/shard_map/finish/pallas_call | solution.py:346
  (1 shorter events, 0.0 us)
Async XLA Ops:
  0.6 3.1 %collective-permute-start.1 = (bf16[1,1,4,4,4096]{4,3,2,1,0:T(4,128)(2,1)}, bf16[1,1,4,4,4096]{4,3,2,1,0:T(4,128)(2,1)S(1)}, u32[]{:S(2)}, u32[]{:S(2)}) collective-permute-start(bf16[1,1,4,4,4096]{4,3,2,1,0:T(4,128)(2,1)} %own_ref.1), channel_id=1, source_target_pairs={{0,4},{4,0},{8,12},{12,8},{16,20},{20,16},{24,28},{28,24},{1,5},{5... | collective-permute-start | bytes 393224 | tf_op jit(solution)/shard_map/ppermute | solution.py:277
  1.1 4.0 %collective-permute-start = (bf16[1,1,4,4,4096]{4,3,2,1,0:T(4,128)(2,1)}, bf16[1,1,4,4,4096]{4,3,2,1,0:T(4,128)(2,1)S(1)}, u32[]{:S(2)}, u32[]{:S(2)}) collective-permute-start(bf16[1,1,4,4,4096]{4,3,2,1,0:T(4,128)(2,1)} %own_ref.1), channel_id=1, source_target_pairs={{4,8},{8,4},{12,16},{16,12},{20,24},{24,20},{5,9},{9,5},{13,17},{1... | collective-permute-start | bytes 393224 | tf_op jit(solution)/shard_map/ppermute | solution.py:276
  1.8 1.9 %copy-start = (bf16[1,1,4,4,4096]{4,3,2,1,0:T(4,128)(2,1)S(1)}, bf16[1,1,4,4,4096]{4,3,2,1,0:T(4,128)(2,1)}, u32[]{:S(2)}) copy-start(bf16[1,1,4,4,4096]{4,3,2,1,0:T(4,128)(2,1)} %own_ref.1) | copy-start | bytes 393220

commit v10 on v9

--- a/solution.py
+++ b/solution.py
@@ -258,14 +258,10 @@
     out_copy.wait()
 
 
-def finish_kernel(parts_ref, grad_ref):
-    wide, half, _ = parts_ref.shape
-    for core in range(2):
-        total = parts_ref[core].astype(jnp.float32)
-        for k in range(core + 2, wide, 2):
-            total = total + parts_ref[k].astype(jnp.float32)
-        for tap in range(27):
-            grad_ref[tap, core * half : (core + 1) * half, :] = total[:, tap * C1 : (tap + 1) * C1]
+def finish_kernel(mine_ref, other_ref, grad_ref):
+    total = mine_ref[...].astype(jnp.float32) + other_ref[...].astype(jnp.float32)
+    for tap in range(27):
+        grad_ref[tap] = total[:, tap * C1 : (tap + 1) * C1]
 
 
 def body(volumes, first_kernel, second_kernel, cotangent):
@@ -274,7 +270,8 @@
     cells_out = cotangent.shape[3]
     scale = 1.0 / math.sqrt(wide * narrow * cells_out)
     across = lax.ppermute(volumes, WIDE, [p for k in range(1, wide - 1, 2) for p in ((k, k + 1), (k + 1, k))])
-    within = lax.ppermute(volumes, WIDE, [p for k in range(0, wide - 1, 2) for p in ((k, k + 1), (k + 1, k))])
+    pairs = [p for k in range(0, wide - 1, 2) for p in ((k, k + 1), (k + 1, k))]
+    within = lax.ppermute(volumes, WIDE, pairs)
     pinned = pl.BlockSpec(memory_space=pltpu.HBM)
     fast = pl.BlockSpec(memory_space=pltpu.VMEM)
     bf16 = functools.partial(jax.ShapeDtypeStruct, dtype=jnp.bfloat16)
@@ -339,16 +336,18 @@
         compiler_params=pltpu.CompilerParams(vmem_limit_bytes=16 * MIB),
         name="far",
     )(across, select, w1_far, w2, cot, first, near, pre)
-    half = rows // 2
-    received = lax.all_to_all(term, ("narrow", "core"), 0, 0, tiled=True)
-    owned = jnp.sum(received.reshape(2 * narrow, half, PACKED).astype(jnp.float32), axis=0).astype(jnp.bfloat16)
-    parts = lax.all_gather(owned, WIDE)
+    received = lax.all_to_all(term, "narrow", 0, 0, tiled=True)
+    owned = jnp.sum(received.reshape(narrow, rows, PACKED).astype(jnp.float32), axis=0).astype(jnp.bfloat16)
+    copies = jnp.broadcast_to(owned[None], (wide // 2, rows, PACKED))
+    parts = lax.all_to_all(copies, "chip", 0, 0, tiled=True)
+    mine = jnp.sum(parts.astype(jnp.float32), axis=0).astype(jnp.bfloat16)
+    other = lax.ppermute(mine, WIDE, pairs)
     weight_grad = pl.pallas_call(
         finish_kernel,
         out_shape=jax.ShapeDtypeStruct((27, rows, C1), jnp.float32),
         compiler_params=pltpu.CompilerParams(vmem_limit_bytes=8 * MIB),
         name="finish",
-    )(parts)
+    )(mine, other)
     return (output, weight_grad)
 
 

time: 34.5 us -> 33.4 us (0.968)
  blocking collectives: 26 us -> 23.7 us
  waiting for transfers between devices: 0.01 us -> 1.19 us
    all_gather x1 -> x0, blocking collectives: 10.1 us -> none  [body(): parts = lax.all_gather(owned, WIDE)]
    all_to_all x1 -> x2, blocking collectives: 16 us -> 23.7 us  [the longest x1 12.1 us: body(): parts = lax.all_to_all(copies, 'chip', 0, 0, tiled=True)]
    ppermute x1 -> x2, waiting for transfers between devices: 0.01 us -> 1.19 us  [the longest x1 1.19 us: body(): other = lax.ppermute(mine, WIDE, pairs)]
  transfers between devices with their start and end apart: 2 -> 3, of which waited for: 0 -> 1; matrix products, arithmetic and copies ran while one was open for 0% -> 0% of each run, Pallas kernels for 9% -> 10%
where the time goes in v10:
time: 33.4 us; the launch traced here: 33.2 us
  blocking collectives  23.7 us (71%)
  Pallas kernels  6.3 us (19%)
  starting transfers between devices  1.25 us (4%)
  waiting for transfers between devices  1.19 us (4%)
  between operations  0.72 us (2%)
    all_to_all x1, blocking collectives, body(): parts = lax.all_to_all(copies, 'chip', 0, 0, tiled=True)  12.1 us
    all_to_all x1, blocking collectives, body(): received = lax.all_to_all(term, 'narrow', 0, 0, tiled=True)  11.6 us
    pallas_call x1, Pallas kernels, body(): pl.pallas_call(functools.partial(far_kernel, wide // 2, scale), in_specs=...  2.27 us
    pallas_call x1, Pallas kernels, body(): pl.pallas_call(prepare_kernel, in_specs=[pinned] * 5, out_specs=(fast,) *...  1.85 us
    pallas_call x1, Pallas kernels, body(): pl.pallas_call(near_kernel, in_specs=[fast] * 5, out_specs=(fast,) * 3, o...  1.39 us
    ppermute x1, waiting for transfers between devices, body(): other = lax.ppermute(mine, WIDE, pairs)  1.19 us
    pallas_call x1, Pallas kernels, body(): pl.pallas_call(finish_kernel, out_shape=jax.ShapeDtypeStruct((27, rows, C...  0.8 us
  transfers between devices with their start and end apart: 3, of which 1 were waited for; matrix products, arithmetic and copies ran while one was open for 0% of the time, Pallas kernels for 10%

profile of v10, /device:TPU:0, one launch (start us, length us, event | category | flops | bytes accessed | tf_op | source)
XLA Modules:
  0.0 33.2 jit_solution(9157784980504057242)
XLA Ops:
  0.6 0.5 %collective-permute-start.1 = (bf16[1,1,4,4,4096]{4,3,2,1,0:T(4,128)(2,1)}, bf16[1,1,4,4,4096]{4,3,2,1,0:T(4,128)(2,1)S(1)}, u32[]{:S(2)}, u32[]{:S(2)}) collective-permute-start(bf16[1,1,4,4,4096]{4,3,2,1,0:T(4,128)(2,1)} %own_ref.1), channel_id=1, source_target_pairs={{0,4},{4,0},{8,12},{12,8},{16,20},{20,16},{24,28},{28,24},{1,5},{5... | collective-permute-start | bytes 393224 | tf_op jit(solution)/shard_map/ppermute | solution.py:274
  1.1 0.7 %collective-permute-start = (bf16[1,1,4,4,4096]{4,3,2,1,0:T(4,128)(2,1)}, bf16[1,1,4,4,4096]{4,3,2,1,0:T(4,128)(2,1)S(1)}, u32[]{:S(2)}, u32[]{:S(2)}) collective-permute-start(bf16[1,1,4,4,4096]{4,3,2,1,0:T(4,128)(2,1)} %own_ref.1), channel_id=1, source_target_pairs={{4,8},{8,4},{12,16},{16,12},{20,24},{24,20},{5,9},{9,5},{13,17},{1... | collective-permute-start | bytes 393224 | tf_op jit(solution)/shard_map/ppermute | solution.py:272
  1.8 0.0 copy-start
  1.8 1.9 %prepare.1 = (bf16[2,64,288]{2,1,0:T(8,128)(2,1)S(1)}, bf16[2,64,144]{2,1,0:T(8,128)(2,1)S(1)}, bf16[2,384,192]{2,1,0:T(8,128)(2,1)S(1)}, bf16[512,512]{1,0:T(8,128)(2,1)S(1)}, bf16[1,1,64,2048]{3,2,1,0:T(8,128)(2,1)S(1)}) custom-call(bf16[27,4,32]{2,1,0:T(4,128)(2,1)} %bitcast.5, bf16[2,108,2048]{2,1,0:T(8,128)(2,1)} %constant.8.clone.place_hbm, ...), custom_call_target="tpu_custom_call" | custom-call | flops 1000000000 | bytes 4194304 | tf_op jit(solution)/shard_map/prepare/pallas_call | solution.py:283
  3.7 0.0 collective-permute-done.1.within_ref
  3.7 0.0 copy-done
  3.7 1.4 %near.1 = (f32[64,1024]{1,0:T(8,128)S(1)}, bf16[192,1024]{1,0:T(8,128)(2,1)S(1)}, f32[128,1024]{1,0:T(8,128)S(1)}) custom-call(bf16[1,1,4,4,4096]{4,3,2,1,0:T(4,128)(2,1)S(1)} %copy-done, bf16[1,1,4,4,4096]{4,3,2,1,0:T(4,128)(2,1)S(1)} %collective-permute-done.1.within_ref, bf16[512,512]{1,0:T(8,128)(2,1)S(1)} %get-tuple-element.12.select_ref, ...), custom_call_target="tpu_custom_call" | custom-call | flops 1000000000 | bytes 4194304 | tf_op jit(solution)/shard_map/near/pallas_call | solution.py:302
  5.1 0.0 collective-permute-done.across_ref
  5.1 2.3 %far.1 = (bf16[1,1,64,2048]{3,2,1,0:T(8,128)(2,1)}, bf16[64,896]{1,0:T(8,128)(2,1)S(1)}) custom-call(bf16[1,1,4,4,4096]{4,3,2,1,0:T(4,128)(2,1)S(1)} %collective-permute-done.across_ref, bf16[512,512]{1,0:T(8,128)(2,1)S(1)} %get-tuple-element.12.select_ref, bf16[2,64,144]{2,1,0:T(8,128)(2,1)S(1)} %get-tuple-element.13.w1_ref, ...), custom_call_target="tpu_custom_call" | custom-call | tf_op jit(solution)/shard_map/far/pallas_call | solution.py:319
  7.4 11.6 %all_to_all.14 = bf16[4,16,896]{2,1,0:T(8,128)(2,1)S(1)} all-to-all(bf16[4,16,896]{2,1,0:T(8,128)(2,1)S(1)} %bitcast.3), channel_id=1, replica_groups=mesh['chip'=4,'core'=2,'narrow'=4] {'narrow'}, dimensions={0} | all-to-all | bytes 229376 | tf_op jit(solution)/shard_map/all_to_all | solution.py:339
  19.0 12.1 %all_to_all.15 = bf16[4,16,896]{2,1,0:T(8,128)(2,1)S(1)} all-to-all(bf16[4,16,896]{2,1,0:T(8,128)(2,1)S(1)} %broadcast_in_dim.2), channel_id=1, replica_groups=mesh['chip'=4,'core'=2,'narrow'=4] {'chip'}, dimensions={0} | all-to-all | bytes 229376 | tf_op jit(solution)/shard_map/all_to_all | solution.py:342
  31.1 0.1 collective-permute-start.2
  31.2 1.2 %collective-permute-done.2.other_ref = bf16[16,896]{1,0:T(8,128)(2,1)S(1)} collective-permute-done((bf16[16,896]{1,0:T(8,128)(2,1)S(1)}, bf16[16,896]{1,0:T(8,128)(2,1)S(1)}, u32[]{:S(2)}, u32[]{:S(2)}) %collective-permute-start.2) | collective-permute-done | bytes 28704 | tf_op jit(solution)/shard_map/ppermute | solution.py:344
  32.4 0.8 %finish.1 = f32[27,16,32]{2,1,0:T(8,128)} custom-call(bf16[16,896]{1,0:T(8,128)(2,1)S(1)} %reduce_sum.25.mine_ref, bf16[16,896]{1,0:T(8,128)(2,1)S(1)} %collective-permute-done.2.other_ref), custom_call_target="tpu_custom_call" | custom-call | tf_op jit(solution)/shard_map/finish/pallas_call | solution.py:345
  (3 shorter events, 0.0 us)
Async XLA Ops:
  0.6 3.1 %collective-permute-start.1 = (bf16[1,1,4,4,4096]{4,3,2,1,0:T(4,128)(2,1)}, bf16[1,1,4,4,4096]{4,3,2,1,0:T(4,128)(2,1)S(1)}, u32[]{:S(2)}, u32[]{:S(2)}) collective-permute-start(bf16[1,1,4,4,4096]{4,3,2,1,0:T(4,128)(2,1)} %own_ref.1), channel_id=1, source_target_pairs={{0,4},{4,0},{8,12},{12,8},{16,20},{20,16},{24,28},{28,24},{1,5},{5... | collective-permute-start | bytes 393224 | tf_op jit(solution)/shard_map/ppermute | solution.py:274
  1.1 4.0 %collective-permute-start = (bf16[1,1,4,4,4096]{4,3,2,1,0:T(4,128)(2,1)}, bf16[1,1,4,4,4096]{4,3,2,1,0:T(4,128)(2,1)S(1)}, u32[]{:S(2)}, u32[]{:S(2)}) collective-permute-start(bf16[1,1,4,4,4096]{4,3,2,1,0:T(4,128)(2,1)} %own_ref.1), channel_id=1, source_target_pairs={{4,8},{8,4},{12,16},{16,12},{20,24},{24,20},{5,9},{9,5},{13,17},{1... | collective-permute-start | bytes 393224 | tf_op jit(solution)/shard_map/ppermute | solution.py:272
  1.8 1.9 %copy-start = (bf16[1,1,4,4,4096]{4,3,2,1,0:T(4,128)(2,1)S(1)}, bf16[1,1,4,4,4096]{4,3,2,1,0:T(4,128)(2,1)}, u32[]{:S(2)}) copy-start(bf16[1,1,4,4,4096]{4,3,2,1,0:T(4,128)(2,1)} %own_ref.1) | copy-start | bytes 393220
  31.1 1.3 %collective-permute-start.2 = (bf16[16,896]{1,0:T(8,128)(2,1)S(1)}, bf16[16,896]{1,0:T(8,128)(2,1)S(1)}, u32[]{:S(2)}, u32[]{:S(2)}) collective-permute-start(bf16[16,896]{1,0:T(8,128)(2,1)S(1)} %reduce_sum.25.mine_ref), channel_id=1, source_target_pairs={{0,4},{4,0},{8,12},{12,8},{16,20},{20,16},{24,28},{28,24},{1,5},{5... | collective-permute-start | bytes 86024 | tf_op jit(solution)/shard_map/ppermute | solution.py:344

commit v11 on v7

--- a/solution.py
+++ b/solution.py
@@ -132,11 +132,15 @@
 
 
 def prepare_kernel(
-    k1_hbm, place_hbm, k2_hbm, select_hbm, cot_hbm, w1_near_ref, w1_far_ref, w2_ref, select_ref, cot_ref,
+    k1_hbm, place_hbm, k2_hbm, select_hbm, cot_hbm, slab_hbm,
+    w1_near_ref, w1_far_ref, w2_ref, select_ref, cot_ref, slab_ref,
     k1_ref, place_ref, k2_ref, k1_rows_ref, sems,
 ):
     odd = lax.axis_index("core")
-    moves = ((k1_hbm, k1_ref), (k2_hbm, k2_ref), (place_hbm.at[odd], place_ref), (select_hbm, select_ref), (cot_hbm, cot_ref))
+    moves = (
+        (k1_hbm, k1_ref), (k2_hbm, k2_ref), (place_hbm.at[odd], place_ref),
+        (select_hbm, select_ref), (cot_hbm, cot_ref), (slab_hbm, slab_ref),
+    )
     copies = [pltpu.make_async_copy(src, dst, sems.at[k]) for k, (src, dst) in enumerate(moves)]
     for copy in copies:
         copy.start()
@@ -171,6 +175,7 @@
         w1_far_ref[q // 2, rows, :] = spread[:, CHUNK * q + 18 * ROWS : CHUNK * q + 27 * ROWS]
     copies[3].wait()
     copies[4].wait()
+    copies[5].wait()
 
 
 def near_kernel(
@@ -194,13 +199,15 @@
 
 
 def far_kernel(
-    chips, scale, across_ref, select_ref, w1_ref, w2_ref, cot_ref, first_ref, near_ref, pre_ref, out_hbm, grad_ref,
+    chips, scale, hop_ref, turn_ref, select_ref, w1_ref, w2_ref, cot_ref, first_ref, near_ref, pre_ref, out_hbm, grad_ref,
     rows_ref, parity_ref, taps_ref, act_ref, columns_ref, rowed_ref, back_ref, sums_ref, out_ref, out_sem,
 ):
     odd = lax.axis_index("core")
-    last = (lax.axis_index("chip") == chips - 1) & (odd == 1)
-    inside = jnp.where(last, 0.0, 1.0)
-    plane_rows(across_ref, rows_ref)
+    chip = lax.axis_index("chip")
+    inside = jnp.where((chip == chips - 1) & (odd == 1), 0.0, 1.0)
+    turned = lax.rem(chip + odd, 2) == 0
+    pl.when(turned)(lambda: plane_rows(turn_ref, rows_ref))
+    pl.when(jnp.logical_not(turned))(lambda: plane_rows(hop_ref, rows_ref))
     strided_taps(rows_ref[...].astype(jnp.bfloat16), select_ref, parity_ref, taps_ref)
     clear_margins(act_ref)
     for n in range(4):
@@ -273,35 +280,37 @@
     narrow = lax.axis_size("narrow")
     cells_out = cotangent.shape[3]
     scale = 1.0 / math.sqrt(wide * narrow * cells_out)
-    across = lax.ppermute(volumes, WIDE, [p for k in range(1, wide - 1, 2) for p in ((k, k + 1), (k + 1, k))])
-    within = lax.ppermute(volumes, WIDE, [p for k in range(0, wide - 1, 2) for p in ((k, k + 1), (k + 1, k))])
+    within, turn, hop = ([p for k in range(first, wide - 1, step) for p in ((k, k + 1), (k + 1, k))] for first, step in ((0, 2), (3, 4), (1, 4)))
+    within = lax.ppermute(volumes, WIDE, within)
+    turn = lax.ppermute(volumes, WIDE, turn)
     pinned = pl.BlockSpec(memory_space=pltpu.HBM)
     fast = pl.BlockSpec(memory_space=pltpu.VMEM)
     bf16 = functools.partial(jax.ShapeDtypeStruct, dtype=jnp.bfloat16)
     f32 = functools.partial(jax.ShapeDtypeStruct, dtype=jnp.float32)
     stored = (
         first_kernel.transpose(0, 2, 1), jnp.asarray(placement(), jnp.bfloat16), second_kernel.transpose(0, 2, 1),
-        jnp.asarray(selection(), jnp.bfloat16), cotangent,
+        jnp.asarray(selection(), jnp.bfloat16), cotangent, volumes,
     )
-    w1_near, w1_far, w2, select, cot = pl.pallas_call(
+    w1_near, w1_far, w2, select, cot, slab = pl.pallas_call(
         prepare_kernel,
-        in_specs=[pinned] * 5,
-        out_specs=(fast,) * 5,
+        in_specs=[pinned] * 6,
+        out_specs=(fast,) * 6,
         out_shape=(
             bf16((2, 2 * C1, 18 * ROWS)), bf16((2, 2 * C1, 9 * ROWS)), bf16((2, 6 * C2, 6 * C1)),
-            bf16((CHUNK, CHUNK)), bf16(cotangent.shape),
+            bf16((CHUNK, CHUNK)), bf16(cotangent.shape), bf16(volumes.shape),
         ),
         scratch_shapes=[
             pltpu.VMEM((27, CIN, C1), jnp.bfloat16),
             pltpu.VMEM((27 * CIN, 4 * CHUNK), jnp.bfloat16),
             pltpu.VMEM((27, C1, C2), jnp.bfloat16),
             pltpu.VMEM((27 * CIN, C1), jnp.float32),
-            pltpu.SemaphoreType.DMA((5,)),
+            pltpu.SemaphoreType.DMA((6,)),
         ],
         compiler_params=pltpu.CompilerParams(vmem_limit_bytes=12 * MIB),
         cost_estimate=pl.CostEstimate(flops=10**9, bytes_accessed=4 * MIB, transcendentals=0),
         name="prepare",
     )(*(pltpu.with_memory_space_constraint(x, pltpu.HBM) for x in stored))
+    hop = lax.ppermute(slab, WIDE, hop)
     first, near, pre = pl.pallas_call(
         near_kernel,
         in_specs=[fast] * 5,
@@ -317,11 +326,11 @@
         compiler_params=pltpu.CompilerParams(vmem_limit_bytes=16 * MIB),
         cost_estimate=pl.CostEstimate(flops=10**9, bytes_accessed=4 * MIB, transcendentals=0),
         name="near",
-    )(volumes, within, select, w1_near, w2)
+    )(slab, within, select, w1_near, w2)
     rows = C2 // narrow
     output, term = pl.pallas_call(
         functools.partial(far_kernel, wide // 2, scale),
-        in_specs=[fast] * 8,
+        in_specs=[fast] * 9,
         out_specs=(pl.BlockSpec(memory_space=pl.ANY), fast),
         out_shape=(bf16((1, 1, C2, cells_out)), bf16((C2, PACKED))),
         scratch_shapes=[
@@ -338,7 +347,7 @@
         ],
         compiler_params=pltpu.CompilerParams(vmem_limit_bytes=16 * MIB),
         name="far",
-    )(across, select, w1_far, w2, cot, first, near, pre)
+    )(hop, turn, select, w1_far, w2, cot, first, near, pre)
     half = rows // 2
     received = lax.all_to_all(term, ("narrow", "core"), 0, 0, tiled=True)
     owned = jnp.sum(received.reshape(2 * narrow, half, PACKED).astype(jnp.float32), axis=0).astype(jnp.bfloat16)

time: 33.2 us -> 34.4 us (1.036)
  starting transfers between devices: 1.17 us -> 1.84 us
  blocking collectives: 24.7 us -> 25.3 us
    ppermute x2 -> x3, starting transfers between devices: 1.17 us -> 1.84 us  [the longest x1 0.67 us: body(): hop = lax.ppermute(slab, WIDE, hop)]
    all_to_all x1, blocking collectives: 16 us -> 16.5 us  [body(): received = lax.all_to_all(term, ('narrow', 'core'), 0, 0, tiled=True)]
  transfers between devices with their start and end apart: 2 -> 3, of which waited for: 0 -> 0; matrix products, arithmetic and copies ran while one was open for 0% -> 0% of each run, Pallas kernels for 10% -> 9%
where the time goes in v11:
time: 34.4 us; the launch traced here: 34.2 us
  blocking collectives  25.3 us (74%)
  Pallas kernels  6.31 us (18%)
  starting transfers between devices  1.84 us (5%)
  between operations  0.7 us (2%)
    all_to_all x1, blocking collectives, body(): received = lax.all_to_all(term, ('narrow', 'core'), 0, 0, tiled=True)  16.5 us
    all_to_all x1, blocking collectives, body(): lax.all_to_all(jnp.broadcast_to(owned[None], (wide, half, PACKED)), WIDE,...  8.79 us
    pallas_call x1, Pallas kernels, body(): pl.pallas_call(functools.partial(far_kernel, wide // 2, scale), in_specs=...  2.31 us
    pallas_call x1, Pallas kernels, body(): pl.pallas_call(prepare_kernel, in_specs=[pinned] * 6, out_specs=(fast,) *...  1.83 us
    pallas_call x1, Pallas kernels, body(): pl.pallas_call(near_kernel, in_specs=[fast] * 5, out_specs=(fast,) * 3, o...  1.38 us
    pallas_call x1, Pallas kernels, body(): pl.pallas_call(finish_kernel, out_shape=jax.ShapeDtypeStruct((27, rows, C...  0.8 us
  transfers between devices with their start and end apart: 3, of which 0 were waited for; matrix products, arithmetic and copies ran while one was open for 0% of the time, Pallas kernels for 9%

profile of v11, /device:TPU:0, one launch (start us, length us, event | category | flops | bytes accessed | tf_op | source)
XLA Modules:
  0.0 34.2 jit_solution(1027692050730515583)
XLA Ops:
  0.6 0.5 %collective-permute-start.2 = (bf16[1,1,4,4,4096]{4,3,2,1,0:T(4,128)(2,1)}, bf16[1,1,4,4,4096]{4,3,2,1,0:T(4,128)(2,1)S(1)}, u32[]{:S(2)}, u32[]{:S(2)}) collective-permute-start(bf16[1,1,4,4,4096]{4,3,2,1,0:T(4,128)(2,1)} %slab_hbm.1), channel_id=1, source_target_pairs={{0,4},{4,0},{8,12},{12,8},{16,20},{20,16},{24,28},{28,24},{1,5},{5... | collective-permute-start | bytes 393224 | tf_op jit(solution)/shard_map/ppermute | solution.py:284
  1.1 0.7 %collective-permute-start.1 = (bf16[1,1,4,4,4096]{4,3,2,1,0:T(4,128)(2,1)}, bf16[1,1,4,4,4096]{4,3,2,1,0:T(4,128)(2,1)S(1)}, u32[]{:S(2)}, u32[]{:S(2)}) collective-permute-start(bf16[1,1,4,4,4096]{4,3,2,1,0:T(4,128)(2,1)} %slab_hbm.1), channel_id=1, source_target_pairs={{12,16},{16,12},{13,17},{17,13},{14,18},{18,14},{15,19},{19,15}} | collective-permute-start | bytes 393224 | tf_op jit(solution)/shard_map/ppermute | solution.py:285
  1.8 1.8 %prepare.1 = (bf16[2,64,288]{2,1,0:T(8,128)(2,1)S(1)}, bf16[2,64,144]{2,1,0:T(8,128)(2,1)S(1)}, bf16[2,384,192]{2,1,0:T(8,128)(2,1)S(1)}, bf16[512,512]{1,0:T(8,...) custom-call(bf16[27,4,32]{2,1,0:T(4,128)(2,1)} %bitcast.5, ...), custom_call_target="tpu_custom_call" | custom-call | flops 1000000000 | bytes 4194304 | tf_op jit(solution)/shard_map/prepare/pallas_call | solution.py:294
  3.6 0.7 %collective-permute-start = (bf16[1,1,4,4,4096]{4,3,2,1,0:T(4,128)(2,1)S(1)}, bf16[1,1,4,4,4096]{4,3,2,1,0:T(4,128)(2,1)S(1)}, u32[]{:S(2)}, u32[]{:S(2)}) collective-permute-start(bf16[1,1,4,4,4096]{4,3,2,1,0:T(4,128)(2,1)S(1)} %get-tuple-element.13.own_ref), channel_id=1, source_target_pairs={{4,8},{8,4},{20,24},{24,20},{5,9},{9,5},{21,25},{25,21},{6,10},{10... | collective-permute-start | bytes 393224 | tf_op jit(solution)/shard_map/ppermute | solution.py:313
  4.3 0.0 collective-permute-done.2.within_ref
  4.3 1.4 %near.1 = (f32[64,1024]{1,0:T(8,128)S(1)}, bf16[192,1024]{1,0:T(8,128)(2,1)S(1)}, f32[128,1024]{1,0:T(8,128)S(1)}) custom-call(bf16[1,1,4,4,4096]{4,3,2,1,0:T(4,128)(2,1)S(1)} %get-tuple-element.13.own_ref, bf16[1,1,4,4,4096]{4,3,2,1,0:T(4,128)(2,1)S(1)} %collective-permute-done.2.within_ref, bf16[512,512]{1,0:T(8,128)(2,1)S(1)} %get-tuple-element.14.select_ref, ...), custom_call_target="tpu_custom_call" | custom-call | flops 1000000000 | bytes 4194304 | tf_op jit(solution)/shard_map/near/pallas_call | solution.py:314
  5.7 0.0 collective-permute-done.1.turn_ref
  5.7 0.0 collective-permute-done.hop_ref
  5.7 2.3 %far.1 = (bf16[1,1,64,2048]{3,2,1,0:T(8,128)(2,1)}, bf16[64,896]{1,0:T(8,128)(2,1)S(1)}) custom-call(bf16[1,1,4,4,4096]{4,3,2,1,0:T(4,128)(2,1)S(1)} %collective-permute-done.hop_ref, bf16[1,1,4,4,4096]{4,3,2,1,0:T(4,128)(2,1)S(1)} %collective-permute-done.1.turn_ref, bf16[512,512]{1,0:T(8,128)(2,1)S(1)} %get-tuple-element.14.select_ref, ...), custom_call_target="tpu_custom_call" | custom-call | tf_op jit(solution)/shard_map/far/pallas_call | solution.py:331
  8.1 16.5 %all_to_all.14 = bf16[8,8,896]{2,1,0:T(8,128)(2,1)S(1)} all-to-all(bf16[8,8,896]{2,1,0:T(8,128)(2,1)S(1)} %bitcast.3), channel_id=1, replica_groups=mesh['chip'=4,'core'=2,'narrow'=4] {'narrow','core'}, dimensions={0} | all-to-all | bytes 229376 | tf_op jit(solution)/shard_map/all_to_all | solution.py:352
  24.6 8.8 %all_to_all.15.parts_ref = bf16[8,8,896]{2,1,0:T(8,128)(2,1)S(1)} all-to-all(bf16[8,8,896]{2,1,0:T(8,128)(2,1)S(1)} %broadcast_in_dim.2), channel_id=1, replica_groups=mesh['chip'=4,'core'=2,'narrow'=4] {'chip','core'}, dimensions={0} | all-to-all | bytes 229376 | tf_op jit(solution)/shard_map/all_to_all | solution.py:354
  33.4 0.8 %finish.1 = f32[27,16,32]{2,1,0:T(8,128)} custom-call(bf16[8,8,896]{2,1,0:T(8,128)(2,1)S(1)} %all_to_all.15.parts_ref), custom_call_target="tpu_custom_call" | custom-call | tf_op jit(solution)/shard_map/finish/pallas_call | solution.py:355
  (2 shorter events, 0.0 us)
Async XLA Ops:
  0.6 3.7 %collective-permute-start.2 = (bf16[1,1,4,4,4096]{4,3,2,1,0:T(4,128)(2,1)}, bf16[1,1,4,4,4096]{4,3,2,1,0:T(4,128)(2,1)S(1)}, u32[]{:S(2)}, u32[]{:S(2)}) collective-permute-start(bf16[1,1,4,4,4096]{4,3,2,1,0:T(4,128)(2,1)} %slab_hbm.1), channel_id=1, source_target_pairs={{0,4},{4,0},{8,12},{12,8},{16,20},{20,16},{24,28},{28,24},{1,5},{5... | collective-permute-start | bytes 393224 | tf_op jit(solution)/shard_map/ppermute | solution.py:284
  1.1 4.6 %collective-permute-start.1 = (bf16[1,1,4,4,4096]{4,3,2,1,0:T(4,128)(2,1)}, bf16[1,1,4,4,4096]{4,3,2,1,0:T(4,128)(2,1)S(1)}, u32[]{:S(2)}, u32[]{:S(2)}) collective-permute-start(bf16[1,1,4,4,4096]{4,3,2,1,0:T(4,128)(2,1)} %slab_hbm.1), channel_id=1, source_target_pairs={{12,16},{16,12},{13,17},{17,13},{14,18},{18,14},{15,19},{19,15}} | collective-permute-start | bytes 393224 | tf_op jit(solution)/shard_map/ppermute | solution.py:285
  3.6 2.1 %collective-permute-start = (bf16[1,1,4,4,4096]{4,3,2,1,0:T(4,128)(2,1)S(1)}, bf16[1,1,4,4,4096]{4,3,2,1,0:T(4,128)(2,1)S(1)}, u32[]{:S(2)}, u32[]{:S(2)}) collective-permute-start(bf16[1,1,4,4,4096]{4,3,2,1,0:T(4,128)(2,1)S(1)} %get-tuple-element.13.own_ref), channel_id=1, source_target_pairs={{4,8},{8,4},{20,24},{24,20},{5,9},{9,5},{21,25},{25,21},{6,10},{10... | collective-permute-start | bytes 393224 | tf_op jit(solution)/shard_map/ppermute | solution.py:313

commit v12 on v11

--- a/solution.py
+++ b/solution.py
@@ -132,14 +132,14 @@
 
 
 def prepare_kernel(
-    k1_hbm, place_hbm, k2_hbm, select_hbm, cot_hbm, slab_hbm,
-    w1_near_ref, w1_far_ref, w2_ref, select_ref, cot_ref, slab_ref,
+    k1_hbm, place_hbm, k2_hbm, select_hbm, cot_hbm,
+    w1_near_ref, w1_far_ref, w2_ref, select_ref, cot_ref,
     k1_ref, place_ref, k2_ref, k1_rows_ref, sems,
 ):
     odd = lax.axis_index("core")
     moves = (
         (k1_hbm, k1_ref), (k2_hbm, k2_ref), (place_hbm.at[odd], place_ref),
-        (select_hbm, select_ref), (cot_hbm, cot_ref), (slab_hbm, slab_ref),
+        (select_hbm, select_ref), (cot_hbm, cot_ref),
     )
     copies = [pltpu.make_async_copy(src, dst, sems.at[k]) for k, (src, dst) in enumerate(moves)]
     for copy in copies:
@@ -175,7 +175,6 @@
         w1_far_ref[q // 2, rows, :] = spread[:, CHUNK * q + 18 * ROWS : CHUNK * q + 27 * ROWS]
     copies[3].wait()
     copies[4].wait()
-    copies[5].wait()
 
 
 def near_kernel(
@@ -280,37 +279,38 @@
     narrow = lax.axis_size("narrow")
     cells_out = cotangent.shape[3]
     scale = 1.0 / math.sqrt(wide * narrow * cells_out)
-    within, turn, hop = ([p for k in range(first, wide - 1, step) for p in ((k, k + 1), (k + 1, k))] for first, step in ((0, 2), (3, 4), (1, 4)))
+    swaps = [[p for k in range(first, wide - 1, step) for p in ((k, k + 1), (k + 1, k))] for first, step in ((0, 2), (3, 4), (1, 4))]
+    within, turn, hop = swaps
     within = lax.ppermute(volumes, WIDE, within)
     turn = lax.ppermute(volumes, WIDE, turn)
+    hop = lax.ppermute(volumes, WIDE, hop)
     pinned = pl.BlockSpec(memory_space=pltpu.HBM)
     fast = pl.BlockSpec(memory_space=pltpu.VMEM)
     bf16 = functools.partial(jax.ShapeDtypeStruct, dtype=jnp.bfloat16)
     f32 = functools.partial(jax.ShapeDtypeStruct, dtype=jnp.float32)
     stored = (
         first_kernel.transpose(0, 2, 1), jnp.asarray(placement(), jnp.bfloat16), second_kernel.transpose(0, 2, 1),
-        jnp.asarray(selection(), jnp.bfloat16), cotangent, volumes,
+        jnp.asarray(selection(), jnp.bfloat16), cotangent,
     )
-    w1_near, w1_far, w2, select, cot, slab = pl.pallas_call(
+    w1_near, w1_far, w2, select, cot = pl.pallas_call(
         prepare_kernel,
-        in_specs=[pinned] * 6,
-        out_specs=(fast,) * 6,
+        in_specs=[pinned] * 5,
+        out_specs=(fast,) * 5,
         out_shape=(
             bf16((2, 2 * C1, 18 * ROWS)), bf16((2, 2 * C1, 9 * ROWS)), bf16((2, 6 * C2, 6 * C1)),
-            bf16((CHUNK, CHUNK)), bf16(cotangent.shape), bf16(volumes.shape),
+            bf16((CHUNK, CHUNK)), bf16(cotangent.shape),
         ),
         scratch_shapes=[
             pltpu.VMEM((27, CIN, C1), jnp.bfloat16),
             pltpu.VMEM((27 * CIN, 4 * CHUNK), jnp.bfloat16),
             pltpu.VMEM((27, C1, C2), jnp.bfloat16),
             pltpu.VMEM((27 * CIN, C1), jnp.float32),
-            pltpu.SemaphoreType.DMA((6,)),
+            pltpu.SemaphoreType.DMA((5,)),
         ],
         compiler_params=pltpu.CompilerParams(vmem_limit_bytes=12 * MIB),
         cost_estimate=pl.CostEstimate(flops=10**9, bytes_accessed=4 * MIB, transcendentals=0),
         name="prepare",
     )(*(pltpu.with_memory_space_constraint(x, pltpu.HBM) for x in stored))
-    hop = lax.ppermute(slab, WIDE, hop)
     first, near, pre = pl.pallas_call(
         near_kernel,
         in_specs=[fast] * 5,
@@ -326,7 +326,7 @@
         compiler_params=pltpu.CompilerParams(vmem_limit_bytes=16 * MIB),
         cost_estimate=pl.CostEstimate(flops=10**9, bytes_accessed=4 * MIB, transcendentals=0),
         name="near",
-    )(slab, within, select, w1_near, w2)
+    )(volumes, within, select, w1_near, w2)
     rows = C2 // narrow
     output, term = pl.pallas_call(
         functools.partial(far_kernel, wide // 2, scale),

time: 34.4 us -> 34.1 us (level)
    all_to_all x1, blocking collectives: 16.5 us -> 15.9 us  [body(): received = lax.all_to_all(term, ('narrow', 'core'), 0, 0, tiled=True)]
  transfers between devices with their start and end apart: 3 -> 3, of which waited for: 0 -> 0; matrix products, arithmetic and copies ran while one was open for 0% -> 0% of each run, Pallas kernels for 9% -> 10%
where the time goes in v12:
time: 34.1 us; the launch traced here: 33.9 us
  blocking collectives  25 us (73%)
  Pallas kernels  6.34 us (19%)
  starting transfers between devices  1.84 us (5%)
  between operations  0.72 us (2%)
    all_to_all x1, blocking collectives, body(): received = lax.all_to_all(term, ('narrow', 'core'), 0, 0, tiled=True)  15.9 us
    all_to_all x1, blocking collectives, body(): lax.all_to_all(jnp.broadcast_to(owned[None], (wide, half, PACKED)), WIDE,...  9.1 us
    pallas_call x1, Pallas kernels, body(): pl.pallas_call(functools.partial(far_kernel, wide // 2, scale), in_specs=...  2.31 us
    pallas_call x1, Pallas kernels, body(): pl.pallas_call(prepare_kernel, in_specs=[pinned] * 5, out_specs=(fast,) *...  1.85 us
    pallas_call x1, Pallas kernels, body(): pl.pallas_call(near_kernel, in_specs=[fast] * 5, out_specs=(fast,) * 3, o...  1.38 us
    pallas_call x1, Pallas kernels, body(): pl.pallas_call(finish_kernel, out_shape=jax.ShapeDtypeStruct((27, rows, C...  0.8 us
  transfers between devices with their start and end apart: 3, of which 0 were waited for; matrix products, arithmetic and copies ran while one was open for 0% of the time, Pallas kernels for 10%

profile of v12, /device:TPU:0, one launch (start us, length us, event | category | flops | bytes accessed | tf_op | source)
XLA Modules:
  0.0 33.9 jit_solution(5997596882799101318)
XLA Ops:
  0.6 0.5 %collective-permute-start.2 = (bf16[1,1,4,4,4096]{4,3,2,1,0:T(4,128)(2,1)}, bf16[1,1,4,4,4096]{4,3,2,1,0:T(4,128)(2,1)S(1)}, u32[]{:S(2)}, u32[]{:S(2)}) collective-permute-start(bf16[1,1,4,4,4096]{4,3,2,1,0:T(4,128)(2,1)} %own_ref.1), channel_id=1, source_target_pairs={{0,4},{4,0},{8,12},{12,8},{16,20},{20,16},{24,28},{28,24},{1,5},{5... | collective-permute-start | bytes 393224 | tf_op jit(solution)/shard_map/ppermute | solution.py:284
  1.1 0.7 %collective-permute-start.1 = (bf16[1,1,4,4,4096]{4,3,2,1,0:T(4,128)(2,1)}, bf16[1,1,4,4,4096]{4,3,2,1,0:T(4,128)(2,1)S(1)}, u32[]{:S(2)}, u32[]{:S(2)}) collective-permute-start(bf16[1,1,4,4,4096]{4,3,2,1,0:T(4,128)(2,1)} %own_ref.1), channel_id=1, source_target_pairs={{12,16},{16,12},{13,17},{17,13},{14,18},{18,14},{15,19},{19,15}} | collective-permute-start | bytes 393224 | tf_op jit(solution)/shard_map/ppermute | solution.py:285
  1.8 0.7 %collective-permute-start = (bf16[1,1,4,4,4096]{4,3,2,1,0:T(4,128)(2,1)}, bf16[1,1,4,4,4096]{4,3,2,1,0:T(4,128)(2,1)S(1)}, u32[]{:S(2)}, u32[]{:S(2)}) collective-permute-start(bf16[1,1,4,4,4096]{4,3,2,1,0:T(4,128)(2,1)} %own_ref.1), channel_id=1, source_target_pairs={{4,8},{8,4},{20,24},{24,20},{5,9},{9,5},{21,25},{25,21},{6,10},{10... | collective-permute-start | bytes 393224 | tf_op jit(solution)/shard_map/ppermute | solution.py:286
  2.5 0.0 copy-start
  2.5 1.9 %prepare.1 = (bf16[2,64,288]{2,1,0:T(8,128)(2,1)S(1)}, bf16[2,64,144]{2,1,0:T(8,128)(2,1)S(1)}, bf16[2,384,192]{2,1,0:T(8,128)(2,1)S(1)}, bf16[512,512]{1,0:T(8,128)(2,1)S(1)}, bf16[1,1,64,2048]{3,2,1,0:T(8,128)(2,1)S(1)}) custom-call(bf16[27,4,32]{2,1,0:T(4,128)(2,1)} %bitcast.5, bf16[2,108,2048]{2,1,0:T(8,128)(2,1)} %constant.7.clone.place_hbm, ...), custom_call_target="tpu_custom_call" | custom-call | flops 1000000000 | bytes 4194304 | tf_op jit(solution)/shard_map/prepare/pallas_call | solution.py:295
  4.4 0.0 collective-permute-done.2.within_ref
  4.4 0.0 copy-done
  4.4 1.4 %near.1 = (f32[64,1024]{1,0:T(8,128)S(1)}, bf16[192,1024]{1,0:T(8,128)(2,1)S(1)}, f32[128,1024]{1,0:T(8,128)S(1)}) custom-call(bf16[1,1,4,4,4096]{4,3,2,1,0:T(4,128)(2,1)S(1)} %copy-done, bf16[1,1,4,4,4096]{4,3,2,1,0:T(4,128)(2,1)S(1)} %collective-permute-done.2.within_ref, bf16[512,512]{1,0:T(8,128)(2,1)S(1)} %get-tuple-element.12.select_ref, ...), custom_call_target="tpu_custom_call" | custom-call | flops 1000000000 | bytes 4194304 | tf_op jit(solution)/shard_map/near/pallas_call | solution.py:314
  5.8 0.0 collective-permute-done.1.turn_ref
  5.8 0.0 collective-permute-done.hop_ref
  5.8 2.3 %far.1 = (bf16[1,1,64,2048]{3,2,1,0:T(8,128)(2,1)}, bf16[64,896]{1,0:T(8,128)(2,1)S(1)}) custom-call(bf16[1,1,4,4,4096]{4,3,2,1,0:T(4,128)(2,1)S(1)} %collective-permute-done.hop_ref, bf16[1,1,4,4,4096]{4,3,2,1,0:T(4,128)(2,1)S(1)} %collective-permute-done.1.turn_ref, bf16[512,512]{1,0:T(8,128)(2,1)S(1)} %get-tuple-element.12.select_ref, ...), custom_call_target="tpu_custom_call" | custom-call | tf_op jit(solution)/shard_map/far/pallas_call | solution.py:331
  8.1 15.9 %all_to_all.14 = bf16[8,8,896]{2,1,0:T(8,128)(2,1)S(1)} all-to-all(bf16[8,8,896]{2,1,0:T(8,128)(2,1)S(1)} %bitcast.3), channel_id=1, replica_groups=mesh['chip'=4,'core'=2,'narrow'=4] {'narrow','core'}, dimensions={0} | all-to-all | bytes 229376 | tf_op jit(solution)/shard_map/all_to_all | solution.py:352
  24.0 9.1 %all_to_all.15.parts_ref = bf16[8,8,896]{2,1,0:T(8,128)(2,1)S(1)} all-to-all(bf16[8,8,896]{2,1,0:T(8,128)(2,1)S(1)} %broadcast_in_dim.2), channel_id=1, replica_groups=mesh['chip'=4,'core'=2,'narrow'=4] {'chip','core'}, dimensions={0} | all-to-all | bytes 229376 | tf_op jit(solution)/shard_map/all_to_all | solution.py:354
  33.1 0.8 %finish.1 = f32[27,16,32]{2,1,0:T(8,128)} custom-call(bf16[8,8,896]{2,1,0:T(8,128)(2,1)S(1)} %all_to_all.15.parts_ref), custom_call_target="tpu_custom_call" | custom-call | tf_op jit(solution)/shard_map/finish/pallas_call | solution.py:355
  (2 shorter events, 0.0 us)
Async XLA Ops:
  0.6 3.7 %collective-permute-start.2 = (bf16[1,1,4,4,4096]{4,3,2,1,0:T(4,128)(2,1)}, bf16[1,1,4,4,4096]{4,3,2,1,0:T(4,128)(2,1)S(1)}, u32[]{:S(2)}, u32[]{:S(2)}) collective-permute-start(bf16[1,1,4,4,4096]{4,3,2,1,0:T(4,128)(2,1)} %own_ref.1), channel_id=1, source_target_pairs={{0,4},{4,0},{8,12},{12,8},{16,20},{20,16},{24,28},{28,24},{1,5},{5... | collective-permute-start | bytes 393224 | tf_op jit(solution)/shard_map/ppermute | solution.py:284
  1.1 4.6 %collective-permute-start.1 = (bf16[1,1,4,4,4096]{4,3,2,1,0:T(4,128)(2,1)}, bf16[1,1,4,4,4096]{4,3,2,1,0:T(4,128)(2,1)S(1)}, u32[]{:S(2)}, u32[]{:S(2)}) collective-permute-start(bf16[1,1,4,4,4096]{4,3,2,1,0:T(4,128)(2,1)} %own_ref.1), channel_id=1, source_target_pairs={{12,16},{16,12},{13,17},{17,13},{14,18},{18,14},{15,19},{19,15}} | collective-permute-start | bytes 393224 | tf_op jit(solution)/shard_map/ppermute | solution.py:285
  1.8 4.0 %collective-permute-start = (bf16[1,1,4,4,4096]{4,3,2,1,0:T(4,128)(2,1)}, bf16[1,1,4,4,4096]{4,3,2,1,0:T(4,128)(2,1)S(1)}, u32[]{:S(2)}, u32[]{:S(2)}) collective-permute-start(bf16[1,1,4,4,4096]{4,3,2,1,0:T(4,128)(2,1)} %own_ref.1), channel_id=1, source_target_pairs={{4,8},{8,4},{20,24},{24,20},{5,9},{9,5},{21,25},{25,21},{6,10},{10... | collective-permute-start | bytes 393224 | tf_op jit(solution)/shard_map/ppermute | solution.py:286
  2.5 1.9 %copy-start = (bf16[1,1,4,4,4096]{4,3,2,1,0:T(4,128)(2,1)S(1)}, bf16[1,1,4,4,4096]{4,3,2,1,0:T(4,128)(2,1)}, u32[]{:S(2)}) copy-start(bf16[1,1,4,4,4096]{4,3,2,1,0:T(4,128)(2,1)} %own_ref.1) | copy-start | bytes 393220

commit v13 on v7

--- a/solution.py
+++ b/solution.py
@@ -193,9 +193,47 @@
         pre_ref[:, 256 * n : 256 * n + 256] = row_sum(rowed_ref, n)
 
 
+def slots():
+    where = {}
+    for a in range(3):
+        for b in range(3):
+            for c in range(3):
+                slot, side = divmod(3 * a + c, 2)
+                where[9 * a + 3 * b + c] = (2 * b + side, slot) if slot < 4 else (6, (0, 2, 1)[b])
+    return where
+
+
+def group_of_lane():
+    return lax.broadcasted_iota(jnp.int32, (C1, LANES), 1) // C1
+
+
+def paired_terms(sums_ref, tile):
+    even = group_of_lane() % 2 == 0
+
+    def plane(q, c):
+        begin = 2 * C1 * c + C1 * (q % 2)
+        return sums_ref[q // 2, begin : begin + C1, tile * LANES : (tile + 1) * LANES]
+
+    terms = [plane(a, c) + pltpu.roll(plane(a + 1, c), 3 * C1, 1) for a in range(3) for c in range(3)]
+    return [jnp.where(even, terms[k], pltpu.roll(terms[k + 1], C1, 1)) for k in range(0, 8, 2)] + [terms[8]]
+
+
+def turned_groups(blocks, scale):
+    flat = (jnp.concatenate(blocks, axis=0) * scale).T
+    return [flat[g * C1 : (g + 1) * C1] for g in range(4)]
+
+
+def gradient_sums(odd, near_ref, far_ref, backs, sums_ref):
+    columns = jnp.concatenate([near_ref[...], far_ref[...]], axis=0)
+    sums = jnp.dot(columns, backs, preferred_element_type=jnp.float32)
+    sums_ref[1 - odd] = sums[0 : 6 * C1]
+    sums_ref[odd] = sums[6 * C1 :]
+
+
 def far_kernel(
-    chips, scale, across_ref, select_ref, w1_ref, w2_ref, cot_ref, first_ref, near_ref, pre_ref, out_hbm, grad_ref,
-    rows_ref, parity_ref, taps_ref, act_ref, columns_ref, rowed_ref, back_ref, sums_ref, out_ref, out_sem,
+    chips, narrow, scale, across_ref, select_ref, w1_ref, w2_ref, cot_ref, first_ref, near_ref, pre_ref,
+    out_ref, give_ref, keep_ref, columns_ref, kept_ref,
+    rows_ref, parity_ref, taps_ref, act_ref, rowed_ref, given_ref, mixed_ref, sums_ref,
 ):
     odd = lax.axis_index("core")
     last = (lax.axis_index("chip") == chips - 1) & (odd == 1)
@@ -212,49 +250,66 @@
         act_ref[C1:, there] = (first_act[C1:] * inside).astype(jnp.bfloat16)
     shifted_columns(act_ref, columns_ref)
     second_layer(w2_ref[odd], columns_ref, rowed_ref)
+
     margin = jnp.zeros((HALF, LANES), jnp.bfloat16)
-    back_ref[0:HALF, :] = margin
-    back_ref[HALF + PLANE :, :] = margin
+    for ref in (given_ref, mixed_ref, kept_ref):
+        ref[HALF : 2 * HALF, :] = margin
+        ref[PLANE : PLANE + HALF, :] = margin
+    half = C2 // (2 * narrow)
+
+    def halves(x):
+        lower = [x[2 * n * half : (2 * n + 1) * half] for n in range(narrow)]
+        upper = [x[(2 * n + 1) * half : (2 * n + 2) * half] for n in range(narrow)]
+        give = jnp.concatenate([jnp.where(odd == 1, l, u) for l, u in zip(lower, upper)], axis=0)
+        keep = jnp.concatenate([jnp.where(odd == 1, u, l) for l, u in zip(lower, upper)], axis=0)
+        return give, keep
+
     for n in range(4):
         pre = pre_ref[:, 256 * n : 256 * n + 256] + row_sum(rowed_ref, n)
         output = leaky_relu(pre).astype(jnp.bfloat16)
         slope = jnp.where(pre > 0, 1.0, neg_slope)
-        backs = []
+        parts = []
         for z in range(2):
             cells = slice(z * PLANE + 256 * n, z * PLANE + 256 * n + 256)
             rows = slice(z * C2, (z + 1) * C2)
             out_ref[0, 0, :, cells] = output[rows]
-            backs.append((cot_ref[0, 0, :, cells].astype(jnp.float32) * slope[rows]).astype(jnp.bfloat16))
-        back_ref[HALF + 256 * n : HALF + 256 * n + 256, :] = jnp.concatenate(backs, axis=0).T
+            parts.append(halves(cot_ref[0, 0, :, cells].astype(jnp.float32) * slope[rows]))
+        order = jnp.concatenate([parts[0][0], parts[1][0], parts[0][1], parts[1][1]], axis=0)
+        back = order.astype(jnp.bfloat16).T
+        other = jnp.concatenate([back[:, C2:], back[:, 0:C2]], axis=1)
+        rows = [slice(256 * n + HALF * b, 256 * n + HALF * b + 256) for b in range(3)]
+        given_ref[rows[0], 0:C2] = back[:, 0:C2]
+        given_ref[rows[1], C2:] = other[:, C2:]
+        mixed_ref[rows[2], :] = back
+        kept_ref[rows[0], 0:C2] = other[:, 0:C2]
+        kept_ref[rows[1], C2:] = back[:, C2:]
+    middle = slice(HALF, HALF + PLANE)
+    gradient_sums(odd, near_ref, columns_ref, jnp.concatenate([given_ref[middle, :], mixed_ref[middle, :]], axis=1), sums_ref)
+    given, mixed = paired_terms(sums_ref, 0), paired_terms(sums_ref, 1)
+    first = turned_groups(given[0:4], scale)
+    second = turned_groups(mixed[0:4], scale)
+    third = turned_groups([given[4], mixed[4], given[4], mixed[4]], scale)
+    group = group_of_lane()
+    tiles = first + second[0:2] + [jnp.where(group < 2, third[0], pltpu.roll(third[2], C2, 1))]
+    for k, tile in enumerate(tiles):
+        give_ref[:, k * LANES : (k + 1) * LANES] = tile.astype(jnp.bfloat16)
+    for k, tile in enumerate((second[2], second[3], third[2])):
+        keep_ref[:, k * LANES : (k + 1) * LANES] = tile
+
+
+def rest_kernel(scale, out_ref, near_ref, far_ref, kept_ref, mixed_ref, out_hbm, keep_ref, sums_ref, out_sem):
     out_copy = pltpu.make_async_copy(out_ref, out_hbm, out_sem)
     out_copy.start()
-    columns = jnp.concatenate([near_ref[...], columns_ref[...]], axis=0)
-    rowed_back = jnp.concatenate([back_ref[(2 - b) * HALF : (2 - b) * HALF + PLANE, :] for b in range(3)], axis=1)
-    sums = jnp.dot(columns, rowed_back, preferred_element_type=jnp.float32)
-    sums_ref[1 - odd] = sums[0 : 6 * C1]
-    sums_ref[odd] = sums[6 * C1 :]
-    low = lax.broadcasted_iota(jnp.int32, (C1, LANES), 1) < C2
-
-    def plane_sums(bc, q):
-        b, c = divmod(bc, 3)
-        begin = 2 * C1 * c + C1 * (q % 2)
-        return sums_ref[q // 2, begin : begin + C1, b * LANES : (b + 1) * LANES]
-
-    def two_taps(first, second):
-        a, bc = divmod(first, 9)
-        here, above = plane_sums(bc, a), pltpu.roll(plane_sums(bc, a + 1), C2, 1)
-        if second > 26:
-            return here + above
-        a, bc = divmod(second, 9)
-        there, beyond = pltpu.roll(plane_sums(bc, a), C2, 1), plane_sums(bc, a + 1)
-        return jnp.where(low, here, there) + jnp.where(low, above, beyond)
-
-    for block in range(4):
-        tall = jnp.concatenate([two_taps(min(8 * block + g, 26), 8 * block + 4 + g) for g in range(4)], axis=0)
-        flat = (tall * scale).T.astype(jnp.bfloat16)
-        grad_ref[:, 2 * block * LANES : (2 * block + 1) * LANES] = flat[0:C2]
-        if block < 3:
-            grad_ref[:, (2 * block + 1) * LANES : (2 * block + 2) * LANES] = flat[C2:]
+    odd = lax.axis_index("core")
+    gradient_sums(odd, near_ref, far_ref, kept_ref[HALF : HALF + PLANE, :], sums_ref)
+    kept = paired_terms(sums_ref, 0)
+    first = turned_groups(kept[0:4], scale)
+    third = turned_groups([kept[4]] * 4, scale)
+    group = group_of_lane()
+    mixed = [mixed_ref[:, k * LANES : (k + 1) * LANES] for k in range(3)]
+    ends = jnp.where(group == 1, mixed[2], jnp.where(group == 0, third[0], pltpu.roll(third[2], C2, 1)))
+    for k, tile in enumerate(first + mixed[0:2] + [ends]):
+        keep_ref[:, k * LANES : (k + 1) * LANES] = tile
     out_copy.wait()
 
 
@@ -264,8 +319,9 @@
         total = parts_ref[core].astype(jnp.float32)
         for k in range(core + 2, wide, 2):
             total = total + parts_ref[k].astype(jnp.float32)
-        for tap in range(27):
-            grad_ref[tap, core * half : (core + 1) * half, :] = total[:, tap * C1 : (tap + 1) * C1]
+        for tap, (tile, slot) in slots().items():
+            begin = tile * LANES + slot * C1
+            grad_ref[tap, core * half : (core + 1) * half, :] = total[:, begin : begin + C1]
 
 
 def body(volumes, first_kernel, second_kernel, cotangent):
@@ -274,7 +330,8 @@
     cells_out = cotangent.shape[3]
     scale = 1.0 / math.sqrt(wide * narrow * cells_out)
     across = lax.ppermute(volumes, WIDE, [p for k in range(1, wide - 1, 2) for p in ((k, k + 1), (k + 1, k))])
-    within = lax.ppermute(volumes, WIDE, [p for k in range(0, wide - 1, 2) for p in ((k, k + 1), (k + 1, k))])
+    pairs = [p for k in range(0, wide - 1, 2) for p in ((k, k + 1), (k + 1, k))]
+    within = lax.ppermute(volumes, WIDE, pairs)
     pinned = pl.BlockSpec(memory_space=pltpu.HBM)
     fast = pl.BlockSpec(memory_space=pltpu.VMEM)
     bf16 = functools.partial(jax.ShapeDtypeStruct, dtype=jnp.bfloat16)
@@ -319,29 +376,43 @@
         name="near",
     )(volumes, within, select, w1_near, w2)
     rows = C2 // narrow
-    output, term = pl.pallas_call(
-        functools.partial(far_kernel, wide // 2, scale),
+    acts, give, mixed, far, kept = pl.pallas_call(
+        functools.partial(far_kernel, wide // 2, narrow, scale),
         in_specs=[fast] * 8,
-        out_specs=(pl.BlockSpec(memory_space=pl.ANY), fast),
-        out_shape=(bf16((1, 1, C2, cells_out)), bf16((C2, PACKED))),
+        out_specs=(fast,) * 5,
+        out_shape=(
+            bf16((1, 1, C2, cells_out)), bf16((C2 // 2, PACKED)), f32((C2 // 2, 3 * LANES)),
+            bf16((6 * C1, PLANE)), bf16((PLANE + 2 * HALF, LANES)),
+        ),
         scratch_shapes=[
             pltpu.VMEM((ROWS, CELLS), jnp.float32),
             pltpu.VMEM((4, ROWS, LANES + PLANE), jnp.bfloat16),
             pltpu.VMEM((9 * ROWS, PLANE), jnp.bfloat16),
             pltpu.VMEM((2 * C1, PLANE + 2 * LANES), jnp.bfloat16),
-            pltpu.VMEM((6 * C1, PLANE), jnp.bfloat16),
             pltpu.VMEM((3, 2 * C2, PLANE + 2 * LANES), jnp.float32),
             pltpu.VMEM((PLANE + 2 * HALF, LANES), jnp.bfloat16),
-            pltpu.VMEM((2, 6 * C1, 3 * LANES), jnp.float32),
-            pltpu.VMEM((1, 1, C2, cells_out), jnp.bfloat16),
-            pltpu.SemaphoreType.DMA,
+            pltpu.VMEM((PLANE + 2 * HALF, LANES), jnp.bfloat16),
+            pltpu.VMEM((2, 6 * C1, 2 * LANES), jnp.float32),
         ],
         compiler_params=pltpu.CompilerParams(vmem_limit_bytes=16 * MIB),
+        cost_estimate=pl.CostEstimate(flops=10**9, bytes_accessed=4 * MIB, transcendentals=0),
         name="far",
     )(across, select, w1_far, w2, cot, first, near, pre)
+    got = lax.ppermute(give, WIDE, pairs)
+    output, keep = pl.pallas_call(
+        functools.partial(rest_kernel, scale),
+        in_specs=[fast] * 5,
+        out_specs=(pl.BlockSpec(memory_space=pl.ANY), fast),
+        out_shape=(bf16((1, 1, C2, cells_out)), f32((C2 // 2, PACKED))),
+        scratch_shapes=[pltpu.VMEM((2, 6 * C1, LANES), jnp.float32), pltpu.SemaphoreType.DMA],
+        compiler_params=pltpu.CompilerParams(vmem_limit_bytes=8 * MIB),
+        cost_estimate=pl.CostEstimate(flops=10**9, bytes_accessed=4 * MIB, transcendentals=0),
+        name="rest",
+    )(acts, near, far, kept, mixed)
     half = rows // 2
-    received = lax.all_to_all(term, ("narrow", "core"), 0, 0, tiled=True)
-    owned = jnp.sum(received.reshape(2 * narrow, half, PACKED).astype(jnp.float32), axis=0).astype(jnp.bfloat16)
+    term = (keep + got.astype(jnp.float32)).astype(jnp.bfloat16)
+    received = lax.all_to_all(term, "narrow", 0, 0, tiled=True)
+    owned = jnp.sum(received.reshape(narrow, half, PACKED).astype(jnp.float32), axis=0).astype(jnp.bfloat16)
     parts = lax.all_to_all(jnp.broadcast_to(owned[None], (wide, half, PACKED)), WIDE, 0, 0, tiled=True)
     weight_grad = pl.pallas_call(
         finish_kernel,

time: 33.2 us -> 33.8 us (1.018)
  blocking collectives: 24.7 us -> 20.3 us
  starting transfers between devices: 1.17 us -> 5.17 us
  Pallas kernels: 6.3 us -> 7.13 us
    all_to_all x1, blocking collectives: 16 us -> 11.6 us  [body(): received = lax.all_to_all(term, 'narrow', 0, 0, tiled=True)]
    ppermute x1 -> x2, starting transfers between devices: 0.52 us -> 4.52 us  [the longest x1 4 us: body(): got = lax.ppermute(give, WIDE, pairs)]
    pallas_call x1 -> x2, Pallas kernels: 2.27 us -> 3.09 us  [the longest x1 2.37 us: body(): pl.pallas_call(functools.partial(far_kernel, wide // 2, narrow, scale), i...]
  transfers between devices with their start and end apart: 2 -> 3, of which waited for: 0 -> 1; matrix products, arithmetic and copies ran while one was open for 0% -> 0% of each run, Pallas kernels for 10% -> 12%
where the time goes in v13:
time: 33.8 us; the launch traced here: 33.6 us
  blocking collectives  20.3 us (60%)
  Pallas kernels  7.13 us (21%)
  starting transfers between devices  5.17 us (15%)
  between operations  0.72 us (2%)
    all_to_all x1, blocking collectives, body(): received = lax.all_to_all(term, 'narrow', 0, 0, tiled=True)  11.6 us
    all_to_all x1, blocking collectives, body(): lax.all_to_all(jnp.broadcast_to(owned[None], (wide, half, PACKED)), WIDE,...  8.72 us
    ppermute x1, starting transfers between devices, body(): got = lax.ppermute(give, WIDE, pairs)  4 us
    pallas_call x1, Pallas kernels, body(): pl.pallas_call(functools.partial(far_kernel, wide // 2, narrow, scale), i...  2.37 us
    pallas_call x1, Pallas kernels, body(): pl.pallas_call(prepare_kernel, in_specs=[pinned] * 5, out_specs=(fast,) *...  1.85 us
    pallas_call x1, Pallas kernels, body(): pl.pallas_call(near_kernel, in_specs=[fast] * 5, out_specs=(fast,) * 3, o...  1.39 us
    pallas_call x1, Pallas kernels, body(): pl.pallas_call(finish_kernel, out_shape=jax.ShapeDtypeStruct((27, rows, C...  0.8 us
    pallas_call x1, Pallas kernels, body(): pl.pallas_call(functools.partial(rest_kernel, scale), in_specs=[fast] * 5...  0.71 us
  transfers between devices with their start and end apart: 3, of which 1 were waited for; matrix products, arithmetic and copies ran while one was open for 0% of the time, Pallas kernels for 12%

profile of v13, /device:TPU:0, one launch (start us, length us, event | category | flops | bytes accessed | tf_op | source)
XLA Modules:
  0.0 33.6 jit_solution(13085516275261625184)
XLA Ops:
  0.6 0.5 %collective-permute-start.1 = (bf16[1,1,4,4,4096]{4,3,2,1,0:T(4,128)(2,1)}, bf16[1,1,4,4,4096]{4,3,2,1,0:T(4,128)(2,1)S(1)}, u32[]{:S(2)}, u32[]{:S(2)}) collective-permute-start(bf16[1,1,4,4,4096]{4,3,2,1,0:T(4,128)(2,1)} %own_ref.1), channel_id=1, source_target_pairs={{0,4},{4,0},{8,12},{12,8},{16,20},{20,16},{24,28},{28,24},{1,5},{5... | collective-permute-start | bytes 393224 | tf_op jit(solution)/shard_map/ppermute | solution.py:334
  1.1 0.7 %collective-permute-start = (bf16[1,1,4,4,4096]{4,3,2,1,0:T(4,128)(2,1)}, bf16[1,1,4,4,4096]{4,3,2,1,0:T(4,128)(2,1)S(1)}, u32[]{:S(2)}, u32[]{:S(2)}) collective-permute-start(bf16[1,1,4,4,4096]{4,3,2,1,0:T(4,128)(2,1)} %own_ref.1), channel_id=1, source_target_pairs={{4,8},{8,4},{12,16},{16,12},{20,24},{24,20},{5,9},{9,5},{13,17},{1... | collective-permute-start | bytes 393224 | tf_op jit(solution)/shard_map/ppermute | solution.py:332
  1.8 0.0 copy-start
  1.8 1.9 %prepare.1 = (bf16[2,64,288]{2,1,0:T(8,128)(2,1)S(1)}, bf16[2,64,144]{2,1,0:T(8,128)(2,1)S(1)}, bf16[2,384,192]{2,1,0:T(8,128)(2,1)S(1)}, bf16[512,512]{1,0:T(8,128)(2,1)S(1)}, bf16[1,1,64,2048]{3,2,1,0:T(8,128)(2,1)S(1)}) custom-call(bf16[27,4,32]{2,1,0:T(4,128)(2,1)} %bitcast.5, bf16[2,108,2048]{2,1,0:T(8,128)(2,1)} %constant.7.clone.place_hbm, ...), custom_call_target="tpu_custom_call" | custom-call | flops 1000000000 | bytes 4194304 | tf_op jit(solution)/shard_map/prepare/pallas_call | solution.py:343
  3.7 0.0 collective-permute-done.1.within_ref
  3.7 0.0 copy-done
  3.7 1.4 %near.1 = (f32[64,1024]{1,0:T(8,128)S(1)}, bf16[192,1024]{1,0:T(8,128)(2,1)S(1)}, f32[128,1024]{1,0:T(8,128)S(1)}) custom-call(bf16[1,1,4,4,4096]{4,3,2,1,0:T(4,128)(2,1)S(1)} %copy-done, bf16[1,1,4,4,4096]{4,3,2,1,0:T(4,128)(2,1)S(1)} %collective-permute-done.1.within_ref, bf16[512,512]{1,0:T(8,128)(2,1)S(1)} %get-tuple-element.17.select_ref, ...), custom_call_target="tpu_custom_call" | custom-call | flops 1000000000 | bytes 4194304 | tf_op jit(solution)/shard_map/near/pallas_call | solution.py:362
  5.1 0.0 collective-permute-done.across_ref
  5.1 2.4 %far.1 = (bf16[1,1,64,2048]{3,2,1,0:T(8,128)(2,1)S(1)}, bf16[32,896]{1,0:T(8,128)(2,1)S(1)}, f32[32,384]{1,0:T(8,128)S(1)}, bf16[192,1024]{1,0:T(8,128)(2,1)S(1)}, bf16[1088,128]{1,0:T(8,128)(2,1)S(1)}) custom-call(bf16[1,1,4,4,4096]{4,3,2,1,0:T(4,128)(2,1)S(1)} %collective-permute-done.across_ref, bf16[512,512]{1,0:T(8,128)(2,1)S(1)} %get-tuple-element.17.select_ref, ...), custom_call_target="tpu_custom_call" | custom-call | flops 1000000000 | bytes 4194304 | tf_op jit(solution)/shard_map/far/pallas_call | solution.py:379
  7.5 4.0 %collective-permute-start.2 = (bf16[32,896]{1,0:T(8,128)(2,1)S(1)}, bf16[32,896]{1,0:T(8,128)(2,1)S(1)}, u32[]{:S(2)}, u32[]{:S(2)}) collective-permute-start(bf16[32,896]{1,0:T(8,128)(2,1)S(1)} %get-tuple-element.31), channel_id=1, source_target_pairs={{0,4},{4,0},{8,12},{12,8},{16,20},{20,16},{24,28},{28,24},{1,5},{5... | collective-permute-start | bytes 172040 | tf_op jit(solution)/shard_map/ppermute | solution.py:401
  11.5 0.7 %rest.1 = (bf16[1,1,64,2048]{3,2,1,0:T(8,128)(2,1)}, f32[32,896]{1,0:T(8,128)S(1)}) custom-call(bf16[1,1,64,2048]{3,2,1,0:T(8,128)(2,1)S(1)} %get-tuple-element.25.out_ref, bf16[192,1024]{1,0:T(8,128)(2,1)S(1)} %get-tuple-element.23.near_ref, bf16[192,1024]{1,0:T(8,128)(2,1)S(1)} %get-tuple-element.26.far_ref, ...), custom_call_target="tpu_custom_call" | custom-call | flops 1000000000 | bytes 4194304 | tf_op jit(solution)/shard_map/rest/pallas_call | solution.py:402
  12.2 0.2 collective-permute-done.2
  12.4 11.6 %all_to_all.14 = bf16[4,8,896]{2,1,0:T(8,128)(2,1)S(1)} all-to-all(bf16[4,8,896]{2,1,0:T(8,128)(2,1)S(1)} %fusion), channel_id=1, replica_groups=mesh['chip'=4,'core'=2,'narrow'=4] {'narrow'}, dimensions={0} | all-to-all | bytes 114688 | tf_op jit(solution)/shard_map/all_to_all | solution.py:414
  24.0 8.7 %all_to_all.15.parts_ref = bf16[8,8,896]{2,1,0:T(8,128)(2,1)S(1)} all-to-all(bf16[8,8,896]{2,1,0:T(8,128)(2,1)S(1)} %broadcast_in_dim.2), channel_id=1, replica_groups=mesh['chip'=4,'core'=2,'narrow'=4] {'chip','core'}, dimensions={0} | all-to-all | bytes 229376 | tf_op jit(solution)/shard_map/all_to_all | solution.py:416
  32.8 0.8 %finish.1 = f32[27,16,32]{2,1,0:T(8,128)} custom-call(bf16[8,8,896]{2,1,0:T(8,128)(2,1)S(1)} %all_to_all.15.parts_ref), custom_call_target="tpu_custom_call" | custom-call | tf_op jit(solution)/shard_map/finish/pallas_call | solution.py:417
  (3 shorter events, 0.0 us)
Async XLA Ops:
  0.6 3.1 %collective-permute-start.1 = (bf16[1,1,4,4,4096]{4,3,2,1,0:T(4,128)(2,1)}, bf16[1,1,4,4,4096]{4,3,2,1,0:T(4,128)(2,1)S(1)}, u32[]{:S(2)}, u32[]{:S(2)}) collective-permute-start(bf16[1,1,4,4,4096]{4,3,2,1,0:T(4,128)(2,1)} %own_ref.1), channel_id=1, source_target_pairs={{0,4},{4,0},{8,12},{12,8},{16,20},{20,16},{24,28},{28,24},{1,5},{5... | collective-permute-start | bytes 393224 | tf_op jit(solution)/shard_map/ppermute | solution.py:334
  1.1 4.0 %collective-permute-start = (bf16[1,1,4,4,4096]{4,3,2,1,0:T(4,128)(2,1)}, bf16[1,1,4,4,4096]{4,3,2,1,0:T(4,128)(2,1)S(1)}, u32[]{:S(2)}, u32[]{:S(2)}) collective-permute-start(bf16[1,1,4,4,4096]{4,3,2,1,0:T(4,128)(2,1)} %own_ref.1), channel_id=1, source_target_pairs={{4,8},{8,4},{12,16},{16,12},{20,24},{24,20},{5,9},{9,5},{13,17},{1... | collective-permute-start | bytes 393224 | tf_op jit(solution)/shard_map/ppermute | solution.py:332
  1.8 1.9 %copy-start = (bf16[1,1,4,4,4096]{4,3,2,1,0:T(4,128)(2,1)S(1)}, bf16[1,1,4,4,4096]{4,3,2,1,0:T(4,128)(2,1)}, u32[]{:S(2)}) copy-start(bf16[1,1,4,4,4096]{4,3,2,1,0:T(4,128)(2,1)} %own_ref.1) | copy-start | bytes 393220
  7.5 4.9 %collective-permute-start.2 = (bf16[32,896]{1,0:T(8,128)(2,1)S(1)}, bf16[32,896]{1,0:T(8,128)(2,1)S(1)}, u32[]{:S(2)}, u32[]{:S(2)}) collective-permute-start(bf16[32,896]{1,0:T(8,128)(2,1)S(1)} %get-tuple-element.31), channel_id=1, source_target_pairs={{0,4},{4,0},{8,12},{12,8},{16,20},{20,16},{24,28},{28,24},{1,5},{5... | collective-permute-start | bytes 172040 | tf_op jit(solution)/shard_map/ppermute | solution.py:401

commit v14 on v13

--- a/solution.py
+++ b/solution.py
@@ -52,6 +52,18 @@
                             column = 18 * ROWS + bc * ROWS + inner
                         table[odd, 9 * a + bc, i, q, column] = 1
     return table.reshape(2, 27 * CIN, 4 * CHUNK)
+
+
+def channel_order(narrow):
+    half = C2 // (2 * narrow)
+    table = np.zeros((2, 2 * C2, 2 * C2), np.float32)
+    for odd in range(2):
+        for z in range(2):
+            for o in range(C2):
+                owner, inner = divmod(o, 2 * half)
+                side, row = divmod(inner, half)
+                table[odd, z * C2 + o, (side == odd) * C2 + z * C1 + owner * half + row] = 1
+    return table
 
 
 def leaky_relu(value):
@@ -106,23 +118,24 @@
         columns_ref[c * 2 * C1 : (c + 1) * 2 * C1, :] = part
 
 
-def second_layer(w2, columns_ref, rowed_ref):
-    blank = jnp.zeros((2 * C2, LANES), jnp.float32)
+def second_layer(w2, columns_ref, turned_ref, rowed_ref):
+    blank = jnp.zeros((HALF, LANES), jnp.float32)
     for b in (0, 2):
-        rowed_ref[b, :, 0:LANES] = blank
-        rowed_ref[b, :, LANES + PLANE :] = blank
-    for n in range(4):
-        sums = jnp.dot(w2, columns_ref[:, 256 * n : 256 * n + 256], preferred_element_type=jnp.float32)
+        rowed_ref[b, 0:HALF, :] = blank
+        rowed_ref[b, HALF + PLANE :, :] = blank
+    for n in range(4):
+        cells = slice(256 * n, 256 * n + 256)
+        turned_ref[cells, :] = columns_ref[:, cells].T
+    for n in range(4):
+        sums = jnp.dot(turned_ref[256 * n : 256 * n + 256, :], w2, preferred_element_type=jnp.float32)
         for b in range(3):
-            rowed_ref[b, :, LANES + 256 * n : LANES + 256 * n + 256] = sums[b * 2 * C2 : (b + 1) * 2 * C2]
+            rowed_ref[b, HALF + 256 * n : HALF + 256 * n + 256, :] = sums[:, b * LANES : (b + 1) * LANES]
 
 
 def row_sum(rowed_ref, n):
-    total = rowed_ref[1, :, LANES + 256 * n : LANES + 256 * n + 256]
-    for b in (0, 2):
-        begin = LANES + HALF * (b - 1) + 256 * n
-        total = total + rowed_ref[b, :, begin : begin + 256]
-    return total
+    begins = [HALF * b + 256 * n for b in range(3)]
+    first, second, third = (rowed_ref[b, begin : begin + 256, :] for b, begin in enumerate(begins))
+    return first + second + third
 
 
 def clear_margins(act_ref):
@@ -132,11 +145,15 @@
 
 
 def prepare_kernel(
-    k1_hbm, place_hbm, k2_hbm, select_hbm, cot_hbm, w1_near_ref, w1_far_ref, w2_ref, select_ref, cot_ref,
-    k1_ref, place_ref, k2_ref, k1_rows_ref, sems,
+    k1_hbm, place_hbm, k2_hbm, select_hbm, cot_hbm, order_hbm,
+    w1_near_ref, w1_far_ref, w2_ref, select_ref, turned_ref, order_ref,
+    k1_ref, place_ref, k2_ref, cot_ref, k1_rows_ref, k2_rows_ref, sems,
 ):
     odd = lax.axis_index("core")
-    moves = ((k1_hbm, k1_ref), (k2_hbm, k2_ref), (place_hbm.at[odd], place_ref), (select_hbm, select_ref), (cot_hbm, cot_ref))
+    moves = (
+        (k1_hbm, k1_ref), (k2_hbm, k2_ref), (order_hbm.at[odd], order_ref),
+        (place_hbm.at[odd], place_ref), (cot_hbm, cot_ref), (select_hbm, select_ref),
+    )
     copies = [pltpu.make_async_copy(src, dst, sems.at[k]) for k, (src, dst) in enumerate(moves)]
     for copy in copies:
         copy.start()
@@ -152,15 +169,18 @@
         upper = jnp.concatenate(k[2 * pair : 2 + 2 * pair], axis=0)
         return jnp.concatenate([lower, upper], axis=1)
 
-    for b in range(3):
-        rows = slice(b * 2 * C2, (b + 1) * 2 * C2)
-        for pair in range(2):
-            both = jnp.concatenate([stacked(3 * b, pair), stacked(3 * b + 1, pair)], axis=0)
-            w2_ref[pair, rows, 0:LANES] = both.T
-        both = jnp.concatenate([stacked(3 * b + 2, 0), stacked(3 * b + 2, 1)], axis=0).T
-        for pair in range(2):
-            w2_ref[pair, rows, LANES : LANES + 2 * C1] = both[:, pair * 2 * C1 : (pair + 1) * 2 * C1]
+    for pair in range(2):
+        for bc in range(9):
+            begin = (9 * pair + bc) * 2 * C1
+            k2_rows_ref[begin : begin + 2 * C1, :] = stacked(bc, pair)
     copies[2].wait()
+    ordered = jnp.dot(k2_rows_ref[...], order_ref[...], preferred_element_type=jnp.float32).astype(jnp.bfloat16)
+    for pair in range(2):
+        for b in range(3):
+            for c in range(3):
+                begin = (9 * pair + 3 * b + c) * 2 * C1
+                w2_ref[pair, c * 2 * C1 : (c + 1) * 2 * C1, b * LANES : (b + 1) * LANES] = ordered[begin : begin + 2 * C1]
+    copies[3].wait()
     spread = lax.dot_general(
         k1_rows_ref[...].astype(jnp.bfloat16), place_ref[...],
         (((0,), (0,)), ((), ())), preferred_element_type=jnp.float32,
@@ -169,13 +189,19 @@
         rows = slice(q % 2 * C1, (q % 2 + 1) * C1)
         w1_near_ref[q // 2, rows, :] = spread[:, CHUNK * q : CHUNK * q + 18 * ROWS]
         w1_far_ref[q // 2, rows, :] = spread[:, CHUNK * q + 18 * ROWS : CHUNK * q + 27 * ROWS]
-    copies[3].wait()
     copies[4].wait()
+    for n in range(4):
+        planes = [cot_ref[0, 0, :, z * PLANE + 256 * n : z * PLANE + 256 * n + 256] for z in range(2)]
+        turned = jnp.concatenate(planes, axis=0).T
+        turned_ref[256 * n : 256 * n + 256, :] = jnp.dot(
+            turned, order_ref[...], preferred_element_type=jnp.float32
+        ).astype(jnp.bfloat16)
+    copies[5].wait()
 
 
 def near_kernel(
     own_ref, within_ref, select_ref, w1_ref, w2_ref, first_ref, columns_ref, pre_ref,
-    rows_ref, parity_ref, taps_ref, act_ref, rowed_ref,
+    rows_ref, parity_ref, taps_ref, act_ref, turned_ref, rowed_ref,
 ):
     odd = lax.axis_index("core")
     plane_rows(own_ref, rows_ref.at[0:ROWS])
@@ -188,9 +214,9 @@
         complete = jnp.dot(w1_ref[1 - odd], taps_ref[:, here], preferred_element_type=jnp.float32)
         act_ref[:, LANES + 256 * n : LANES + 256 * n + 256] = leaky_relu(complete).astype(jnp.bfloat16)
     shifted_columns(act_ref, columns_ref)
-    second_layer(w2_ref[1 - odd], columns_ref, rowed_ref)
-    for n in range(4):
-        pre_ref[:, 256 * n : 256 * n + 256] = row_sum(rowed_ref, n)
+    second_layer(w2_ref[1 - odd], columns_ref, turned_ref, rowed_ref)
+    for n in range(4):
+        pre_ref[256 * n : 256 * n + 256, :] = row_sum(rowed_ref, n)
 
 
 def slots():
@@ -231,9 +257,9 @@
 
 
 def far_kernel(
-    chips, narrow, scale, across_ref, select_ref, w1_ref, w2_ref, cot_ref, first_ref, near_ref, pre_ref,
-    out_ref, give_ref, keep_ref, columns_ref, kept_ref,
-    rows_ref, parity_ref, taps_ref, act_ref, rowed_ref, given_ref, mixed_ref, sums_ref,
+    chips, scale, across_ref, select_ref, w1_ref, w2_ref, cot_ref, first_ref, near_ref, near_pre_ref,
+    pre_ref, give_ref, keep_ref, columns_ref, kept_ref,
+    rows_ref, parity_ref, taps_ref, act_ref, turned_ref, rowed_ref, given_ref, mixed_ref, sums_ref,
 ):
     odd = lax.axis_index("core")
     last = (lax.axis_index("chip") == chips - 1) & (odd == 1)
@@ -249,33 +275,17 @@
         act_ref[0:C1, there] = first_act[0:C1].astype(jnp.bfloat16)
         act_ref[C1:, there] = (first_act[C1:] * inside).astype(jnp.bfloat16)
     shifted_columns(act_ref, columns_ref)
-    second_layer(w2_ref[odd], columns_ref, rowed_ref)
+    second_layer(w2_ref[odd], columns_ref, turned_ref, rowed_ref)
 
     margin = jnp.zeros((HALF, LANES), jnp.bfloat16)
     for ref in (given_ref, mixed_ref, kept_ref):
         ref[HALF : 2 * HALF, :] = margin
         ref[PLANE : PLANE + HALF, :] = margin
-    half = C2 // (2 * narrow)
-
-    def halves(x):
-        lower = [x[2 * n * half : (2 * n + 1) * half] for n in range(narrow)]
-        upper = [x[(2 * n + 1) * half : (2 * n + 2) * half] for n in range(narrow)]
-        give = jnp.concatenate([jnp.where(odd == 1, l, u) for l, u in zip(lower, upper)], axis=0)
-        keep = jnp.concatenate([jnp.where(odd == 1, u, l) for l, u in zip(lower, upper)], axis=0)
-        return give, keep
-
-    for n in range(4):
-        pre = pre_ref[:, 256 * n : 256 * n + 256] + row_sum(rowed_ref, n)
-        output = leaky_relu(pre).astype(jnp.bfloat16)
-        slope = jnp.where(pre > 0, 1.0, neg_slope)
-        parts = []
-        for z in range(2):
-            cells = slice(z * PLANE + 256 * n, z * PLANE + 256 * n + 256)
-            rows = slice(z * C2, (z + 1) * C2)
-            out_ref[0, 0, :, cells] = output[rows]
-            parts.append(halves(cot_ref[0, 0, :, cells].astype(jnp.float32) * slope[rows]))
-        order = jnp.concatenate([parts[0][0], parts[1][0], parts[0][1], parts[1][1]], axis=0)
-        back = order.astype(jnp.bfloat16).T
+    for n in range(4):
+        cells = slice(256 * n, 256 * n + 256)
+        pre = near_pre_ref[cells, :] + row_sum(rowed_ref, n)
+        pre_ref[cells, :] = pre
+        back = (cot_ref[cells, :].astype(jnp.float32) * jnp.where(pre > 0, 1.0, neg_slope)).astype(jnp.bfloat16)
         other = jnp.concatenate([back[:, C2:], back[:, 0:C2]], axis=1)
         rows = [slice(256 * n + HALF * b, 256 * n + HALF * b + 256) for b in range(3)]
         given_ref[rows[0], 0:C2] = back[:, 0:C2]
@@ -297,7 +307,16 @@
         keep_ref[:, k * LANES : (k + 1) * LANES] = tile
 
 
-def rest_kernel(scale, out_ref, near_ref, far_ref, kept_ref, mixed_ref, out_hbm, keep_ref, sums_ref, out_sem):
+def rest_kernel(
+    scale, pre_ref, order_ref, near_ref, far_ref, kept_ref, mixed_ref, out_hbm, keep_ref, sums_ref, out_ref, out_sem,
+):
+    for n in range(4):
+        output = leaky_relu(pre_ref[256 * n : 256 * n + 256, :]).astype(jnp.bfloat16)
+        ordered = lax.dot_general(
+            order_ref[...], output, (((1,), (1,)), ((), ())), preferred_element_type=jnp.float32
+        ).astype(jnp.bfloat16)
+        for z in range(2):
+            out_ref[0, 0, :, z * PLANE + 256 * n : z * PLANE + 256 * n + 256] = ordered[z * C2 : (z + 1) * C2]
     out_copy = pltpu.make_async_copy(out_ref, out_hbm, out_sem)
     out_copy.start()
     odd = lax.axis_index("core")
@@ -338,22 +357,24 @@
     f32 = functools.partial(jax.ShapeDtypeStruct, dtype=jnp.float32)
     stored = (
         first_kernel.transpose(0, 2, 1), jnp.asarray(placement(), jnp.bfloat16), second_kernel.transpose(0, 2, 1),
-        jnp.asarray(selection(), jnp.bfloat16), cotangent,
+        jnp.asarray(selection(), jnp.bfloat16), cotangent, jnp.asarray(channel_order(narrow), jnp.bfloat16),
     )
-    w1_near, w1_far, w2, select, cot = pl.pallas_call(
+    w1_near, w1_far, w2, select, cot, order = pl.pallas_call(
         prepare_kernel,
-        in_specs=[pinned] * 5,
-        out_specs=(fast,) * 5,
+        in_specs=[pinned] * 6,
+        out_specs=(fast,) * 6,
         out_shape=(
-            bf16((2, 2 * C1, 18 * ROWS)), bf16((2, 2 * C1, 9 * ROWS)), bf16((2, 6 * C2, 6 * C1)),
-            bf16((CHUNK, CHUNK)), bf16(cotangent.shape),
+            bf16((2, 2 * C1, 18 * ROWS)), bf16((2, 2 * C1, 9 * ROWS)), bf16((2, 6 * C1, 6 * C2)),
+            bf16((CHUNK, CHUNK)), bf16((PLANE, 2 * C2)), bf16((2 * C2, 2 * C2)),
         ),
         scratch_shapes=[
             pltpu.VMEM((27, CIN, C1), jnp.bfloat16),
             pltpu.VMEM((27 * CIN, 4 * CHUNK), jnp.bfloat16),
             pltpu.VMEM((27, C1, C2), jnp.bfloat16),
+            pltpu.VMEM(cotangent.shape, jnp.bfloat16),
             pltpu.VMEM((27 * CIN, C1), jnp.float32),
-            pltpu.SemaphoreType.DMA((5,)),
+            pltpu.VMEM((36 * C1, 2 * C2), jnp.bfloat16),
+            pltpu.SemaphoreType.DMA((6,)),
         ],
         compiler_params=pltpu.CompilerParams(vmem_limit_bytes=12 * MIB),
         cost_estimate=pl.CostEstimate(flops=10**9, bytes_accessed=4 * MIB, transcendentals=0),
@@ -363,25 +384,26 @@
         near_kernel,
         in_specs=[fast] * 5,
         out_specs=(fast,) * 3,
-        out_shape=(f32((2 * C1, PLANE)), bf16((6 * C1, PLANE)), f32((2 * C2, PLANE))),
+        out_shape=(f32((2 * C1, PLANE)), bf16((6 * C1, PLANE)), f32((PLANE, 2 * C2))),
         scratch_shapes=[
             pltpu.VMEM((2 * ROWS, CELLS), jnp.float32),
             pltpu.VMEM((4, 2 * ROWS, LANES + PLANE), jnp.bfloat16),
             pltpu.VMEM((18 * ROWS, PLANE), jnp.bfloat16),
             pltpu.VMEM((2 * C1, PLANE + 2 * LANES), jnp.bfloat16),
-            pltpu.VMEM((3, 2 * C2, PLANE + 2 * LANES), jnp.float32),
+            pltpu.VMEM((PLANE, 6 * C1), jnp.bfloat16),
+            pltpu.VMEM((3, PLANE + 2 * HALF, LANES), jnp.float32),
         ],
         compiler_params=pltpu.CompilerParams(vmem_limit_bytes=16 * MIB),
         cost_estimate=pl.CostEstimate(flops=10**9, bytes_accessed=4 * MIB, transcendentals=0),
         name="near",
     )(volumes, within, select, w1_near, w2)
     rows = C2 // narrow
-    acts, give, mixed, far, kept = pl.pallas_call(
-        functools.partial(far_kernel, wide // 2, narrow, scale),
+    pre, give, mixed, far, kept = pl.pallas_call(
+        functools.partial(far_kernel, wide // 2, scale),
         in_specs=[fast] * 8,
         out_specs=(fast,) * 5,
         out_shape=(
-            bf16((1, 1, C2, cells_out)), bf16((C2 // 2, PACKED)), f32((C2 // 2, 3 * LANES)),
+            f32((PLANE, 2 * C2)), bf16((C2 // 2, PACKED)), f32((C2 // 2, 3 * LANES)),
             bf16((6 * C1, PLANE)), bf16((PLANE + 2 * HALF, LANES)),
         ),
         scratch_shapes=[
@@ -389,7 +411,8 @@
             pltpu.VMEM((4, ROWS, LANES + PLANE), jnp.bfloat16),
             pltpu.VMEM((9 * ROWS, PLANE), jnp.bfloat16),
             pltpu.VMEM((2 * C1, PLANE + 2 * LANES), jnp.bfloat16),
-            pltpu.VMEM((3, 2 * C2, PLANE + 2 * LANES), jnp.float32),
+            pltpu.VMEM((PLANE, 6 * C1), jnp.bfloat16),
+            pltpu.VMEM((3, PLANE + 2 * HALF, LANES), jnp.float32),
             pltpu.VMEM((PLANE + 2 * HALF, LANES), jnp.bfloat16),
             pltpu.VMEM((PLANE + 2 * HALF, LANES), jnp.bfloat16),
             pltpu.VMEM((2, 6 * C1, 2 * LANES), jnp.float32),
@@ -401,14 +424,18 @@
     got = lax.ppermute(give, WIDE, pairs)
     output, keep = pl.pallas_call(
         functools.partial(rest_kernel, scale),
-        in_specs=[fast] * 5,
+        in_specs=[fast] * 6,
         out_specs=(pl.BlockSpec(memory_space=pl.ANY), fast),
         out_shape=(bf16((1, 1, C2, cells_out)), f32((C2 // 2, PACKED))),
-        scratch_shapes=[pltpu.VMEM((2, 6 * C1, LANES), jnp.float32), pltpu.SemaphoreType.DMA],
+        scratch_shapes=[
+            pltpu.VMEM((2, 6 * C1, LANES), jnp.float32),
+            pltpu.VMEM((1, 1, C2, cells_out), jnp.bfloat16),
+            pltpu.SemaphoreType.DMA,
+        ],
         compiler_params=pltpu.CompilerParams(vmem_limit_bytes=8 * MIB),
         cost_estimate=pl.CostEstimate(flops=10**9, bytes_accessed=4 * MIB, transcendentals=0),
         name="rest",
-    )(acts, near, far, kept, mixed)
+    )(pre, order, near, far, kept, mixed)
     half = rows // 2
     term = (keep + got.astype(jnp.float32)).astype(jnp.bfloat16)
     received = lax.all_to_all(term, "narrow", 0, 0, tiled=True)

time: 33.8 us -> 33.4 us (0.988)
  transfers between devices with their start and end apart: 3 -> 3, of which waited for: 1 -> 0; matrix products, arithmetic and copies ran while one was open for 0% -> 0% of each run, Pallas kernels for 12% -> 13%
where the time goes in v14:
time: 33.4 us; the launch traced here: 33.2 us
  blocking collectives  20.1 us (60%)
  Pallas kernels  7.24 us (22%)
  starting transfers between devices  5.1 us (15%)
  between operations  0.72 us (2%)
    all_to_all x1, blocking collectives, body(): received = lax.all_to_all(term, 'narrow', 0, 0, tiled=True)  11.4 us
    all_to_all x1, blocking collectives, body(): lax.all_to_all(jnp.broadcast_to(owned[None], (wide, half, PACKED)), WIDE,...  8.64 us
    ppermute x1, starting transfers between devices, body(): got = lax.ppermute(give, WIDE, pairs)  3.93 us
    pallas_call x1, Pallas kernels, body(): pl.pallas_call(prepare_kernel, in_specs=[pinned] * 6, out_specs=(fast,) *...  2.09 us
    pallas_call x1, Pallas kernels, body(): pl.pallas_call(functools.partial(far_kernel, wide // 2, scale), in_specs=...  2.02 us
    pallas_call x1, Pallas kernels, body(): pl.pallas_call(near_kernel, in_specs=[fast] * 5, out_specs=(fast,) * 3, o...  1.39 us
    pallas_call x1, Pallas kernels, body(): pl.pallas_call(functools.partial(rest_kernel, scale), in_specs=[fast] * 6...  0.95 us
    pallas_call x1, Pallas kernels, body(): pl.pallas_call(finish_kernel, out_shape=jax.ShapeDtypeStruct((27, rows, C...  0.8 us
  transfers between devices with their start and end apart: 3, of which 0 were waited for; matrix products, arithmetic and copies ran while one was open for 0% of the time, Pallas kernels for 13%

profile of v14, /device:TPU:0, one launch (start us, length us, event | category | flops | bytes accessed | tf_op | source)
XLA Modules:
  0.0 33.2 jit_solution(193674835563725872)
XLA Ops:
  0.6 0.5 %collective-permute-start.1 = (bf16[1,1,4,4,4096]{4,3,2,1,0:T(4,128)(2,1)}, bf16[1,1,4,4,4096]{4,3,2,1,0:T(4,128)(2,1)S(1)}, u32[]{:S(2)}, u32[]{:S(2)}) collective-permute-start(bf16[1,1,4,4,4096]{4,3,2,1,0:T(4,128)(2,1)} %own_ref.1), channel_id=1, source_target_pairs={{0,4},{4,0},{8,12},{12,8},{16,20},{20,16},{24,28},{28,24},{1,5},{5... | collective-permute-start | bytes 393224 | tf_op jit(solution)/shard_map/ppermute | solution.py:353
  1.1 0.7 %collective-permute-start = (bf16[1,1,4,4,4096]{4,3,2,1,0:T(4,128)(2,1)}, bf16[1,1,4,4,4096]{4,3,2,1,0:T(4,128)(2,1)S(1)}, u32[]{:S(2)}, u32[]{:S(2)}) collective-permute-start(bf16[1,1,4,4,4096]{4,3,2,1,0:T(4,128)(2,1)} %own_ref.1), channel_id=1, source_target_pairs={{4,8},{8,4},{12,16},{16,12},{20,24},{24,20},{5,9},{9,5},{13,17},{1... | collective-permute-start | bytes 393224 | tf_op jit(solution)/shard_map/ppermute | solution.py:351
  1.8 0.0 copy-start
  1.8 2.1 %prepare.1 = (bf16[2,64,288]{2,1,0:T(8,128)(2,1)S(1)}, bf16[2,64,144]{2,1,0:T(8,128)(2,1)S(1)}, bf16[2,192,384]{2,1,0:T(8,128)(2,1)S(1)}, bf16[512,512]{1,0:T(8,...) custom-call(bf16[27,4,32]{2,1,0:T(4,128)(2,1)} %bitcast.5, ...), custom_call_target="tpu_custom_call" | custom-call | flops 1000000000 | bytes 4194304 | tf_op jit(solution)/shard_map/prepare/pallas_call | solution.py:362
  3.9 0.0 collective-permute-done.1.within_ref
  3.9 0.0 copy-done
  3.9 1.4 %near.1 = (f32[64,1024]{1,0:T(8,128)S(1)}, bf16[192,1024]{1,0:T(8,128)(2,1)S(1)}, f32[1024,128]{1,0:T(8,128)S(1)}) custom-call(bf16[1,1,4,4,4096]{4,3,2,1,0:T(4,128)(2,1)S(1)} %copy-done, bf16[1,1,4,4,4096]{4,3,2,1,0:T(4,128)(2,1)S(1)} %collective-permute-done.1.within_ref, bf16[512,512]{1,0:T(8,128)(2,1)S(1)} %get-tuple-element.18.select_ref, ...), custom_call_target="tpu_custom_call" | custom-call | flops 1000000000 | bytes 4194304 | tf_op jit(solution)/shard_map/near/pallas_call | solution.py:383
  5.3 0.0 collective-permute-done.across_ref
  5.3 2.0 %far.1 = (f32[1024,128]{1,0:T(8,128)S(1)}, bf16[32,896]{1,0:T(8,128)(2,1)S(1)}, f32[32,384]{1,0:T(8,128)S(1)}, bf16[192,1024]{1,0:T(8,128)(2,1)S(1)}, bf16[1088,128]{1,0:T(8,128)(2,1)S(1)}) custom-call(bf16[1,1,4,4,4096]{4,3,2,1,0:T(4,128)(2,1)S(1)} %collective-permute-done.across_ref, bf16[512,512]{1,0:T(8,128)(2,1)S(1)} %get-tuple-element.18.select_ref, ...), custom_call_target="tpu_custom_call" | custom-call | flops 1000000000 | bytes 4194304 | tf_op jit(solution)/shard_map/far/pallas_call | solution.py:401
  7.4 3.9 %collective-permute-start.2 = (bf16[32,896]{1,0:T(8,128)(2,1)S(1)}, bf16[32,896]{1,0:T(8,128)(2,1)S(1)}, u32[]{:S(2)}, u32[]{:S(2)}) collective-permute-start(bf16[32,896]{1,0:T(8,128)(2,1)S(1)} %get-tuple-element.33), channel_id=1, source_target_pairs={{0,4},{4,0},{8,12},{12,8},{16,20},{20,16},{24,28},{28,24},{1,5},{5... | collective-permute-start | bytes 172040 | tf_op jit(solution)/shard_map/ppermute | solution.py:424
  11.3 1.0 %rest.1 = (bf16[1,1,64,2048]{3,2,1,0:T(8,128)(2,1)}, f32[32,896]{1,0:T(8,128)S(1)}) custom-call(f32[1024,128]{1,0:T(8,128)S(1)} %get-tuple-element.26.pre_ref, bf16[128,128]{1,0:T(8,128)(2,1)S(1)} %get-tuple-element.27.order_ref, bf16[192,1024]{1,0:T(8,128)(2,1)S(1)} %get-tuple-element.24.near_ref, bf16[192,1024]{1,0:T(8,128)(2,1)S(1)} %get-tuple-element.28.far_ref, ...), custom_call_target="tpu_custom_call" | custom-call | flops 1000000000 | bytes 4194304 | tf_op jit(solution)/shard_map/rest/pallas_call | solution.py:425
  12.2 0.0 collective-permute-done.2
  12.3 11.4 %all_to_all.14 = bf16[4,8,896]{2,1,0:T(8,128)(2,1)S(1)} all-to-all(bf16[4,8,896]{2,1,0:T(8,128)(2,1)S(1)} %fusion), channel_id=1, replica_groups=mesh['chip'=4,'core'=2,'narrow'=4] {'narrow'}, dimensions={0} | all-to-all | bytes 114688 | tf_op jit(solution)/shard_map/all_to_all | solution.py:441
  23.8 8.6 %all_to_all.15.parts_ref = bf16[8,8,896]{2,1,0:T(8,128)(2,1)S(1)} all-to-all(bf16[8,8,896]{2,1,0:T(8,128)(2,1)S(1)} %broadcast_in_dim.2), channel_id=1, replica_groups=mesh['chip'=4,'core'=2,'narrow'=4] {'chip','core'}, dimensions={0} | all-to-all | bytes 229376 | tf_op jit(solution)/shard_map/all_to_all | solution.py:443
  32.4 0.8 %finish.1 = f32[27,16,32]{2,1,0:T(8,128)} custom-call(bf16[8,8,896]{2,1,0:T(8,128)(2,1)S(1)} %all_to_all.15.parts_ref), custom_call_target="tpu_custom_call" | custom-call | tf_op jit(solution)/shard_map/finish/pallas_call | solution.py:444
  (3 shorter events, 0.0 us)
Async XLA Ops:
  0.6 3.3 %collective-permute-start.1 = (bf16[1,1,4,4,4096]{4,3,2,1,0:T(4,128)(2,1)}, bf16[1,1,4,4,4096]{4,3,2,1,0:T(4,128)(2,1)S(1)}, u32[]{:S(2)}, u32[]{:S(2)}) collective-permute-start(bf16[1,1,4,4,4096]{4,3,2,1,0:T(4,128)(2,1)} %own_ref.1), channel_id=1, source_target_pairs={{0,4},{4,0},{8,12},{12,8},{16,20},{20,16},{24,28},{28,24},{1,5},{5... | collective-permute-start | bytes 393224 | tf_op jit(solution)/shard_map/ppermute | solution.py:353
  1.1 4.2 %collective-permute-start = (bf16[1,1,4,4,4096]{4,3,2,1,0:T(4,128)(2,1)}, bf16[1,1,4,4,4096]{4,3,2,1,0:T(4,128)(2,1)S(1)}, u32[]{:S(2)}, u32[]{:S(2)}) collective-permute-start(bf16[1,1,4,4,4096]{4,3,2,1,0:T(4,128)(2,1)} %own_ref.1), channel_id=1, source_target_pairs={{4,8},{8,4},{12,16},{16,12},{20,24},{24,20},{5,9},{9,5},{13,17},{1... | collective-permute-start | bytes 393224 | tf_op jit(solution)/shard_map/ppermute | solution.py:351
  1.8 2.1 %copy-start = (bf16[1,1,4,4,4096]{4,3,2,1,0:T(4,128)(2,1)S(1)}, bf16[1,1,4,4,4096]{4,3,2,1,0:T(4,128)(2,1)}, u32[]{:S(2)}) copy-start(bf16[1,1,4,4,4096]{4,3,2,1,0:T(4,128)(2,1)} %own_ref.1) | copy-start | bytes 393220
  7.4 4.9 %collective-permute-start.2 = (bf16[32,896]{1,0:T(8,128)(2,1)S(1)}, bf16[32,896]{1,0:T(8,128)(2,1)S(1)}, u32[]{:S(2)}, u32[]{:S(2)}) collective-permute-start(bf16[32,896]{1,0:T(8,128)(2,1)S(1)} %get-tuple-element.33), channel_id=1, source_target_pairs={{0,4},{4,0},{8,12},{12,8},{16,20},{20,16},{24,28},{28,24},{1,5},{5... | collective-permute-start | bytes 172040 | tf_op jit(solution)/shard_map/ppermute | solution.py:424

commit v15 on v14

--- a/solution.py
+++ b/solution.py
@@ -18,7 +18,8 @@
 PLANE = 1024
 LANES = 128
 ROWS = CIN * PLANES
-CHUNK = 512
+CHUNK = 256
+TABLE = 512
 PACKED = 7 * LANES
 MIB = 2**20
 WIDE = ("chip", "core")
@@ -26,17 +27,17 @@
 
 
 def selection():
-    table = np.zeros((CHUNK, 2, 2, 4, HALF), np.float32)
+    table = np.zeros((CHUNK, 2, 2, 2, HALF), np.float32)
     for py in range(2):
         for px in range(2):
-            for row in range(4):
+            for row in range(2):
                 for col in range(HALF):
                     table[(2 * row + py) * 64 + 2 * col + px, py, px, row, col] = 1
     return table.reshape(CHUNK, CHUNK)
 
 
 def placement():
-    table = np.zeros((2, 27, CIN, 4, CHUNK), np.float32)
+    table = np.zeros((2, 27, CIN, 4, TABLE), np.float32)
     for odd in range(2):
         for a in range(3):
             for bc in range(9):
@@ -51,7 +52,7 @@
                         else:
                             column = 18 * ROWS + bc * ROWS + inner
                         table[odd, 9 * a + bc, i, q, column] = 1
-    return table.reshape(2, 27 * CIN, 4 * CHUNK)
+    return table.reshape(2, 27 * CIN, 4 * TABLE)
 
 
 def channel_order(narrow):
@@ -85,18 +86,16 @@
 def strided_taps(rows, select_ref, parity_ref, taps_ref):
     count = rows.shape[0]
     left_ok, _ = column_masks()
-    chunks = jnp.concatenate([rows[:, CHUNK * j : CHUNK * (j + 1)] for j in range(8)], axis=0)
+    chunks = jnp.concatenate([rows[:, CHUNK * j : CHUNK * (j + 1)] for j in range(16)], axis=0)
     for p in range(4):
         parity_ref[p, :, 0:LANES] = jnp.zeros((count, LANES), jnp.bfloat16)
-    for py in range(2):
-        parts = jnp.dot(
-            chunks, select_ref[:, 256 * py : 256 * py + 256], preferred_element_type=jnp.float32
-        ).astype(jnp.bfloat16)
-        for px in range(2):
-            for j in range(8):
-                parity_ref[2 * py + px, :, LANES * (j + 1) : LANES * (j + 2)] = parts[
-                    j * count : (j + 1) * count, px * LANES : (px + 1) * LANES
-                ]
+    parts = jnp.dot(chunks, select_ref[...], preferred_element_type=jnp.float32).astype(jnp.bfloat16)
+    for j in range(16):
+        for p in range(4):
+            begin = LANES + j * LANES // 2
+            parity_ref[p, :, begin : begin + LANES // 2] = parts[
+                j * count : (j + 1) * count, p * LANES // 2 : (p + 1) * LANES // 2
+            ]
     for b in range(3):
         for c in range(3):
             begin = LANES - HALF * (b == 0) - (c == 0)
@@ -187,8 +186,8 @@
     ).astype(jnp.bfloat16)
     for q in range(4):
         rows = slice(q % 2 * C1, (q % 2 + 1) * C1)
-        w1_near_ref[q // 2, rows, :] = spread[:, CHUNK * q : CHUNK * q + 18 * ROWS]
-        w1_far_ref[q // 2, rows, :] = spread[:, CHUNK * q + 18 * ROWS : CHUNK * q + 27 * ROWS]
+        w1_near_ref[q // 2, rows, :] = spread[:, TABLE * q : TABLE * q + 18 * ROWS]
+        w1_far_ref[q // 2, rows, :] = spread[:, TABLE * q + 18 * ROWS : TABLE * q + 27 * ROWS]
     copies[4].wait()
     for n in range(4):
         planes = [cot_ref[0, 0, :, z * PLANE + 256 * n : z * PLANE + 256 * n + 256] for z in range(2)]
@@ -332,15 +331,10 @@
     out_copy.wait()
 
 
-def finish_kernel(parts_ref, grad_ref):
-    wide, half, _ = parts_ref.shape
-    for core in range(2):
-        total = parts_ref[core].astype(jnp.float32)
-        for k in range(core + 2, wide, 2):
-            total = total + parts_ref[k].astype(jnp.float32)
-        for tap, (tile, slot) in slots().items():
-            begin = tile * LANES + slot * C1
-            grad_ref[tap, core * half : (core + 1) * half, :] = total[:, begin : begin + C1]
+def finish_kernel(total_ref, grad_ref):
+    for tap, (tile, slot) in slots().items():
+        begin = tile * LANES + slot * C1
+        grad_ref[tap] = total_ref[:, begin : begin + C1]
 
 
 def body(volumes, first_kernel, second_kernel, cotangent):
@@ -369,7 +363,7 @@
         ),
         scratch_shapes=[
             pltpu.VMEM((27, CIN, C1), jnp.bfloat16),
-            pltpu.VMEM((27 * CIN, 4 * CHUNK), jnp.bfloat16),
+            pltpu.VMEM((27 * CIN, 4 * TABLE), jnp.bfloat16),
             pltpu.VMEM((27, C1, C2), jnp.bfloat16),
             pltpu.VMEM(cotangent.shape, jnp.bfloat16),
             pltpu.VMEM((27 * CIN, C1), jnp.float32),
@@ -441,12 +435,13 @@
     received = lax.all_to_all(term, "narrow", 0, 0, tiled=True)
     owned = jnp.sum(received.reshape(narrow, half, PACKED).astype(jnp.float32), axis=0).astype(jnp.bfloat16)
     parts = lax.all_to_all(jnp.broadcast_to(owned[None], (wide, half, PACKED)), WIDE, 0, 0, tiled=True)
+    total = jnp.sum(parts.reshape(wide // 2, rows, PACKED).astype(jnp.float32), axis=0)
     weight_grad = pl.pallas_call(
         finish_kernel,
         out_shape=jax.ShapeDtypeStruct((27, rows, C1), jnp.float32),
         compiler_params=pltpu.CompilerParams(vmem_limit_bytes=8 * MIB),
         name="finish",
-    )(parts)
+    )(total)
     return (output, weight_grad)
 
 

time: 33.4 us -> 33.5 us (level)
  Pallas kernels: 7.24 us -> 7.62 us
  transfers between devices with their start and end apart: 3 -> 3, of which waited for: 0 -> 0; matrix products, arithmetic and copies ran while one was open for 0% -> 0% of each run, Pallas kernels for 13% -> 14%
where the time goes in v15:
time: 33.5 us; the launch traced here: 33.3 us
  blocking collectives  19.8 us (59%)
  Pallas kernels  7.62 us (23%)
  starting transfers between devices  5.1 us (15%)
  between operations  0.72 us (2%)
    all_to_all x1, blocking collectives, body(): received = lax.all_to_all(term, 'narrow', 0, 0, tiled=True)  11.2 us
    all_to_all x1, blocking collectives, body(): lax.all_to_all(jnp.broadcast_to(owned[None], (wide, half, PACKED)), WIDE,...  8.63 us
    ppermute x1, starting transfers between devices, body(): got = lax.ppermute(give, WIDE, pairs)  3.93 us
    pallas_call x1, Pallas kernels, body(): pl.pallas_call(functools.partial(far_kernel, wide // 2, scale), in_specs=...  2.12 us
    pallas_call x1, Pallas kernels, body(): pl.pallas_call(prepare_kernel, in_specs=[pinned] * 6, out_specs=(fast,) *...  2.09 us
    pallas_call x1, Pallas kernels, body(): pl.pallas_call(near_kernel, in_specs=[fast] * 5, out_specs=(fast,) * 3, o...  1.67 us
    pallas_call x1, Pallas kernels, body(): pl.pallas_call(functools.partial(rest_kernel, scale), in_specs=[fast] * 6...  0.95 us
    pallas_call x1, Pallas kernels, body(): pl.pallas_call(finish_kernel, out_shape=jax.ShapeDtypeStruct((27, rows, C...  0.79 us
  transfers between devices with their start and end apart: 3, of which 0 were waited for; matrix products, arithmetic and copies ran while one was open for 0% of the time, Pallas kernels for 14%

profile of v15, /device:TPU:0, one launch (start us, length us, event | category | flops | bytes accessed | tf_op | source)
XLA Modules:
  0.0 33.3 jit_solution(741347832400123012)
XLA Ops:
  0.6 0.5 %collective-permute-start.1 = (bf16[1,1,4,4,4096]{4,3,2,1,0:T(4,128)(2,1)}, bf16[1,1,4,4,4096]{4,3,2,1,0:T(4,128)(2,1)S(1)}, u32[]{:S(2)}, u32[]{:S(2)}) collective-permute-start(bf16[1,1,4,4,4096]{4,3,2,1,0:T(4,128)(2,1)} %own_ref.1), channel_id=1, source_target_pairs={{0,4},{4,0},{8,12},{12,8},{16,20},{20,16},{24,28},{28,24},{1,5},{5... | collective-permute-start | bytes 393224 | tf_op jit(solution)/shard_map/ppermute | solution.py:347
  1.1 0.7 %collective-permute-start = (bf16[1,1,4,4,4096]{4,3,2,1,0:T(4,128)(2,1)}, bf16[1,1,4,4,4096]{4,3,2,1,0:T(4,128)(2,1)S(1)}, u32[]{:S(2)}, u32[]{:S(2)}) collective-permute-start(bf16[1,1,4,4,4096]{4,3,2,1,0:T(4,128)(2,1)} %own_ref.1), channel_id=1, source_target_pairs={{4,8},{8,4},{12,16},{16,12},{20,24},{24,20},{5,9},{9,5},{13,17},{1... | collective-permute-start | bytes 393224 | tf_op jit(solution)/shard_map/ppermute | solution.py:345
  1.8 0.0 copy-start
  1.8 2.1 %prepare.1 = (bf16[2,64,288]{2,1,0:T(8,128)(2,1)S(1)}, bf16[2,64,144]{2,1,0:T(8,128)(2,1)S(1)}, bf16[2,192,384]{2,1,0:T(8,128)(2,1)S(1)}, bf16[256,256]{1,0:T(8,...) custom-call(bf16[27,4,32]{2,1,0:T(4,128)(2,1)} %bitcast.10, ...), custom_call_target="tpu_custom_call" | custom-call | flops 1000000000 | bytes 4194304 | tf_op jit(solution)/shard_map/prepare/pallas_call | solution.py:356
  3.9 0.0 collective-permute-done.1.within_ref
  3.9 0.0 copy-done
  3.9 1.7 %near.1 = (f32[64,1024]{1,0:T(8,128)S(1)}, bf16[192,1024]{1,0:T(8,128)(2,1)S(1)}, f32[1024,128]{1,0:T(8,128)S(1)}) custom-call(bf16[1,1,4,4,4096]{4,3,2,1,0:T(4,128)(2,1)S(1)} %copy-done, bf16[1,1,4,4,4096]{4,3,2,1,0:T(4,128)(2,1)S(1)} %collective-permute-done.1.within_ref, bf16[256,256]{1,0:T(8,128)(2,1)S(1)} %get-tuple-element.18.select_ref, ...), custom_call_target="tpu_custom_call" | custom-call | flops 1000000000 | bytes 4194304 | tf_op jit(solution)/shard_map/near/pallas_call | solution.py:377
  5.6 0.0 collective-permute-done.across_ref
  5.6 2.1 %far.1 = (f32[1024,128]{1,0:T(8,128)S(1)}, bf16[32,896]{1,0:T(8,128)(2,1)S(1)}, f32[32,384]{1,0:T(8,128)S(1)}, bf16[192,1024]{1,0:T(8,128)(2,1)S(1)}, bf16[1088,128]{1,0:T(8,128)(2,1)S(1)}) custom-call(bf16[1,1,4,4,4096]{4,3,2,1,0:T(4,128)(2,1)S(1)} %collective-permute-done.across_ref, bf16[256,256]{1,0:T(8,128)(2,1)S(1)} %get-tuple-element.18.select_ref, ...), custom_call_target="tpu_custom_call" | custom-call | flops 1000000000 | bytes 4194304 | tf_op jit(solution)/shard_map/far/pallas_call | solution.py:395
  7.7 3.9 %collective-permute-start.2 = (bf16[32,896]{1,0:T(8,128)(2,1)S(1)}, bf16[32,896]{1,0:T(8,128)(2,1)S(1)}, u32[]{:S(2)}, u32[]{:S(2)}) collective-permute-start(bf16[32,896]{1,0:T(8,128)(2,1)S(1)} %get-tuple-element.33), channel_id=1, source_target_pairs={{0,4},{4,0},{8,12},{12,8},{16,20},{20,16},{24,28},{28,24},{1,5},{5... | collective-permute-start | bytes 172040 | tf_op jit(solution)/shard_map/ppermute | solution.py:418
  11.7 1.0 %rest.1 = (bf16[1,1,64,2048]{3,2,1,0:T(8,128)(2,1)}, f32[32,896]{1,0:T(8,128)S(1)}) custom-call(f32[1024,128]{1,0:T(8,128)S(1)} %get-tuple-element.26.pre_ref, bf16[128,128]{1,0:T(8,128)(2,1)S(1)} %get-tuple-element.27.order_ref, bf16[192,1024]{1,0:T(8,128)(2,1)S(1)} %get-tuple-element.24.near_ref, bf16[192,1024]{1,0:T(8,128)(2,1)S(1)} %get-tuple-element.28.far_ref, ...), custom_call_target="tpu_custom_call" | custom-call | flops 1000000000 | bytes 4194304 | tf_op jit(solution)/shard_map/rest/pallas_call | solution.py:419
  12.6 0.0 collective-permute-done.2
  12.7 11.2 %all_to_all.14 = bf16[4,8,896]{2,1,0:T(8,128)(2,1)S(1)} all-to-all(bf16[4,8,896]{2,1,0:T(8,128)(2,1)S(1)} %fusion), channel_id=1, replica_groups=mesh['chip'=4,'core'=2,'narrow'=4] {'narrow'}, dimensions={0} | all-to-all | bytes 114688 | tf_op jit(solution)/shard_map/all_to_all | solution.py:435
  23.9 8.6 %all_to_all.15 = bf16[8,8,896]{2,1,0:T(8,128)(2,1)S(1)} all-to-all(bf16[8,8,896]{2,1,0:T(8,128)(2,1)S(1)} %broadcast_in_dim.2), channel_id=1, replica_groups=mesh['chip'=4,'core'=2,'narrow'=4] {'chip','core'}, dimensions={0} | all-to-all | bytes 229376 | tf_op jit(solution)/shard_map/all_to_all | solution.py:437
  32.5 0.8 %finish.1 = f32[27,16,32]{2,1,0:T(8,128)} custom-call(f32[16,896]{1,0:T(8,128)S(1)} %convert_reduce_fusion.total_ref), custom_call_target="tpu_custom_call" | custom-call | tf_op jit(solution)/shard_map/finish/pallas_call | solution.py:439
  (4 shorter events, 0.1 us)
Async XLA Ops:
  0.6 3.3 %collective-permute-start.1 = (bf16[1,1,4,4,4096]{4,3,2,1,0:T(4,128)(2,1)}, bf16[1,1,4,4,4096]{4,3,2,1,0:T(4,128)(2,1)S(1)}, u32[]{:S(2)}, u32[]{:S(2)}) collective-permute-start(bf16[1,1,4,4,4096]{4,3,2,1,0:T(4,128)(2,1)} %own_ref.1), channel_id=1, source_target_pairs={{0,4},{4,0},{8,12},{12,8},{16,20},{20,16},{24,28},{28,24},{1,5},{5... | collective-permute-start | bytes 393224 | tf_op jit(solution)/shard_map/ppermute | solution.py:347
  1.1 4.5 %collective-permute-start = (bf16[1,1,4,4,4096]{4,3,2,1,0:T(4,128)(2,1)}, bf16[1,1,4,4,4096]{4,3,2,1,0:T(4,128)(2,1)S(1)}, u32[]{:S(2)}, u32[]{:S(2)}) collective-permute-start(bf16[1,1,4,4,4096]{4,3,2,1,0:T(4,128)(2,1)} %own_ref.1), channel_id=1, source_target_pairs={{4,8},{8,4},{12,16},{16,12},{20,24},{24,20},{5,9},{9,5},{13,17},{1... | collective-permute-start | bytes 393224 | tf_op jit(solution)/shard_map/ppermute | solution.py:345
  1.8 2.1 %copy-start = (bf16[1,1,4,4,4096]{4,3,2,1,0:T(4,128)(2,1)S(1)}, bf16[1,1,4,4,4096]{4,3,2,1,0:T(4,128)(2,1)}, u32[]{:S(2)}) copy-start(bf16[1,1,4,4,4096]{4,3,2,1,0:T(4,128)(2,1)} %own_ref.1) | copy-start | bytes 393220
  7.7 4.9 %collective-permute-start.2 = (bf16[32,896]{1,0:T(8,128)(2,1)S(1)}, bf16[32,896]{1,0:T(8,128)(2,1)S(1)}, u32[]{:S(2)}, u32[]{:S(2)}) collective-permute-start(bf16[32,896]{1,0:T(8,128)(2,1)S(1)} %get-tuple-element.33), channel_id=1, source_target_pairs={{0,4},{4,0},{8,12},{12,8},{16,20},{20,16},{24,28},{28,24},{1,5},{5... | collective-permute-start | bytes 172040 | tf_op jit(solution)/shard_map/ppermute | solution.py:418

commit v16 on v14

--- a/solution.py
+++ b/solution.py
@@ -70,9 +70,8 @@
     return jnp.where(value > 0, value, neg_slope * value)
 
 
-def plane_rows(volume_ref, rows_ref):
-    for i in range(CIN):
-        rows_ref[PLANES * i : PLANES * (i + 1), :] = volume_ref[0, 0, i].astype(jnp.float32)
+def plane_rows(volume_ref):
+    return jnp.concatenate([volume_ref[0, 0, i] for i in range(CIN)], axis=0)
 
 
 def column_masks():
@@ -201,12 +200,11 @@
 
 def near_kernel(
     own_ref, within_ref, select_ref, w1_ref, w2_ref, first_ref, columns_ref, pre_ref,
-    rows_ref, parity_ref, taps_ref, act_ref, turned_ref, rowed_ref,
+    parity_ref, taps_ref, act_ref, turned_ref, rowed_ref,
 ):
     odd = lax.axis_index("core")
-    plane_rows(own_ref, rows_ref.at[0:ROWS])
-    plane_rows(within_ref, rows_ref.at[ROWS : 2 * ROWS])
-    strided_taps(rows_ref[...].astype(jnp.bfloat16), select_ref, parity_ref, taps_ref)
+    rows = jnp.concatenate([plane_rows(own_ref), plane_rows(within_ref)], axis=0)
+    strided_taps(rows, select_ref, parity_ref, taps_ref)
     clear_margins(act_ref)
     for n in range(4):
         here = slice(256 * n, 256 * n + 256)
@@ -249,6 +247,11 @@
     return [flat[g * C1 : (g + 1) * C1] for g in range(4)]
 
 
+def first_two_rows(left_ref, right_ref):
+    low = lax.broadcasted_iota(jnp.int32, (1, LANES), 1) < C2
+    return jnp.where(low, left_ref[2 * HALF : 2 * HALF + PLANE, :], right_ref[HALF : HALF + PLANE, :])
+
+
 def gradient_sums(odd, near_ref, far_ref, backs, sums_ref):
     columns = jnp.concatenate([near_ref[...], far_ref[...]], axis=0)
     sums = jnp.dot(columns, backs, preferred_element_type=jnp.float32)
@@ -258,14 +261,13 @@
 
 def far_kernel(
     chips, scale, across_ref, select_ref, w1_ref, w2_ref, cot_ref, first_ref, near_ref, near_pre_ref,
-    pre_ref, give_ref, keep_ref, columns_ref, kept_ref,
-    rows_ref, parity_ref, taps_ref, act_ref, turned_ref, rowed_ref, given_ref, mixed_ref, sums_ref,
+    pre_ref, give_ref, keep_ref, columns_ref, back_ref, swapped_ref,
+    parity_ref, taps_ref, act_ref, turned_ref, rowed_ref, sums_ref,
 ):
     odd = lax.axis_index("core")
     last = (lax.axis_index("chip") == chips - 1) & (odd == 1)
     inside = jnp.where(last, 0.0, 1.0)
-    plane_rows(across_ref, rows_ref)
-    strided_taps(rows_ref[...].astype(jnp.bfloat16), select_ref, parity_ref, taps_ref)
+    strided_taps(plane_rows(across_ref), select_ref, parity_ref, taps_ref)
     clear_margins(act_ref)
     for n in range(4):
         here = slice(256 * n, 256 * n + 256)
@@ -278,23 +280,20 @@
     second_layer(w2_ref[odd], columns_ref, turned_ref, rowed_ref)
 
     margin = jnp.zeros((HALF, LANES), jnp.bfloat16)
-    for ref in (given_ref, mixed_ref, kept_ref):
-        ref[HALF : 2 * HALF, :] = margin
-        ref[PLANE : PLANE + HALF, :] = margin
+    for ref in (back_ref, swapped_ref):
+        ref[0:HALF, :] = margin
+        ref[HALF + PLANE :, :] = margin
     for n in range(4):
         cells = slice(256 * n, 256 * n + 256)
         pre = near_pre_ref[cells, :] + row_sum(rowed_ref, n)
         pre_ref[cells, :] = pre
         back = (cot_ref[cells, :].astype(jnp.float32) * jnp.where(pre > 0, 1.0, neg_slope)).astype(jnp.bfloat16)
-        other = jnp.concatenate([back[:, C2:], back[:, 0:C2]], axis=1)
-        rows = [slice(256 * n + HALF * b, 256 * n + HALF * b + 256) for b in range(3)]
-        given_ref[rows[0], 0:C2] = back[:, 0:C2]
-        given_ref[rows[1], C2:] = other[:, C2:]
-        mixed_ref[rows[2], :] = back
-        kept_ref[rows[0], 0:C2] = other[:, 0:C2]
-        kept_ref[rows[1], C2:] = back[:, C2:]
-    middle = slice(HALF, HALF + PLANE)
-    gradient_sums(odd, near_ref, columns_ref, jnp.concatenate([given_ref[middle, :], mixed_ref[middle, :]], axis=1), sums_ref)
+        here = slice(HALF + 256 * n, HALF + 256 * n + 256)
+        back_ref[here, :] = back
+        swapped_ref[here, :] = jnp.concatenate([back[:, C2:], back[:, 0:C2]], axis=1)
+    given = first_two_rows(back_ref, swapped_ref)
+    mixed = back_ref[0:PLANE, :]
+    gradient_sums(odd, near_ref, columns_ref, jnp.concatenate([given, mixed], axis=1), sums_ref)
     given, mixed = paired_terms(sums_ref, 0), paired_terms(sums_ref, 1)
     first = turned_groups(given[0:4], scale)
     second = turned_groups(mixed[0:4], scale)
@@ -308,7 +307,7 @@
 
 
 def rest_kernel(
-    scale, pre_ref, order_ref, near_ref, far_ref, kept_ref, mixed_ref, out_hbm, keep_ref, sums_ref, out_ref, out_sem,
+    scale, pre_ref, order_ref, near_ref, far_ref, back_ref, swapped_ref, mixed_ref, out_hbm, keep_ref, sums_ref, out_ref, out_sem,
 ):
     for n in range(4):
         output = leaky_relu(pre_ref[256 * n : 256 * n + 256, :]).astype(jnp.bfloat16)
@@ -320,7 +319,7 @@
     out_copy = pltpu.make_async_copy(out_ref, out_hbm, out_sem)
     out_copy.start()
     odd = lax.axis_index("core")
-    gradient_sums(odd, near_ref, far_ref, kept_ref[HALF : HALF + PLANE, :], sums_ref)
+    gradient_sums(odd, near_ref, far_ref, first_two_rows(swapped_ref, back_ref), sums_ref)
     kept = paired_terms(sums_ref, 0)
     first = turned_groups(kept[0:4], scale)
     third = turned_groups([kept[4]] * 4, scale)
@@ -332,15 +331,19 @@
     out_copy.wait()
 
 
-def finish_kernel(parts_ref, grad_ref):
-    wide, half, _ = parts_ref.shape
-    for core in range(2):
-        total = parts_ref[core].astype(jnp.float32)
-        for k in range(core + 2, wide, 2):
-            total = total + parts_ref[k].astype(jnp.float32)
-        for tap, (tile, slot) in slots().items():
+def finish_kernel(total_ref, grad_hbm, grad_ref, sems):
+    where = slots()
+    copies = []
+    for k in range(3):
+        for tap in range(9 * k, 9 * k + 9):
+            tile, slot = where[tap]
             begin = tile * LANES + slot * C1
-            grad_ref[tap, core * half : (core + 1) * half, :] = total[:, begin : begin + C1]
+            grad_ref[tap] = total_ref[:, begin : begin + C1]
+        here = slice(9 * k, 9 * k + 9)
+        copies.append(pltpu.make_async_copy(grad_ref.at[here], grad_hbm.at[here], sems.at[k]))
+        copies[k].start()
+    for copy in copies:
+        copy.wait()
 
 
 def body(volumes, first_kernel, second_kernel, cotangent):
@@ -386,7 +389,6 @@
         out_specs=(fast,) * 3,
         out_shape=(f32((2 * C1, PLANE)), bf16((6 * C1, PLANE)), f32((PLANE, 2 * C2))),
         scratch_shapes=[
-            pltpu.VMEM((2 * ROWS, CELLS), jnp.float32),
             pltpu.VMEM((4, 2 * ROWS, LANES + PLANE), jnp.bfloat16),
             pltpu.VMEM((18 * ROWS, PLANE), jnp.bfloat16),
             pltpu.VMEM((2 * C1, PLANE + 2 * LANES), jnp.bfloat16),
@@ -398,23 +400,20 @@
         name="near",
     )(volumes, within, select, w1_near, w2)
     rows = C2 // narrow
-    pre, give, mixed, far, kept = pl.pallas_call(
+    pre, give, mixed, far, back, swapped = pl.pallas_call(
         functools.partial(far_kernel, wide // 2, scale),
         in_specs=[fast] * 8,
-        out_specs=(fast,) * 5,
+        out_specs=(fast,) * 6,
         out_shape=(
             f32((PLANE, 2 * C2)), bf16((C2 // 2, PACKED)), f32((C2 // 2, 3 * LANES)),
-            bf16((6 * C1, PLANE)), bf16((PLANE + 2 * HALF, LANES)),
+            bf16((6 * C1, PLANE)), bf16((PLANE + 2 * HALF, LANES)), bf16((PLANE + 2 * HALF, LANES)),
         ),
         scratch_shapes=[
-            pltpu.VMEM((ROWS, CELLS), jnp.float32),
             pltpu.VMEM((4, ROWS, LANES + PLANE), jnp.bfloat16),
             pltpu.VMEM((9 * ROWS, PLANE), jnp.bfloat16),
             pltpu.VMEM((2 * C1, PLANE + 2 * LANES), jnp.bfloat16),
             pltpu.VMEM((PLANE, 6 * C1), jnp.bfloat16),
             pltpu.VMEM((3, PLANE + 2 * HALF, LANES), jnp.float32),
-            pltpu.VMEM((PLANE + 2 * HALF, LANES), jnp.bfloat16),
-            pltpu.VMEM((PLANE + 2 * HALF, LANES), jnp.bfloat16),
             pltpu.VMEM((2, 6 * C1, 2 * LANES), jnp.float32),
         ],
         compiler_params=pltpu.CompilerParams(vmem_limit_bytes=16 * MIB),
@@ -424,7 +423,7 @@
     got = lax.ppermute(give, WIDE, pairs)
     output, keep = pl.pallas_call(
         functools.partial(rest_kernel, scale),
-        in_specs=[fast] * 6,
+        in_specs=[fast] * 7,
         out_specs=(pl.BlockSpec(memory_space=pl.ANY), fast),
         out_shape=(bf16((1, 1, C2, cells_out)), f32((C2 // 2, PACKED))),
         scratch_shapes=[
@@ -435,18 +434,22 @@
         compiler_params=pltpu.CompilerParams(vmem_limit_bytes=8 * MIB),
         cost_estimate=pl.CostEstimate(flops=10**9, bytes_accessed=4 * MIB, transcendentals=0),
         name="rest",
-    )(pre, order, near, far, kept, mixed)
+    )(pre, order, near, far, back, swapped, mixed)
     half = rows // 2
     term = (keep + got.astype(jnp.float32)).astype(jnp.bfloat16)
     received = lax.all_to_all(term, "narrow", 0, 0, tiled=True)
     owned = jnp.sum(received.reshape(narrow, half, PACKED).astype(jnp.float32), axis=0).astype(jnp.bfloat16)
     parts = lax.all_to_all(jnp.broadcast_to(owned[None], (wide, half, PACKED)), WIDE, 0, 0, tiled=True)
+    total = jnp.sum(parts.reshape(wide // 2, rows, PACKED).astype(jnp.float32), axis=0)
     weight_grad = pl.pallas_call(
         finish_kernel,
-        out_shape=jax.ShapeDtypeStruct((27, rows, C1), jnp.float32),
+        in_specs=[fast],
+        out_specs=pl.BlockSpec(memory_space=pl.ANY),
+        out_shape=f32((27, rows, C1)),
+        scratch_shapes=[pltpu.VMEM((27, rows, C1), jnp.float32), pltpu.SemaphoreType.DMA((3,))],
         compiler_params=pltpu.CompilerParams(vmem_limit_bytes=8 * MIB),
         name="finish",
-    )(parts)
+    )(total)
     return (output, weight_grad)
 
 

time: 33.4 us -> 33.4 us (level)
  no operation moved by 1% of the time
where the time goes in v16:
time: 33.4 us; the launch traced here: 33.2 us
  blocking collectives  20.1 us (60%)
  Pallas kernels  7.21 us (22%)
  starting transfers between devices  5.11 us (15%)
  between operations  0.72 us (2%)
    all_to_all x1, blocking collectives, body(): received = lax.all_to_all(term, 'narrow', 0, 0, tiled=True)  11.4 us
    all_to_all x1, blocking collectives, body(): lax.all_to_all(jnp.broadcast_to(owned[None], (wide, half, PACKED)), WIDE,...  8.62 us
    ppermute x1, starting transfers between devices, body(): got = lax.ppermute(give, WIDE, pairs)  3.94 us
    pallas_call x1, Pallas kernels, body(): pl.pallas_call(prepare_kernel, in_specs=[pinned] * 6, out_specs=(fast,) *...  2.09 us
    pallas_call x1, Pallas kernels, body(): pl.pallas_call(functools.partial(far_kernel, wide // 2, scale), in_specs=...  2 us
    pallas_call x1, Pallas kernels, body(): pl.pallas_call(near_kernel, in_specs=[fast] * 5, out_specs=(fast,) * 3, o...  1.39 us
    pallas_call x1, Pallas kernels, body(): pl.pallas_call(functools.partial(rest_kernel, scale), in_specs=[fast] * 7...  0.96 us
    pallas_call x1, Pallas kernels, body(): pl.pallas_call(finish_kernel, in_specs=[fast], out_specs=pl.BlockSpec(mem...  0.78 us
  transfers between devices with their start and end apart: 3, of which 0 were waited for; matrix products, arithmetic and copies ran while one was open for 0% of the time, Pallas kernels for 13%

profile of v16, /device:TPU:0, one launch (start us, length us, event | category | flops | bytes accessed | tf_op | source)
XLA Modules:
  0.0 33.2 jit_solution(13450467832963142180)
XLA Ops:
  0.6 0.5 %collective-permute-start.1 = (bf16[1,1,4,4,4096]{4,3,2,1,0:T(4,128)(2,1)}, bf16[1,1,4,4,4096]{4,3,2,1,0:T(4,128)(2,1)S(1)}, u32[]{:S(2)}, u32[]{:S(2)}) collective-permute-start(bf16[1,1,4,4,4096]{4,3,2,1,0:T(4,128)(2,1)} %own_ref.1), channel_id=1, source_target_pairs={{0,4},{4,0},{8,12},{12,8},{16,20},{20,16},{24,28},{28,24},{1,5},{5... | collective-permute-start | bytes 393224 | tf_op jit(solution)/shard_map/ppermute | solution.py:356
  1.1 0.7 %collective-permute-start = (bf16[1,1,4,4,4096]{4,3,2,1,0:T(4,128)(2,1)}, bf16[1,1,4,4,4096]{4,3,2,1,0:T(4,128)(2,1)S(1)}, u32[]{:S(2)}, u32[]{:S(2)}) collective-permute-start(bf16[1,1,4,4,4096]{4,3,2,1,0:T(4,128)(2,1)} %own_ref.1), channel_id=1, source_target_pairs={{4,8},{8,4},{12,16},{16,12},{20,24},{24,20},{5,9},{9,5},{13,17},{1... | collective-permute-start | bytes 393224 | tf_op jit(solution)/shard_map/ppermute | solution.py:354
  1.8 0.0 copy-start
  1.8 2.1 %prepare.1 = (bf16[2,64,288]{2,1,0:T(8,128)(2,1)S(1)}, bf16[2,64,144]{2,1,0:T(8,128)(2,1)S(1)}, bf16[2,192,384]{2,1,0:T(8,128)(2,1)S(1)}, bf16[512,512]{1,0:T(8,...) custom-call(bf16[27,4,32]{2,1,0:T(4,128)(2,1)} %bitcast.10, ...), custom_call_target="tpu_custom_call" | custom-call | flops 1000000000 | bytes 4194304 | tf_op jit(solution)/shard_map/prepare/pallas_call | solution.py:365
  3.9 0.0 collective-permute-done.1.within_ref
  3.9 0.0 copy-done
  3.9 1.4 %near.1 = (f32[64,1024]{1,0:T(8,128)S(1)}, bf16[192,1024]{1,0:T(8,128)(2,1)S(1)}, f32[1024,128]{1,0:T(8,128)S(1)}) custom-call(bf16[1,1,4,4,4096]{4,3,2,1,0:T(4,128)(2,1)S(1)} %copy-done, bf16[1,1,4,4,4096]{4,3,2,1,0:T(4,128)(2,1)S(1)} %collective-permute-done.1.within_ref, bf16[512,512]{1,0:T(8,128)(2,1)S(1)} %get-tuple-element.19.select_ref, ...), custom_call_target="tpu_custom_call" | custom-call | flops 1000000000 | bytes 4194304 | tf_op jit(solution)/shard_map/near/pallas_call | solution.py:386
  5.3 0.0 collective-permute-done.across_ref
  5.3 2.0 %far.1 = (f32[1024,128]{1,0:T(8,128)S(1)}, bf16[32,896]{1,0:T(8,128)(2,1)S(1)}, f32[32,384]{1,0:T(8,128)S(1)}, bf16[192,1024]{1,0:T(8,128)(2,1)S(1)}, bf16[1088,...) custom-call(bf16[1,1,4,4,4096]{4,3,2,1,0:T(4,128)(2,1)S(1)} %collective-permute-done.across_ref, ...), custom_call_target="tpu_custom_call" | custom-call | flops 1000000000 | bytes 4194304 | tf_op jit(solution)/shard_map/far/pallas_call | solution.py:403
  7.3 3.9 %collective-permute-start.2 = (bf16[32,896]{1,0:T(8,128)(2,1)S(1)}, bf16[32,896]{1,0:T(8,128)(2,1)S(1)}, u32[]{:S(2)}, u32[]{:S(2)}) collective-permute-start(bf16[32,896]{1,0:T(8,128)(2,1)S(1)} %get-tuple-element.35), channel_id=1, source_target_pairs={{0,4},{4,0},{8,12},{12,8},{16,20},{20,16},{24,28},{28,24},{1,5},{5... | collective-permute-start | bytes 172040 | tf_op jit(solution)/shard_map/ppermute | solution.py:423
  11.3 1.0 %rest.1 = (bf16[1,1,64,2048]{3,2,1,0:T(8,128)(2,1)}, f32[32,896]{1,0:T(8,128)S(1)}) custom-call(f32[1024,128]{1,0:T(8,128)S(1)} %get-tuple-element.27.pre_ref, bf16[128,128]{1,0:T(8,128)(2,1)S(1)} %get-tuple-element.28.order_ref, bf16[192,1024]{1,0:T(8,128)(2,1)S(1)} %get-tuple-element.25.near_ref, bf16[192,1024]{1,0:T(8,128)(2,1)S(1)} %get-tuple-element.29.far_ref, ...), custom_call_target="tpu_custom_call" | custom-call | flops 1000000000 | bytes 4194304 | tf_op jit(solution)/shard_map/rest/pallas_call | solution.py:424
  12.2 0.0 collective-permute-done.2
  12.3 11.4 %all_to_all.14 = bf16[4,8,896]{2,1,0:T(8,128)(2,1)S(1)} all-to-all(bf16[4,8,896]{2,1,0:T(8,128)(2,1)S(1)} %fusion), channel_id=1, replica_groups=mesh['chip'=4,'core'=2,'narrow'=4] {'narrow'}, dimensions={0} | all-to-all | bytes 114688 | tf_op jit(solution)/shard_map/all_to_all | solution.py:440
  23.7 8.6 %all_to_all.15 = bf16[8,8,896]{2,1,0:T(8,128)(2,1)S(1)} all-to-all(bf16[8,8,896]{2,1,0:T(8,128)(2,1)S(1)} %broadcast_in_dim.2), channel_id=1, replica_groups=mesh['chip'=4,'core'=2,'narrow'=4] {'chip','core'}, dimensions={0} | all-to-all | bytes 229376 | tf_op jit(solution)/shard_map/all_to_all | solution.py:442
  32.4 0.8 %finish.1 = f32[27,16,32]{2,1,0:T(8,128)} custom-call(f32[16,896]{1,0:T(8,128)S(1)} %convert_reduce_fusion.total_ref), custom_call_target="tpu_custom_call" | custom-call | tf_op jit(solution)/shard_map/finish/pallas_call | solution.py:444
  (4 shorter events, 0.1 us)
Async XLA Ops:
  0.6 3.3 %collective-permute-start.1 = (bf16[1,1,4,4,4096]{4,3,2,1,0:T(4,128)(2,1)}, bf16[1,1,4,4,4096]{4,3,2,1,0:T(4,128)(2,1)S(1)}, u32[]{:S(2)}, u32[]{:S(2)}) collective-permute-start(bf16[1,1,4,4,4096]{4,3,2,1,0:T(4,128)(2,1)} %own_ref.1), channel_id=1, source_target_pairs={{0,4},{4,0},{8,12},{12,8},{16,20},{20,16},{24,28},{28,24},{1,5},{5... | collective-permute-start | bytes 393224 | tf_op jit(solution)/shard_map/ppermute | solution.py:356
  1.1 4.2 %collective-permute-start = (bf16[1,1,4,4,4096]{4,3,2,1,0:T(4,128)(2,1)}, bf16[1,1,4,4,4096]{4,3,2,1,0:T(4,128)(2,1)S(1)}, u32[]{:S(2)}, u32[]{:S(2)}) collective-permute-start(bf16[1,1,4,4,4096]{4,3,2,1,0:T(4,128)(2,1)} %own_ref.1), channel_id=1, source_target_pairs={{4,8},{8,4},{12,16},{16,12},{20,24},{24,20},{5,9},{9,5},{13,17},{1... | collective-permute-start | bytes 393224 | tf_op jit(solution)/shard_map/ppermute | solution.py:354
  1.8 2.1 %copy-start = (bf16[1,1,4,4,4096]{4,3,2,1,0:T(4,128)(2,1)S(1)}, bf16[1,1,4,4,4096]{4,3,2,1,0:T(4,128)(2,1)}, u32[]{:S(2)}) copy-start(bf16[1,1,4,4,4096]{4,3,2,1,0:T(4,128)(2,1)} %own_ref.1) | copy-start | bytes 393220
  7.3 4.9 %collective-permute-start.2 = (bf16[32,896]{1,0:T(8,128)(2,1)S(1)}, bf16[32,896]{1,0:T(8,128)(2,1)S(1)}, u32[]{:S(2)}, u32[]{:S(2)}) collective-permute-start(bf16[32,896]{1,0:T(8,128)(2,1)S(1)} %get-tuple-element.35), channel_id=1, source_target_pairs={{0,4},{4,0},{8,12},{12,8},{16,20},{20,16},{24,28},{28,24},{1,5},{5... | collective-permute-start | bytes 172040 | tf_op jit(solution)/shard_map/ppermute | solution.py:423

commit v17 on v7

--- a/solution.py
+++ b/solution.py
@@ -58,9 +58,8 @@
     return jnp.where(value > 0, value, neg_slope * value)
 
 
-def plane_rows(volume_ref, rows_ref):
-    for i in range(CIN):
-        rows_ref[PLANES * i : PLANES * (i + 1), :] = volume_ref[0, 0, i].astype(jnp.float32)
+def plane_rows(volume_ref):
+    return jnp.concatenate([volume_ref[0, 0, i] for i in range(CIN)], axis=0)
 
 
 def column_masks():
@@ -106,23 +105,24 @@
         columns_ref[c * 2 * C1 : (c + 1) * 2 * C1, :] = part
 
 
-def second_layer(w2, columns_ref, rowed_ref):
-    blank = jnp.zeros((2 * C2, LANES), jnp.float32)
+def second_layer(w2, columns_ref, turned_ref, rowed_ref):
+    blank = jnp.zeros((HALF, LANES), jnp.float32)
     for b in (0, 2):
-        rowed_ref[b, :, 0:LANES] = blank
-        rowed_ref[b, :, LANES + PLANE :] = blank
-    for n in range(4):
-        sums = jnp.dot(w2, columns_ref[:, 256 * n : 256 * n + 256], preferred_element_type=jnp.float32)
+        rowed_ref[b, 0:HALF, :] = blank
+        rowed_ref[b, HALF + PLANE :, :] = blank
+    for n in range(4):
+        cells = slice(256 * n, 256 * n + 256)
+        turned_ref[cells, :] = columns_ref[:, cells].T
+    for n in range(4):
+        sums = jnp.dot(turned_ref[256 * n : 256 * n + 256, :], w2, preferred_element_type=jnp.float32)
         for b in range(3):
-            rowed_ref[b, :, LANES + 256 * n : LANES + 256 * n + 256] = sums[b * 2 * C2 : (b + 1) * 2 * C2]
+            rowed_ref[b, HALF + 256 * n : HALF + 256 * n + 256, :] = sums[:, b * LANES : (b + 1) * LANES]
 
 
 def row_sum(rowed_ref, n):
-    total = rowed_ref[1, :, LANES + 256 * n : LANES + 256 * n + 256]
-    for b in (0, 2):
-        begin = LANES + HALF * (b - 1) + 256 * n
-        total = total + rowed_ref[b, :, begin : begin + 256]
-    return total
+    begins = [HALF * b + 256 * n for b in range(3)]
+    first, second, third = (rowed_ref[b, begin : begin + 256, :] for b, begin in enumerate(begins))
+    return first + second + third
 
 
 def clear_margins(act_ref):
@@ -132,11 +132,14 @@
 
 
 def prepare_kernel(
-    k1_hbm, place_hbm, k2_hbm, select_hbm, cot_hbm, w1_near_ref, w1_far_ref, w2_ref, select_ref, cot_ref,
-    k1_ref, place_ref, k2_ref, k1_rows_ref, sems,
+    k1_hbm, place_hbm, k2_hbm, select_hbm, cot_hbm,
+    w1_near_ref, w1_far_ref, w2_ref, select_ref, turned_ref,
+    k1_ref, place_ref, k2_ref, cot_ref, k1_rows_ref, sems,
 ):
     odd = lax.axis_index("core")
-    moves = ((k1_hbm, k1_ref), (k2_hbm, k2_ref), (place_hbm.at[odd], place_ref), (select_hbm, select_ref), (cot_hbm, cot_ref))
+    moves = (
+        (k1_hbm, k1_ref), (k2_hbm, k2_ref), (place_hbm.at[odd], place_ref), (cot_hbm, cot_ref), (select_hbm, select_ref),
+    )
     copies = [pltpu.make_async_copy(src, dst, sems.at[k]) for k, (src, dst) in enumerate(moves)]
     for copy in copies:
         copy.start()
@@ -152,14 +155,10 @@
         upper = jnp.concatenate(k[2 * pair : 2 + 2 * pair], axis=0)
         return jnp.concatenate([lower, upper], axis=1)
 
-    for b in range(3):
-        rows = slice(b * 2 * C2, (b + 1) * 2 * C2)
-        for pair in range(2):
-            both = jnp.concatenate([stacked(3 * b, pair), stacked(3 * b + 1, pair)], axis=0)
-            w2_ref[pair, rows, 0:LANES] = both.T
-        both = jnp.concatenate([stacked(3 * b + 2, 0), stacked(3 * b + 2, 1)], axis=0).T
-        for pair in range(2):
-            w2_ref[pair, rows, LANES : LANES + 2 * C1] = both[:, pair * 2 * C1 : (pair + 1) * 2 * C1]
+    for pair in range(2):
+        for b in range(3):
+            for c in range(3):
+                w2_ref[pair, c * 2 * C1 : (c + 1) * 2 * C1, b * LANES : (b + 1) * LANES] = stacked(3 * b + c, pair)
     copies[2].wait()
     spread = lax.dot_general(
         k1_rows_ref[...].astype(jnp.bfloat16), place_ref[...],
@@ -170,17 +169,19 @@
         w1_near_ref[q // 2, rows, :] = spread[:, CHUNK * q : CHUNK * q + 18 * ROWS]
         w1_far_ref[q // 2, rows, :] = spread[:, CHUNK * q + 18 * ROWS : CHUNK * q + 27 * ROWS]
     copies[3].wait()
+    for n in range(4):
+        planes = [cot_ref[0, 0, :, z * PLANE + 256 * n : z * PLANE + 256 * n + 256] for z in range(2)]
+        turned_ref[256 * n : 256 * n + 256, :] = jnp.concatenate(planes, axis=0).T
     copies[4].wait()
 
 
 def near_kernel(
     own_ref, within_ref, select_ref, w1_ref, w2_ref, first_ref, columns_ref, pre_ref,
-    rows_ref, parity_ref, taps_ref, act_ref, rowed_ref,
+    parity_ref, taps_ref, act_ref, turned_ref, rowed_ref,
 ):
     odd = lax.axis_index("core")
-    plane_rows(own_ref, rows_ref.at[0:ROWS])
-    plane_rows(within_ref, rows_ref.at[ROWS : 2 * ROWS])
-    strided_taps(rows_ref[...].astype(jnp.bfloat16), select_ref, parity_ref, taps_ref)
+    rows = jnp.concatenate([plane_rows(own_ref), plane_rows(within_ref)], axis=0)
+    strided_taps(rows, select_ref, parity_ref, taps_ref)
     clear_margins(act_ref)
     for n in range(4):
         here = slice(256 * n, 256 * n + 256)
@@ -188,20 +189,19 @@
         complete = jnp.dot(w1_ref[1 - odd], taps_ref[:, here], preferred_element_type=jnp.float32)
         act_ref[:, LANES + 256 * n : LANES + 256 * n + 256] = leaky_relu(complete).astype(jnp.bfloat16)
     shifted_columns(act_ref, columns_ref)
-    second_layer(w2_ref[1 - odd], columns_ref, rowed_ref)
-    for n in range(4):
-        pre_ref[:, 256 * n : 256 * n + 256] = row_sum(rowed_ref, n)
+    second_layer(w2_ref[1 - odd], columns_ref, turned_ref, rowed_ref)
+    for n in range(4):
+        pre_ref[256 * n : 256 * n + 256, :] = row_sum(rowed_ref, n)
 
 
 def far_kernel(
-    chips, scale, across_ref, select_ref, w1_ref, w2_ref, cot_ref, first_ref, near_ref, pre_ref, out_hbm, grad_ref,
-    rows_ref, parity_ref, taps_ref, act_ref, columns_ref, rowed_ref, back_ref, sums_ref, out_ref, out_sem,
+    chips, scale, across_ref, select_ref, w1_ref, w2_ref, cot_ref, first_ref, near_ref, near_pre_ref, out_hbm, grad_ref,
+    parity_ref, taps_ref, act_ref, columns_ref, turned_ref, rowed_ref, back_ref, sums_ref, out_ref, out_sem,
 ):
     odd = lax.axis_index("core")
     last = (lax.axis_index("chip") == chips - 1) & (odd == 1)
     inside = jnp.where(last, 0.0, 1.0)
-    plane_rows(across_ref, rows_ref)
-    strided_taps(rows_ref[...].astype(jnp.bfloat16), select_ref, parity_ref, taps_ref)
+    strided_taps(plane_rows(across_ref), select_ref, parity_ref, taps_ref)
     clear_margins(act_ref)
     for n in range(4):
         here = slice(256 * n, 256 * n + 256)
@@ -211,21 +211,18 @@
         act_ref[0:C1, there] = first_act[0:C1].astype(jnp.bfloat16)
         act_ref[C1:, there] = (first_act[C1:] * inside).astype(jnp.bfloat16)
     shifted_columns(act_ref, columns_ref)
-    second_layer(w2_ref[odd], columns_ref, rowed_ref)
+    second_layer(w2_ref[odd], columns_ref, turned_ref, rowed_ref)
     margin = jnp.zeros((HALF, LANES), jnp.bfloat16)
     back_ref[0:HALF, :] = margin
     back_ref[HALF + PLANE :, :] = margin
     for n in range(4):
-        pre = pre_ref[:, 256 * n : 256 * n + 256] + row_sum(rowed_ref, n)
-        output = leaky_relu(pre).astype(jnp.bfloat16)
-        slope = jnp.where(pre > 0, 1.0, neg_slope)
-        backs = []
+        cells = slice(256 * n, 256 * n + 256)
+        pre = near_pre_ref[cells, :] + row_sum(rowed_ref, n)
+        back = cot_ref[cells, :].astype(jnp.float32) * jnp.where(pre > 0, 1.0, neg_slope)
+        back_ref[HALF + 256 * n : HALF + 256 * n + 256, :] = back.astype(jnp.bfloat16)
+        output = leaky_relu(pre).astype(jnp.bfloat16).T
         for z in range(2):
-            cells = slice(z * PLANE + 256 * n, z * PLANE + 256 * n + 256)
-            rows = slice(z * C2, (z + 1) * C2)
-            out_ref[0, 0, :, cells] = output[rows]
-            backs.append((cot_ref[0, 0, :, cells].astype(jnp.float32) * slope[rows]).astype(jnp.bfloat16))
-        back_ref[HALF + 256 * n : HALF + 256 * n + 256, :] = jnp.concatenate(backs, axis=0).T
+            out_ref[0, 0, :, z * PLANE + 256 * n : z * PLANE + 256 * n + 256] = output[z * C2 : (z + 1) * C2]
     out_copy = pltpu.make_async_copy(out_ref, out_hbm, out_sem)
     out_copy.start()
     columns = jnp.concatenate([near_ref[...], columns_ref[...]], axis=0)
@@ -258,14 +255,16 @@
     out_copy.wait()
 
 
-def finish_kernel(parts_ref, grad_ref):
-    wide, half, _ = parts_ref.shape
-    for core in range(2):
-        total = parts_ref[core].astype(jnp.float32)
-        for k in range(core + 2, wide, 2):
-            total = total + parts_ref[k].astype(jnp.float32)
-        for tap in range(27):
-            grad_ref[tap, core * half : (core + 1) * half, :] = total[:, tap * C1 : (tap + 1) * C1]
+def finish_kernel(total_ref, grad_hbm, grad_ref, sems):
+    copies = []
+    for k in range(3):
+        for tap in range(9 * k, 9 * k + 9):
+            grad_ref[tap] = total_ref[:, tap * C1 : (tap + 1) * C1]
+        here = slice(9 * k, 9 * k + 9)
+        copies.append(pltpu.make_async_copy(grad_ref.at[here], grad_hbm.at[here], sems.at[k]))
+        copies[k].start()
+    for copy in copies:
+        copy.wait()
 
 
 def body(volumes, first_kernel, second_kernel, cotangent):
@@ -274,7 +273,8 @@
     cells_out = cotangent.shape[3]
     scale = 1.0 / math.sqrt(wide * narrow * cells_out)
     across = lax.ppermute(volumes, WIDE, [p for k in range(1, wide - 1, 2) for p in ((k, k + 1), (k + 1, k))])
-    within = lax.ppermute(volumes, WIDE, [p for k in range(0, wide - 1, 2) for p in ((k, k + 1), (k + 1, k))])
+    pairs = [p for k in range(0, wide - 1, 2) for p in ((k, k + 1), (k + 1, k))]
+    within = lax.ppermute(volumes, WIDE, pairs)
     pinned = pl.BlockSpec(memory_space=pltpu.HBM)
     fast = pl.BlockSpec(memory_space=pltpu.VMEM)
     bf16 = functools.partial(jax.ShapeDtypeStruct, dtype=jnp.bfloat16)
@@ -288,13 +288,14 @@
         in_specs=[pinned] * 5,
         out_specs=(fast,) * 5,
         out_shape=(
-            bf16((2, 2 * C1, 18 * ROWS)), bf16((2, 2 * C1, 9 * ROWS)), bf16((2, 6 * C2, 6 * C1)),
-            bf16((CHUNK, CHUNK)), bf16(cotangent.shape),
+            bf16((2, 2 * C1, 18 * ROWS)), bf16((2, 2 * C1, 9 * ROWS)), bf16((2, 6 * C1, 6 * C2)),
+            bf16((CHUNK, CHUNK)), bf16((PLANE, 2 * C2)),
         ),
         scratch_shapes=[
             pltpu.VMEM((27, CIN, C1), jnp.bfloat16),
             pltpu.VMEM((27 * CIN, 4 * CHUNK), jnp.bfloat16),
             pltpu.VMEM((27, C1, C2), jnp.bfloat16),
+            pltpu.VMEM(cotangent.shape, jnp.bfloat16),
             pltpu.VMEM((27 * CIN, C1), jnp.float32),
             pltpu.SemaphoreType.DMA((5,)),
         ],
@@ -306,13 +307,13 @@
         near_kernel,
         in_specs=[fast] * 5,
         out_specs=(fast,) * 3,
-        out_shape=(f32((2 * C1, PLANE)), bf16((6 * C1, PLANE)), f32((2 * C2, PLANE))),
+        out_shape=(f32((2 * C1, PLANE)), bf16((6 * C1, PLANE)), f32((PLANE, 2 * C2))),
         scratch_shapes=[
-            pltpu.VMEM((2 * ROWS, CELLS), jnp.float32),
             pltpu.VMEM((4, 2 * ROWS, LANES + PLANE), jnp.bfloat16),
             pltpu.VMEM((18 * ROWS, PLANE), jnp.bfloat16),
             pltpu.VMEM((2 * C1, PLANE + 2 * LANES), jnp.bfloat16),
-            pltpu.VMEM((3, 2 * C2, PLANE + 2 * LANES), jnp.float32),
+            pltpu.VMEM((PLANE, 6 * C1), jnp.bfloat16),
+            pltpu.VMEM((3, PLANE + 2 * HALF, LANES), jnp.float32),
         ],
         compiler_params=pltpu.CompilerParams(vmem_limit_bytes=16 * MIB),
         cost_estimate=pl.CostEstimate(flops=10**9, bytes_accessed=4 * MIB, transcendentals=0),
@@ -325,12 +326,12 @@
         out_specs=(pl.BlockSpec(memory_space=pl.ANY), fast),
         out_shape=(bf16((1, 1, C2, cells_out)), bf16((C2, PACKED))),
         scratch_shapes=[
-            pltpu.VMEM((ROWS, CELLS), jnp.float32),
             pltpu.VMEM((4, ROWS, LANES + PLANE), jnp.bfloat16),
             pltpu.VMEM((9 * ROWS, PLANE), jnp.bfloat16),
             pltpu.VMEM((2 * C1, PLANE + 2 * LANES), jnp.bfloat16),
             pltpu.VMEM((6 * C1, PLANE), jnp.bfloat16),
-            pltpu.VMEM((3, 2 * C2, PLANE + 2 * LANES), jnp.float32),
+            pltpu.VMEM((PLANE, 6 * C1), jnp.bfloat16),
+            pltpu.VMEM((3, PLANE + 2 * HALF, LANES), jnp.float32),
             pltpu.VMEM((PLANE + 2 * HALF, LANES), jnp.bfloat16),
             pltpu.VMEM((2, 6 * C1, 3 * LANES), jnp.float32),
             pltpu.VMEM((1, 1, C2, cells_out), jnp.bfloat16),
@@ -343,12 +344,16 @@
     received = lax.all_to_all(term, ("narrow", "core"), 0, 0, tiled=True)
     owned = jnp.sum(received.reshape(2 * narrow, half, PACKED).astype(jnp.float32), axis=0).astype(jnp.bfloat16)
     parts = lax.all_to_all(jnp.broadcast_to(owned[None], (wide, half, PACKED)), WIDE, 0, 0, tiled=True)
+    total = jnp.sum(parts.reshape(wide // 2, rows, PACKED).astype(jnp.float32), axis=0)
     weight_grad = pl.pallas_call(
         finish_kernel,
-        out_shape=jax.ShapeDtypeStruct((27, rows, C1), jnp.float32),
+        in_specs=[fast],
+        out_specs=pl.BlockSpec(memory_space=pl.ANY),
+        out_shape=f32((27, rows, C1)),
+        scratch_shapes=[pltpu.VMEM((27, rows, C1), jnp.float32), pltpu.SemaphoreType.DMA((3,))],
         compiler_params=pltpu.CompilerParams(vmem_limit_bytes=8 * MIB),
         name="finish",
-    )(parts)
+    )(total)
     return (output, weight_grad)
 
 

time: 33.2 us -> 33.2 us (level)
  transfers between devices with their start and end apart: 2 -> 2, of which waited for: 0 -> 0; matrix products, arithmetic and copies ran while one was open for 0% -> 0% of each run, Pallas kernels for 10% -> 9%
where the time goes in v17:
time: 33.2 us; the launch traced here: 33 us
  blocking collectives  24.9 us (75%)
  Pallas kernels  6.12 us (18%)
  starting transfers between devices  1.17 us (4%)
  between operations  0.7 us (2%)
    all_to_all x1, blocking collectives, body(): received = lax.all_to_all(term, ('narrow', 'core'), 0, 0, tiled=True)  16.2 us
    all_to_all x1, blocking collectives, body(): lax.all_to_all(jnp.broadcast_to(owned[None], (wide, half, PACKED)), WIDE,...  8.76 us
    pallas_call x1, Pallas kernels, body(): pl.pallas_call(functools.partial(far_kernel, wide // 2, scale), in_specs=...  2.28 us
    pallas_call x1, Pallas kernels, body(): pl.pallas_call(prepare_kernel, in_specs=[pinned] * 5, out_specs=(fast,) *...  1.66 us
    pallas_call x1, Pallas kernels, body(): pl.pallas_call(near_kernel, in_specs=[fast] * 5, out_specs=(fast,) * 3, o...  1.39 us
    pallas_call x1, Pallas kernels, body(): pl.pallas_call(finish_kernel, in_specs=[fast], out_specs=pl.BlockSpec(mem...  0.79 us
  transfers between devices with their start and end apart: 2, of which 0 were waited for; matrix products, arithmetic and copies ran while one was open for 0% of the time, Pallas kernels for 9%

profile of v17, /device:TPU:0, one launch (start us, length us, event | category | flops | bytes accessed | tf_op | source)
XLA Modules:
  0.0 33.0 jit_solution(11760894146193462348)
XLA Ops:
  0.6 0.5 %collective-permute-start.1 = (bf16[1,1,4,4,4096]{4,3,2,1,0:T(4,128)(2,1)}, bf16[1,1,4,4,4096]{4,3,2,1,0:T(4,128)(2,1)S(1)}, u32[]{:S(2)}, u32[]{:S(2)}) collective-permute-start(bf16[1,1,4,4,4096]{4,3,2,1,0:T(4,128)(2,1)} %own_ref.1), channel_id=1, source_target_pairs={{0,4},{4,0},{8,12},{12,8},{16,20},{20,16},{24,28},{28,24},{1,5},{5... | collective-permute-start | bytes 393224 | tf_op jit(solution)/shard_map/ppermute | solution.py:277
  1.1 0.7 %collective-permute-start = (bf16[1,1,4,4,4096]{4,3,2,1,0:T(4,128)(2,1)}, bf16[1,1,4,4,4096]{4,3,2,1,0:T(4,128)(2,1)S(1)}, u32[]{:S(2)}, u32[]{:S(2)}) collective-permute-start(bf16[1,1,4,4,4096]{4,3,2,1,0:T(4,128)(2,1)} %own_ref.1), channel_id=1, source_target_pairs={{4,8},{8,4},{12,16},{16,12},{20,24},{24,20},{5,9},{9,5},{13,17},{1... | collective-permute-start | bytes 393224 | tf_op jit(solution)/shard_map/ppermute | solution.py:275
  1.8 0.0 copy-start
  1.8 1.7 %prepare.1 = (bf16[2,64,288]{2,1,0:T(8,128)(2,1)S(1)}, bf16[2,64,144]{2,1,0:T(8,128)(2,1)S(1)}, bf16[2,192,384]{2,1,0:T(8,128)(2,1)S(1)}, bf16[512,512]{1,0:T(8,128)(2,1)S(1)}, bf16[1024,128]{1,0:T(8,128)(2,1)S(1)}) custom-call(bf16[27,4,32]{2,1,0:T(4,128)(2,1)} %bitcast.10, bf16[2,108,2048]{2,1,0:T(8,128)(2,1)} %constant.8.clone.place_hbm, ...), custom_call_target="tpu_custom_call" | custom-call | flops 1000000000 | bytes 4194304 | tf_op jit(solution)/shard_map/prepare/pallas_call | solution.py:286
  3.5 0.0 collective-permute-done.1.within_ref
  3.5 0.0 copy-done
  3.5 1.4 %near.1 = (f32[64,1024]{1,0:T(8,128)S(1)}, bf16[192,1024]{1,0:T(8,128)(2,1)S(1)}, f32[1024,128]{1,0:T(8,128)S(1)}) custom-call(bf16[1,1,4,4,4096]{4,3,2,1,0:T(4,128)(2,1)S(1)} %copy-done, bf16[1,1,4,4,4096]{4,3,2,1,0:T(4,128)(2,1)S(1)} %collective-permute-done.1.within_ref, bf16[512,512]{1,0:T(8,128)(2,1)S(1)} %get-tuple-element.12.select_ref, ...), custom_call_target="tpu_custom_call" | custom-call | flops 1000000000 | bytes 4194304 | tf_op jit(solution)/shard_map/near/pallas_call | solution.py:306
  4.9 0.0 collective-permute-done.across_ref
  4.9 2.3 %far.1 = (bf16[1,1,64,2048]{3,2,1,0:T(8,128)(2,1)}, bf16[64,896]{1,0:T(8,128)(2,1)S(1)}) custom-call(bf16[1,1,4,4,4096]{4,3,2,1,0:T(4,128)(2,1)S(1)} %collective-permute-done.across_ref, bf16[512,512]{1,0:T(8,128)(2,1)S(1)} %get-tuple-element.12.select_ref, bf16[2,64,144]{2,1,0:T(8,128)(2,1)S(1)} %get-tuple-element.13.w1_ref, ...), custom_call_target="tpu_custom_call" | custom-call | tf_op jit(solution)/shard_map/far/pallas_call | solution.py:323
  7.2 16.2 %all_to_all.14 = bf16[8,8,896]{2,1,0:T(8,128)(2,1)S(1)} all-to-all(bf16[8,8,896]{2,1,0:T(8,128)(2,1)S(1)} %bitcast.7), channel_id=1, replica_groups=mesh['chip'=4,'core'=2,'narrow'=4] {'narrow','core'}, dimensions={0} | all-to-all | bytes 229376 | tf_op jit(solution)/shard_map/all_to_all | solution.py:344
  23.4 8.8 %all_to_all.15 = bf16[8,8,896]{2,1,0:T(8,128)(2,1)S(1)} all-to-all(bf16[8,8,896]{2,1,0:T(8,128)(2,1)S(1)} %broadcast_in_dim.2), channel_id=1, replica_groups=mesh['chip'=4,'core'=2,'narrow'=4] {'chip','core'}, dimensions={0} | all-to-all | bytes 229376 | tf_op jit(solution)/shard_map/all_to_all | solution.py:346
  32.2 0.8 %finish.1 = f32[27,16,32]{2,1,0:T(8,128)} custom-call(f32[16,896]{1,0:T(8,128)S(1)} %convert_reduce_fusion.total_ref), custom_call_target="tpu_custom_call" | custom-call | tf_op jit(solution)/shard_map/finish/pallas_call | solution.py:348
  (3 shorter events, 0.1 us)
Async XLA Ops:
  0.6 2.9 %collective-permute-start.1 = (bf16[1,1,4,4,4096]{4,3,2,1,0:T(4,128)(2,1)}, bf16[1,1,4,4,4096]{4,3,2,1,0:T(4,128)(2,1)S(1)}, u32[]{:S(2)}, u32[]{:S(2)}) collective-permute-start(bf16[1,1,4,4,4096]{4,3,2,1,0:T(4,128)(2,1)} %own_ref.1), channel_id=1, source_target_pairs={{0,4},{4,0},{8,12},{12,8},{16,20},{20,16},{24,28},{28,24},{1,5},{5... | collective-permute-start | bytes 393224 | tf_op jit(solution)/shard_map/ppermute | solution.py:277
  1.1 3.8 %collective-permute-start = (bf16[1,1,4,4,4096]{4,3,2,1,0:T(4,128)(2,1)}, bf16[1,1,4,4,4096]{4,3,2,1,0:T(4,128)(2,1)S(1)}, u32[]{:S(2)}, u32[]{:S(2)}) collective-permute-start(bf16[1,1,4,4,4096]{4,3,2,1,0:T(4,128)(2,1)} %own_ref.1), channel_id=1, source_target_pairs={{4,8},{8,4},{12,16},{16,12},{20,24},{24,20},{5,9},{9,5},{13,17},{1... | collective-permute-start | bytes 393224 | tf_op jit(solution)/shard_map/ppermute | solution.py:275
  1.8 1.7 %copy-start = (bf16[1,1,4,4,4096]{4,3,2,1,0:T(4,128)(2,1)S(1)}, bf16[1,1,4,4,4096]{4,3,2,1,0:T(4,128)(2,1)}, u32[]{:S(2)}) copy-start(bf16[1,1,4,4,4096]{4,3,2,1,0:T(4,128)(2,1)} %own_ref.1) | copy-start | bytes 393220

commit v18 on v17

--- a/solution.py
+++ b/solution.py
@@ -131,6 +131,14 @@
     act_ref[:, LANES + PLANE :] = margin
 
 
+def fetch_kernel(slab_hbm, low_ref, high_ref, sems):
+    copies = [pltpu.make_async_copy(slab_hbm.at[:, :, 2 * k : 2 * k + 2], ref, sems.at[k]) for k, ref in enumerate((low_ref, high_ref))]
+    for copy in copies:
+        copy.start()
+    for copy in copies:
+        copy.wait()
+
+
 def prepare_kernel(
     k1_hbm, place_hbm, k2_hbm, select_hbm, cot_hbm,
     w1_near_ref, w1_far_ref, w2_ref, select_ref, turned_ref,
@@ -176,11 +184,12 @@
 
 
 def near_kernel(
-    own_ref, within_ref, select_ref, w1_ref, w2_ref, first_ref, columns_ref, pre_ref,
+    own_ref, own2_ref, within_ref, within2_ref, select_ref, w1_ref, w2_ref, first_ref, columns_ref, pre_ref,
     parity_ref, taps_ref, act_ref, turned_ref, rowed_ref,
 ):
     odd = lax.axis_index("core")
-    rows = jnp.concatenate([plane_rows(own_ref), plane_rows(within_ref)], axis=0)
+    slabs = (own_ref, own2_ref, within_ref, within2_ref)
+    rows = jnp.concatenate([ref[0, 0, i] for ref in slabs for i in range(2)], axis=0)
     strided_taps(rows, select_ref, parity_ref, taps_ref)
     clear_margins(act_ref)
     for n in range(4):
@@ -273,12 +282,21 @@
     cells_out = cotangent.shape[3]
     scale = 1.0 / math.sqrt(wide * narrow * cells_out)
     across = lax.ppermute(volumes, WIDE, [p for k in range(1, wide - 1, 2) for p in ((k, k + 1), (k + 1, k))])
-    pairs = [p for k in range(0, wide - 1, 2) for p in ((k, k + 1), (k + 1, k))]
-    within = lax.ppermute(volumes, WIDE, pairs)
     pinned = pl.BlockSpec(memory_space=pltpu.HBM)
     fast = pl.BlockSpec(memory_space=pltpu.VMEM)
     bf16 = functools.partial(jax.ShapeDtypeStruct, dtype=jnp.bfloat16)
     f32 = functools.partial(jax.ShapeDtypeStruct, dtype=jnp.float32)
+    slabs = pl.pallas_call(
+        fetch_kernel,
+        in_specs=[pinned],
+        out_specs=(fast, fast),
+        out_shape=(bf16((1, 1, 2, PLANES, CELLS)),) * 2,
+        scratch_shapes=[pltpu.SemaphoreType.DMA((2,))],
+        compiler_params=pltpu.CompilerParams(vmem_limit_bytes=4 * MIB),
+        name="fetch",
+    )(pltpu.with_memory_space_constraint(volumes, pltpu.HBM))
+    pairs = [p for k in range(0, wide - 1, 2) for p in ((k, k + 1), (k + 1, k))]
+    withins = [lax.ppermute(slab, WIDE, pairs) for slab in slabs]
     stored = (
         first_kernel.transpose(0, 2, 1), jnp.asarray(placement(), jnp.bfloat16), second_kernel.transpose(0, 2, 1),
         jnp.asarray(selection(), jnp.bfloat16), cotangent,
@@ -305,7 +323,7 @@
     )(*(pltpu.with_memory_space_constraint(x, pltpu.HBM) for x in stored))
     first, near, pre = pl.pallas_call(
         near_kernel,
-        in_specs=[fast] * 5,
+        in_specs=[fast] * 7,
         out_specs=(fast,) * 3,
         out_shape=(f32((2 * C1, PLANE)), bf16((6 * C1, PLANE)), f32((PLANE, 2 * C2))),
         scratch_shapes=[
@@ -316,9 +334,8 @@
             pltpu.VMEM((3, PLANE + 2 * HALF, LANES), jnp.float32),
         ],
         compiler_params=pltpu.CompilerParams(vmem_limit_bytes=16 * MIB),
-        cost_estimate=pl.CostEstimate(flops=10**9, bytes_accessed=4 * MIB, transcendentals=0),
         name="near",
-    )(volumes, within, select, w1_near, w2)
+    )(*slabs, *withins, select, w1_near, w2)
     rows = C2 // narrow
     output, term = pl.pallas_call(
         functools.partial(far_kernel, wide // 2, scale),

time: 33.2 us -> 33.5 us (level)
  blocking collectives: 24.9 us -> 20.3 us
  starting transfers between devices: 1.17 us -> 5.12 us
  Pallas kernels: 6.12 us -> 6.97 us
    all_to_all x1, blocking collectives: 16.2 us -> 11.3 us  [body(): received = lax.all_to_all(term, ('narrow', 'core'), 0, 0, tiled=True)]
    ppermute x1 -> x2, starting transfers between devices: 0.52 us -> 4.45 us  [body(): withins = [lax.ppermute(slab, WIDE, pairs) for slab in slabs]]
    pallas_call x1 -> x2, Pallas kernels: 1.39 us -> 2.28 us  [the longest x1 1.39 us: body(): pl.pallas_call(near_kernel, in_specs=[fast] * 7, out_specs=(fast,) * 3, o...]
  transfers between devices with their start and end apart: 2 -> 3, of which waited for: 0 -> 0; matrix products, arithmetic and copies ran while one was open for 0% -> 0% of each run, Pallas kernels for 9% -> 12%
where the time goes in v18:
time: 33.5 us; the launch traced here: 33.2 us
  blocking collectives  20.3 us (61%)
  Pallas kernels  6.97 us (21%)
  starting transfers between devices  5.12 us (15%)
  between operations  0.7 us (2%)
    all_to_all x1, blocking collectives, body(): received = lax.all_to_all(term, ('narrow', 'core'), 0, 0, tiled=True)  11.3 us
    all_to_all x1, blocking collectives, body(): lax.all_to_all(jnp.broadcast_to(owned[None], (wide, half, PACKED)), WIDE,...  9.04 us
    ppermute x2, starting transfers between devices, body(): withins = [lax.ppermute(slab, WIDE, pairs) for slab in slabs]  4.45 us
    pallas_call x1, Pallas kernels, body(): pl.pallas_call(functools.partial(far_kernel, wide // 2, scale), in_specs=...  2.28 us
    pallas_call x1, Pallas kernels, body(): pl.pallas_call(prepare_kernel, in_specs=[pinned] * 5, out_specs=(fast,) *...  1.62 us
    pallas_call x1, Pallas kernels, body(): pl.pallas_call(near_kernel, in_specs=[fast] * 7, out_specs=(fast,) * 3, o...  1.39 us
    pallas_call x1, Pallas kernels, body(): pl.pallas_call(fetch_kernel, in_specs=[pinned], out_specs=(fast, fast), o...  0.89 us
    pallas_call x1, Pallas kernels, body(): pl.pallas_call(finish_kernel, in_specs=[fast], out_specs=pl.BlockSpec(mem...  0.79 us
  transfers between devices with their start and end apart: 3, of which 0 were waited for; matrix products, arithmetic and copies ran while one was open for 0% of the time, Pallas kernels for 12%

profile of v18, /device:TPU:0, one launch (start us, length us, event | category | flops | bytes accessed | tf_op | source)
XLA Modules:
  0.0 33.2 jit_solution(11896552969747294724)
XLA Ops:
  0.6 0.7 %collective-permute-start = (bf16[1,1,4,4,4096]{4,3,2,1,0:T(4,128)(2,1)}, bf16[1,1,4,4,4096]{4,3,2,1,0:T(4,128)(2,1)S(1)}, u32[]{:S(2)}, u32[]{:S(2)}) collective-permute-start(bf16[1,1,4,4,4096]{4,3,2,1,0:T(4,128)(2,1)} %slab_hbm.1), channel_id=1, source_target_pairs={{4,8},{8,4},{12,16},{16,12},{20,24},{24,20},{5,9},{9,5},{13,17},{1... | collective-permute-start | bytes 393224 | tf_op jit(solution)/shard_map/ppermute | solution.py:284
  1.3 0.9 %fetch.1 = (bf16[1,1,2,4,4096]{4,3,2,1,0:T(4,128)(2,1)S(1)}, bf16[1,1,2,4,4096]{4,3,2,1,0:T(4,128)(2,1)S(1)}) custom-call(bf16[1,1,4,4,4096]{4,3,2,1,0:T(4,128)(2,1)} %slab_hbm.1), custom_call_target="tpu_custom_call" | custom-call | tf_op jit(solution)/shard_map/fetch/pallas_call | solution.py:289
  2.2 4.4 %collective-permute-start.1 = (bf16[1,1,2,4,4096]{4,3,2,1,0:T(4,128)(2,1)S(1)}, bf16[1,1,2,4,4096]{4,3,2,1,0:T(4,128)(2,1)S(1)}, u32[]{:S(2)}, u32[]{:S(2)}) collective-permute-start(bf16[1,1,2,4,4096]{4,3,2,1,0:T(4,128)(2,1)S(1)} %get-tuple-element.18.own_ref), channel_id=1, source_target_pairs={{0,4},{4,0},{8,12},{12,8},{16,20},{20,16},{24,28},{28,24},{1,5},{5... | collective-permute-start | bytes 196616 | tf_op jit(solution)/shard_map/ppermute | solution.py:299
  6.6 0.1 collective-permute-start.2
  6.7 1.6 %prepare.1 = (bf16[2,64,288]{2,1,0:T(8,128)(2,1)S(1)}, bf16[2,64,144]{2,1,0:T(8,128)(2,1)S(1)}, bf16[2,192,384]{2,1,0:T(8,128)(2,1)S(1)}, bf16[512,512]{1,0:T(8,128)(2,1)S(1)}, bf16[1024,128]{1,0:T(8,128)(2,1)S(1)}) custom-call(bf16[27,4,32]{2,1,0:T(4,128)(2,1)} %bitcast.10, bf16[2,108,2048]{2,1,0:T(8,128)(2,1)} %constant.8.clone.place_hbm, ...), custom_call_target="tpu_custom_call" | custom-call | flops 1000000000 | bytes 4194304 | tf_op jit(solution)/shard_map/prepare/pallas_call | solution.py:304
  8.3 0.0 collective-permute-done.1.within_ref
  8.3 0.0 collective-permute-done.2.within2_ref
  8.3 1.4 %near.1 = (f32[64,1024]{1,0:T(8,128)S(1)}, bf16[192,1024]{1,0:T(8,128)(2,1)S(1)}, f32[1024,128]{1,0:T(8,128)S(1)}) custom-call(bf16[1,1,2,4,4096]{4,3,2,1,0:T(4,128)(2,1)S(1)} %get-tuple-element.18.own_ref, bf16[1,1,2,4,4096]{4,3,2,1,0:T(4,128)(2,1)S(1)} %get-tuple-element.19.own2_ref, bf16[1,1,2,4,4096]{4,3,2,1,0:T(4,128)(2,1)S(1)} %collective-permute-done.1.within_ref, ...), custom_call_target="tpu_custom_call" | custom-call | tf_op jit(solution)/shard_map/near/pallas_call | solution.py:324
  9.7 0.0 collective-permute-done.across_ref
  9.7 2.3 %far.1 = (bf16[1,1,64,2048]{3,2,1,0:T(8,128)(2,1)}, bf16[64,896]{1,0:T(8,128)(2,1)S(1)}) custom-call(bf16[1,1,4,4,4096]{4,3,2,1,0:T(4,128)(2,1)S(1)} %collective-permute-done.across_ref, bf16[512,512]{1,0:T(8,128)(2,1)S(1)} %get-tuple-element.14.select_ref, bf16[2,64,144]{2,1,0:T(8,128)(2,1)S(1)} %get-tuple-element.15.w1_ref, ...), custom_call_target="tpu_custom_call" | custom-call | tf_op jit(solution)/shard_map/far/pallas_call | solution.py:340
  12.0 11.3 %all_to_all.14 = bf16[8,8,896]{2,1,0:T(8,128)(2,1)S(1)} all-to-all(bf16[8,8,896]{2,1,0:T(8,128)(2,1)S(1)} %bitcast.7), channel_id=1, replica_groups=mesh['chip'=4,'core'=2,'narrow'=4] {'narrow','core'}, dimensions={0} | all-to-all | bytes 229376 | tf_op jit(solution)/shard_map/all_to_all | solution.py:361
  23.3 9.0 %all_to_all.15 = bf16[8,8,896]{2,1,0:T(8,128)(2,1)S(1)} all-to-all(bf16[8,8,896]{2,1,0:T(8,128)(2,1)S(1)} %broadcast_in_dim.2), channel_id=1, replica_groups=mesh['chip'=4,'core'=2,'narrow'=4] {'chip','core'}, dimensions={0} | all-to-all | bytes 229376 | tf_op jit(solution)/shard_map/all_to_all | solution.py:363
  32.4 0.8 %finish.1 = f32[27,16,32]{2,1,0:T(8,128)} custom-call(f32[16,896]{1,0:T(8,128)S(1)} %convert_reduce_fusion.total_ref), custom_call_target="tpu_custom_call" | custom-call | tf_op jit(solution)/shard_map/finish/pallas_call | solution.py:365
  (3 shorter events, 0.1 us)
Async XLA Ops:
  0.6 9.1 %collective-permute-start = (bf16[1,1,4,4,4096]{4,3,2,1,0:T(4,128)(2,1)}, bf16[1,1,4,4,4096]{4,3,2,1,0:T(4,128)(2,1)S(1)}, u32[]{:S(2)}, u32[]{:S(2)}) collective-permute-start(bf16[1,1,4,4,4096]{4,3,2,1,0:T(4,128)(2,1)} %slab_hbm.1), channel_id=1, source_target_pairs={{4,8},{8,4},{12,16},{16,12},{20,24},{24,20},{5,9},{9,5},{13,17},{1... | collective-permute-start | bytes 393224 | tf_op jit(solution)/shard_map/ppermute | solution.py:284
  2.2 6.1 %collective-permute-start.1 = (bf16[1,1,2,4,4096]{4,3,2,1,0:T(4,128)(2,1)S(1)}, bf16[1,1,2,4,4096]{4,3,2,1,0:T(4,128)(2,1)S(1)}, u32[]{:S(2)}, u32[]{:S(2)}) collective-permute-start(bf16[1,1,2,4,4096]{4,3,2,1,0:T(4,128)(2,1)S(1)} %get-tuple-element.18.own_ref), channel_id=1, source_target_pairs={{0,4},{4,0},{8,12},{12,8},{16,20},{20,16},{24,28},{28,24},{1,5},{5... | collective-permute-start | bytes 196616 | tf_op jit(solution)/shard_map/ppermute | solution.py:299
  6.6 1.7 %collective-permute-start.2 = (bf16[1,1,2,4,4096]{4,3,2,1,0:T(4,128)(2,1)S(1)}, bf16[1,1,2,4,4096]{4,3,2,1,0:T(4,128)(2,1)S(1)}, u32[]{:S(2)}, u32[]{:S(2)}) collective-permute-start(bf16[1,1,2,4,4096]{4,3,2,1,0:T(4,128)(2,1)S(1)} %get-tuple-element.19.own2_ref), channel_id=1, source_target_pairs={{0,4},{4,0},{8,12},{12,8},{16,20},{20,16},{24,28},{28,24},{1,5},{5... | collective-permute-start | bytes 196616 | tf_op jit(solution)/shard_map/ppermute | solution.py:299

commit v19 on v17

--- a/solution.py
+++ b/solution.py
@@ -194,8 +194,18 @@
         pre_ref[256 * n : 256 * n + 256, :] = row_sum(rowed_ref, n)
 
 
+def emit_activations(pre_ref, out_ref, out_hbm, sem):
+    for n in range(4):
+        output = leaky_relu(pre_ref[256 * n : 256 * n + 256, :]).astype(jnp.bfloat16).T
+        for z in range(2):
+            out_ref[0, 0, :, z * PLANE + 256 * n : z * PLANE + 256 * n + 256] = output[z * C2 : (z + 1) * C2]
+    copy = pltpu.make_async_copy(out_ref, out_hbm, sem)
+    copy.start()
+    copy.wait()
+
+
 def far_kernel(
-    chips, scale, across_ref, select_ref, w1_ref, w2_ref, cot_ref, first_ref, near_ref, near_pre_ref, out_hbm, grad_ref,
+    chips, narrow, scale, across_ref, select_ref, w1_ref, w2_ref, cot_ref, first_ref, near_ref, near_pre_ref, out_hbm, grad_ref, pre_ref,
     parity_ref, taps_ref, act_ref, columns_ref, turned_ref, rowed_ref, back_ref, sums_ref, out_ref, out_sem,
 ):
     odd = lax.axis_index("core")
@@ -218,13 +228,9 @@
     for n in range(4):
         cells = slice(256 * n, 256 * n + 256)
         pre = near_pre_ref[cells, :] + row_sum(rowed_ref, n)
+        pre_ref[cells, :] = pre
         back = cot_ref[cells, :].astype(jnp.float32) * jnp.where(pre > 0, 1.0, neg_slope)
         back_ref[HALF + 256 * n : HALF + 256 * n + 256, :] = back.astype(jnp.bfloat16)
-        output = leaky_relu(pre).astype(jnp.bfloat16).T
-        for z in range(2):
-            out_ref[0, 0, :, z * PLANE + 256 * n : z * PLANE + 256 * n + 256] = output[z * C2 : (z + 1) * C2]
-    out_copy = pltpu.make_async_copy(out_ref, out_hbm, out_sem)
-    out_copy.start()
     columns = jnp.concatenate([near_ref[...], columns_ref[...]], axis=0)
     rowed_back = jnp.concatenate([back_ref[(2 - b) * HALF : (2 - b) * HALF + PLANE, :] for b in range(3)], axis=1)
     sums = jnp.dot(columns, rowed_back, preferred_element_type=jnp.float32)
@@ -252,10 +258,12 @@
         grad_ref[:, 2 * block * LANES : (2 * block + 1) * LANES] = flat[0:C2]
         if block < 3:
             grad_ref[:, (2 * block + 1) * LANES : (2 * block + 2) * LANES] = flat[C2:]
-    out_copy.wait()
-
-
-def finish_kernel(total_ref, grad_hbm, grad_ref, sems):
+    early = lax.axis_index("narrow") < narrow - 1
+    pl.when(early)(lambda: emit_activations(pre_ref, out_ref, out_hbm, out_sem))
+
+
+def finish_kernel(narrow, total_ref, pre_ref, begun_hbm, grad_hbm, out_hbm, grad_ref, out_ref, sems, out_sem):
+    del begun_hbm
     copies = []
     for k in range(3):
         for tap in range(9 * k, 9 * k + 9):
@@ -263,6 +271,8 @@
         here = slice(9 * k, 9 * k + 9)
         copies.append(pltpu.make_async_copy(grad_ref.at[here], grad_hbm.at[here], sems.at[k]))
         copies[k].start()
+    late = lax.axis_index("narrow") == narrow - 1
+    pl.when(late)(lambda: emit_activations(pre_ref, out_ref, out_hbm, out_sem))
     for copy in copies:
         copy.wait()
 
@@ -320,11 +330,11 @@
         name="near",
     )(volumes, within, select, w1_near, w2)
     rows = C2 // narrow
-    output, term = pl.pallas_call(
-        functools.partial(far_kernel, wide // 2, scale),
+    begun, term, pre = pl.pallas_call(
+        functools.partial(far_kernel, wide // 2, narrow, scale),
         in_specs=[fast] * 8,
-        out_specs=(pl.BlockSpec(memory_space=pl.ANY), fast),
-        out_shape=(bf16((1, 1, C2, cells_out)), bf16((C2, PACKED))),
+        out_specs=(pl.BlockSpec(memory_space=pl.ANY), fast, fast),
+        out_shape=(bf16((1, 1, C2, cells_out)), bf16((C2, PACKED)), f32((PLANE, 2 * C2))),
         scratch_shapes=[
             pltpu.VMEM((4, ROWS, LANES + PLANE), jnp.bfloat16),
             pltpu.VMEM((9 * ROWS, PLANE), jnp.bfloat16),
@@ -345,15 +355,22 @@
     owned = jnp.sum(received.reshape(2 * narrow, half, PACKED).astype(jnp.float32), axis=0).astype(jnp.bfloat16)
     parts = lax.all_to_all(jnp.broadcast_to(owned[None], (wide, half, PACKED)), WIDE, 0, 0, tiled=True)
     total = jnp.sum(parts.reshape(wide // 2, rows, PACKED).astype(jnp.float32), axis=0)
-    weight_grad = pl.pallas_call(
-        finish_kernel,
-        in_specs=[fast],
-        out_specs=pl.BlockSpec(memory_space=pl.ANY),
-        out_shape=f32((27, rows, C1)),
-        scratch_shapes=[pltpu.VMEM((27, rows, C1), jnp.float32), pltpu.SemaphoreType.DMA((3,))],
+    anywhere = pl.BlockSpec(memory_space=pl.ANY)
+    weight_grad, output = pl.pallas_call(
+        functools.partial(finish_kernel, narrow),
+        in_specs=[fast, fast, anywhere],
+        out_specs=(anywhere, anywhere),
+        out_shape=(f32((27, rows, C1)), bf16((1, 1, C2, cells_out))),
+        scratch_shapes=[
+            pltpu.VMEM((27, rows, C1), jnp.float32),
+            pltpu.VMEM((1, 1, C2, cells_out), jnp.bfloat16),
+            pltpu.SemaphoreType.DMA((3,)),
+            pltpu.SemaphoreType.DMA,
+        ],
+        input_output_aliases={2: 1},
         compiler_params=pltpu.CompilerParams(vmem_limit_bytes=8 * MIB),
         name="finish",
-    )(total)
+    )(total, pre, begun)
     return (output, weight_grad)
 
 

time: 33.2 us -> 32.8 us (0.988)
  blocking collectives: 24.9 us -> 24.1 us
  Pallas kernels: 6.12 us -> 6.58 us
    all_to_all x1, blocking collectives: 16.2 us -> 15.4 us  [body(): received = lax.all_to_all(term, ('narrow', 'core'), 0, 0, tiled=True)]
    pallas_call x2, Pallas kernels: 3.07 us -> 3.52 us  [the longest x1 2.72 us: body(): pl.pallas_call(functools.partial(far_kernel, wide // 2, narrow, scale), i...]
where the time goes in v19:
time: 32.8 us; the launch traced here: 32.6 us
  blocking collectives  24.1 us (73%)
  Pallas kernels  6.58 us (20%)
  starting transfers between devices  1.17 us (4%)
  between operations  0.7 us (2%)
    all_to_all x1, blocking collectives, body(): received = lax.all_to_all(term, ('narrow', 'core'), 0, 0, tiled=True)  15.4 us
    all_to_all x1, blocking collectives, body(): lax.all_to_all(jnp.broadcast_to(owned[None], (wide, half, PACKED)), WIDE,...  8.76 us
    pallas_call x1, Pallas kernels, body(): pl.pallas_call(functools.partial(far_kernel, wide // 2, narrow, scale), i...  2.72 us
    pallas_call x1, Pallas kernels, body(): pl.pallas_call(prepare_kernel, in_specs=[pinned] * 5, out_specs=(fast,) *...  1.66 us
    pallas_call x1, Pallas kernels, body(): pl.pallas_call(near_kernel, in_specs=[fast] * 5, out_specs=(fast,) * 3, o...  1.4 us
    pallas_call x1, Pallas kernels, body(): pl.pallas_call(functools.partial(finish_kernel, narrow), in_specs=[fast,...  0.8 us
    ppermute x1, starting transfers between devices, body(): lax.ppermute(volumes, WIDE, [p for k in range(1, wide - 1, 2) for p in ((...  0.66 us
  transfers between devices with their start and end apart: 2, of which 0 were waited for; matrix products, arithmetic and copies ran while one was open for 0% of the time, Pallas kernels for 9%

profile of v19, /device:TPU:0, one launch (start us, length us, event | category | flops | bytes accessed | tf_op | source)
XLA Modules:
  0.0 32.6 jit_solution(11514187698241429638)
XLA Ops:
  0.6 0.5 %collective-permute-start.1 = (bf16[1,1,4,4,4096]{4,3,2,1,0:T(4,128)(2,1)}, bf16[1,1,4,4,4096]{4,3,2,1,0:T(4,128)(2,1)S(1)}, u32[]{:S(2)}, u32[]{:S(2)}) collective-permute-start(bf16[1,1,4,4,4096]{4,3,2,1,0:T(4,128)(2,1)} %own_ref.1), channel_id=1, source_target_pairs={{0,4},{4,0},{8,12},{12,8},{16,20},{20,16},{24,28},{28,24},{1,5},{5... | collective-permute-start | bytes 393224 | tf_op jit(solution)/shard_map/ppermute | solution.py:287
  1.1 0.7 %collective-permute-start = (bf16[1,1,4,4,4096]{4,3,2,1,0:T(4,128)(2,1)}, bf16[1,1,4,4,4096]{4,3,2,1,0:T(4,128)(2,1)S(1)}, u32[]{:S(2)}, u32[]{:S(2)}) collective-permute-start(bf16[1,1,4,4,4096]{4,3,2,1,0:T(4,128)(2,1)} %own_ref.1), channel_id=1, source_target_pairs={{4,8},{8,4},{12,16},{16,12},{20,24},{24,20},{5,9},{9,5},{13,17},{1... | collective-permute-start | bytes 393224 | tf_op jit(solution)/shard_map/ppermute | solution.py:285
  1.8 0.0 copy-start
  1.8 1.7 %prepare.1 = (bf16[2,64,288]{2,1,0:T(8,128)(2,1)S(1)}, bf16[2,64,144]{2,1,0:T(8,128)(2,1)S(1)}, bf16[2,192,384]{2,1,0:T(8,128)(2,1)S(1)}, bf16[512,512]{1,0:T(8,128)(2,1)S(1)}, bf16[1024,128]{1,0:T(8,128)(2,1)S(1)}) custom-call(bf16[27,4,32]{2,1,0:T(4,128)(2,1)} %bitcast.10, bf16[2,108,2048]{2,1,0:T(8,128)(2,1)} %constant.8.clone.place_hbm, ...), custom_call_target="tpu_custom_call" | custom-call | flops 1000000000 | bytes 4194304 | tf_op jit(solution)/shard_map/prepare/pallas_call | solution.py:296
  3.5 0.0 collective-permute-done.1.within_ref
  3.5 0.0 copy-done
  3.5 1.4 %near.1 = (f32[64,1024]{1,0:T(8,128)S(1)}, bf16[192,1024]{1,0:T(8,128)(2,1)S(1)}, f32[1024,128]{1,0:T(8,128)S(1)}) custom-call(bf16[1,1,4,4,4096]{4,3,2,1,0:T(4,128)(2,1)S(1)} %copy-done, bf16[1,1,4,4,4096]{4,3,2,1,0:T(4,128)(2,1)S(1)} %collective-permute-done.1.within_ref, bf16[512,512]{1,0:T(8,128)(2,1)S(1)} %get-tuple-element.15.select_ref, ...), custom_call_target="tpu_custom_call" | custom-call | flops 1000000000 | bytes 4194304 | tf_op jit(solution)/shard_map/near/pallas_call | solution.py:316
  4.9 0.0 collective-permute-done.across_ref
  4.9 2.7 %far.1 = (bf16[1,1,64,2048]{3,2,1,0:T(8,128)(2,1)}, bf16[64,896]{1,0:T(8,128)(2,1)S(1)}, f32[1024,128]{1,0:T(8,128)S(1)}) custom-call(bf16[1,1,4,4,4096]{4,3,2,1,0:T(4,128)(2,1)S(1)} %collective-permute-done.across_ref, bf16[512,512]{1,0:T(8,128)(2,1)S(1)} %get-tuple-element.15.select_ref, bf16[2,64,144]{2,1,0:T(8,128)(2,1)S(1)} %get-tuple-element.16.w1_ref, ...), custom_call_target="tpu_custom_call" | custom-call | tf_op jit(solution)/shard_map/far/pallas_call | solution.py:333
  7.7 15.4 %all_to_all.14 = bf16[8,8,896]{2,1,0:T(8,128)(2,1)S(1)} all-to-all(bf16[8,8,896]{2,1,0:T(8,128)(2,1)S(1)} %bitcast.7), channel_id=1, replica_groups=mesh['chip'=4,'core'=2,'narrow'=4] {'narrow','core'}, dimensions={0} | all-to-all | bytes 229376 | tf_op jit(solution)/shard_map/all_to_all | solution.py:354
  23.0 8.8 %all_to_all.15 = bf16[8,8,896]{2,1,0:T(8,128)(2,1)S(1)} all-to-all(bf16[8,8,896]{2,1,0:T(8,128)(2,1)S(1)} %broadcast_in_dim.2), channel_id=1, replica_groups=mesh['chip'=4,'core'=2,'narrow'=4] {'chip','core'}, dimensions={0} | all-to-all | bytes 229376 | tf_op jit(solution)/shard_map/all_to_all | solution.py:356
  31.8 0.8 %finish.1 = (f32[27,16,32]{2,1,0:T(8,128)}, bf16[1,1,64,2048]{3,2,1,0:T(8,128)(2,1)}) custom-call(f32[16,896]{1,0:T(8,128)S(1)} %convert_reduce_fusion.total_ref, f32[1024,128]{1,0:T(8,128)S(1)} %get-tuple-element.24.pre_ref, bf16[1,1,64,2048]{3,2,1,0:T(8,128)(2,1)} %get-tuple-element.25.begun_hbm), custom_call_target="tpu_custom_call", output_to_operand_aliasing={{1}: (2, {})} | custom-call | tf_op jit(solution)/shard_map/finish/pallas_call | solution.py:359
  (3 shorter events, 0.1 us)
Async XLA Ops:
  0.6 2.9 %collective-permute-start.1 = (bf16[1,1,4,4,4096]{4,3,2,1,0:T(4,128)(2,1)}, bf16[1,1,4,4,4096]{4,3,2,1,0:T(4,128)(2,1)S(1)}, u32[]{:S(2)}, u32[]{:S(2)}) collective-permute-start(bf16[1,1,4,4,4096]{4,3,2,1,0:T(4,128)(2,1)} %own_ref.1), channel_id=1, source_target_pairs={{0,4},{4,0},{8,12},{12,8},{16,20},{20,16},{24,28},{28,24},{1,5},{5... | collective-permute-start | bytes 393224 | tf_op jit(solution)/shard_map/ppermute | solution.py:287
  1.1 3.8 %collective-permute-start = (bf16[1,1,4,4,4096]{4,3,2,1,0:T(4,128)(2,1)}, bf16[1,1,4,4,4096]{4,3,2,1,0:T(4,128)(2,1)S(1)}, u32[]{:S(2)}, u32[]{:S(2)}) collective-permute-start(bf16[1,1,4,4,4096]{4,3,2,1,0:T(4,128)(2,1)} %own_ref.1), channel_id=1, source_target_pairs={{4,8},{8,4},{12,16},{16,12},{20,24},{24,20},{5,9},{9,5},{13,17},{1... | collective-permute-start | bytes 393224 | tf_op jit(solution)/shard_map/ppermute | solution.py:285
  1.8 1.7 %copy-start = (bf16[1,1,4,4,4096]{4,3,2,1,0:T(4,128)(2,1)S(1)}, bf16[1,1,4,4,4096]{4,3,2,1,0:T(4,128)(2,1)}, u32[]{:S(2)}) copy-start(bf16[1,1,4,4,4096]{4,3,2,1,0:T(4,128)(2,1)} %own_ref.1) | copy-start | bytes 393220

commit v20 on v19

--- a/solution.py
+++ b/solution.py
@@ -205,7 +205,7 @@
 
 
 def far_kernel(
-    chips, narrow, scale, across_ref, select_ref, w1_ref, w2_ref, cot_ref, first_ref, near_ref, near_pre_ref, out_hbm, grad_ref, pre_ref,
+    chips, scale, across_ref, select_ref, w1_ref, w2_ref, cot_ref, first_ref, near_ref, near_pre_ref, out_hbm, grad_ref, pre_ref,
     parity_ref, taps_ref, act_ref, columns_ref, turned_ref, rowed_ref, back_ref, sums_ref, out_ref, out_sem,
 ):
     odd = lax.axis_index("core")
@@ -258,11 +258,11 @@
         grad_ref[:, 2 * block * LANES : (2 * block + 1) * LANES] = flat[0:C2]
         if block < 3:
             grad_ref[:, (2 * block + 1) * LANES : (2 * block + 2) * LANES] = flat[C2:]
-    early = lax.axis_index("narrow") < narrow - 1
+    early = lax.axis_index("narrow") == 0
     pl.when(early)(lambda: emit_activations(pre_ref, out_ref, out_hbm, out_sem))
 
 
-def finish_kernel(narrow, total_ref, pre_ref, begun_hbm, grad_hbm, out_hbm, grad_ref, out_ref, sems, out_sem):
+def finish_kernel(total_ref, pre_ref, begun_hbm, grad_hbm, out_hbm, grad_ref, out_ref, sems, out_sem):
     del begun_hbm
     copies = []
     for k in range(3):
@@ -271,7 +271,7 @@
         here = slice(9 * k, 9 * k + 9)
         copies.append(pltpu.make_async_copy(grad_ref.at[here], grad_hbm.at[here], sems.at[k]))
         copies[k].start()
-    late = lax.axis_index("narrow") == narrow - 1
+    late = lax.axis_index("narrow") > 0
     pl.when(late)(lambda: emit_activations(pre_ref, out_ref, out_hbm, out_sem))
     for copy in copies:
         copy.wait()
@@ -331,7 +331,7 @@
     )(volumes, within, select, w1_near, w2)
     rows = C2 // narrow
     begun, term, pre = pl.pallas_call(
-        functools.partial(far_kernel, wide // 2, narrow, scale),
+        functools.partial(far_kernel, wide // 2, scale),
         in_specs=[fast] * 8,
         out_specs=(pl.BlockSpec(memory_space=pl.ANY), fast, fast),
         out_shape=(bf16((1, 1, C2, cells_out)), bf16((C2, PACKED)), f32((PLANE, 2 * C2))),
@@ -357,7 +357,7 @@
     total = jnp.sum(parts.reshape(wide // 2, rows, PACKED).astype(jnp.float32), axis=0)
     anywhere = pl.BlockSpec(memory_space=pl.ANY)
     weight_grad, output = pl.pallas_call(
-        functools.partial(finish_kernel, narrow),
+        finish_kernel,
         in_specs=[fast, fast, anywhere],
         out_specs=(anywhere, anywhere),
         out_shape=(f32((27, rows, C1)), bf16((1, 1, C2, cells_out))),

time: 32.8 us -> 32.8 us (level)
  no operation moved by 1% of the time
where the time goes in v20:
time: 32.8 us; the launch traced here: 32.6 us
  blocking collectives  24.1 us (73%)
  Pallas kernels  6.58 us (20%)
  starting transfers between devices  1.17 us (4%)
  between operations  0.7 us (2%)
    all_to_all x1, blocking collectives, body(): received = lax.all_to_all(term, ('narrow', 'core'), 0, 0, tiled=True)  15.4 us
    all_to_all x1, blocking collectives, body(): lax.all_to_all(jnp.broadcast_to(owned[None], (wide, half, PACKED)), WIDE,...  8.76 us
    pallas_call x1, Pallas kernels, body(): pl.pallas_call(functools.partial(far_kernel, wide // 2, scale), in_specs=...  2.72 us
    pallas_call x1, Pallas kernels, body(): pl.pallas_call(prepare_kernel, in_specs=[pinned] * 5, out_specs=(fast,) *...  1.66 us
    pallas_call x1, Pallas kernels, body(): pl.pallas_call(near_kernel, in_specs=[fast] * 5, out_specs=(fast,) * 3, o...  1.4 us
    pallas_call x1, Pallas kernels, body(): pl.pallas_call(finish_kernel, in_specs=[fast, fast, anywhere], out_specs=...  0.8 us
    ppermute x1, starting transfers between devices, body(): lax.ppermute(volumes, WIDE, [p for k in range(1, wide - 1, 2) for p in ((...  0.66 us
  transfers between devices with their start and end apart: 2, of which 0 were waited for; matrix products, arithmetic and copies ran while one was open for 0% of the time, Pallas kernels for 9%

profile of v20, /device:TPU:0, one launch (start us, length us, event | category | flops | bytes accessed | tf_op | source)
XLA Modules:
  0.0 32.6 jit_solution(14848621238051523948)
XLA Ops:
  0.6 0.5 %collective-permute-start.1 = (bf16[1,1,4,4,4096]{4,3,2,1,0:T(4,128)(2,1)}, bf16[1,1,4,4,4096]{4,3,2,1,0:T(4,128)(2,1)S(1)}, u32[]{:S(2)}, u32[]{:S(2)}) collective-permute-start(bf16[1,1,4,4,4096]{4,3,2,1,0:T(4,128)(2,1)} %own_ref.1), channel_id=1, source_target_pairs={{0,4},{4,0},{8,12},{12,8},{16,20},{20,16},{24,28},{28,24},{1,5},{5... | collective-permute-start | bytes 393224 | tf_op jit(solution)/shard_map/ppermute | solution.py:287
  1.1 0.7 %collective-permute-start = (bf16[1,1,4,4,4096]{4,3,2,1,0:T(4,128)(2,1)}, bf16[1,1,4,4,4096]{4,3,2,1,0:T(4,128)(2,1)S(1)}, u32[]{:S(2)}, u32[]{:S(2)}) collective-permute-start(bf16[1,1,4,4,4096]{4,3,2,1,0:T(4,128)(2,1)} %own_ref.1), channel_id=1, source_target_pairs={{4,8},{8,4},{12,16},{16,12},{20,24},{24,20},{5,9},{9,5},{13,17},{1... | collective-permute-start | bytes 393224 | tf_op jit(solution)/shard_map/ppermute | solution.py:285
  1.8 0.0 copy-start
  1.8 1.7 %prepare.1 = (bf16[2,64,288]{2,1,0:T(8,128)(2,1)S(1)}, bf16[2,64,144]{2,1,0:T(8,128)(2,1)S(1)}, bf16[2,192,384]{2,1,0:T(8,128)(2,1)S(1)}, bf16[512,512]{1,0:T(8,128)(2,1)S(1)}, bf16[1024,128]{1,0:T(8,128)(2,1)S(1)}) custom-call(bf16[27,4,32]{2,1,0:T(4,128)(2,1)} %bitcast.10, bf16[2,108,2048]{2,1,0:T(8,128)(2,1)} %constant.8.clone.place_hbm, ...), custom_call_target="tpu_custom_call" | custom-call | flops 1000000000 | bytes 4194304 | tf_op jit(solution)/shard_map/prepare/pallas_call | solution.py:296
  3.5 0.0 collective-permute-done.1.within_ref
  3.5 0.0 copy-done
  3.5 1.4 %near.1 = (f32[64,1024]{1,0:T(8,128)S(1)}, bf16[192,1024]{1,0:T(8,128)(2,1)S(1)}, f32[1024,128]{1,0:T(8,128)S(1)}) custom-call(bf16[1,1,4,4,4096]{4,3,2,1,0:T(4,128)(2,1)S(1)} %copy-done, bf16[1,1,4,4,4096]{4,3,2,1,0:T(4,128)(2,1)S(1)} %collective-permute-done.1.within_ref, bf16[512,512]{1,0:T(8,128)(2,1)S(1)} %get-tuple-element.15.select_ref, ...), custom_call_target="tpu_custom_call" | custom-call | flops 1000000000 | bytes 4194304 | tf_op jit(solution)/shard_map/near/pallas_call | solution.py:316
  4.9 0.0 collective-permute-done.across_ref
  4.9 2.7 %far.1 = (bf16[1,1,64,2048]{3,2,1,0:T(8,128)(2,1)}, bf16[64,896]{1,0:T(8,128)(2,1)S(1)}, f32[1024,128]{1,0:T(8,128)S(1)}) custom-call(bf16[1,1,4,4,4096]{4,3,2,1,0:T(4,128)(2,1)S(1)} %collective-permute-done.across_ref, bf16[512,512]{1,0:T(8,128)(2,1)S(1)} %get-tuple-element.15.select_ref, bf16[2,64,144]{2,1,0:T(8,128)(2,1)S(1)} %get-tuple-element.16.w1_ref, ...), custom_call_target="tpu_custom_call" | custom-call | tf_op jit(solution)/shard_map/far/pallas_call | solution.py:333
  7.7 15.4 %all_to_all.14 = bf16[8,8,896]{2,1,0:T(8,128)(2,1)S(1)} all-to-all(bf16[8,8,896]{2,1,0:T(8,128)(2,1)S(1)} %bitcast.7), channel_id=1, replica_groups=mesh['chip'=4,'core'=2,'narrow'=4] {'narrow','core'}, dimensions={0} | all-to-all | bytes 229376 | tf_op jit(solution)/shard_map/all_to_all | solution.py:354
  23.0 8.8 %all_to_all.15 = bf16[8,8,896]{2,1,0:T(8,128)(2,1)S(1)} all-to-all(bf16[8,8,896]{2,1,0:T(8,128)(2,1)S(1)} %broadcast_in_dim.2), channel_id=1, replica_groups=mesh['chip'=4,'core'=2,'narrow'=4] {'chip','core'}, dimensions={0} | all-to-all | bytes 229376 | tf_op jit(solution)/shard_map/all_to_all | solution.py:356
  31.8 0.8 %finish.1 = (f32[27,16,32]{2,1,0:T(8,128)}, bf16[1,1,64,2048]{3,2,1,0:T(8,128)(2,1)}) custom-call(f32[16,896]{1,0:T(8,128)S(1)} %convert_reduce_fusion.total_ref, f32[1024,128]{1,0:T(8,128)S(1)} %get-tuple-element.24.pre_ref, bf16[1,1,64,2048]{3,2,1,0:T(8,128)(2,1)} %get-tuple-element.25.begun_hbm), custom_call_target="tpu_custom_call", output_to_operand_aliasing={{1}: (2, {})} | custom-call | tf_op jit(solution)/shard_map/finish/pallas_call | solution.py:359
  (3 shorter events, 0.1 us)
Async XLA Ops:
  0.6 2.9 %collective-permute-start.1 = (bf16[1,1,4,4,4096]{4,3,2,1,0:T(4,128)(2,1)}, bf16[1,1,4,4,4096]{4,3,2,1,0:T(4,128)(2,1)S(1)}, u32[]{:S(2)}, u32[]{:S(2)}) collective-permute-start(bf16[1,1,4,4,4096]{4,3,2,1,0:T(4,128)(2,1)} %own_ref.1), channel_id=1, source_target_pairs={{0,4},{4,0},{8,12},{12,8},{16,20},{20,16},{24,28},{28,24},{1,5},{5... | collective-permute-start | bytes 393224 | tf_op jit(solution)/shard_map/ppermute | solution.py:287
  1.1 3.8 %collective-permute-start = (bf16[1,1,4,4,4096]{4,3,2,1,0:T(4,128)(2,1)}, bf16[1,1,4,4,4096]{4,3,2,1,0:T(4,128)(2,1)S(1)}, u32[]{:S(2)}, u32[]{:S(2)}) collective-permute-start(bf16[1,1,4,4,4096]{4,3,2,1,0:T(4,128)(2,1)} %own_ref.1), channel_id=1, source_target_pairs={{4,8},{8,4},{12,16},{16,12},{20,24},{24,20},{5,9},{9,5},{13,17},{1... | collective-permute-start | bytes 393224 | tf_op jit(solution)/shard_map/ppermute | solution.py:285
  1.8 1.7 %copy-start = (bf16[1,1,4,4,4096]{4,3,2,1,0:T(4,128)(2,1)S(1)}, bf16[1,1,4,4,4096]{4,3,2,1,0:T(4,128)(2,1)}, u32[]{:S(2)}) copy-start(bf16[1,1,4,4,4096]{4,3,2,1,0:T(4,128)(2,1)} %own_ref.1) | copy-start | bytes 393220

commit v21 on v20

--- a/solution.py
+++ b/solution.py
@@ -206,7 +206,7 @@
 
 def far_kernel(
     chips, scale, across_ref, select_ref, w1_ref, w2_ref, cot_ref, first_ref, near_ref, near_pre_ref, out_hbm, grad_ref, pre_ref,
-    parity_ref, taps_ref, act_ref, columns_ref, turned_ref, rowed_ref, back_ref, sums_ref, out_ref, out_sem,
+    parity_ref, taps_ref, act_ref, columns_ref, turned_ref, rowed_ref, back_ref, swapped_ref, out_ref, out_sem,
 ):
     odd = lax.axis_index("core")
     last = (lax.axis_index("chip") == chips - 1) & (odd == 1)
@@ -220,46 +220,57 @@
         there = slice(LANES + 256 * n, LANES + 256 * n + 256)
         act_ref[0:C1, there] = first_act[0:C1].astype(jnp.bfloat16)
         act_ref[C1:, there] = (first_act[C1:] * inside).astype(jnp.bfloat16)
-    shifted_columns(act_ref, columns_ref)
-    second_layer(w2_ref[odd], columns_ref, turned_ref, rowed_ref)
+    columns_ref[1 - odd] = near_ref[...]
+    shifted_columns(act_ref, columns_ref.at[odd])
+    second_layer(w2_ref[odd], columns_ref.at[odd], turned_ref, rowed_ref)
     margin = jnp.zeros((HALF, LANES), jnp.bfloat16)
-    back_ref[0:HALF, :] = margin
-    back_ref[HALF + PLANE :, :] = margin
+    for ref in (back_ref, swapped_ref):
+        ref[0:HALF, :] = margin
+        ref[HALF + PLANE :, :] = margin
     for n in range(4):
         cells = slice(256 * n, 256 * n + 256)
         pre = near_pre_ref[cells, :] + row_sum(rowed_ref, n)
         pre_ref[cells, :] = pre
-        back = cot_ref[cells, :].astype(jnp.float32) * jnp.where(pre > 0, 1.0, neg_slope)
-        back_ref[HALF + 256 * n : HALF + 256 * n + 256, :] = back.astype(jnp.bfloat16)
-    columns = jnp.concatenate([near_ref[...], columns_ref[...]], axis=0)
-    rowed_back = jnp.concatenate([back_ref[(2 - b) * HALF : (2 - b) * HALF + PLANE, :] for b in range(3)], axis=1)
-    sums = jnp.dot(columns, rowed_back, preferred_element_type=jnp.float32)
-    sums_ref[1 - odd] = sums[0 : 6 * C1]
-    sums_ref[odd] = sums[6 * C1 :]
-    low = lax.broadcasted_iota(jnp.int32, (C1, LANES), 1) < C2
-
-    def plane_sums(bc, q):
-        b, c = divmod(bc, 3)
+        back = (cot_ref[cells, :].astype(jnp.float32) * jnp.where(pre > 0, 1.0, neg_slope)).astype(jnp.bfloat16)
+        here = slice(HALF + 256 * n, HALF + 256 * n + 256)
+        back_ref[here, :] = back
+        swapped_ref[here, :] = jnp.concatenate([back[:, C2:], back[:, 0:C2]], axis=1)
+    low = lax.broadcasted_iota(jnp.int32, (1, LANES), 1) < C2
+    rows_of = [slice((2 - b) * HALF, (2 - b) * HALF + PLANE) for b in range(3)]
+    operands = []
+    for left_ref, right_ref in ((back_ref, swapped_ref), (swapped_ref, back_ref)):
+        first_two = jnp.where(low, left_ref[rows_of[0], :], right_ref[rows_of[1], :])
+        operands.append(jnp.concatenate([first_two, left_ref[rows_of[2], :]], axis=1))
+
+    def plane_columns(q, c):
         begin = 2 * C1 * c + C1 * (q % 2)
-        return sums_ref[q // 2, begin : begin + C1, b * LANES : (b + 1) * LANES]
-
-    def two_taps(first, second):
-        a, bc = divmod(first, 9)
-        here, above = plane_sums(bc, a), pltpu.roll(plane_sums(bc, a + 1), C2, 1)
-        if second > 26:
-            return here + above
-        a, bc = divmod(second, 9)
-        there, beyond = pltpu.roll(plane_sums(bc, a), C2, 1), plane_sums(bc, a + 1)
-        return jnp.where(low, here, there) + jnp.where(low, above, beyond)
-
-    for block in range(4):
-        tall = jnp.concatenate([two_taps(min(8 * block + g, 26), 8 * block + 4 + g) for g in range(4)], axis=0)
-        flat = (tall * scale).T.astype(jnp.bfloat16)
-        grad_ref[:, 2 * block * LANES : (2 * block + 1) * LANES] = flat[0:C2]
-        if block < 3:
-            grad_ref[:, (2 * block + 1) * LANES : (2 * block + 2) * LANES] = flat[C2:]
+        return columns_ref[q // 2, begin : begin + C1, :]
+
+    columns = [jnp.concatenate([plane_columns(a + z, c) for a in range(3) for c in range(3)], axis=0) for z in range(2)]
+    sums = scale * jnp.dot(
+        jnp.concatenate(columns, axis=1), jnp.concatenate(operands, axis=0), preferred_element_type=jnp.float32
+    )
+    left, right, ends = sums[0:256, 0:LANES], sums[0:256, LANES:], sums[256:]
+    turned = [left[0:LANES].T, left[LANES:].T]
+    third = jnp.where(low, right[0:LANES], pltpu.roll(right[LANES:], C2, 1)).T
+    fourth = jnp.concatenate([ends[:, 0:LANES], ends[:, LANES:]] * 2, axis=0).T
+    group = lax.broadcasted_iota(jnp.int32, (1, LANES), 1) // C1
+    tiles = [turned[0][0:C2], turned[1][0:C2], turned[0][C2:], turned[1][C2:], third[0:C2], third[C2:]]
+    tiles.append(jnp.where(group < 2, fourth[0:C2], pltpu.roll(fourth[C2:], C2, 1)))
+    for k, tile in enumerate(tiles):
+        grad_ref[:, k * LANES : (k + 1) * LANES] = tile.astype(jnp.bfloat16)
     early = lax.axis_index("narrow") == 0
     pl.when(early)(lambda: emit_activations(pre_ref, out_ref, out_hbm, out_sem))
+
+
+def slots():
+    where = []
+    for a in range(3):
+        for b in range(3):
+            for c in range(3):
+                tile, group = divmod(3 * a + c, 4)
+                where.append((2 * b + tile, group) if tile < 2 else (6, (0, 2, 1)[b]))
+    return where
 
 
 def finish_kernel(total_ref, pre_ref, begun_hbm, grad_hbm, out_hbm, grad_ref, out_ref, sems, out_sem):
@@ -267,7 +278,9 @@
     copies = []
     for k in range(3):
         for tap in range(9 * k, 9 * k + 9):
-            grad_ref[tap] = total_ref[:, tap * C1 : (tap + 1) * C1]
+            tile, slot = slots()[tap]
+            begin = tile * LANES + slot * C1
+            grad_ref[tap] = total_ref[:, begin : begin + C1]
         here = slice(9 * k, 9 * k + 9)
         copies.append(pltpu.make_async_copy(grad_ref.at[here], grad_hbm.at[here], sems.at[k]))
         copies[k].start()
@@ -339,11 +352,11 @@
             pltpu.VMEM((4, ROWS, LANES + PLANE), jnp.bfloat16),
             pltpu.VMEM((9 * ROWS, PLANE), jnp.bfloat16),
             pltpu.VMEM((2 * C1, PLANE + 2 * LANES), jnp.bfloat16),
-            pltpu.VMEM((6 * C1, PLANE), jnp.bfloat16),
+            pltpu.VMEM((2, 6 * C1, PLANE), jnp.bfloat16),
             pltpu.VMEM((PLANE, 6 * C1), jnp.bfloat16),
             pltpu.VMEM((3, PLANE + 2 * HALF, LANES), jnp.float32),
             pltpu.VMEM((PLANE + 2 * HALF, LANES), jnp.bfloat16),
-            pltpu.VMEM((2, 6 * C1, 3 * LANES), jnp.float32),
+            pltpu.VMEM((PLANE + 2 * HALF, LANES), jnp.bfloat16),
             pltpu.VMEM((1, 1, C2, cells_out), jnp.bfloat16),
             pltpu.SemaphoreType.DMA,
         ],

time: 32.8 us -> 32.8 us (level)
  no operation moved by 1% of the time
where the time goes in v21:
time: 32.8 us; the launch traced here: 32.6 us
  blocking collectives  24.1 us (73%)
  Pallas kernels  6.55 us (20%)
  starting transfers between devices  1.17 us (4%)
  between operations  0.7 us (2%)
    all_to_all x1, blocking collectives, body(): received = lax.all_to_all(term, ('narrow', 'core'), 0, 0, tiled=True)  15.3 us
    all_to_all x1, blocking collectives, body(): lax.all_to_all(jnp.broadcast_to(owned[None], (wide, half, PACKED)), WIDE,...  8.76 us
    pallas_call x1, Pallas kernels, body(): pl.pallas_call(functools.partial(far_kernel, wide // 2, scale), in_specs=...  2.69 us
    pallas_call x1, Pallas kernels, body(): pl.pallas_call(prepare_kernel, in_specs=[pinned] * 5, out_specs=(fast,) *...  1.66 us
    pallas_call x1, Pallas kernels, body(): pl.pallas_call(near_kernel, in_specs=[fast] * 5, out_specs=(fast,) * 3, o...  1.4 us
    pallas_call x1, Pallas kernels, body(): pl.pallas_call(finish_kernel, in_specs=[fast, fast, anywhere], out_specs=...  0.8 us
    ppermute x1, starting transfers between devices, body(): lax.ppermute(volumes, WIDE, [p for k in range(1, wide - 1, 2) for p in ((...  0.66 us
  transfers between devices with their start and end apart: 2, of which 0 were waited for; matrix products, arithmetic and copies ran while one was open for 0% of the time, Pallas kernels for 9%

profile of v21, /device:TPU:0, one launch (start us, length us, event | category | flops | bytes accessed | tf_op | source)
XLA Modules:
  0.0 32.6 jit_solution(4244123205730605386)
XLA Ops:
  0.6 0.5 %collective-permute-start.1 = (bf16[1,1,4,4,4096]{4,3,2,1,0:T(4,128)(2,1)}, bf16[1,1,4,4,4096]{4,3,2,1,0:T(4,128)(2,1)S(1)}, u32[]{:S(2)}, u32[]{:S(2)}) collective-permute-start(bf16[1,1,4,4,4096]{4,3,2,1,0:T(4,128)(2,1)} %own_ref.1), channel_id=1, source_target_pairs={{0,4},{4,0},{8,12},{12,8},{16,20},{20,16},{24,28},{28,24},{1,5},{5... | collective-permute-start | bytes 393224 | tf_op jit(solution)/shard_map/ppermute | solution.py:300
  1.1 0.7 %collective-permute-start = (bf16[1,1,4,4,4096]{4,3,2,1,0:T(4,128)(2,1)}, bf16[1,1,4,4,4096]{4,3,2,1,0:T(4,128)(2,1)S(1)}, u32[]{:S(2)}, u32[]{:S(2)}) collective-permute-start(bf16[1,1,4,4,4096]{4,3,2,1,0:T(4,128)(2,1)} %own_ref.1), channel_id=1, source_target_pairs={{4,8},{8,4},{12,16},{16,12},{20,24},{24,20},{5,9},{9,5},{13,17},{1... | collective-permute-start | bytes 393224 | tf_op jit(solution)/shard_map/ppermute | solution.py:298
  1.8 0.0 copy-start
  1.8 1.7 %prepare.1 = (bf16[2,64,288]{2,1,0:T(8,128)(2,1)S(1)}, bf16[2,64,144]{2,1,0:T(8,128)(2,1)S(1)}, bf16[2,192,384]{2,1,0:T(8,128)(2,1)S(1)}, bf16[512,512]{1,0:T(8,128)(2,1)S(1)}, bf16[1024,128]{1,0:T(8,128)(2,1)S(1)}) custom-call(bf16[27,4,32]{2,1,0:T(4,128)(2,1)} %bitcast.10, bf16[2,108,2048]{2,1,0:T(8,128)(2,1)} %constant.8.clone.place_hbm, ...), custom_call_target="tpu_custom_call" | custom-call | flops 1000000000 | bytes 4194304 | tf_op jit(solution)/shard_map/prepare/pallas_call | solution.py:309
  3.5 0.0 collective-permute-done.1.within_ref
  3.5 0.0 copy-done
  3.5 1.4 %near.1 = (f32[64,1024]{1,0:T(8,128)S(1)}, bf16[192,1024]{1,0:T(8,128)(2,1)S(1)}, f32[1024,128]{1,0:T(8,128)S(1)}) custom-call(bf16[1,1,4,4,4096]{4,3,2,1,0:T(4,128)(2,1)S(1)} %copy-done, bf16[1,1,4,4,4096]{4,3,2,1,0:T(4,128)(2,1)S(1)} %collective-permute-done.1.within_ref, bf16[512,512]{1,0:T(8,128)(2,1)S(1)} %get-tuple-element.15.select_ref, ...), custom_call_target="tpu_custom_call" | custom-call | flops 1000000000 | bytes 4194304 | tf_op jit(solution)/shard_map/near/pallas_call | solution.py:329
  4.9 0.0 collective-permute-done.across_ref
  4.9 2.7 %far.1 = (bf16[1,1,64,2048]{3,2,1,0:T(8,128)(2,1)}, bf16[64,896]{1,0:T(8,128)(2,1)S(1)}, f32[1024,128]{1,0:T(8,128)S(1)}) custom-call(bf16[1,1,4,4,4096]{4,3,2,1,0:T(4,128)(2,1)S(1)} %collective-permute-done.across_ref, bf16[512,512]{1,0:T(8,128)(2,1)S(1)} %get-tuple-element.15.select_ref, bf16[2,64,144]{2,1,0:T(8,128)(2,1)S(1)} %get-tuple-element.16.w1_ref, ...), custom_call_target="tpu_custom_call" | custom-call | tf_op jit(solution)/shard_map/far/pallas_call | solution.py:346
  7.6 15.3 %all_to_all.14 = bf16[8,8,896]{2,1,0:T(8,128)(2,1)S(1)} all-to-all(bf16[8,8,896]{2,1,0:T(8,128)(2,1)S(1)} %bitcast.7), channel_id=1, replica_groups=mesh['chip'=4,'core'=2,'narrow'=4] {'narrow','core'}, dimensions={0} | all-to-all | bytes 229376 | tf_op jit(solution)/shard_map/all_to_all | solution.py:367
  23.0 8.8 %all_to_all.15 = bf16[8,8,896]{2,1,0:T(8,128)(2,1)S(1)} all-to-all(bf16[8,8,896]{2,1,0:T(8,128)(2,1)S(1)} %broadcast_in_dim.2), channel_id=1, replica_groups=mesh['chip'=4,'core'=2,'narrow'=4] {'chip','core'}, dimensions={0} | all-to-all | bytes 229376 | tf_op jit(solution)/shard_map/all_to_all | solution.py:369
  31.8 0.8 %finish.1 = (f32[27,16,32]{2,1,0:T(8,128)}, bf16[1,1,64,2048]{3,2,1,0:T(8,128)(2,1)}) custom-call(f32[16,896]{1,0:T(8,128)S(1)} %convert_reduce_fusion.total_ref, f32[1024,128]{1,0:T(8,128)S(1)} %get-tuple-element.24.pre_ref, bf16[1,1,64,2048]{3,2,1,0:T(8,128)(2,1)} %get-tuple-element.25.begun_hbm), custom_call_target="tpu_custom_call", output_to_operand_aliasing={{1}: (2, {})} | custom-call | tf_op jit(solution)/shard_map/finish/pallas_call | solution.py:372
  (3 shorter events, 0.1 us)
Async XLA Ops:
  0.6 2.9 %collective-permute-start.1 = (bf16[1,1,4,4,4096]{4,3,2,1,0:T(4,128)(2,1)}, bf16[1,1,4,4,4096]{4,3,2,1,0:T(4,128)(2,1)S(1)}, u32[]{:S(2)}, u32[]{:S(2)}) collective-permute-start(bf16[1,1,4,4,4096]{4,3,2,1,0:T(4,128)(2,1)} %own_ref.1), channel_id=1, source_target_pairs={{0,4},{4,0},{8,12},{12,8},{16,20},{20,16},{24,28},{28,24},{1,5},{5... | collective-permute-start | bytes 393224 | tf_op jit(solution)/shard_map/ppermute | solution.py:300
  1.1 3.8 %collective-permute-start = (bf16[1,1,4,4,4096]{4,3,2,1,0:T(4,128)(2,1)}, bf16[1,1,4,4,4096]{4,3,2,1,0:T(4,128)(2,1)S(1)}, u32[]{:S(2)}, u32[]{:S(2)}) collective-permute-start(bf16[1,1,4,4,4096]{4,3,2,1,0:T(4,128)(2,1)} %own_ref.1), channel_id=1, source_target_pairs={{4,8},{8,4},{12,16},{16,12},{20,24},{24,20},{5,9},{9,5},{13,17},{1... | collective-permute-start | bytes 393224 | tf_op jit(solution)/shard_map/ppermute | solution.py:298
  1.8 1.7 %copy-start = (bf16[1,1,4,4,4096]{4,3,2,1,0:T(4,128)(2,1)S(1)}, bf16[1,1,4,4,4096]{4,3,2,1,0:T(4,128)(2,1)}, u32[]{:S(2)}) copy-start(bf16[1,1,4,4,4096]{4,3,2,1,0:T(4,128)(2,1)} %own_ref.1) | copy-start | bytes 393220

commit v22 on v21

--- a/solution.py
+++ b/solution.py
@@ -19,9 +19,10 @@
 LANES = 128
 ROWS = CIN * PLANES
 CHUNK = 512
-PACKED = 7 * LANES
+PACKED = 8 * LANES
 MIB = 2**20
-WIDE = ("chip", "core")
+WIDE = ("row", "column", "core")
+PART = 256
 neg_slope = 0.3
 
 
@@ -52,6 +53,10 @@
                             column = 18 * ROWS + bc * ROWS + inner
                         table[odd, 9 * a + bc, i, q, column] = 1
     return table.reshape(2, 27 * CIN, 4 * CHUNK)
+
+
+def chip_index():
+    return 2 * lax.axis_index("row") + lax.axis_index("column")
 
 
 def leaky_relu(value):
@@ -209,7 +214,7 @@
     parity_ref, taps_ref, act_ref, columns_ref, turned_ref, rowed_ref, back_ref, swapped_ref, out_ref, out_sem,
 ):
     odd = lax.axis_index("core")
-    last = (lax.axis_index("chip") == chips - 1) & (odd == 1)
+    last = (chip_index() == chips - 1) & (odd == 1)
     inside = jnp.where(last, 0.0, 1.0)
     strided_taps(plane_rows(across_ref), select_ref, parity_ref, taps_ref)
     clear_margins(act_ref)
@@ -257,8 +262,13 @@
     group = lax.broadcasted_iota(jnp.int32, (1, LANES), 1) // C1
     tiles = [turned[0][0:C2], turned[1][0:C2], turned[0][C2:], turned[1][C2:], third[0:C2], third[C2:]]
     tiles.append(jnp.where(group < 2, fourth[0:C2], pltpu.roll(fourth[C2:], C2, 1)))
-    for k, tile in enumerate(tiles):
-        grad_ref[:, k * LANES : (k + 1) * LANES] = tile.astype(jnp.bfloat16)
+    tiles.append(tiles[-1])
+    owners = grad_ref.shape[0] // 4
+    rows = C2 // owners
+    for n in range(owners):
+        for k, tile in enumerate(tiles):
+            lanes = slice(k % 2 * LANES, k % 2 * LANES + LANES)
+            grad_ref[4 * n + k // 2, :, lanes] = tile[n * rows : (n + 1) * rows].astype(jnp.bfloat16)
     early = lax.axis_index("narrow") == 0
     pl.when(early)(lambda: emit_activations(pre_ref, out_ref, out_hbm, out_sem))
 
@@ -279,8 +289,8 @@
     for k in range(3):
         for tap in range(9 * k, 9 * k + 9):
             tile, slot = slots()[tap]
-            begin = tile * LANES + slot * C1
-            grad_ref[tap] = total_ref[:, begin : begin + C1]
+            begin = tile % 2 * LANES + slot * C1
+            grad_ref[tap] = total_ref[tile // 2, :, begin : begin + C1]
         here = slice(9 * k, 9 * k + 9)
         copies.append(pltpu.make_async_copy(grad_ref.at[here], grad_hbm.at[here], sems.at[k]))
         copies[k].start()
@@ -347,7 +357,7 @@
         functools.partial(far_kernel, wide // 2, scale),
         in_specs=[fast] * 8,
         out_specs=(pl.BlockSpec(memory_space=pl.ANY), fast, fast),
-        out_shape=(bf16((1, 1, C2, cells_out)), bf16((C2, PACKED)), f32((PLANE, 2 * C2))),
+        out_shape=(bf16((1, 1, C2, cells_out)), bf16((4 * narrow, rows, PART)), f32((PLANE, 2 * C2))),
         scratch_shapes=[
             pltpu.VMEM((4, ROWS, LANES + PLANE), jnp.bfloat16),
             pltpu.VMEM((9 * ROWS, PLANE), jnp.bfloat16),
@@ -363,11 +373,10 @@
         compiler_params=pltpu.CompilerParams(vmem_limit_bytes=16 * MIB),
         name="far",
     )(across, select, w1_far, w2, cot, first, near, pre)
-    half = rows // 2
-    received = lax.all_to_all(term, ("narrow", "core"), 0, 0, tiled=True)
-    owned = jnp.sum(received.reshape(2 * narrow, half, PACKED).astype(jnp.float32), axis=0).astype(jnp.bfloat16)
-    parts = lax.all_to_all(jnp.broadcast_to(owned[None], (wide, half, PACKED)), WIDE, 0, 0, tiled=True)
-    total = jnp.sum(parts.reshape(wide // 2, rows, PACKED).astype(jnp.float32), axis=0)
+    received = lax.all_to_all(term, ("narrow", "column", "core"), 0, 0, tiled=True)
+    owned = jnp.sum(received.astype(jnp.float32), axis=0).astype(jnp.bfloat16)
+    parts = lax.all_to_all(jnp.broadcast_to(owned[None], (wide, rows, PART)), WIDE, 0, 0, tiled=True)
+    total = jnp.sum(parts.reshape(wide // 4, 4, rows, PART).astype(jnp.float32), axis=0)
     anywhere = pl.BlockSpec(memory_space=pl.ANY)
     weight_grad, output = pl.pallas_call(
         finish_kernel,
@@ -389,7 +398,7 @@
 
 def solution(mesh):
     wide, narrow = mesh.devices.shape
-    split = jax.sharding.Mesh(mesh.devices.reshape(wide // 2, 2, narrow), ("chip", "core", "narrow"))
+    split = jax.sharding.Mesh(mesh.devices.reshape(wide // 4, 2, 2, narrow), WIDE + ("narrow",))
     return jax.shard_map(
         body,
         mesh=split,

time: 32.8 us -> 34.4 us (1.049)
  blocking collectives: 24.1 us -> 25.7 us
    all_to_all x2, blocking collectives: 24.1 us -> 25.7 us  [the longest x1 18.3 us: body(): lax.all_to_all(term, ('narrow', 'column', 'core'), 0, 0, tiled=True)]
where the time goes in v22:
time: 34.4 us; the launch traced here: 34.2 us
  blocking collectives  25.7 us (75%)
  Pallas kernels  6.54 us (19%)
  starting transfers between devices  1.17 us (3%)
  between operations  0.7 us (2%)
    all_to_all x1, blocking collectives, body(): lax.all_to_all(term, ('narrow', 'column', 'core'), 0, 0, tiled=True)  18.3 us
    all_to_all x1, blocking collectives, body(): lax.all_to_all(jnp.broadcast_to(owned[None], (wide, rows, PART)), WIDE, 0...  7.4 us
    pallas_call x1, Pallas kernels, body(): pl.pallas_call(functools.partial(far_kernel, wide // 2, scale), in_specs=...  2.69 us
    pallas_call x1, Pallas kernels, body(): pl.pallas_call(prepare_kernel, in_specs=[pinned] * 5, out_specs=(fast,) *...  1.66 us
    pallas_call x1, Pallas kernels, body(): pl.pallas_call(near_kernel, in_specs=[fast] * 5, out_specs=(fast,) * 3, o...  1.39 us
    pallas_call x1, Pallas kernels, body(): pl.pallas_call(finish_kernel, in_specs=[fast, fast, anywhere], out_specs=...  0.8 us
  transfers between devices with their start and end apart: 2, of which 0 were waited for; matrix products, arithmetic and copies ran while one was open for 0% of the time, Pallas kernels for 9%

profile of v22, /device:TPU:0, one launch (start us, length us, event | category | flops | bytes accessed | tf_op | source)
XLA Modules:
  0.0 34.2 jit_solution(647299597589576231)
XLA Ops:
  0.6 0.5 %collective-permute-start.1 = (bf16[1,1,4,4,4096]{4,3,2,1,0:T(4,128)(2,1)}, bf16[1,1,4,4,4096]{4,3,2,1,0:T(4,128)(2,1)S(1)}, u32[]{:S(2)}, u32[]{:S(2)}) collective-permute-start(bf16[1,1,4,4,4096]{4,3,2,1,0:T(4,128)(2,1)} %own_ref.1), channel_id=1, source_target_pairs={{0,4},{4,0},{8,12},{12,8},{16,20},{20,16},{24,28},{28,24},{1,5},{5... | collective-permute-start | bytes 393224 | tf_op jit(solution)/shard_map/ppermute | solution.py:310
  1.1 0.7 %collective-permute-start = (bf16[1,1,4,4,4096]{4,3,2,1,0:T(4,128)(2,1)}, bf16[1,1,4,4,4096]{4,3,2,1,0:T(4,128)(2,1)S(1)}, u32[]{:S(2)}, u32[]{:S(2)}) collective-permute-start(bf16[1,1,4,4,4096]{4,3,2,1,0:T(4,128)(2,1)} %own_ref.1), channel_id=1, source_target_pairs={{4,8},{8,4},{12,16},{16,12},{20,24},{24,20},{5,9},{9,5},{13,17},{1... | collective-permute-start | bytes 393224 | tf_op jit(solution)/shard_map/ppermute | solution.py:308
  1.8 0.0 copy-start
  1.8 1.7 %prepare.1 = (bf16[2,64,288]{2,1,0:T(8,128)(2,1)S(1)}, bf16[2,64,144]{2,1,0:T(8,128)(2,1)S(1)}, bf16[2,192,384]{2,1,0:T(8,128)(2,1)S(1)}, bf16[512,512]{1,0:T(8,128)(2,1)S(1)}, bf16[1024,128]{1,0:T(8,128)(2,1)S(1)}) custom-call(bf16[27,4,32]{2,1,0:T(4,128)(2,1)} %bitcast.6, bf16[2,108,2048]{2,1,0:T(8,128)(2,1)} %constant.8.clone.place_hbm, ...), custom_call_target="tpu_custom_call" | custom-call | flops 1000000000 | bytes 4194304 | tf_op jit(solution)/shard_map/prepare/pallas_call | solution.py:319
  3.5 0.0 collective-permute-done.1.within_ref
  3.5 0.0 copy-done
  3.5 1.4 %near.1 = (f32[64,1024]{1,0:T(8,128)S(1)}, bf16[192,1024]{1,0:T(8,128)(2,1)S(1)}, f32[1024,128]{1,0:T(8,128)S(1)}) custom-call(bf16[1,1,4,4,4096]{4,3,2,1,0:T(4,128)(2,1)S(1)} %copy-done, bf16[1,1,4,4,4096]{4,3,2,1,0:T(4,128)(2,1)S(1)} %collective-permute-done.1.within_ref, bf16[512,512]{1,0:T(8,128)(2,1)S(1)} %get-tuple-element.15.select_ref, ...), custom_call_target="tpu_custom_call" | custom-call | flops 1000000000 | bytes 4194304 | tf_op jit(solution)/shard_map/near/pallas_call | solution.py:339
  4.9 0.0 collective-permute-done.across_ref
  4.9 2.7 %far.1 = (bf16[1,1,64,2048]{3,2,1,0:T(8,128)(2,1)}, bf16[16,16,256]{2,1,0:T(8,128)(2,1)S(1)}, f32[1024,128]{1,0:T(8,128)S(1)}) custom-call(bf16[1,1,4,4,4096]{4,3,2,1,0:T(4,128)(2,1)S(1)} %collective-permute-done.across_ref, bf16[512,512]{1,0:T(8,128)(2,1)S(1)} %get-tuple-element.15.select_ref, bf16[2,64,144]{2,1,0:T(8,128)(2,1)S(1)} %get-tuple-element.16.w1_ref, ...), custom_call_target="tpu_custom_call" | custom-call | tf_op jit(solution)/shard_map/far/pallas_call | solution.py:356
  7.6 18.3 %all_to_all.10 = bf16[16,16,256]{2,1,0:T(8,128)(2,1)S(1)} all-to-all(bf16[16,16,256]{2,1,0:T(8,128)(2,1)S(1)} %get-tuple-element.23), channel_id=1, replica_groups=mesh['row'=2,'column'=2,'core'=2,'narrow'=4] {'narrow','column','core'}, dimensions={0} | all-to-all | bytes 262144 | tf_op jit(solution)/shard_map/all_to_all | solution.py:376
  26.0 7.4 %all_to_all.11 = bf16[8,16,256]{2,1,0:T(8,128)(2,1)S(1)} all-to-all(bf16[8,16,256]{2,1,0:T(8,128)(2,1)S(1)} %broadcast_in_dim.2), channel_id=1, replica_groups=mesh['row'=2,'column'=2,'core'=2,'narrow'=4] {'row','column','core'}, dimensions={0} | all-to-all | bytes 131072 | tf_op jit(solution)/shard_map/all_to_all | solution.py:378
  33.4 0.8 %finish.1 = (f32[27,16,32]{2,1,0:T(8,128)}, bf16[1,1,64,2048]{3,2,1,0:T(8,128)(2,1)}) custom-call(f32[4,16,256]{2,1,0:T(8,128)S(1)} %convert_reduce_fusion.total_ref, f32[1024,128]{1,0:T(8,128)S(1)} %get-tuple-element.24.pre_ref, bf16[1,1,64,2048]{3,2,1,0:T(8,128)(2,1)} %get-tuple-element.25.begun_hbm), custom_call_target="tpu_custom_call", output_to_operand_aliasing={{1}: (2, {})} | custom-call | tf_op jit(solution)/shard_map/finish/pallas_call | solution.py:381
  (3 shorter events, 0.0 us)
Async XLA Ops:
  0.6 2.9 %collective-permute-start.1 = (bf16[1,1,4,4,4096]{4,3,2,1,0:T(4,128)(2,1)}, bf16[1,1,4,4,4096]{4,3,2,1,0:T(4,128)(2,1)S(1)}, u32[]{:S(2)}, u32[]{:S(2)}) collective-permute-start(bf16[1,1,4,4,4096]{4,3,2,1,0:T(4,128)(2,1)} %own_ref.1), channel_id=1, source_target_pairs={{0,4},{4,0},{8,12},{12,8},{16,20},{20,16},{24,28},{28,24},{1,5},{5... | collective-permute-start | bytes 393224 | tf_op jit(solution)/shard_map/ppermute | solution.py:310
  1.1 3.8 %collective-permute-start = (bf16[1,1,4,4,4096]{4,3,2,1,0:T(4,128)(2,1)}, bf16[1,1,4,4,4096]{4,3,2,1,0:T(4,128)(2,1)S(1)}, u32[]{:S(2)}, u32[]{:S(2)}) collective-permute-start(bf16[1,1,4,4,4096]{4,3,2,1,0:T(4,128)(2,1)} %own_ref.1), channel_id=1, source_target_pairs={{4,8},{8,4},{12,16},{16,12},{20,24},{24,20},{5,9},{9,5},{13,17},{1... | collective-permute-start | bytes 393224 | tf_op jit(solution)/shard_map/ppermute | solution.py:308
  1.8 1.7 %copy-start = (bf16[1,1,4,4,4096]{4,3,2,1,0:T(4,128)(2,1)S(1)}, bf16[1,1,4,4,4096]{4,3,2,1,0:T(4,128)(2,1)}, u32[]{:S(2)}) copy-start(bf16[1,1,4,4,4096]{4,3,2,1,0:T(4,128)(2,1)} %own_ref.1) | copy-start | bytes 393220

commit v23 on v21

--- a/solution.py
+++ b/solution.py
@@ -43,7 +43,7 @@
                 for i in range(CIN):
                     for q in range(4):
                         slab, plane = divmod(2 * q + a + 1, PLANES)
-                        inner = i * PLANES + plane
+                        inner = (plane - (slab == 0)) * CIN + i
                         if slab == 1:
                             column = bc * 2 * ROWS + inner
                         elif (slab == 0) == (odd == 1):
@@ -58,8 +58,8 @@
     return jnp.where(value > 0, value, neg_slope * value)
 
 
-def plane_rows(volume_ref):
-    return jnp.concatenate([volume_ref[0, 0, i] for i in range(CIN)], axis=0)
+def padded_rows(planes):
+    return jnp.concatenate(planes + [jnp.zeros((CIN, CELLS), jnp.bfloat16)], axis=0)
 
 
 def column_masks():
@@ -131,6 +131,21 @@
     act_ref[:, LANES + PLANE :] = margin
 
 
+def pack_kernel(slab_hbm, own_ref, across_ref, within_ref, within_last_ref, slab_ref, sem):
+    copy = pltpu.make_async_copy(slab_hbm, slab_ref, sem)
+    copy.start()
+    copy.wait()
+    odd = lax.axis_index("core")
+    channels = [slab_ref[0, 0, i].astype(jnp.float32) for i in range(CIN)]
+    for p in range(PLANES):
+        own_ref[p] = jnp.concatenate([x[p : p + 1] for x in channels], axis=0).astype(jnp.bfloat16)
+    for k in range(3):
+        across_ref[k] = own_ref[k + odd]
+    for k in range(2):
+        within_ref[k] = own_ref[k + 1 - odd]
+    within_last_ref[0] = own_ref[3 - odd]
+
+
 def prepare_kernel(
     k1_hbm, place_hbm, k2_hbm, select_hbm, cot_hbm,
     w1_near_ref, w1_far_ref, w2_ref, select_ref, turned_ref,
@@ -176,11 +191,11 @@
 
 
 def near_kernel(
-    own_ref, within_ref, select_ref, w1_ref, w2_ref, first_ref, columns_ref, pre_ref,
+    own_ref, within_ref, within_last_ref, select_ref, w1_ref, w2_ref, first_ref, columns_ref, pre_ref,
     parity_ref, taps_ref, act_ref, turned_ref, rowed_ref,
 ):
     odd = lax.axis_index("core")
-    rows = jnp.concatenate([plane_rows(own_ref), plane_rows(within_ref)], axis=0)
+    rows = padded_rows([own_ref[p] for p in range(PLANES)] + [within_ref[0], within_ref[1], within_last_ref[0]])
     strided_taps(rows, select_ref, parity_ref, taps_ref)
     clear_margins(act_ref)
     for n in range(4):
@@ -211,7 +226,7 @@
     odd = lax.axis_index("core")
     last = (lax.axis_index("chip") == chips - 1) & (odd == 1)
     inside = jnp.where(last, 0.0, 1.0)
-    strided_taps(plane_rows(across_ref), select_ref, parity_ref, taps_ref)
+    strided_taps(padded_rows([across_ref[k] for k in range(3)]), select_ref, parity_ref, taps_ref)
     clear_margins(act_ref)
     for n in range(4):
         here = slice(256 * n, 256 * n + 256)
@@ -295,13 +310,23 @@
     narrow = lax.axis_size("narrow")
     cells_out = cotangent.shape[3]
     scale = 1.0 / math.sqrt(wide * narrow * cells_out)
-    across = lax.ppermute(volumes, WIDE, [p for k in range(1, wide - 1, 2) for p in ((k, k + 1), (k + 1, k))])
-    pairs = [p for k in range(0, wide - 1, 2) for p in ((k, k + 1), (k + 1, k))]
-    within = lax.ppermute(volumes, WIDE, pairs)
     pinned = pl.BlockSpec(memory_space=pltpu.HBM)
     fast = pl.BlockSpec(memory_space=pltpu.VMEM)
     bf16 = functools.partial(jax.ShapeDtypeStruct, dtype=jnp.bfloat16)
     f32 = functools.partial(jax.ShapeDtypeStruct, dtype=jnp.float32)
+    own, across, within, within_last = pl.pallas_call(
+        pack_kernel,
+        in_specs=[pinned],
+        out_specs=(fast,) * 4,
+        out_shape=tuple(bf16((planes, CIN, CELLS)) for planes in (PLANES, 3, 2, 1)),
+        scratch_shapes=[pltpu.VMEM(volumes.shape, jnp.bfloat16), pltpu.SemaphoreType.DMA],
+        compiler_params=pltpu.CompilerParams(vmem_limit_bytes=8 * MIB),
+        name="pack",
+    )(pltpu.with_memory_space_constraint(volumes, pltpu.HBM))
+    across = lax.ppermute(across, WIDE, [p for k in range(1, wide - 1, 2) for p in ((k, k + 1), (k + 1, k))])
+    pairs = [p for k in range(0, wide - 1, 2) for p in ((k, k + 1), (k + 1, k))]
+    within = lax.ppermute(within, WIDE, pairs)
+    within_last = lax.ppermute(within_last, WIDE, pairs)
     stored = (
         first_kernel.transpose(0, 2, 1), jnp.asarray(placement(), jnp.bfloat16), second_kernel.transpose(0, 2, 1),
         jnp.asarray(selection(), jnp.bfloat16), cotangent,
@@ -328,7 +353,7 @@
     )(*(pltpu.with_memory_space_constraint(x, pltpu.HBM) for x in stored))
     first, near, pre = pl.pallas_call(
         near_kernel,
-        in_specs=[fast] * 5,
+        in_specs=[fast] * 6,
         out_specs=(fast,) * 3,
         out_shape=(f32((2 * C1, PLANE)), bf16((6 * C1, PLANE)), f32((PLANE, 2 * C2))),
         scratch_shapes=[
@@ -339,9 +364,8 @@
             pltpu.VMEM((3, PLANE + 2 * HALF, LANES), jnp.float32),
         ],
         compiler_params=pltpu.CompilerParams(vmem_limit_bytes=16 * MIB),
-        cost_estimate=pl.CostEstimate(flops=10**9, bytes_accessed=4 * MIB, transcendentals=0),
         name="near",
-    )(volumes, within, select, w1_near, w2)
+    )(own, within, within_last, select, w1_near, w2)
     rows = C2 // narrow
     begun, term, pre = pl.pallas_call(
         functools.partial(far_kernel, wide // 2, scale),

time: 32.8 us -> 33.2 us (1.012)
  blocking collectives: 24.1 us -> 19.5 us
  starting transfers between devices: 1.17 us -> 5.11 us
  Pallas kernels: 6.55 us -> 7.6 us
    all_to_all x1, blocking collectives: 15.3 us -> 10.5 us  [body(): received = lax.all_to_all(term, ('narrow', 'core'), 0, 0, tiled=True)]
    ppermute x2 -> x3, starting transfers between devices: 1.17 us -> 5.11 us  [the longest x1 4.36 us: body(): within_last = lax.ppermute(within_last, WIDE, pairs)]
    pallas_call x1 -> x2, Pallas kernels: 1.4 us -> 2.49 us  [the longest x1 1.39 us: body(): pl.pallas_call(near_kernel, in_specs=[fast] * 6, out_specs=(fast,) * 3, o...]
  transfers between devices with their start and end apart: 2 -> 3, of which waited for: 0 -> 0; matrix products, arithmetic and copies ran while one was open for 0% -> 0% of each run, Pallas kernels for 9% -> 9%
where the time goes in v23:
time: 33.2 us; the launch traced here: 33 us
  blocking collectives  19.5 us (59%)
  Pallas kernels  7.6 us (23%)
  starting transfers between devices  5.11 us (15%)
  between operations  0.7 us (2%)
    all_to_all x1, blocking collectives, body(): received = lax.all_to_all(term, ('narrow', 'core'), 0, 0, tiled=True)  10.5 us
    all_to_all x1, blocking collectives, body(): lax.all_to_all(jnp.broadcast_to(owned[None], (wide, half, PACKED)), WIDE,...  9.05 us
    ppermute x1, starting transfers between devices, body(): within_last = lax.ppermute(within_last, WIDE, pairs)  4.36 us
    pallas_call x1, Pallas kernels, body(): pl.pallas_call(functools.partial(far_kernel, wide // 2, scale), in_specs=...  2.68 us
    pallas_call x1, Pallas kernels, body(): pl.pallas_call(prepare_kernel, in_specs=[pinned] * 5, out_specs=(fast,) *...  1.63 us
    pallas_call x1, Pallas kernels, body(): pl.pallas_call(near_kernel, in_specs=[fast] * 6, out_specs=(fast,) * 3, o...  1.39 us
    pallas_call x1, Pallas kernels, body(): pl.pallas_call(pack_kernel, in_specs=[pinned], out_specs=(fast,) * 4, out...  1.1 us
    pallas_call x1, Pallas kernels, body(): pl.pallas_call(finish_kernel, in_specs=[fast, fast, anywhere], out_specs=...  0.8 us
  transfers between devices with their start and end apart: 3, of which 0 were waited for; matrix products, arithmetic and copies ran while one was open for 0% of the time, Pallas kernels for 9%

profile of v23, /device:TPU:0, one launch (start us, length us, event | category | flops | bytes accessed | tf_op | source)
XLA Modules:
  0.0 33.0 jit_solution(12774635044837804676)
XLA Ops:
  0.6 1.1 %pack.1 = (bf16[4,4,4096]{2,1,0:T(4,128)(2,1)S(1)}, bf16[3,4,4096]{2,1,0:T(4,128)(2,1)S(1)}, bf16[2,4,4096]{2,1,0:T(4,128)(2,1)S(1)}, bf16[1,4,4096]{2,1,0:T(4,128)(2,1)S(1)}) custom-call(bf16[1,1,4,4,4096]{4,3,2,1,0:T(4,128)(2,1)} %slab_hbm.1), custom_call_target="tpu_custom_call" | custom-call | tf_op jit(solution)/shard_map/pack/pallas_call | solution.py:317
  1.7 0.7 %collective-permute-start = (bf16[3,4,4096]{2,1,0:T(4,128)(2,1)S(1)}, bf16[3,4,4096]{2,1,0:T(4,128)(2,1)S(1)}, u32[]{:S(2)}, u32[]{:S(2)}) collective-permute-start(bf16[3,4,4096]{2,1,0:T(4,128)(2,1)S(1)} %get-tuple-element.19), channel_id=1, source_target_pairs={{4,8},{8,4},{12,16},{16,12},{20,24},{24,20},{5,9},{9,5},{13,17},{1... | collective-permute-start | bytes 294920 | tf_op jit(solution)/shard_map/ppermute | solution.py:326
  2.4 4.4 %collective-permute-start.2 = (bf16[1,4,4096]{2,1,0:T(4,128)(2,1)S(1)}, bf16[1,4,4096]{2,1,0:T(4,128)(2,1)S(1)}, u32[]{:S(2)}, u32[]{:S(2)}) collective-permute-start(bf16[1,4,4096]{2,1,0:T(4,128)(2,1)S(1)} %get-tuple-element.26), channel_id=1, source_target_pairs={{0,4},{4,0},{8,12},{12,8},{16,20},{20,16},{24,28},{28,24},{1,5},{5... | collective-permute-start | bytes 98312 | tf_op jit(solution)/shard_map/ppermute | solution.py:329
  6.8 0.1 collective-permute-start.1
  6.8 1.6 %prepare.1 = (bf16[2,64,288]{2,1,0:T(8,128)(2,1)S(1)}, bf16[2,64,144]{2,1,0:T(8,128)(2,1)S(1)}, bf16[2,192,384]{2,1,0:T(8,128)(2,1)S(1)}, bf16[512,512]{1,0:T(8,128)(2,1)S(1)}, bf16[1024,128]{1,0:T(8,128)(2,1)S(1)}) custom-call(bf16[27,4,32]{2,1,0:T(4,128)(2,1)} %bitcast.10, bf16[2,108,2048]{2,1,0:T(8,128)(2,1)} %constant.8.clone.place_hbm, ...), custom_call_target="tpu_custom_call" | custom-call | flops 1000000000 | bytes 4194304 | tf_op jit(solution)/shard_map/prepare/pallas_call | solution.py:334
  8.5 0.0 collective-permute-done.2.within_last_ref
  8.5 0.0 collective-permute-done.1.within_ref
  8.5 1.4 %near.1 = (f32[64,1024]{1,0:T(8,128)S(1)}, bf16[192,1024]{1,0:T(8,128)(2,1)S(1)}, f32[1024,128]{1,0:T(8,128)S(1)}) custom-call(bf16[4,4,4096]{2,1,0:T(4,128)(2,1)S(1)} %get-tuple-element.24.own_ref, bf16[2,4,4096]{2,1,0:T(4,128)(2,1)S(1)} %collective-permute-done.1.within_ref, bf16[1,4,4096]{2,1,0:T(4,128)(2,1)S(1)} %collective-permute-done.2.within_last_ref, ...), custom_call_target="tpu_custom_call" | custom-call | tf_op jit(solution)/shard_map/near/pallas_call | solution.py:354
  9.9 0.0 collective-permute-done.across_ref
  9.9 2.7 %far.1 = (bf16[1,1,64,2048]{3,2,1,0:T(8,128)(2,1)}, bf16[64,896]{1,0:T(8,128)(2,1)S(1)}, f32[1024,128]{1,0:T(8,128)S(1)}) custom-call(bf16[3,4,4096]{2,1,0:T(4,128)(2,1)S(1)} %collective-permute-done.across_ref, bf16[512,512]{1,0:T(8,128)(2,1)S(1)} %get-tuple-element.20.select_ref, bf16[2,64,144]{2,1,0:T(8,128)(2,1)S(1)} %get-tuple-element.21.w1_ref, ...), custom_call_target="tpu_custom_call" | custom-call | tf_op jit(solution)/shard_map/far/pallas_call | solution.py:370
  12.6 10.5 %all_to_all.14 = bf16[8,8,896]{2,1,0:T(8,128)(2,1)S(1)} all-to-all(bf16[8,8,896]{2,1,0:T(8,128)(2,1)S(1)} %bitcast.7), channel_id=1, replica_groups=mesh['chip'=4,'core'=2,'narrow'=4] {'narrow','core'}, dimensions={0} | all-to-all | bytes 229376 | tf_op jit(solution)/shard_map/all_to_all | solution.py:391
  23.1 9.1 %all_to_all.15 = bf16[8,8,896]{2,1,0:T(8,128)(2,1)S(1)} all-to-all(bf16[8,8,896]{2,1,0:T(8,128)(2,1)S(1)} %broadcast_in_dim.2), channel_id=1, replica_groups=mesh['chip'=4,'core'=2,'narrow'=4] {'chip','core'}, dimensions={0} | all-to-all | bytes 229376 | tf_op jit(solution)/shard_map/all_to_all | solution.py:393
  32.2 0.8 %finish.1 = (f32[27,16,32]{2,1,0:T(8,128)}, bf16[1,1,64,2048]{3,2,1,0:T(8,128)(2,1)}) custom-call(f32[16,896]{1,0:T(8,128)S(1)} %convert_reduce_fusion.total_ref, f32[1024,128]{1,0:T(8,128)S(1)} %get-tuple-element.32.pre_ref, bf16[1,1,64,2048]{3,2,1,0:T(8,128)(2,1)} %get-tuple-element.33.begun_hbm), custom_call_target="tpu_custom_call", output_to_operand_aliasing={{1}: (2, {})} | custom-call | tf_op jit(solution)/shard_map/finish/pallas_call | solution.py:396
  (3 shorter events, 0.1 us)
Async XLA Ops:
  1.7 8.2 %collective-permute-start = (bf16[3,4,4096]{2,1,0:T(4,128)(2,1)S(1)}, bf16[3,4,4096]{2,1,0:T(4,128)(2,1)S(1)}, u32[]{:S(2)}, u32[]{:S(2)}) collective-permute-start(bf16[3,4,4096]{2,1,0:T(4,128)(2,1)S(1)} %get-tuple-element.19), channel_id=1, source_target_pairs={{4,8},{8,4},{12,16},{16,12},{20,24},{24,20},{5,9},{9,5},{13,17},{1... | collective-permute-start | bytes 294920 | tf_op jit(solution)/shard_map/ppermute | solution.py:326
  2.4 6.1 %collective-permute-start.2 = (bf16[1,4,4096]{2,1,0:T(4,128)(2,1)S(1)}, bf16[1,4,4096]{2,1,0:T(4,128)(2,1)S(1)}, u32[]{:S(2)}, u32[]{:S(2)}) collective-permute-start(bf16[1,4,4096]{2,1,0:T(4,128)(2,1)S(1)} %get-tuple-element.26), channel_id=1, source_target_pairs={{0,4},{4,0},{8,12},{12,8},{16,20},{20,16},{24,28},{28,24},{1,5},{5... | collective-permute-start | bytes 98312 | tf_op jit(solution)/shard_map/ppermute | solution.py:329
  6.8 1.7 %collective-permute-start.1 = (bf16[2,4,4096]{2,1,0:T(4,128)(2,1)S(1)}, bf16[2,4,4096]{2,1,0:T(4,128)(2,1)S(1)}, u32[]{:S(2)}, u32[]{:S(2)}) collective-permute-start(bf16[2,4,4096]{2,1,0:T(4,128)(2,1)S(1)} %get-tuple-element.25), channel_id=1, source_target_pairs={{0,4},{4,0},{8,12},{12,8},{16,20},{20,16},{24,28},{28,24},{1,5},{5... | collective-permute-start | bytes 196616 | tf_op jit(solution)/shard_map/ppermute | solution.py:328

commit v24 on v21

--- a/solution.py
+++ b/solution.py
@@ -49,17 +49,13 @@
                         elif (slab == 0) == (odd == 1):
                             column = bc * 2 * ROWS + ROWS + inner
                         else:
-                            column = 18 * ROWS + bc * ROWS + inner
+                            column = 18 * ROWS + bc * ROWS + (plane - (slab == 0)) * CIN + i
                         table[odd, 9 * a + bc, i, q, column] = 1
     return table.reshape(2, 27 * CIN, 4 * CHUNK)
 
 
 def leaky_relu(value):
     return jnp.where(value > 0, value, neg_slope * value)
-
-
-def plane_rows(volume_ref):
-    return jnp.concatenate([volume_ref[0, 0, i] for i in range(CIN)], axis=0)
 
 
 def column_masks():
@@ -131,6 +127,24 @@
     act_ref[:, LANES + PLANE :] = margin
 
 
+def pack_kernel(slab_hbm, across_ref, low_ref, high_ref, rows_ref, sems):
+    odd = lax.axis_index("core")
+    places = [(ref, k) for ref in (low_ref, high_ref) for k in range(CIN // 2)]
+    copies = [pltpu.make_async_copy(slab_hbm.at[0, 0, i], ref.at[k], sems.at[i]) for i, (ref, k) in enumerate(places)]
+    for copy in copies:
+        copy.start()
+    for i, (ref, k) in enumerate(places):
+        copies[i].wait()
+        planes = ref[k].astype(jnp.float32)
+        for j in range(CELLS // LANES):
+            begin = j * ROWS + PLANES * i
+            rows_ref[begin : begin + PLANES, :] = planes[:, j * LANES : (j + 1) * LANES]
+    for k in range(3):
+        for j in range(CELLS // LANES):
+            channels = rows_ref[pl.ds(j * ROWS + k + odd, CIN, stride=PLANES), :]
+            across_ref[k, :, j * LANES : (j + 1) * LANES] = channels.astype(jnp.bfloat16)
+
+
 def prepare_kernel(
     k1_hbm, place_hbm, k2_hbm, select_hbm, cot_hbm,
     w1_near_ref, w1_far_ref, w2_ref, select_ref, turned_ref,
@@ -176,11 +190,12 @@
 
 
 def near_kernel(
-    own_ref, within_ref, select_ref, w1_ref, w2_ref, first_ref, columns_ref, pre_ref,
+    own_low_ref, own_high_ref, low_ref, high_ref, select_ref, w1_ref, w2_ref, first_ref, columns_ref, pre_ref,
     parity_ref, taps_ref, act_ref, turned_ref, rowed_ref,
 ):
     odd = lax.axis_index("core")
-    rows = jnp.concatenate([plane_rows(own_ref), plane_rows(within_ref)], axis=0)
+    slabs = (own_low_ref, own_high_ref, low_ref, high_ref)
+    rows = jnp.concatenate([ref[k] for ref in slabs for k in range(CIN // 2)], axis=0)
     strided_taps(rows, select_ref, parity_ref, taps_ref)
     clear_margins(act_ref)
     for n in range(4):
@@ -211,7 +226,9 @@
     odd = lax.axis_index("core")
     last = (lax.axis_index("chip") == chips - 1) & (odd == 1)
     inside = jnp.where(last, 0.0, 1.0)
-    strided_taps(plane_rows(across_ref), select_ref, parity_ref, taps_ref)
+    blank = jnp.zeros((CIN, CELLS), jnp.bfloat16)
+    rows = jnp.concatenate([across_ref[k] for k in range(3)] + [blank], axis=0)
+    strided_taps(rows, select_ref, parity_ref, taps_ref)
     clear_margins(act_ref)
     for n in range(4):
         here = slice(256 * n, 256 * n + 256)
@@ -295,13 +312,23 @@
     narrow = lax.axis_size("narrow")
     cells_out = cotangent.shape[3]
     scale = 1.0 / math.sqrt(wide * narrow * cells_out)
-    across = lax.ppermute(volumes, WIDE, [p for k in range(1, wide - 1, 2) for p in ((k, k + 1), (k + 1, k))])
-    pairs = [p for k in range(0, wide - 1, 2) for p in ((k, k + 1), (k + 1, k))]
-    within = lax.ppermute(volumes, WIDE, pairs)
     pinned = pl.BlockSpec(memory_space=pltpu.HBM)
     fast = pl.BlockSpec(memory_space=pltpu.VMEM)
     bf16 = functools.partial(jax.ShapeDtypeStruct, dtype=jnp.bfloat16)
     f32 = functools.partial(jax.ShapeDtypeStruct, dtype=jnp.float32)
+    halves = bf16((CIN // 2, PLANES, CELLS))
+    across, low, high = pl.pallas_call(
+        pack_kernel,
+        in_specs=[pinned],
+        out_specs=(fast,) * 3,
+        out_shape=(bf16((3, CIN, CELLS)), halves, halves),
+        scratch_shapes=[pltpu.VMEM((CELLS // LANES * ROWS, LANES), jnp.float32), pltpu.SemaphoreType.DMA((CIN,))],
+        compiler_params=pltpu.CompilerParams(vmem_limit_bytes=8 * MIB),
+        name="pack",
+    )(pltpu.with_memory_space_constraint(volumes, pltpu.HBM))
+    across = lax.ppermute(across, WIDE, [p for k in range(1, wide - 1, 2) for p in ((k, k + 1), (k + 1, k))])
+    pairs = [p for k in range(0, wide - 1, 2) for p in ((k, k + 1), (k + 1, k))]
+    within = [lax.ppermute(half, WIDE, pairs) for half in (low, high)]
     stored = (
         first_kernel.transpose(0, 2, 1), jnp.asarray(placement(), jnp.bfloat16), second_kernel.transpose(0, 2, 1),
         jnp.asarray(selection(), jnp.bfloat16), cotangent,
@@ -328,7 +355,7 @@
     )(*(pltpu.with_memory_space_constraint(x, pltpu.HBM) for x in stored))
     first, near, pre = pl.pallas_call(
         near_kernel,
-        in_specs=[fast] * 5,
+        in_specs=[fast] * 7,
         out_specs=(fast,) * 3,
         out_shape=(f32((2 * C1, PLANE)), bf16((6 * C1, PLANE)), f32((PLANE, 2 * C2))),
         scratch_shapes=[
@@ -339,9 +366,8 @@
             pltpu.VMEM((3, PLANE + 2 * HALF, LANES), jnp.float32),
         ],
         compiler_params=pltpu.CompilerParams(vmem_limit_bytes=16 * MIB),
-        cost_estimate=pl.CostEstimate(flops=10**9, bytes_accessed=4 * MIB, transcendentals=0),
         name="near",
-    )(volumes, within, select, w1_near, w2)
+    )(low, high, *within, select, w1_near, w2)
     rows = C2 // narrow
     begun, term, pre = pl.pallas_call(
         functools.partial(far_kernel, wide // 2, scale),

time: 32.8 us -> 33.1 us (level)
  blocking collectives: 24.1 us -> 19.5 us
  starting transfers between devices: 1.17 us -> 5.11 us
  Pallas kernels: 6.55 us -> 7.41 us
    all_to_all x1, blocking collectives: 15.3 us -> 10.5 us  [body(): received = lax.all_to_all(term, ('narrow', 'core'), 0, 0, tiled=True)]
    ppermute x2 -> x3, starting transfers between devices: 1.17 us -> 5.11 us  [the longest x2 4.44 us: body(): within = [lax.ppermute(half, WIDE, pairs) for half in (low, high)]]
    pallas_call x1 -> x2, Pallas kernels: 1.4 us -> 2.3 us  [the longest x1 1.39 us: body(): pl.pallas_call(near_kernel, in_specs=[fast] * 7, out_specs=(fast,) * 3, o...]
  transfers between devices with their start and end apart: 2 -> 3, of which waited for: 0 -> 0; matrix products, arithmetic and copies ran while one was open for 0% -> 0% of each run, Pallas kernels for 9% -> 9%
where the time goes in v24:
time: 33.1 us; the launch traced here: 32.8 us
  blocking collectives  19.5 us (59%)
  Pallas kernels  7.41 us (22%)
  starting transfers between devices  5.11 us (15%)
  between operations  0.7 us (2%)
    all_to_all x1, blocking collectives, body(): received = lax.all_to_all(term, ('narrow', 'core'), 0, 0, tiled=True)  10.5 us
    all_to_all x1, blocking collectives, body(): lax.all_to_all(jnp.broadcast_to(owned[None], (wide, half, PACKED)), WIDE,...  9.05 us
    ppermute x2, starting transfers between devices, body(): within = [lax.ppermute(half, WIDE, pairs) for half in (low, high)]  4.44 us
    pallas_call x1, Pallas kernels, body(): pl.pallas_call(functools.partial(far_kernel, wide // 2, scale), in_specs=...  2.69 us
    pallas_call x1, Pallas kernels, body(): pl.pallas_call(prepare_kernel, in_specs=[pinned] * 5, out_specs=(fast,) *...  1.63 us
    pallas_call x1, Pallas kernels, body(): pl.pallas_call(near_kernel, in_specs=[fast] * 7, out_specs=(fast,) * 3, o...  1.39 us
    pallas_call x1, Pallas kernels, body(): pl.pallas_call(pack_kernel, in_specs=[pinned], out_specs=(fast,) * 3, out...  0.91 us
    pallas_call x1, Pallas kernels, body(): pl.pallas_call(finish_kernel, in_specs=[fast, fast, anywhere], out_specs=...  0.8 us
  transfers between devices with their start and end apart: 3, of which 0 were waited for; matrix products, arithmetic and copies ran while one was open for 0% of the time, Pallas kernels for 9%

profile of v24, /device:TPU:0, one launch (start us, length us, event | category | flops | bytes accessed | tf_op | source)
XLA Modules:
  0.0 32.8 jit_solution(10546880919049326589)
XLA Ops:
  0.6 0.9 %pack.1 = (bf16[3,4,4096]{2,1,0:T(4,128)(2,1)S(1)}, bf16[2,4,4096]{2,1,0:T(4,128)(2,1)S(1)}, bf16[2,4,4096]{2,1,0:T(4,128)(2,1)S(1)}) custom-call(bf16[1,1,4,4,4096]{4,3,2,1,0:T(4,128)(2,1)} %slab_hbm.1), custom_call_target="tpu_custom_call" | custom-call | tf_op jit(solution)/shard_map/pack/pallas_call | solution.py:320
  1.5 0.7 %collective-permute-start = (bf16[3,4,4096]{2,1,0:T(4,128)(2,1)S(1)}, bf16[3,4,4096]{2,1,0:T(4,128)(2,1)S(1)}, u32[]{:S(2)}, u32[]{:S(2)}) collective-permute-start(bf16[3,4,4096]{2,1,0:T(4,128)(2,1)S(1)} %get-tuple-element.18), channel_id=1, source_target_pairs={{4,8},{8,4},{12,16},{16,12},{20,24},{24,20},{5,9},{9,5},{13,17},{1... | collective-permute-start | bytes 294920 | tf_op jit(solution)/shard_map/ppermute | solution.py:329
  2.2 4.4 %collective-permute-start.1 = (bf16[2,4,4096]{2,1,0:T(4,128)(2,1)S(1)}, bf16[2,4,4096]{2,1,0:T(4,128)(2,1)S(1)}, u32[]{:S(2)}, u32[]{:S(2)}) collective-permute-start(bf16[2,4,4096]{2,1,0:T(4,128)(2,1)S(1)} %get-tuple-element.23.own_low_ref), channel_id=1, source_target_pairs={{0,4},{4,0},{8,12},{12,8},{16,20},{20,16},{24,28},{28,24},{1,5},{5... | collective-permute-start | bytes 196616 | tf_op jit(solution)/shard_map/ppermute | solution.py:331
  6.6 0.1 collective-permute-start.2
  6.7 1.6 %prepare.1 = (bf16[2,64,288]{2,1,0:T(8,128)(2,1)S(1)}, bf16[2,64,144]{2,1,0:T(8,128)(2,1)S(1)}, bf16[2,192,384]{2,1,0:T(8,128)(2,1)S(1)}, bf16[512,512]{1,0:T(8,128)(2,1)S(1)}, bf16[1024,128]{1,0:T(8,128)(2,1)S(1)}) custom-call(bf16[27,4,32]{2,1,0:T(4,128)(2,1)} %bitcast.10, bf16[2,108,2048]{2,1,0:T(8,128)(2,1)} %constant.8.clone.place_hbm, ...), custom_call_target="tpu_custom_call" | custom-call | flops 1000000000 | bytes 4194304 | tf_op jit(solution)/shard_map/prepare/pallas_call | solution.py:336
  8.3 0.0 collective-permute-done.1.low_ref
  8.3 0.0 collective-permute-done.2.high_ref
  8.3 1.4 %near.1 = (f32[64,1024]{1,0:T(8,128)S(1)}, bf16[192,1024]{1,0:T(8,128)(2,1)S(1)}, f32[1024,128]{1,0:T(8,128)S(1)}) custom-call(bf16[2,4,4096]{2,1,0:T(4,128)(2,1)S(1)} %get-tuple-element.23.own_low_ref, bf16[2,4,4096]{2,1,0:T(4,128)(2,1)S(1)} %get-tuple-element.24.own_high_ref, bf16[2,4,4096]{2,1,0:T(4,128)(2,1)S(1)} %collective-permute-done.1.low_ref, ...), custom_call_target="tpu_custom_call" | custom-call | tf_op jit(solution)/shard_map/near/pallas_call | solution.py:356
  9.7 0.0 collective-permute-done.across_ref
  9.7 2.7 %far.1 = (bf16[1,1,64,2048]{3,2,1,0:T(8,128)(2,1)}, bf16[64,896]{1,0:T(8,128)(2,1)S(1)}, f32[1024,128]{1,0:T(8,128)S(1)}) custom-call(bf16[3,4,4096]{2,1,0:T(4,128)(2,1)S(1)} %collective-permute-done.across_ref, bf16[512,512]{1,0:T(8,128)(2,1)S(1)} %get-tuple-element.19.select_ref, bf16[2,64,144]{2,1,0:T(8,128)(2,1)S(1)} %get-tuple-element.20.w1_ref, ...), custom_call_target="tpu_custom_call" | custom-call | tf_op jit(solution)/shard_map/far/pallas_call | solution.py:372
  12.4 10.5 %all_to_all.14 = bf16[8,8,896]{2,1,0:T(8,128)(2,1)S(1)} all-to-all(bf16[8,8,896]{2,1,0:T(8,128)(2,1)S(1)} %bitcast.7), channel_id=1, replica_groups=mesh['chip'=4,'core'=2,'narrow'=4] {'narrow','core'}, dimensions={0} | all-to-all | bytes 229376 | tf_op jit(solution)/shard_map/all_to_all | solution.py:393
  22.9 9.1 %all_to_all.15 = bf16[8,8,896]{2,1,0:T(8,128)(2,1)S(1)} all-to-all(bf16[8,8,896]{2,1,0:T(8,128)(2,1)S(1)} %broadcast_in_dim.2), channel_id=1, replica_groups=mesh['chip'=4,'core'=2,'narrow'=4] {'chip','core'}, dimensions={0} | all-to-all | bytes 229376 | tf_op jit(solution)/shard_map/all_to_all | solution.py:395
  32.0 0.8 %finish.1 = (f32[27,16,32]{2,1,0:T(8,128)}, bf16[1,1,64,2048]{3,2,1,0:T(8,128)(2,1)}) custom-call(f32[16,896]{1,0:T(8,128)S(1)} %convert_reduce_fusion.total_ref, f32[1024,128]{1,0:T(8,128)S(1)} %get-tuple-element.30.pre_ref, bf16[1,1,64,2048]{3,2,1,0:T(8,128)(2,1)} %get-tuple-element.31.begun_hbm), custom_call_target="tpu_custom_call", output_to_operand_aliasing={{1}: (2, {})} | custom-call | tf_op jit(solution)/shard_map/finish/pallas_call | solution.py:398
  (3 shorter events, 0.1 us)
Async XLA Ops:
  1.5 8.2 %collective-permute-start = (bf16[3,4,4096]{2,1,0:T(4,128)(2,1)S(1)}, bf16[3,4,4096]{2,1,0:T(4,128)(2,1)S(1)}, u32[]{:S(2)}, u32[]{:S(2)}) collective-permute-start(bf16[3,4,4096]{2,1,0:T(4,128)(2,1)S(1)} %get-tuple-element.18), channel_id=1, source_target_pairs={{4,8},{8,4},{12,16},{16,12},{20,24},{24,20},{5,9},{9,5},{13,17},{1... | collective-permute-start | bytes 294920 | tf_op jit(solution)/shard_map/ppermute | solution.py:329
  2.2 6.1 %collective-permute-start.1 = (bf16[2,4,4096]{2,1,0:T(4,128)(2,1)S(1)}, bf16[2,4,4096]{2,1,0:T(4,128)(2,1)S(1)}, u32[]{:S(2)}, u32[]{:S(2)}) collective-permute-start(bf16[2,4,4096]{2,1,0:T(4,128)(2,1)S(1)} %get-tuple-element.23.own_low_ref), channel_id=1, source_target_pairs={{0,4},{4,0},{8,12},{12,8},{16,20},{20,16},{24,28},{28,24},{1,5},{5... | collective-permute-start | bytes 196616 | tf_op jit(solution)/shard_map/ppermute | solution.py:331
  6.6 1.7 %collective-permute-start.2 = (bf16[2,4,4096]{2,1,0:T(4,128)(2,1)S(1)}, bf16[2,4,4096]{2,1,0:T(4,128)(2,1)S(1)}, u32[]{:S(2)}, u32[]{:S(2)}) collective-permute-start(bf16[2,4,4096]{2,1,0:T(4,128)(2,1)S(1)} %get-tuple-element.24.own_high_ref), channel_id=1, source_target_pairs={{0,4},{4,0},{8,12},{12,8},{16,20},{20,16},{24,28},{28,24},{1,5},{5... | collective-permute-start | bytes 196616 | tf_op jit(solution)/shard_map/ppermute | solution.py:331

commit v25 on v24

--- a/solution.py
+++ b/solution.py
@@ -127,15 +127,14 @@
     act_ref[:, LANES + PLANE :] = margin
 
 
-def pack_kernel(slab_hbm, across_ref, low_ref, high_ref, rows_ref, sems):
+def pack_kernel(slab_hbm, across_ref, slab_ref, rows_ref, sems):
     odd = lax.axis_index("core")
-    places = [(ref, k) for ref in (low_ref, high_ref) for k in range(CIN // 2)]
-    copies = [pltpu.make_async_copy(slab_hbm.at[0, 0, i], ref.at[k], sems.at[i]) for i, (ref, k) in enumerate(places)]
+    copies = [pltpu.make_async_copy(slab_hbm.at[0, 0, i], slab_ref.at[i], sems.at[i]) for i in range(CIN)]
     for copy in copies:
         copy.start()
-    for i, (ref, k) in enumerate(places):
+    for i in range(CIN):
         copies[i].wait()
-        planes = ref[k].astype(jnp.float32)
+        planes = slab_ref[i].astype(jnp.float32)
         for j in range(CELLS // LANES):
             begin = j * ROWS + PLANES * i
             rows_ref[begin : begin + PLANES, :] = planes[:, j * LANES : (j + 1) * LANES]
@@ -190,12 +189,11 @@
 
 
 def near_kernel(
-    own_low_ref, own_high_ref, low_ref, high_ref, select_ref, w1_ref, w2_ref, first_ref, columns_ref, pre_ref,
+    own_ref, within_ref, select_ref, w1_ref, w2_ref, first_ref, columns_ref, pre_ref,
     parity_ref, taps_ref, act_ref, turned_ref, rowed_ref,
 ):
     odd = lax.axis_index("core")
-    slabs = (own_low_ref, own_high_ref, low_ref, high_ref)
-    rows = jnp.concatenate([ref[k] for ref in slabs for k in range(CIN // 2)], axis=0)
+    rows = jnp.concatenate([ref[i] for ref in (own_ref, within_ref) for i in range(CIN)], axis=0)
     strided_taps(rows, select_ref, parity_ref, taps_ref)
     clear_margins(act_ref)
     for n in range(4):
@@ -316,19 +314,17 @@
     fast = pl.BlockSpec(memory_space=pltpu.VMEM)
     bf16 = functools.partial(jax.ShapeDtypeStruct, dtype=jnp.bfloat16)
     f32 = functools.partial(jax.ShapeDtypeStruct, dtype=jnp.float32)
-    halves = bf16((CIN // 2, PLANES, CELLS))
-    across, low, high = pl.pallas_call(
+    across, slab = pl.pallas_call(
         pack_kernel,
         in_specs=[pinned],
-        out_specs=(fast,) * 3,
-        out_shape=(bf16((3, CIN, CELLS)), halves, halves),
+        out_specs=(fast,) * 2,
+        out_shape=(bf16((3, CIN, CELLS)), bf16((CIN, PLANES, CELLS))),
         scratch_shapes=[pltpu.VMEM((CELLS // LANES * ROWS, LANES), jnp.float32), pltpu.SemaphoreType.DMA((CIN,))],
         compiler_params=pltpu.CompilerParams(vmem_limit_bytes=8 * MIB),
         name="pack",
     )(pltpu.with_memory_space_constraint(volumes, pltpu.HBM))
     across = lax.ppermute(across, WIDE, [p for k in range(1, wide - 1, 2) for p in ((k, k + 1), (k + 1, k))])
-    pairs = [p for k in range(0, wide - 1, 2) for p in ((k, k + 1), (k + 1, k))]
-    within = [lax.ppermute(half, WIDE, pairs) for half in (low, high)]
+    within = lax.ppermute(slab, WIDE, [p for k in range(0, wide - 1, 2) for p in ((k, k + 1), (k + 1, k))])
     stored = (
         first_kernel.transpose(0, 2, 1), jnp.asarray(placement(), jnp.bfloat16), second_kernel.transpose(0, 2, 1),
         jnp.asarray(selection(), jnp.bfloat16), cotangent,
@@ -355,7 +351,7 @@
     )(*(pltpu.with_memory_space_constraint(x, pltpu.HBM) for x in stored))
     first, near, pre = pl.pallas_call(
         near_kernel,
-        in_specs=[fast] * 7,
+        in_specs=[fast] * 5,
         out_specs=(fast,) * 3,
         out_shape=(f32((2 * C1, PLANE)), bf16((6 * C1, PLANE)), f32((PLANE, 2 * C2))),
         scratch_shapes=[
@@ -367,7 +363,7 @@
         ],
         compiler_params=pltpu.CompilerParams(vmem_limit_bytes=16 * MIB),
         name="near",
-    )(low, high, *within, select, w1_near, w2)
+    )(slab, within, select, w1_near, w2)
     rows = C2 // narrow
     begun, term, pre = pl.pallas_call(
         functools.partial(far_kernel, wide // 2, scale),

time: 33.1 us -> 32.9 us (level)
  starting transfers between devices: 5.11 us -> 1.17 us
  blocking collectives: 19.5 us -> 23.2 us
    all_to_all x1, blocking collectives: 10.5 us -> 14.5 us  [body(): received = lax.all_to_all(term, ('narrow', 'core'), 0, 0, tiled=True)]
    ppermute x2 -> x1, starting transfers between devices: 4.44 us -> 0.52 us  [body(): lax.ppermute(slab, WIDE, [p for k in range(0, wide - 1, 2) for p in ((k,...]
  transfers between devices with their start and end apart: 3 -> 2, of which waited for: 0 -> 0; matrix products, arithmetic and copies ran while one was open for 0% -> 0% of each run, Pallas kernels for 9% -> 9%
where the time goes in v25:
time: 32.9 us; the launch traced here: 32.6 us
  blocking collectives  23.2 us (71%)
  Pallas kernels  7.42 us (23%)
  starting transfers between devices  1.17 us (4%)
  between operations  0.69 us (2%)
    all_to_all x1, blocking collectives, body(): received = lax.all_to_all(term, ('narrow', 'core'), 0, 0, tiled=True)  14.5 us
    all_to_all x1, blocking collectives, body(): lax.all_to_all(jnp.broadcast_to(owned[None], (wide, half, PACKED)), WIDE,...  8.76 us
    pallas_call x1, Pallas kernels, body(): pl.pallas_call(functools.partial(far_kernel, wide // 2, scale), in_specs=...  2.69 us
    pallas_call x1, Pallas kernels, body(): pl.pallas_call(prepare_kernel, in_specs=[pinned] * 5, out_specs=(fast,) *...  1.63 us
    pallas_call x1, Pallas kernels, body(): pl.pallas_call(near_kernel, in_specs=[fast] * 5, out_specs=(fast,) * 3, o...  1.39 us
    pallas_call x1, Pallas kernels, body(): pl.pallas_call(pack_kernel, in_specs=[pinned], out_specs=(fast,) * 2, out...  0.91 us
    pallas_call x1, Pallas kernels, body(): pl.pallas_call(finish_kernel, in_specs=[fast, fast, anywhere], out_specs=...  0.8 us
  transfers between devices with their start and end apart: 2, of which 0 were waited for; matrix products, arithmetic and copies ran while one was open for 0% of the time, Pallas kernels for 9%

profile of v25, /device:TPU:0, one launch (start us, length us, event | category | flops | bytes accessed | tf_op | source)
XLA Modules:
  0.0 32.6 jit_solution(833720680216256031)
XLA Ops:
  0.6 0.9 %pack.1 = (bf16[3,4,4096]{2,1,0:T(4,128)(2,1)S(1)}, bf16[4,4,4096]{2,1,0:T(4,128)(2,1)S(1)}) custom-call(bf16[1,1,4,4,4096]{4,3,2,1,0:T(4,128)(2,1)} %slab_hbm.1), custom_call_target="tpu_custom_call" | custom-call | tf_op jit(solution)/shard_map/pack/pallas_call | solution.py:317
  1.5 0.5 %collective-permute-start.1 = (bf16[4,4,4096]{2,1,0:T(4,128)(2,1)S(1)}, bf16[4,4,4096]{2,1,0:T(4,128)(2,1)S(1)}, u32[]{:S(2)}, u32[]{:S(2)}) collective-permute-start(bf16[4,4,4096]{2,1,0:T(4,128)(2,1)S(1)} %get-tuple-element.22.own_ref), channel_id=1, source_target_pairs={{0,4},{4,0},{8,12},{12,8},{16,20},{20,16},{24,28},{28,24},{1,5},{5... | collective-permute-start | bytes 393224 | tf_op jit(solution)/shard_map/ppermute | solution.py:327
  2.1 0.7 %collective-permute-start = (bf16[3,4,4096]{2,1,0:T(4,128)(2,1)S(1)}, bf16[3,4,4096]{2,1,0:T(4,128)(2,1)S(1)}, u32[]{:S(2)}, u32[]{:S(2)}) collective-permute-start(bf16[3,4,4096]{2,1,0:T(4,128)(2,1)S(1)} %get-tuple-element.17), channel_id=1, source_target_pairs={{4,8},{8,4},{12,16},{16,12},{20,24},{24,20},{5,9},{9,5},{13,17},{1... | collective-permute-start | bytes 294920 | tf_op jit(solution)/shard_map/ppermute | solution.py:326
  2.7 1.6 %prepare.1 = (bf16[2,64,288]{2,1,0:T(8,128)(2,1)S(1)}, bf16[2,64,144]{2,1,0:T(8,128)(2,1)S(1)}, bf16[2,192,384]{2,1,0:T(8,128)(2,1)S(1)}, bf16[512,512]{1,0:T(8,128)(2,1)S(1)}, bf16[1024,128]{1,0:T(8,128)(2,1)S(1)}) custom-call(bf16[27,4,32]{2,1,0:T(4,128)(2,1)} %bitcast.10, bf16[2,108,2048]{2,1,0:T(8,128)(2,1)} %constant.8.clone.place_hbm, ...), custom_call_target="tpu_custom_call" | custom-call | flops 1000000000 | bytes 4194304 | tf_op jit(solution)/shard_map/prepare/pallas_call | solution.py:332
  4.4 0.0 collective-permute-done.1.within_ref
  4.4 1.4 %near.1 = (f32[64,1024]{1,0:T(8,128)S(1)}, bf16[192,1024]{1,0:T(8,128)(2,1)S(1)}, f32[1024,128]{1,0:T(8,128)S(1)}) custom-call(bf16[4,4,4096]{2,1,0:T(4,128)(2,1)S(1)} %get-tuple-element.22.own_ref, bf16[4,4,4096]{2,1,0:T(4,128)(2,1)S(1)} %collective-permute-done.1.within_ref, bf16[512,512]{1,0:T(8,128)(2,1)S(1)} %get-tuple-element.18.select_ref, ...), custom_call_target="tpu_custom_call" | custom-call | tf_op jit(solution)/shard_map/near/pallas_call | solution.py:352
  5.8 0.0 collective-permute-done.across_ref
  5.8 2.7 %far.1 = (bf16[1,1,64,2048]{3,2,1,0:T(8,128)(2,1)}, bf16[64,896]{1,0:T(8,128)(2,1)S(1)}, f32[1024,128]{1,0:T(8,128)S(1)}) custom-call(bf16[3,4,4096]{2,1,0:T(4,128)(2,1)S(1)} %collective-permute-done.across_ref, bf16[512,512]{1,0:T(8,128)(2,1)S(1)} %get-tuple-element.18.select_ref, bf16[2,64,144]{2,1,0:T(8,128)(2,1)S(1)} %get-tuple-element.19.w1_ref, ...), custom_call_target="tpu_custom_call" | custom-call | tf_op jit(solution)/shard_map/far/pallas_call | solution.py:368
  8.5 14.5 %all_to_all.14 = bf16[8,8,896]{2,1,0:T(8,128)(2,1)S(1)} all-to-all(bf16[8,8,896]{2,1,0:T(8,128)(2,1)S(1)} %bitcast.7), channel_id=1, replica_groups=mesh['chip'=4,'core'=2,'narrow'=4] {'narrow','core'}, dimensions={0} | all-to-all | bytes 229376 | tf_op jit(solution)/shard_map/all_to_all | solution.py:389
  23.0 8.8 %all_to_all.15 = bf16[8,8,896]{2,1,0:T(8,128)(2,1)S(1)} all-to-all(bf16[8,8,896]{2,1,0:T(8,128)(2,1)S(1)} %broadcast_in_dim.2), channel_id=1, replica_groups=mesh['chip'=4,'core'=2,'narrow'=4] {'chip','core'}, dimensions={0} | all-to-all | bytes 229376 | tf_op jit(solution)/shard_map/all_to_all | solution.py:391
  31.8 0.8 %finish.1 = (f32[27,16,32]{2,1,0:T(8,128)}, bf16[1,1,64,2048]{3,2,1,0:T(8,128)(2,1)}) custom-call(f32[16,896]{1,0:T(8,128)S(1)} %convert_reduce_fusion.total_ref, f32[1024,128]{1,0:T(8,128)S(1)} %get-tuple-element.28.pre_ref, bf16[1,1,64,2048]{3,2,1,0:T(8,128)(2,1)} %get-tuple-element.29.begun_hbm), custom_call_target="tpu_custom_call", output_to_operand_aliasing={{1}: (2, {})} | custom-call | tf_op jit(solution)/shard_map/finish/pallas_call | solution.py:394
  (3 shorter events, 0.1 us)
Async XLA Ops:
  1.5 2.8 %collective-permute-start.1 = (bf16[4,4,4096]{2,1,0:T(4,128)(2,1)S(1)}, bf16[4,4,4096]{2,1,0:T(4,128)(2,1)S(1)}, u32[]{:S(2)}, u32[]{:S(2)}) collective-permute-start(bf16[4,4,4096]{2,1,0:T(4,128)(2,1)S(1)} %get-tuple-element.22.own_ref), channel_id=1, source_target_pairs={{0,4},{4,0},{8,12},{12,8},{16,20},{20,16},{24,28},{28,24},{1,5},{5... | collective-permute-start | bytes 393224 | tf_op jit(solution)/shard_map/ppermute | solution.py:327
  2.1 3.7 %collective-permute-start = (bf16[3,4,4096]{2,1,0:T(4,128)(2,1)S(1)}, bf16[3,4,4096]{2,1,0:T(4,128)(2,1)S(1)}, u32[]{:S(2)}, u32[]{:S(2)}) collective-permute-start(bf16[3,4,4096]{2,1,0:T(4,128)(2,1)S(1)} %get-tuple-element.17), channel_id=1, source_target_pairs={{4,8},{8,4},{12,16},{16,12},{20,24},{24,20},{5,9},{9,5},{13,17},{1... | collective-permute-start | bytes 294920 | tf_op jit(solution)/shard_map/ppermute | solution.py:326

commit v26 on v25

--- a/solution.py
+++ b/solution.py
@@ -129,19 +129,25 @@
 
 def pack_kernel(slab_hbm, across_ref, slab_ref, rows_ref, sems):
     odd = lax.axis_index("core")
-    copies = [pltpu.make_async_copy(slab_hbm.at[0, 0, i], slab_ref.at[i], sems.at[i]) for i in range(CIN)]
+    quarter = CELLS // 4
+    parts = [(i, slice(n * quarter, (n + 1) * quarter)) for n in range(4) for i in range(CIN)]
+    copies = [
+        pltpu.make_async_copy(slab_hbm.at[0, 0, i, :, cells], slab_ref.at[i, :, cells], sems.at[k])
+        for k, (i, cells) in enumerate(parts)
+    ]
     for copy in copies:
         copy.start()
-    for i in range(CIN):
-        copies[i].wait()
-        planes = slab_ref[i].astype(jnp.float32)
-        for j in range(CELLS // LANES):
-            begin = j * ROWS + PLANES * i
-            rows_ref[begin : begin + PLANES, :] = planes[:, j * LANES : (j + 1) * LANES]
-    for k in range(3):
-        for j in range(CELLS // LANES):
-            channels = rows_ref[pl.ds(j * ROWS + k + odd, CIN, stride=PLANES), :]
-            across_ref[k, :, j * LANES : (j + 1) * LANES] = channels.astype(jnp.bfloat16)
+    for n in range(4):
+        tiles = range(n * quarter // LANES, (n + 1) * quarter // LANES)
+        for i in range(CIN):
+            copies[CIN * n + i].wait()
+            for j in tiles:
+                begin = j * ROWS + PLANES * i
+                rows_ref[begin : begin + PLANES, :] = slab_ref[i, :, j * LANES : (j + 1) * LANES].astype(jnp.float32)
+        for k in range(3):
+            for j in tiles:
+                channels = rows_ref[pl.ds(j * ROWS + k + odd, CIN, stride=PLANES), :]
+                across_ref[k, :, j * LANES : (j + 1) * LANES] = channels.astype(jnp.bfloat16)
 
 
 def prepare_kernel(
@@ -319,7 +325,7 @@
         in_specs=[pinned],
         out_specs=(fast,) * 2,
         out_shape=(bf16((3, CIN, CELLS)), bf16((CIN, PLANES, CELLS))),
-        scratch_shapes=[pltpu.VMEM((CELLS // LANES * ROWS, LANES), jnp.float32), pltpu.SemaphoreType.DMA((CIN,))],
+        scratch_shapes=[pltpu.VMEM((CELLS // LANES * ROWS, LANES), jnp.float32), pltpu.SemaphoreType.DMA((4 * CIN,))],
         compiler_params=pltpu.CompilerParams(vmem_limit_bytes=8 * MIB),
         name="pack",
     )(pltpu.with_memory_space_constraint(volumes, pltpu.HBM))

time: 32.9 us -> 33 us (level)
  no operation moved by 1% of the time
where the time goes in v26:
time: 33 us; the launch traced here: 32.7 us
  blocking collectives  23.2 us (70%)
  Pallas kernels  7.55 us (23%)
  starting transfers between devices  1.17 us (4%)
  between operations  0.69 us (2%)
    all_to_all x1, blocking collectives, body(): received = lax.all_to_all(term, ('narrow', 'core'), 0, 0, tiled=True)  14.5 us
    all_to_all x1, blocking collectives, body(): lax.all_to_all(jnp.broadcast_to(owned[None], (wide, half, PACKED)), WIDE,...  8.75 us
    pallas_call x1, Pallas kernels, body(): pl.pallas_call(functools.partial(far_kernel, wide // 2, scale), in_specs=...  2.69 us
    pallas_call x1, Pallas kernels, body(): pl.pallas_call(prepare_kernel, in_specs=[pinned] * 5, out_specs=(fast,) *...  1.64 us
    pallas_call x1, Pallas kernels, body(): pl.pallas_call(near_kernel, in_specs=[fast] * 5, out_specs=(fast,) * 3, o...  1.39 us
    pallas_call x1, Pallas kernels, body(): pl.pallas_call(pack_kernel, in_specs=[pinned], out_specs=(fast,) * 2, out...  1.04 us
    pallas_call x1, Pallas kernels, body(): pl.pallas_call(finish_kernel, in_specs=[fast, fast, anywhere], out_specs=...  0.8 us
  transfers between devices with their start and end apart: 2, of which 0 were waited for; matrix products, arithmetic and copies ran while one was open for 0% of the time, Pallas kernels for 9%

profile of v26, /device:TPU:0, one launch (start us, length us, event | category | flops | bytes accessed | tf_op | source)
XLA Modules:
  0.0 32.7 jit_solution(4588395720917141993)
XLA Ops:
  0.6 1.0 %pack.1 = (bf16[3,4,4096]{2,1,0:T(4,128)(2,1)S(1)}, bf16[4,4,4096]{2,1,0:T(4,128)(2,1)S(1)}) custom-call(bf16[1,1,4,4,4096]{4,3,2,1,0:T(4,128)(2,1)} %slab_hbm.1), custom_call_target="tpu_custom_call" | custom-call | tf_op jit(solution)/shard_map/pack/pallas_call | solution.py:323
  1.7 0.5 %collective-permute-start.1 = (bf16[4,4,4096]{2,1,0:T(4,128)(2,1)S(1)}, bf16[4,4,4096]{2,1,0:T(4,128)(2,1)S(1)}, u32[]{:S(2)}, u32[]{:S(2)}) collective-permute-start(bf16[4,4,4096]{2,1,0:T(4,128)(2,1)S(1)} %get-tuple-element.22.own_ref), channel_id=1, source_target_pairs={{0,4},{4,0},{8,12},{12,8},{16,20},{20,16},{24,28},{28,24},{1,5},{5... | collective-permute-start | bytes 393224 | tf_op jit(solution)/shard_map/ppermute | solution.py:333
  2.2 0.7 %collective-permute-start = (bf16[3,4,4096]{2,1,0:T(4,128)(2,1)S(1)}, bf16[3,4,4096]{2,1,0:T(4,128)(2,1)S(1)}, u32[]{:S(2)}, u32[]{:S(2)}) collective-permute-start(bf16[3,4,4096]{2,1,0:T(4,128)(2,1)S(1)} %get-tuple-element.17), channel_id=1, source_target_pairs={{4,8},{8,4},{12,16},{16,12},{20,24},{24,20},{5,9},{9,5},{13,17},{1... | collective-permute-start | bytes 294920 | tf_op jit(solution)/shard_map/ppermute | solution.py:332
  2.9 1.6 %prepare.1 = (bf16[2,64,288]{2,1,0:T(8,128)(2,1)S(1)}, bf16[2,64,144]{2,1,0:T(8,128)(2,1)S(1)}, bf16[2,192,384]{2,1,0:T(8,128)(2,1)S(1)}, bf16[512,512]{1,0:T(8,128)(2,1)S(1)}, bf16[1024,128]{1,0:T(8,128)(2,1)S(1)}) custom-call(bf16[27,4,32]{2,1,0:T(4,128)(2,1)} %bitcast.10, bf16[2,108,2048]{2,1,0:T(8,128)(2,1)} %constant.8.clone.place_hbm, ...), custom_call_target="tpu_custom_call" | custom-call | flops 1000000000 | bytes 4194304 | tf_op jit(solution)/shard_map/prepare/pallas_call | solution.py:338
  4.5 0.0 collective-permute-done.1.within_ref
  4.5 1.4 %near.1 = (f32[64,1024]{1,0:T(8,128)S(1)}, bf16[192,1024]{1,0:T(8,128)(2,1)S(1)}, f32[1024,128]{1,0:T(8,128)S(1)}) custom-call(bf16[4,4,4096]{2,1,0:T(4,128)(2,1)S(1)} %get-tuple-element.22.own_ref, bf16[4,4,4096]{2,1,0:T(4,128)(2,1)S(1)} %collective-permute-done.1.within_ref, bf16[512,512]{1,0:T(8,128)(2,1)S(1)} %get-tuple-element.18.select_ref, ...), custom_call_target="tpu_custom_call" | custom-call | tf_op jit(solution)/shard_map/near/pallas_call | solution.py:358
  5.9 0.0 collective-permute-done.across_ref
  5.9 2.7 %far.1 = (bf16[1,1,64,2048]{3,2,1,0:T(8,128)(2,1)}, bf16[64,896]{1,0:T(8,128)(2,1)S(1)}, f32[1024,128]{1,0:T(8,128)S(1)}) custom-call(bf16[3,4,4096]{2,1,0:T(4,128)(2,1)S(1)} %collective-permute-done.across_ref, bf16[512,512]{1,0:T(8,128)(2,1)S(1)} %get-tuple-element.18.select_ref, bf16[2,64,144]{2,1,0:T(8,128)(2,1)S(1)} %get-tuple-element.19.w1_ref, ...), custom_call_target="tpu_custom_call" | custom-call | tf_op jit(solution)/shard_map/far/pallas_call | solution.py:374
  8.6 14.5 %all_to_all.14 = bf16[8,8,896]{2,1,0:T(8,128)(2,1)S(1)} all-to-all(bf16[8,8,896]{2,1,0:T(8,128)(2,1)S(1)} %bitcast.7), channel_id=1, replica_groups=mesh['chip'=4,'core'=2,'narrow'=4] {'narrow','core'}, dimensions={0} | all-to-all | bytes 229376 | tf_op jit(solution)/shard_map/all_to_all | solution.py:395
  23.1 8.7 %all_to_all.15 = bf16[8,8,896]{2,1,0:T(8,128)(2,1)S(1)} all-to-all(bf16[8,8,896]{2,1,0:T(8,128)(2,1)S(1)} %broadcast_in_dim.2), channel_id=1, replica_groups=mesh['chip'=4,'core'=2,'narrow'=4] {'chip','core'}, dimensions={0} | all-to-all | bytes 229376 | tf_op jit(solution)/shard_map/all_to_all | solution.py:397
  31.9 0.8 %finish.1 = (f32[27,16,32]{2,1,0:T(8,128)}, bf16[1,1,64,2048]{3,2,1,0:T(8,128)(2,1)}) custom-call(f32[16,896]{1,0:T(8,128)S(1)} %convert_reduce_fusion.total_ref, f32[1024,128]{1,0:T(8,128)S(1)} %get-tuple-element.28.pre_ref, bf16[1,1,64,2048]{3,2,1,0:T(8,128)(2,1)} %get-tuple-element.29.begun_hbm), custom_call_target="tpu_custom_call", output_to_operand_aliasing={{1}: (2, {})} | custom-call | tf_op jit(solution)/shard_map/finish/pallas_call | solution.py:400
  (3 shorter events, 0.1 us)
Async XLA Ops:
  1.7 2.8 %collective-permute-start.1 = (bf16[4,4,4096]{2,1,0:T(4,128)(2,1)S(1)}, bf16[4,4,4096]{2,1,0:T(4,128)(2,1)S(1)}, u32[]{:S(2)}, u32[]{:S(2)}) collective-permute-start(bf16[4,4,4096]{2,1,0:T(4,128)(2,1)S(1)} %get-tuple-element.22.own_ref), channel_id=1, source_target_pairs={{0,4},{4,0},{8,12},{12,8},{16,20},{20,16},{24,28},{28,24},{1,5},{5... | collective-permute-start | bytes 393224 | tf_op jit(solution)/shard_map/ppermute | solution.py:333
  2.2 3.7 %collective-permute-start = (bf16[3,4,4096]{2,1,0:T(4,128)(2,1)S(1)}, bf16[3,4,4096]{2,1,0:T(4,128)(2,1)S(1)}, u32[]{:S(2)}, u32[]{:S(2)}) collective-permute-start(bf16[3,4,4096]{2,1,0:T(4,128)(2,1)S(1)} %get-tuple-element.17), channel_id=1, source_target_pairs={{4,8},{8,4},{12,16},{16,12},{20,24},{24,20},{5,9},{9,5},{13,17},{1... | collective-permute-start | bytes 294920 | tf_op jit(solution)/shard_map/ppermute | solution.py:332

commit v27 on v21

--- a/solution.py
+++ b/solution.py
@@ -55,7 +55,7 @@
 
 
 def leaky_relu(value):
-    return jnp.where(value > 0, value, neg_slope * value)
+    return jnp.maximum(value, neg_slope * value)
 
 
 def plane_rows(volume_ref):
@@ -105,24 +105,19 @@
         columns_ref[c * 2 * C1 : (c + 1) * 2 * C1, :] = part
 
 
-def second_layer(w2, columns_ref, turned_ref, rowed_ref):
-    blank = jnp.zeros((HALF, LANES), jnp.float32)
-    for b in (0, 2):
-        rowed_ref[b, 0:HALF, :] = blank
-        rowed_ref[b, HALF + PLANE :, :] = blank
-    for n in range(4):
-        cells = slice(256 * n, 256 * n + 256)
-        turned_ref[cells, :] = columns_ref[:, cells].T
-    for n in range(4):
-        sums = jnp.dot(turned_ref[256 * n : 256 * n + 256, :], w2, preferred_element_type=jnp.float32)
-        for b in range(3):
-            rowed_ref[b, HALF + 256 * n : HALF + 256 * n + 256, :] = sums[:, b * LANES : (b + 1) * LANES]
-
-
-def row_sum(rowed_ref, n):
-    begins = [HALF * b + 256 * n for b in range(3)]
-    first, second, third = (rowed_ref[b, begin : begin + 256, :] for b, begin in enumerate(begins))
-    return first + second + third
+def turn_columns(columns_ref, turned_ref):
+    margin = jnp.zeros((HALF, 2 * LANES), jnp.bfloat16)
+    turned_ref[0:HALF, :] = margin
+    turned_ref[HALF + PLANE :, :] = margin
+    blank = jnp.zeros((2 * C1, 256), jnp.bfloat16)
+    for n in range(4):
+        channels = jnp.concatenate([columns_ref[:, 256 * n : 256 * n + 256], blank], axis=0)
+        turned_ref[HALF + 256 * n : HALF + 256 * n + 256, :] = channels.T
+
+
+def second_layer(w2, turned_ref, n):
+    views = [turned_ref[HALF * b + 256 * n : HALF * b + 256 * n + 256, :] for b in range(3)]
+    return jnp.dot(jnp.concatenate(views, axis=1), w2, preferred_element_type=jnp.float32)
 
 
 def clear_margins(act_ref):
@@ -157,8 +152,10 @@
 
     for pair in range(2):
         for b in range(3):
+            begin = 2 * LANES * b
             for c in range(3):
-                w2_ref[pair, c * 2 * C1 : (c + 1) * 2 * C1, b * LANES : (b + 1) * LANES] = stacked(3 * b + c, pair)
+                w2_ref[pair, begin + c * 2 * C1 : begin + (c + 1) * 2 * C1, :] = stacked(3 * b + c, pair)
+            w2_ref[pair, begin + 6 * C1 : begin + 2 * LANES, :] = jnp.zeros((2 * C1, LANES), jnp.bfloat16)
     copies[2].wait()
     spread = lax.dot_general(
         k1_rows_ref[...].astype(jnp.bfloat16), place_ref[...],
@@ -177,7 +174,7 @@
 
 def near_kernel(
     own_ref, within_ref, select_ref, w1_ref, w2_ref, first_ref, columns_ref, pre_ref,
-    parity_ref, taps_ref, act_ref, turned_ref, rowed_ref,
+    parity_ref, taps_ref, act_ref, turned_ref,
 ):
     odd = lax.axis_index("core")
     rows = jnp.concatenate([plane_rows(own_ref), plane_rows(within_ref)], axis=0)
@@ -189,9 +186,9 @@
         complete = jnp.dot(w1_ref[1 - odd], taps_ref[:, here], preferred_element_type=jnp.float32)
         act_ref[:, LANES + 256 * n : LANES + 256 * n + 256] = leaky_relu(complete).astype(jnp.bfloat16)
     shifted_columns(act_ref, columns_ref)
-    second_layer(w2_ref[1 - odd], columns_ref, turned_ref, rowed_ref)
-    for n in range(4):
-        pre_ref[256 * n : 256 * n + 256, :] = row_sum(rowed_ref, n)
+    turn_columns(columns_ref, turned_ref)
+    for n in range(4):
+        pre_ref[256 * n : 256 * n + 256, :] = second_layer(w2_ref[1 - odd], turned_ref, n)
 
 
 def emit_activations(pre_ref, out_ref, out_hbm, sem):
@@ -206,7 +203,7 @@
 
 def far_kernel(
     chips, scale, across_ref, select_ref, w1_ref, w2_ref, cot_ref, first_ref, near_ref, near_pre_ref, out_hbm, grad_ref, pre_ref,
-    parity_ref, taps_ref, act_ref, columns_ref, turned_ref, rowed_ref, back_ref, swapped_ref, out_ref, out_sem,
+    parity_ref, taps_ref, act_ref, columns_ref, turned_ref, back_ref, swapped_ref, out_ref, out_sem,
 ):
     odd = lax.axis_index("core")
     last = (lax.axis_index("chip") == chips - 1) & (odd == 1)
@@ -222,14 +219,14 @@
         act_ref[C1:, there] = (first_act[C1:] * inside).astype(jnp.bfloat16)
     columns_ref[1 - odd] = near_ref[...]
     shifted_columns(act_ref, columns_ref.at[odd])
-    second_layer(w2_ref[odd], columns_ref.at[odd], turned_ref, rowed_ref)
+    turn_columns(columns_ref.at[odd], turned_ref)
     margin = jnp.zeros((HALF, LANES), jnp.bfloat16)
     for ref in (back_ref, swapped_ref):
         ref[0:HALF, :] = margin
         ref[HALF + PLANE :, :] = margin
     for n in range(4):
         cells = slice(256 * n, 256 * n + 256)
-        pre = near_pre_ref[cells, :] + row_sum(rowed_ref, n)
+        pre = near_pre_ref[cells, :] + second_layer(w2_ref[odd], turned_ref, n)
         pre_ref[cells, :] = pre
         back = (cot_ref[cells, :].astype(jnp.float32) * jnp.where(pre > 0, 1.0, neg_slope)).astype(jnp.bfloat16)
         here = slice(HALF + 256 * n, HALF + 256 * n + 256)
@@ -311,7 +308,7 @@
         in_specs=[pinned] * 5,
         out_specs=(fast,) * 5,
         out_shape=(
-            bf16((2, 2 * C1, 18 * ROWS)), bf16((2, 2 * C1, 9 * ROWS)), bf16((2, 6 * C1, 6 * C2)),
+            bf16((2, 2 * C1, 18 * ROWS)), bf16((2, 2 * C1, 9 * ROWS)), bf16((2, 6 * LANES, 2 * C2)),
             bf16((CHUNK, CHUNK)), bf16((PLANE, 2 * C2)),
         ),
         scratch_shapes=[
@@ -335,8 +332,7 @@
             pltpu.VMEM((4, 2 * ROWS, LANES + PLANE), jnp.bfloat16),
             pltpu.VMEM((18 * ROWS, PLANE), jnp.bfloat16),
             pltpu.VMEM((2 * C1, PLANE + 2 * LANES), jnp.bfloat16),
-            pltpu.VMEM((PLANE, 6 * C1), jnp.bfloat16),
-            pltpu.VMEM((3, PLANE + 2 * HALF, LANES), jnp.float32),
+            pltpu.VMEM((PLANE + 2 * HALF, 2 * LANES), jnp.bfloat16),
         ],
         compiler_params=pltpu.CompilerParams(vmem_limit_bytes=16 * MIB),
         cost_estimate=pl.CostEstimate(flops=10**9, bytes_accessed=4 * MIB, transcendentals=0),
@@ -353,8 +349,7 @@
             pltpu.VMEM((9 * ROWS, PLANE), jnp.bfloat16),
             pltpu.VMEM((2 * C1, PLANE + 2 * LANES), jnp.bfloat16),
             pltpu.VMEM((2, 6 * C1, PLANE), jnp.bfloat16),
-            pltpu.VMEM((PLANE, 6 * C1), jnp.bfloat16),
-            pltpu.VMEM((3, PLANE + 2 * HALF, LANES), jnp.float32),
+            pltpu.VMEM((PLANE + 2 * HALF, 2 * LANES), jnp.bfloat16),
             pltpu.VMEM((PLANE + 2 * HALF, LANES), jnp.bfloat16),
             pltpu.VMEM((PLANE + 2 * HALF, LANES), jnp.bfloat16),
             pltpu.VMEM((1, 1, C2, cells_out), jnp.bfloat16),

time: 32.8 us -> 32.9 us (level)
  transfers between devices with their start and end apart: 2 -> 2, of which waited for: 0 -> 0; matrix products, arithmetic and copies ran while one was open for 0% -> 0% of each run, Pallas kernels for 9% -> 10%
where the time goes in v27:
time: 32.9 us; the launch traced here: 32.7 us
  blocking collectives  24 us (73%)
  Pallas kernels  6.76 us (21%)
  starting transfers between devices  1.17 us (4%)
  between operations  0.7 us (2%)
    all_to_all x1, blocking collectives, body(): received = lax.all_to_all(term, ('narrow', 'core'), 0, 0, tiled=True)  15.2 us
    all_to_all x1, blocking collectives, body(): lax.all_to_all(jnp.broadcast_to(owned[None], (wide, half, PACKED)), WIDE,...  8.76 us
    pallas_call x1, Pallas kernels, body(): pl.pallas_call(functools.partial(far_kernel, wide // 2, scale), in_specs=...  2.78 us
    pallas_call x1, Pallas kernels, body(): pl.pallas_call(prepare_kernel, in_specs=[pinned] * 5, out_specs=(fast,) *...  1.66 us
    pallas_call x1, Pallas kernels, body(): pl.pallas_call(near_kernel, in_specs=[fast] * 5, out_specs=(fast,) * 3, o...  1.52 us
    pallas_call x1, Pallas kernels, body(): pl.pallas_call(finish_kernel, in_specs=[fast, fast, anywhere], out_specs=...  0.8 us
  transfers between devices with their start and end apart: 2, of which 0 were waited for; matrix products, arithmetic and copies ran while one was open for 0% of the time, Pallas kernels for 10%

profile of v27, /device:TPU:0, one launch (start us, length us, event | category | flops | bytes accessed | tf_op | source)
XLA Modules:
  0.0 32.7 jit_solution(3453028751564234630)
XLA Ops:
  0.6 0.5 %collective-permute-start.1 = (bf16[1,1,4,4,4096]{4,3,2,1,0:T(4,128)(2,1)}, bf16[1,1,4,4,4096]{4,3,2,1,0:T(4,128)(2,1)S(1)}, u32[]{:S(2)}, u32[]{:S(2)}) collective-permute-start(bf16[1,1,4,4,4096]{4,3,2,1,0:T(4,128)(2,1)} %own_ref.1), channel_id=1, source_target_pairs={{0,4},{4,0},{8,12},{12,8},{16,20},{20,16},{24,28},{28,24},{1,5},{5... | collective-permute-start | bytes 393224 | tf_op jit(solution)/shard_map/ppermute | solution.py:297
  1.1 0.7 %collective-permute-start = (bf16[1,1,4,4,4096]{4,3,2,1,0:T(4,128)(2,1)}, bf16[1,1,4,4,4096]{4,3,2,1,0:T(4,128)(2,1)S(1)}, u32[]{:S(2)}, u32[]{:S(2)}) collective-permute-start(bf16[1,1,4,4,4096]{4,3,2,1,0:T(4,128)(2,1)} %own_ref.1), channel_id=1, source_target_pairs={{4,8},{8,4},{12,16},{16,12},{20,24},{24,20},{5,9},{9,5},{13,17},{1... | collective-permute-start | bytes 393224 | tf_op jit(solution)/shard_map/ppermute | solution.py:295
  1.8 0.0 copy-start
  1.8 1.7 %prepare.1 = (bf16[2,64,288]{2,1,0:T(8,128)(2,1)S(1)}, bf16[2,64,144]{2,1,0:T(8,128)(2,1)S(1)}, bf16[2,768,128]{2,1,0:T(8,128)(2,1)S(1)}, bf16[512,512]{1,0:T(8,128)(2,1)S(1)}, bf16[1024,128]{1,0:T(8,128)(2,1)S(1)}) custom-call(bf16[27,4,32]{2,1,0:T(4,128)(2,1)} %bitcast.10, bf16[2,108,2048]{2,1,0:T(8,128)(2,1)} %constant.8.clone.place_hbm, ...), custom_call_target="tpu_custom_call" | custom-call | flops 1000000000 | bytes 4194304 | tf_op jit(solution)/shard_map/prepare/pallas_call | solution.py:306
  3.5 0.0 collective-permute-done.1.within_ref
  3.5 0.0 copy-done
  3.5 1.5 %near.1 = (f32[64,1024]{1,0:T(8,128)S(1)}, bf16[192,1024]{1,0:T(8,128)(2,1)S(1)}, f32[1024,128]{1,0:T(8,128)S(1)}) custom-call(bf16[1,1,4,4,4096]{4,3,2,1,0:T(4,128)(2,1)S(1)} %copy-done, bf16[1,1,4,4,4096]{4,3,2,1,0:T(4,128)(2,1)S(1)} %collective-permute-done.1.within_ref, bf16[512,512]{1,0:T(8,128)(2,1)S(1)} %get-tuple-element.15.select_ref, ...), custom_call_target="tpu_custom_call" | custom-call | flops 1000000000 | bytes 4194304 | tf_op jit(solution)/shard_map/near/pallas_call | solution.py:326
  5.0 0.0 collective-permute-done.across_ref
  5.0 2.8 %far.1 = (bf16[1,1,64,2048]{3,2,1,0:T(8,128)(2,1)}, bf16[64,896]{1,0:T(8,128)(2,1)S(1)}, f32[1024,128]{1,0:T(8,128)S(1)}) custom-call(bf16[1,1,4,4,4096]{4,3,2,1,0:T(4,128)(2,1)S(1)} %collective-permute-done.across_ref, bf16[512,512]{1,0:T(8,128)(2,1)S(1)} %get-tuple-element.15.select_ref, bf16[2,64,144]{2,1,0:T(8,128)(2,1)S(1)} %get-tuple-element.16.w1_ref, ...), custom_call_target="tpu_custom_call" | custom-call | tf_op jit(solution)/shard_map/far/pallas_call | solution.py:342
  7.8 15.2 %all_to_all.14 = bf16[8,8,896]{2,1,0:T(8,128)(2,1)S(1)} all-to-all(bf16[8,8,896]{2,1,0:T(8,128)(2,1)S(1)} %bitcast.7), channel_id=1, replica_groups=mesh['chip'=4,'core'=2,'narrow'=4] {'narrow','core'}, dimensions={0} | all-to-all | bytes 229376 | tf_op jit(solution)/shard_map/all_to_all | solution.py:362
  23.1 8.8 %all_to_all.15 = bf16[8,8,896]{2,1,0:T(8,128)(2,1)S(1)} all-to-all(bf16[8,8,896]{2,1,0:T(8,128)(2,1)S(1)} %broadcast_in_dim.2), channel_id=1, replica_groups=mesh['chip'=4,'core'=2,'narrow'=4] {'chip','core'}, dimensions={0} | all-to-all | bytes 229376 | tf_op jit(solution)/shard_map/all_to_all | solution.py:364
  31.9 0.8 %finish.1 = (f32[27,16,32]{2,1,0:T(8,128)}, bf16[1,1,64,2048]{3,2,1,0:T(8,128)(2,1)}) custom-call(f32[16,896]{1,0:T(8,128)S(1)} %convert_reduce_fusion.total_ref, f32[1024,128]{1,0:T(8,128)S(1)} %get-tuple-element.24.pre_ref, bf16[1,1,64,2048]{3,2,1,0:T(8,128)(2,1)} %get-tuple-element.25.begun_hbm), custom_call_target="tpu_custom_call", output_to_operand_aliasing={{1}: (2, {})} | custom-call | tf_op jit(solution)/shard_map/finish/pallas_call | solution.py:367
  (3 shorter events, 0.1 us)
Async XLA Ops:
  0.6 2.9 %collective-permute-start.1 = (bf16[1,1,4,4,4096]{4,3,2,1,0:T(4,128)(2,1)}, bf16[1,1,4,4,4096]{4,3,2,1,0:T(4,128)(2,1)S(1)}, u32[]{:S(2)}, u32[]{:S(2)}) collective-permute-start(bf16[1,1,4,4,4096]{4,3,2,1,0:T(4,128)(2,1)} %own_ref.1), channel_id=1, source_target_pairs={{0,4},{4,0},{8,12},{12,8},{16,20},{20,16},{24,28},{28,24},{1,5},{5... | collective-permute-start | bytes 393224 | tf_op jit(solution)/shard_map/ppermute | solution.py:297
  1.1 3.9 %collective-permute-start = (bf16[1,1,4,4,4096]{4,3,2,1,0:T(4,128)(2,1)}, bf16[1,1,4,4,4096]{4,3,2,1,0:T(4,128)(2,1)S(1)}, u32[]{:S(2)}, u32[]{:S(2)}) collective-permute-start(bf16[1,1,4,4,4096]{4,3,2,1,0:T(4,128)(2,1)} %own_ref.1), channel_id=1, source_target_pairs={{4,8},{8,4},{12,16},{16,12},{20,24},{24,20},{5,9},{9,5},{13,17},{1... | collective-permute-start | bytes 393224 | tf_op jit(solution)/shard_map/ppermute | solution.py:295
  1.8 1.7 %copy-start = (bf16[1,1,4,4,4096]{4,3,2,1,0:T(4,128)(2,1)S(1)}, bf16[1,1,4,4,4096]{4,3,2,1,0:T(4,128)(2,1)}, u32[]{:S(2)}) copy-start(bf16[1,1,4,4,4096]{4,3,2,1,0:T(4,128)(2,1)} %own_ref.1) | copy-start | bytes 393220

commit v28 on v25

--- a/solution.py
+++ b/solution.py
@@ -55,7 +55,7 @@
 
 
 def leaky_relu(value):
-    return jnp.where(value > 0, value, neg_slope * value)
+    return jnp.maximum(value, neg_slope * value)
 
 
 def column_masks():

time: 32.9 us -> 32.9 us (level)
  no operation moved by 1% of the time
where the time goes in v28:
time: 32.9 us; the launch traced here: 32.6 us
  blocking collectives  23.2 us (71%)
  Pallas kernels  7.41 us (23%)
  starting transfers between devices  1.17 us (4%)
  between operations  0.69 us (2%)
    all_to_all x1, blocking collectives, body(): received = lax.all_to_all(term, ('narrow', 'core'), 0, 0, tiled=True)  14.5 us
    all_to_all x1, blocking collectives, body(): lax.all_to_all(jnp.broadcast_to(owned[None], (wide, half, PACKED)), WIDE,...  8.76 us
    pallas_call x1, Pallas kernels, body(): pl.pallas_call(functools.partial(far_kernel, wide // 2, scale), in_specs=...  2.67 us
    pallas_call x1, Pallas kernels, body(): pl.pallas_call(prepare_kernel, in_specs=[pinned] * 5, out_specs=(fast,) *...  1.63 us
    pallas_call x1, Pallas kernels, body(): pl.pallas_call(near_kernel, in_specs=[fast] * 5, out_specs=(fast,) * 3, o...  1.39 us
    pallas_call x1, Pallas kernels, body(): pl.pallas_call(pack_kernel, in_specs=[pinned], out_specs=(fast,) * 2, out...  0.91 us
    pallas_call x1, Pallas kernels, body(): pl.pallas_call(finish_kernel, in_specs=[fast, fast, anywhere], out_specs=...  0.8 us
  transfers between devices with their start and end apart: 2, of which 0 were waited for; matrix products, arithmetic and copies ran while one was open for 0% of the time, Pallas kernels for 9%

profile of v28, /device:TPU:0, one launch (start us, length us, event | category | flops | bytes accessed | tf_op | source)
XLA Modules:
  0.0 32.6 jit_solution(9770992202535481260)
XLA Ops:
  0.6 0.9 %pack.1 = (bf16[3,4,4096]{2,1,0:T(4,128)(2,1)S(1)}, bf16[4,4,4096]{2,1,0:T(4,128)(2,1)S(1)}) custom-call(bf16[1,1,4,4,4096]{4,3,2,1,0:T(4,128)(2,1)} %slab_hbm.1), custom_call_target="tpu_custom_call" | custom-call | tf_op jit(solution)/shard_map/pack/pallas_call | solution.py:317
  1.5 0.5 %collective-permute-start.1 = (bf16[4,4,4096]{2,1,0:T(4,128)(2,1)S(1)}, bf16[4,4,4096]{2,1,0:T(4,128)(2,1)S(1)}, u32[]{:S(2)}, u32[]{:S(2)}) collective-permute-start(bf16[4,4,4096]{2,1,0:T(4,128)(2,1)S(1)} %get-tuple-element.22.own_ref), channel_id=1, source_target_pairs={{0,4},{4,0},{8,12},{12,8},{16,20},{20,16},{24,28},{28,24},{1,5},{5... | collective-permute-start | bytes 393224 | tf_op jit(solution)/shard_map/ppermute | solution.py:327
  2.1 0.7 %collective-permute-start = (bf16[3,4,4096]{2,1,0:T(4,128)(2,1)S(1)}, bf16[3,4,4096]{2,1,0:T(4,128)(2,1)S(1)}, u32[]{:S(2)}, u32[]{:S(2)}) collective-permute-start(bf16[3,4,4096]{2,1,0:T(4,128)(2,1)S(1)} %get-tuple-element.17), channel_id=1, source_target_pairs={{4,8},{8,4},{12,16},{16,12},{20,24},{24,20},{5,9},{9,5},{13,17},{1... | collective-permute-start | bytes 294920 | tf_op jit(solution)/shard_map/ppermute | solution.py:326
  2.7 1.6 %prepare.1 = (bf16[2,64,288]{2,1,0:T(8,128)(2,1)S(1)}, bf16[2,64,144]{2,1,0:T(8,128)(2,1)S(1)}, bf16[2,192,384]{2,1,0:T(8,128)(2,1)S(1)}, bf16[512,512]{1,0:T(8,128)(2,1)S(1)}, bf16[1024,128]{1,0:T(8,128)(2,1)S(1)}) custom-call(bf16[27,4,32]{2,1,0:T(4,128)(2,1)} %bitcast.10, bf16[2,108,2048]{2,1,0:T(8,128)(2,1)} %constant.8.clone.place_hbm, ...), custom_call_target="tpu_custom_call" | custom-call | flops 1000000000 | bytes 4194304 | tf_op jit(solution)/shard_map/prepare/pallas_call | solution.py:332
  4.4 0.0 collective-permute-done.1.within_ref
  4.4 1.4 %near.1 = (f32[64,1024]{1,0:T(8,128)S(1)}, bf16[192,1024]{1,0:T(8,128)(2,1)S(1)}, f32[1024,128]{1,0:T(8,128)S(1)}) custom-call(bf16[4,4,4096]{2,1,0:T(4,128)(2,1)S(1)} %get-tuple-element.22.own_ref, bf16[4,4,4096]{2,1,0:T(4,128)(2,1)S(1)} %collective-permute-done.1.within_ref, bf16[512,512]{1,0:T(8,128)(2,1)S(1)} %get-tuple-element.18.select_ref, ...), custom_call_target="tpu_custom_call" | custom-call | tf_op jit(solution)/shard_map/near/pallas_call | solution.py:352
  5.8 0.0 collective-permute-done.across_ref
  5.8 2.7 %far.1 = (bf16[1,1,64,2048]{3,2,1,0:T(8,128)(2,1)}, bf16[64,896]{1,0:T(8,128)(2,1)S(1)}, f32[1024,128]{1,0:T(8,128)S(1)}) custom-call(bf16[3,4,4096]{2,1,0:T(4,128)(2,1)S(1)} %collective-permute-done.across_ref, bf16[512,512]{1,0:T(8,128)(2,1)S(1)} %get-tuple-element.18.select_ref, bf16[2,64,144]{2,1,0:T(8,128)(2,1)S(1)} %get-tuple-element.19.w1_ref, ...), custom_call_target="tpu_custom_call" | custom-call | tf_op jit(solution)/shard_map/far/pallas_call | solution.py:368
  8.5 14.5 %all_to_all.14 = bf16[8,8,896]{2,1,0:T(8,128)(2,1)S(1)} all-to-all(bf16[8,8,896]{2,1,0:T(8,128)(2,1)S(1)} %bitcast.7), channel_id=1, replica_groups=mesh['chip'=4,'core'=2,'narrow'=4] {'narrow','core'}, dimensions={0} | all-to-all | bytes 229376 | tf_op jit(solution)/shard_map/all_to_all | solution.py:389
  23.0 8.8 %all_to_all.15 = bf16[8,8,896]{2,1,0:T(8,128)(2,1)S(1)} all-to-all(bf16[8,8,896]{2,1,0:T(8,128)(2,1)S(1)} %broadcast_in_dim.2), channel_id=1, replica_groups=mesh['chip'=4,'core'=2,'narrow'=4] {'chip','core'}, dimensions={0} | all-to-all | bytes 229376 | tf_op jit(solution)/shard_map/all_to_all | solution.py:391
  31.8 0.8 %finish.1 = (f32[27,16,32]{2,1,0:T(8,128)}, bf16[1,1,64,2048]{3,2,1,0:T(8,128)(2,1)}) custom-call(f32[16,896]{1,0:T(8,128)S(1)} %convert_reduce_fusion.total_ref, f32[1024,128]{1,0:T(8,128)S(1)} %get-tuple-element.28.pre_ref, bf16[1,1,64,2048]{3,2,1,0:T(8,128)(2,1)} %get-tuple-element.29.begun_hbm), custom_call_target="tpu_custom_call", output_to_operand_aliasing={{1}: (2, {})} | custom-call | tf_op jit(solution)/shard_map/finish/pallas_call | solution.py:394
  (3 shorter events, 0.1 us)
Async XLA Ops:
  1.5 2.8 %collective-permute-start.1 = (bf16[4,4,4096]{2,1,0:T(4,128)(2,1)S(1)}, bf16[4,4,4096]{2,1,0:T(4,128)(2,1)S(1)}, u32[]{:S(2)}, u32[]{:S(2)}) collective-permute-start(bf16[4,4,4096]{2,1,0:T(4,128)(2,1)S(1)} %get-tuple-element.22.own_ref), channel_id=1, source_target_pairs={{0,4},{4,0},{8,12},{12,8},{16,20},{20,16},{24,28},{28,24},{1,5},{5... | collective-permute-start | bytes 393224 | tf_op jit(solution)/shard_map/ppermute | solution.py:327
  2.1 3.7 %collective-permute-start = (bf16[3,4,4096]{2,1,0:T(4,128)(2,1)S(1)}, bf16[3,4,4096]{2,1,0:T(4,128)(2,1)S(1)}, u32[]{:S(2)}, u32[]{:S(2)}) collective-permute-start(bf16[3,4,4096]{2,1,0:T(4,128)(2,1)S(1)} %get-tuple-element.17), channel_id=1, source_target_pairs={{4,8},{8,4},{12,16},{16,12},{20,24},{24,20},{5,9},{9,5},{13,17},{1... | collective-permute-start | bytes 294920 | tf_op jit(solution)/shard_map/ppermute | solution.py:326

commit v29 on v21

--- a/solution.py
+++ b/solution.py
@@ -55,7 +55,7 @@
 
 
 def leaky_relu(value):
-    return jnp.where(value > 0, value, neg_slope * value)
+    return jnp.maximum(value, neg_slope * value)
 
 
 def plane_rows(volume_ref):

time: 32.8 us -> 32.8 us (level)
  no operation moved by 1% of the time
where the time goes in v29:
time: 32.8 us; the launch traced here: 32.6 us
  blocking collectives  24.1 us (73%)
  Pallas kernels  6.53 us (20%)
  starting transfers between devices  1.17 us (4%)
  between operations  0.7 us (2%)
    all_to_all x1, blocking collectives, body(): received = lax.all_to_all(term, ('narrow', 'core'), 0, 0, tiled=True)  15.4 us
    all_to_all x1, blocking collectives, body(): lax.all_to_all(jnp.broadcast_to(owned[None], (wide, half, PACKED)), WIDE,...  8.76 us
    pallas_call x1, Pallas kernels, body(): pl.pallas_call(functools.partial(far_kernel, wide // 2, scale), in_specs=...  2.67 us
    pallas_call x1, Pallas kernels, body(): pl.pallas_call(prepare_kernel, in_specs=[pinned] * 5, out_specs=(fast,) *...  1.66 us
    pallas_call x1, Pallas kernels, body(): pl.pallas_call(near_kernel, in_specs=[fast] * 5, out_specs=(fast,) * 3, o...  1.39 us
    pallas_call x1, Pallas kernels, body(): pl.pallas_call(finish_kernel, in_specs=[fast, fast, anywhere], out_specs=...  0.8 us
    ppermute x1, starting transfers between devices, body(): lax.ppermute(volumes, WIDE, [p for k in range(1, wide - 1, 2) for p in ((...  0.66 us
  transfers between devices with their start and end apart: 2, of which 0 were waited for; matrix products, arithmetic and copies ran while one was open for 0% of the time, Pallas kernels for 9%

profile of v29, /device:TPU:0, one launch (start us, length us, event | category | flops | bytes accessed | tf_op | source)
XLA Modules:
  0.0 32.6 jit_solution(6830031270981671948)
XLA Ops:
  0.6 0.5 %collective-permute-start.1 = (bf16[1,1,4,4,4096]{4,3,2,1,0:T(4,128)(2,1)}, bf16[1,1,4,4,4096]{4,3,2,1,0:T(4,128)(2,1)S(1)}, u32[]{:S(2)}, u32[]{:S(2)}) collective-permute-start(bf16[1,1,4,4,4096]{4,3,2,1,0:T(4,128)(2,1)} %own_ref.1), channel_id=1, source_target_pairs={{0,4},{4,0},{8,12},{12,8},{16,20},{20,16},{24,28},{28,24},{1,5},{5... | collective-permute-start | bytes 393224 | tf_op jit(solution)/shard_map/ppermute | solution.py:300
  1.1 0.7 %collective-permute-start = (bf16[1,1,4,4,4096]{4,3,2,1,0:T(4,128)(2,1)}, bf16[1,1,4,4,4096]{4,3,2,1,0:T(4,128)(2,1)S(1)}, u32[]{:S(2)}, u32[]{:S(2)}) collective-permute-start(bf16[1,1,4,4,4096]{4,3,2,1,0:T(4,128)(2,1)} %own_ref.1), channel_id=1, source_target_pairs={{4,8},{8,4},{12,16},{16,12},{20,24},{24,20},{5,9},{9,5},{13,17},{1... | collective-permute-start | bytes 393224 | tf_op jit(solution)/shard_map/ppermute | solution.py:298
  1.8 0.0 copy-start
  1.8 1.7 %prepare.1 = (bf16[2,64,288]{2,1,0:T(8,128)(2,1)S(1)}, bf16[2,64,144]{2,1,0:T(8,128)(2,1)S(1)}, bf16[2,192,384]{2,1,0:T(8,128)(2,1)S(1)}, bf16[512,512]{1,0:T(8,128)(2,1)S(1)}, bf16[1024,128]{1,0:T(8,128)(2,1)S(1)}) custom-call(bf16[27,4,32]{2,1,0:T(4,128)(2,1)} %bitcast.10, bf16[2,108,2048]{2,1,0:T(8,128)(2,1)} %constant.8.clone.place_hbm, ...), custom_call_target="tpu_custom_call" | custom-call | flops 1000000000 | bytes 4194304 | tf_op jit(solution)/shard_map/prepare/pallas_call | solution.py:309
  3.5 0.0 collective-permute-done.1.within_ref
  3.5 0.0 copy-done
  3.5 1.4 %near.1 = (f32[64,1024]{1,0:T(8,128)S(1)}, bf16[192,1024]{1,0:T(8,128)(2,1)S(1)}, f32[1024,128]{1,0:T(8,128)S(1)}) custom-call(bf16[1,1,4,4,4096]{4,3,2,1,0:T(4,128)(2,1)S(1)} %copy-done, bf16[1,1,4,4,4096]{4,3,2,1,0:T(4,128)(2,1)S(1)} %collective-permute-done.1.within_ref, bf16[512,512]{1,0:T(8,128)(2,1)S(1)} %get-tuple-element.15.select_ref, ...), custom_call_target="tpu_custom_call" | custom-call | flops 1000000000 | bytes 4194304 | tf_op jit(solution)/shard_map/near/pallas_call | solution.py:329
  4.9 0.0 collective-permute-done.across_ref
  4.9 2.7 %far.1 = (bf16[1,1,64,2048]{3,2,1,0:T(8,128)(2,1)}, bf16[64,896]{1,0:T(8,128)(2,1)S(1)}, f32[1024,128]{1,0:T(8,128)S(1)}) custom-call(bf16[1,1,4,4,4096]{4,3,2,1,0:T(4,128)(2,1)S(1)} %collective-permute-done.across_ref, bf16[512,512]{1,0:T(8,128)(2,1)S(1)} %get-tuple-element.15.select_ref, bf16[2,64,144]{2,1,0:T(8,128)(2,1)S(1)} %get-tuple-element.16.w1_ref, ...), custom_call_target="tpu_custom_call" | custom-call | tf_op jit(solution)/shard_map/far/pallas_call | solution.py:346
  7.6 15.4 %all_to_all.14 = bf16[8,8,896]{2,1,0:T(8,128)(2,1)S(1)} all-to-all(bf16[8,8,896]{2,1,0:T(8,128)(2,1)S(1)} %bitcast.7), channel_id=1, replica_groups=mesh['chip'=4,'core'=2,'narrow'=4] {'narrow','core'}, dimensions={0} | all-to-all | bytes 229376 | tf_op jit(solution)/shard_map/all_to_all | solution.py:367
  23.0 8.8 %all_to_all.15 = bf16[8,8,896]{2,1,0:T(8,128)(2,1)S(1)} all-to-all(bf16[8,8,896]{2,1,0:T(8,128)(2,1)S(1)} %broadcast_in_dim.2), channel_id=1, replica_groups=mesh['chip'=4,'core'=2,'narrow'=4] {'chip','core'}, dimensions={0} | all-to-all | bytes 229376 | tf_op jit(solution)/shard_map/all_to_all | solution.py:369
  31.8 0.8 %finish.1 = (f32[27,16,32]{2,1,0:T(8,128)}, bf16[1,1,64,2048]{3,2,1,0:T(8,128)(2,1)}) custom-call(f32[16,896]{1,0:T(8,128)S(1)} %convert_reduce_fusion.total_ref, f32[1024,128]{1,0:T(8,128)S(1)} %get-tuple-element.24.pre_ref, bf16[1,1,64,2048]{3,2,1,0:T(8,128)(2,1)} %get-tuple-element.25.begun_hbm), custom_call_target="tpu_custom_call", output_to_operand_aliasing={{1}: (2, {})} | custom-call | tf_op jit(solution)/shard_map/finish/pallas_call | solution.py:372
  (3 shorter events, 0.1 us)
Async XLA Ops:
  0.6 2.9 %collective-permute-start.1 = (bf16[1,1,4,4,4096]{4,3,2,1,0:T(4,128)(2,1)}, bf16[1,1,4,4,4096]{4,3,2,1,0:T(4,128)(2,1)S(1)}, u32[]{:S(2)}, u32[]{:S(2)}) collective-permute-start(bf16[1,1,4,4,4096]{4,3,2,1,0:T(4,128)(2,1)} %own_ref.1), channel_id=1, source_target_pairs={{0,4},{4,0},{8,12},{12,8},{16,20},{20,16},{24,28},{28,24},{1,5},{5... | collective-permute-start | bytes 393224 | tf_op jit(solution)/shard_map/ppermute | solution.py:300
  1.1 3.8 %collective-permute-start = (bf16[1,1,4,4,4096]{4,3,2,1,0:T(4,128)(2,1)}, bf16[1,1,4,4,4096]{4,3,2,1,0:T(4,128)(2,1)S(1)}, u32[]{:S(2)}, u32[]{:S(2)}) collective-permute-start(bf16[1,1,4,4,4096]{4,3,2,1,0:T(4,128)(2,1)} %own_ref.1), channel_id=1, source_target_pairs={{4,8},{8,4},{12,16},{16,12},{20,24},{24,20},{5,9},{9,5},{13,17},{1... | collective-permute-start | bytes 393224 | tf_op jit(solution)/shard_map/ppermute | solution.py:298
  1.8 1.7 %copy-start = (bf16[1,1,4,4,4096]{4,3,2,1,0:T(4,128)(2,1)S(1)}, bf16[1,1,4,4,4096]{4,3,2,1,0:T(4,128)(2,1)}, u32[]{:S(2)}) copy-start(bf16[1,1,4,4,4096]{4,3,2,1,0:T(4,128)(2,1)} %own_ref.1) | copy-start | bytes 393220

commit v30 on v29

--- a/solution.py
+++ b/solution.py
@@ -205,7 +205,7 @@
 
 
 def far_kernel(
-    chips, scale, across_ref, select_ref, w1_ref, w2_ref, cot_ref, first_ref, near_ref, near_pre_ref, out_hbm, grad_ref, pre_ref,
+    chips, across_ref, select_ref, w1_ref, w2_ref, cot_ref, first_ref, near_ref, near_pre_ref, out_hbm, grad_ref, pre_ref,
     parity_ref, taps_ref, act_ref, columns_ref, turned_ref, rowed_ref, back_ref, swapped_ref, out_ref, out_sem,
 ):
     odd = lax.axis_index("core")
@@ -247,7 +247,7 @@
         return columns_ref[q // 2, begin : begin + C1, :]
 
     columns = [jnp.concatenate([plane_columns(a + z, c) for a in range(3) for c in range(3)], axis=0) for z in range(2)]
-    sums = scale * jnp.dot(
+    sums = jnp.dot(
         jnp.concatenate(columns, axis=1), jnp.concatenate(operands, axis=0), preferred_element_type=jnp.float32
     )
     left, right, ends = sums[0:256, 0:LANES], sums[0:256, LANES:], sums[256:]
@@ -344,7 +344,7 @@
     )(volumes, within, select, w1_near, w2)
     rows = C2 // narrow
     begun, term, pre = pl.pallas_call(
-        functools.partial(far_kernel, wide // 2, scale),
+        functools.partial(far_kernel, wide // 2),
         in_specs=[fast] * 8,
         out_specs=(pl.BlockSpec(memory_space=pl.ANY), fast, fast),
         out_shape=(bf16((1, 1, C2, cells_out)), bf16((C2, PACKED)), f32((PLANE, 2 * C2))),
@@ -367,7 +367,7 @@
     received = lax.all_to_all(term, ("narrow", "core"), 0, 0, tiled=True)
     owned = jnp.sum(received.reshape(2 * narrow, half, PACKED).astype(jnp.float32), axis=0).astype(jnp.bfloat16)
     parts = lax.all_to_all(jnp.broadcast_to(owned[None], (wide, half, PACKED)), WIDE, 0, 0, tiled=True)
-    total = jnp.sum(parts.reshape(wide // 2, rows, PACKED).astype(jnp.float32), axis=0)
+    total = scale * jnp.sum(parts.reshape(wide // 2, rows, PACKED).astype(jnp.float32), axis=0)
     anywhere = pl.BlockSpec(memory_space=pl.ANY)
     weight_grad, output = pl.pallas_call(
         finish_kernel,

time: 32.8 us -> 32.8 us (level)
  no operation moved by 1% of the time
where the time goes in v30:
time: 32.8 us; the launch traced here: 32.6 us
  blocking collectives  24.1 us (73%)
  Pallas kernels  6.52 us (20%)
  starting transfers between devices  1.17 us (4%)
  between operations  0.71 us (2%)
    all_to_all x1, blocking collectives, body(): received = lax.all_to_all(term, ('narrow', 'core'), 0, 0, tiled=True)  15.4 us
    all_to_all x1, blocking collectives, body(): lax.all_to_all(jnp.broadcast_to(owned[None], (wide, half, PACKED)), WIDE,...  8.76 us
    pallas_call x1, Pallas kernels, body(): pl.pallas_call(functools.partial(far_kernel, wide // 2), in_specs=[fast]...  2.67 us
    pallas_call x1, Pallas kernels, body(): pl.pallas_call(prepare_kernel, in_specs=[pinned] * 5, out_specs=(fast,) *...  1.66 us
    pallas_call x1, Pallas kernels, body(): pl.pallas_call(near_kernel, in_specs=[fast] * 5, out_specs=(fast,) * 3, o...  1.39 us
    pallas_call x1, Pallas kernels, body(): pl.pallas_call(finish_kernel, in_specs=[fast, fast, anywhere], out_specs=...  0.8 us
    ppermute x1, starting transfers between devices, body(): lax.ppermute(volumes, WIDE, [p for k in range(1, wide - 1, 2) for p in ((...  0.66 us
  transfers between devices with their start and end apart: 2, of which 0 were waited for; matrix products, arithmetic and copies ran while one was open for 0% of the time, Pallas kernels for 9%

profile of v30, /device:TPU:0, one launch (start us, length us, event | category | flops | bytes accessed | tf_op | source)
XLA Modules:
  0.0 32.6 jit_solution(15845777189551163832)
XLA Ops:
  0.6 0.5 %collective-permute-start.1 = (bf16[1,1,4,4,4096]{4,3,2,1,0:T(4,128)(2,1)}, bf16[1,1,4,4,4096]{4,3,2,1,0:T(4,128)(2,1)S(1)}, u32[]{:S(2)}, u32[]{:S(2)}) collective-permute-start(bf16[1,1,4,4,4096]{4,3,2,1,0:T(4,128)(2,1)} %own_ref.1), channel_id=1, source_target_pairs={{0,4},{4,0},{8,12},{12,8},{16,20},{20,16},{24,28},{28,24},{1,5},{5... | collective-permute-start | bytes 393224 | tf_op jit(solution)/shard_map/ppermute | solution.py:300
  1.1 0.7 %collective-permute-start = (bf16[1,1,4,4,4096]{4,3,2,1,0:T(4,128)(2,1)}, bf16[1,1,4,4,4096]{4,3,2,1,0:T(4,128)(2,1)S(1)}, u32[]{:S(2)}, u32[]{:S(2)}) collective-permute-start(bf16[1,1,4,4,4096]{4,3,2,1,0:T(4,128)(2,1)} %own_ref.1), channel_id=1, source_target_pairs={{4,8},{8,4},{12,16},{16,12},{20,24},{24,20},{5,9},{9,5},{13,17},{1... | collective-permute-start | bytes 393224 | tf_op jit(solution)/shard_map/ppermute | solution.py:298
  1.8 0.0 copy-start
  1.8 1.7 %prepare.1 = (bf16[2,64,288]{2,1,0:T(8,128)(2,1)S(1)}, bf16[2,64,144]{2,1,0:T(8,128)(2,1)S(1)}, bf16[2,192,384]{2,1,0:T(8,128)(2,1)S(1)}, bf16[512,512]{1,0:T(8,128)(2,1)S(1)}, bf16[1024,128]{1,0:T(8,128)(2,1)S(1)}) custom-call(bf16[27,4,32]{2,1,0:T(4,128)(2,1)} %bitcast.10, bf16[2,108,2048]{2,1,0:T(8,128)(2,1)} %constant.10.clone.place_hbm, ...), custom_call_target="tpu_custom_call" | custom-call | flops 1000000000 | bytes 4194304 | tf_op jit(solution)/shard_map/prepare/pallas_call | solution.py:309
  3.5 0.0 collective-permute-done.1.within_ref
  3.5 0.0 copy-done
  3.5 1.4 %near.1 = (f32[64,1024]{1,0:T(8,128)S(1)}, bf16[192,1024]{1,0:T(8,128)(2,1)S(1)}, f32[1024,128]{1,0:T(8,128)S(1)}) custom-call(bf16[1,1,4,4,4096]{4,3,2,1,0:T(4,128)(2,1)S(1)} %copy-done, bf16[1,1,4,4,4096]{4,3,2,1,0:T(4,128)(2,1)S(1)} %collective-permute-done.1.within_ref, bf16[512,512]{1,0:T(8,128)(2,1)S(1)} %get-tuple-element.15.select_ref, ...), custom_call_target="tpu_custom_call" | custom-call | flops 1000000000 | bytes 4194304 | tf_op jit(solution)/shard_map/near/pallas_call | solution.py:329
  4.9 0.0 collective-permute-done.across_ref
  4.9 2.7 %far.1 = (bf16[1,1,64,2048]{3,2,1,0:T(8,128)(2,1)}, bf16[64,896]{1,0:T(8,128)(2,1)S(1)}, f32[1024,128]{1,0:T(8,128)S(1)}) custom-call(bf16[1,1,4,4,4096]{4,3,2,1,0:T(4,128)(2,1)S(1)} %collective-permute-done.across_ref, bf16[512,512]{1,0:T(8,128)(2,1)S(1)} %get-tuple-element.15.select_ref, bf16[2,64,144]{2,1,0:T(8,128)(2,1)S(1)} %get-tuple-element.16.w1_ref, ...), custom_call_target="tpu_custom_call" | custom-call | tf_op jit(solution)/shard_map/far/pallas_call | solution.py:346
  7.6 15.4 %all_to_all.14 = bf16[8,8,896]{2,1,0:T(8,128)(2,1)S(1)} all-to-all(bf16[8,8,896]{2,1,0:T(8,128)(2,1)S(1)} %bitcast.7), channel_id=1, replica_groups=mesh['chip'=4,'core'=2,'narrow'=4] {'narrow','core'}, dimensions={0} | all-to-all | bytes 229376 | tf_op jit(solution)/shard_map/all_to_all | solution.py:367
  23.0 8.8 %all_to_all.15 = bf16[8,8,896]{2,1,0:T(8,128)(2,1)S(1)} all-to-all(bf16[8,8,896]{2,1,0:T(8,128)(2,1)S(1)} %broadcast_in_dim.2), channel_id=1, replica_groups=mesh['chip'=4,'core'=2,'narrow'=4] {'chip','core'}, dimensions={0} | all-to-all | bytes 229376 | tf_op jit(solution)/shard_map/all_to_all | solution.py:369
  31.8 0.8 %finish.1 = (f32[27,16,32]{2,1,0:T(8,128)}, bf16[1,1,64,2048]{3,2,1,0:T(8,128)(2,1)}) custom-call(f32[16,896]{1,0:T(8,128)S(1)} %broadcast_multiply_fusion.total_ref, f32[1024,128]{1,0:T(8,128)S(1)} %get-tuple-element.24.pre_ref, bf16[1,1,64,2048]{3,2,1,0:T(8,128)(2,1)} %get-tuple-element.25.begun_hbm), custom_call_target="tpu_custom_call", output_to_operand_aliasing={{1}: (2, {})} | custom-call | tf_op jit(solution)/shard_map/finish/pallas_call | solution.py:372
  (4 shorter events, 0.1 us)
Async XLA Ops:
  0.6 2.9 %collective-permute-start.1 = (bf16[1,1,4,4,4096]{4,3,2,1,0:T(4,128)(2,1)}, bf16[1,1,4,4,4096]{4,3,2,1,0:T(4,128)(2,1)S(1)}, u32[]{:S(2)}, u32[]{:S(2)}) collective-permute-start(bf16[1,1,4,4,4096]{4,3,2,1,0:T(4,128)(2,1)} %own_ref.1), channel_id=1, source_target_pairs={{0,4},{4,0},{8,12},{12,8},{16,20},{20,16},{24,28},{28,24},{1,5},{5... | collective-permute-start | bytes 393224 | tf_op jit(solution)/shard_map/ppermute | solution.py:300
  1.1 3.8 %collective-permute-start = (bf16[1,1,4,4,4096]{4,3,2,1,0:T(4,128)(2,1)}, bf16[1,1,4,4,4096]{4,3,2,1,0:T(4,128)(2,1)S(1)}, u32[]{:S(2)}, u32[]{:S(2)}) collective-permute-start(bf16[1,1,4,4,4096]{4,3,2,1,0:T(4,128)(2,1)} %own_ref.1), channel_id=1, source_target_pairs={{4,8},{8,4},{12,16},{16,12},{20,24},{24,20},{5,9},{9,5},{13,17},{1... | collective-permute-start | bytes 393224 | tf_op jit(solution)/shard_map/ppermute | solution.py:298
  1.8 1.7 %copy-start = (bf16[1,1,4,4,4096]{4,3,2,1,0:T(4,128)(2,1)S(1)}, bf16[1,1,4,4,4096]{4,3,2,1,0:T(4,128)(2,1)}, u32[]{:S(2)}) copy-start(bf16[1,1,4,4,4096]{4,3,2,1,0:T(4,128)(2,1)} %own_ref.1) | copy-start | bytes 393220
